TPU v7x, 32 devices: a whole 2x2x4 slice. The times are simulated.
32 devices in a mesh: req: 8 (over z, y), head: 4 (over x, core).
Axes of the slice: x: 2, y: 2, z: 4, core: 2. Of those that a mesh axis runs over, the one named last changes fastest.
Arguments:
- tokens: bfloat16 [64, 1024], P('req'), may hold values from -6 to 6
- lengths: int32 [64], P('req'), may hold values from 1 to 512, as said below
- slot_owner: int32 [64], P('req'), may hold values from 0 to 63, as said below
- positions: int32 [64], P('req'), may hold values from 0 to 8191
- variates: int32 [64], P('req'), may hold values from 0 to 7
- cache_variates: int32 [64, 512], P('req'), may hold values from 0 to 7
- kv_cache: bfloat16 [2, 2, 64, 512, 1024], P(None, None, 'req', None, 'head'), may hold values from -6 to 6
- attn_gain: float32 [2, 1024], replicated, may hold values from 0.1 to 1.9
- ffn_gain: float32 [2, 1024], replicated, may hold values from 0.1 to 1.9
- qkv_weight: bfloat16 [2, 1024, 3072], P(None, None, 'head'), may hold values from -0.1875 to 0.1875
- out_weight: bfloat16 [2, 1024, 1024], P(None, 'head'), may hold values from -0.1875 to 0.1875
- gate_up_weight: bfloat16 [2, 2, 1024, 4096], P(None, None, None, 'head'), may hold values from -0.1875 to 0.1875
- down_weight: bfloat16 [2, 4096, 1024], P(None, 'head'), may hold values from -0.09375 to 0.09375
- variate_bias: float32 [2, 2, 16], P(None, None, 'head'), may hold values from -2 to 300
Outputs:
- next_states: bfloat16 [64, 1024], P(('req', 'head'))
Inputs may be any that keep to these rules, and one draw needn't show every extreme that they name: `lengths`: live cache positions of each request; the largest is exactly 512 in every draw. `slot_owner`: each request is held in exactly one slot; taken in an order of non-increasing length, the requests fill slot t of every req index in turn t = 0, 1, ..., the req indices in rising order on even turns and in falling order on odd ones; no two slots of one req index hold requests of the same device of next_states (the same 2 consecutive requests).
All inputs are finite; a program needn't handle non-finite values.
Results may differ from a plain program's by a relative error of at most 0.02.
Values may be sent and summed in bfloat16 or wider, within the bound.
No kernel may reach another device: no remote copies, remote signals or barrier semaphores. Data moves between devices by JAX's collectives and lax.ppermute only.
A program may use at most 64 MiB of HBM per device.

v0:
```python
import jax
import jax.numpy as jnp
from jax import lax
from jax.sharding import PartitionSpec as P

HD = 64
LAYERS = 2


neg_fill = -1e30


def rms_scale(stream, gain_row):
    return stream * lax.rsqrt(jnp.mean(stream * stream, axis=-1, keepdims=True) + 1e-06) * gain_row


def rotary(vectors, time_ids):
    half_width = vectors.shape[-1] // 2
    frequency = 10000.0 ** (-2.0 * jnp.arange(half_width, dtype=jnp.float32) / vectors.shape[-1])
    angles = time_ids.astype(jnp.float32)[:, None, None] * frequency[None, None, :]
    cosine = jnp.cos(angles)
    sine_part = jnp.sin(angles)
    front_half = vectors[..., :half_width]
    back_half = vectors[..., half_width:]
    return jnp.concatenate(
        [front_half * cosine - back_half * sine_part, front_half * sine_part + back_half * cosine],
        axis=-1,
    )


def attend(
    queries,
    key_new,
    value_new,
    cached_keys,
    cached_values,
    cache_var,
    cache_lengths,
    variate_ids,
    same_bias,
    diff_bias,
):
    row_count, cache_len, width = cached_keys.shape
    local_heads = queries.shape[1]
    score_scale = HD ** (-0.5)
    diagonal_mask = jnp.eye(local_heads, dtype=jnp.bfloat16)
    q_block = (queries[:, :, :, None] * diagonal_mask[None, :, None, :]).reshape(
        row_count, local_heads * HD, local_heads
    )
    raw_scores = jnp.einsum(
        "rcf,rfh->rch", cached_keys, q_block, preferred_element_type=jnp.float32
    )
    score_bias = jnp.where(
        (cache_var == variate_ids[:, None])[:, :, None],
        same_bias[None, None, :],
        diff_bias[None, None, :],
    )
    scores = raw_scores * score_scale + score_bias
    live_mask = jnp.arange(cache_len, dtype=jnp.int32)[None, :] < cache_lengths[:, None]
    scores = jnp.where(live_mask[:, :, None], scores, neg_fill)
    self_score = (
        jnp.sum(queries.astype(jnp.float32) * key_new.astype(jnp.float32), axis=-1) * score_scale
        + same_bias[None, :]
    )
    row_top = jnp.maximum(jnp.max(scores, axis=1), self_score)
    weights = jnp.exp(scores - row_top[:, None, :])
    self_weight = jnp.exp(self_score - row_top)
    denominator = jnp.sum(weights, axis=1) + self_weight
    probs_bf16 = (weights / denominator[:, None, :]).astype(jnp.bfloat16)
    self_prob = (self_weight / denominator).astype(jnp.bfloat16)
    mixed_full = jnp.einsum(
        "rch,rcf->rhf", probs_bf16, cached_values, preferred_element_type=jnp.float32
    )
    mask_float = diagonal_mask.astype(jnp.float32)
    mixed_heads = jnp.sum(
        mixed_full.reshape(row_count, local_heads, local_heads, HD) * mask_float[None, :, :, None],
        axis=2,
    )
    mixed_heads = mixed_heads + self_prob.astype(jnp.float32)[:, :, None] * value_new.astype(
        jnp.float32
    )
    return mixed_heads.reshape(row_count, local_heads * HD).astype(jnp.bfloat16)


def per_device(
    tokens,
    lengths,
    slot_owner,
    positions,
    variates,
    cache_variates,
    kv_cache,
    attn_gain,
    ffn_gain,
    qkv_weight,
    out_weight,
    gate_up_weight,
    down_weight,
    variate_bias,
):
    head_count = lax.axis_size("head")
    head_place = lax.axis_index("head")
    slot_count = slot_owner.shape[0]
    token_share = slot_count // head_count
    all_lengths, all_times, all_variates, all_owners = (
        lax.all_gather(lengths, "req", axis=0, tiled=True),
        lax.all_gather(positions, "req", axis=0, tiled=True),
        lax.all_gather(variates, "req", axis=0, tiled=True),
        lax.all_gather(slot_owner, "req", axis=0, tiled=True),
    )
    all_tokens = lax.all_gather(tokens, "req", axis=0, tiled=True)
    slot_tokens = jnp.take(all_tokens, slot_owner, axis=0).astype(jnp.float32)
    cache_lengths = jnp.take(all_lengths, slot_owner)
    time_ids = jnp.take(all_times, slot_owner)
    variate_ids = jnp.take(all_variates, slot_owner)
    residual = lax.dynamic_slice_in_dim(slot_tokens, head_place * token_share, token_share, 0)
    local_heads = kv_cache.shape[-1] // HD
    for layer_index in range(LAYERS):
        if layer_index == 0:
            normed = rms_scale(slot_tokens, attn_gain[0]).astype(jnp.bfloat16)
        else:
            normed = lax.all_gather(
                rms_scale(residual, attn_gain[layer_index]).astype(jnp.bfloat16),
                "head",
                axis=0,
                tiled=True,
            )
        projected = jnp.dot(normed, qkv_weight[layer_index], preferred_element_type=jnp.float32)
        projected = projected.reshape(slot_count, local_heads, 3, HD)
        queries = rotary(projected[:, :, 0], time_ids).astype(jnp.bfloat16)
        key_new = rotary(projected[:, :, 1], time_ids).astype(jnp.bfloat16)
        value_new = projected[:, :, 2].astype(jnp.bfloat16)
        attended = attend(
            queries,
            key_new,
            value_new,
            kv_cache[layer_index, 0],
            kv_cache[layer_index, 1],
            cache_variates,
            cache_lengths,
            variate_ids,
            variate_bias[layer_index, 0],
            variate_bias[layer_index, 1],
        )
        out_partial = jnp.dot(attended, out_weight[layer_index], preferred_element_type=jnp.float32)
        residual = residual + lax.psum_scatter(
            out_partial.astype(jnp.bfloat16), "head", scatter_dimension=0, tiled=True
        ).astype(jnp.float32)
        ffn_input = lax.all_gather(
            rms_scale(residual, ffn_gain[layer_index]).astype(jnp.bfloat16),
            "head",
            axis=0,
            tiled=True,
        )
        paired = jnp.einsum(
            "rd,gdf->grf",
            ffn_input,
            gate_up_weight[layer_index],
            preferred_element_type=jnp.float32,
        )
        hidden = (jax.nn.silu(paired[0]) * paired[1]).astype(jnp.bfloat16)
        ffn_partial = jnp.dot(hidden, down_weight[layer_index], preferred_element_type=jnp.float32)
        residual = residual + lax.psum_scatter(
            ffn_partial.astype(jnp.bfloat16), "head", scatter_dimension=0, tiled=True
        ).astype(jnp.float32)
    final_rows = residual.astype(jnp.bfloat16)
    own_place = lax.axis_index("req") * head_count + head_place
    request_ids = own_place * token_share + jnp.arange(token_share, dtype=jnp.int32)
    matches = all_owners[None, :] == request_ids[:, None]
    slot_index = jnp.sum(
        jnp.where(matches, jnp.arange(all_owners.shape[0], dtype=jnp.int32)[None, :], 0), axis=1
    )
    everything = lax.all_gather(final_rows, ("req", "head"), axis=0, tiled=True)
    return jnp.take(everything, slot_index, axis=0)


def solution(mesh):
    return jax.shard_map(
        per_device,
        mesh=mesh,
        in_specs=(
            P("req", None),
            P("req"),
            P("req"),
            P("req"),
            P("req"),
            P("req", None),
            P(None, None, "req", None, "head"),
            P(),
            P(),
            P(None, None, "head"),
            P(None, "head", None),
            P(None, None, None, "head"),
            P(None, "head", None),
            P(None, None, "head"),
        ),
        out_specs=P(("req", "head"), None),
        check_vma=False,
    )
```

profile of v0, /device:TPU:0, one launch (start us, length us, event | category | flops | bytes accessed | tf_op | source)
XLA Modules:
  0.0 180.6 jit_solution(14930641685591788002)
XLA Ops:
  0.0 1.2 dynamic-slice
  1.9 0.9 dynamic-update-slice
  2.8 0.8 dynamic-update-slice.1
  3.6 0.8 dynamic-update-slice.2
  4.4 0.8 dynamic-update-slice.3
  5.3 13.1 %all-reduce.8 = (s32[64]{0:T(128)S(1)}, s32[64]{0:T(128)S(1)}, s32[64]{0:T(128)S(1)}, s32[64]{0:T(128)S(1)}) all-reduce(s32[64]{0:T(128)S(1)} %dynamic-update-slice.3, s32[64]{0:T(128)S(1)} %dynamic-update-slice.1, s32[64]{0:T(128)S(1)} %dynamic-update-slice.2, s32[64]{0:T(128)S(1)} %dynamic-update-slice), channel_id=1, replica_groups=mesh['req'=8,'head'=4] {'req'}, use_global_device_ids=true, to_apply=%add.3 | all-reduce | flops 256 | bytes 2048
  18.3 0.7 compare_select_fusion.1
  19.0 0.6 gather_fusion.3
  19.6 0.7 select_convert_fusion
  20.3 30.7 %all_gather.28 = bf16[64,1024]{1,0:T(8,128)(2,1)S(1)} all-gather(bf16[8,1024]{1,0:T(8,128)(2,1)} %param.16), channel_id=1, replica_groups=mesh['req'=8,'head'=4] {'req'}, dimensions={0}, use_global_device_ids=true | all-gather | bytes 147456 | tf_op jit(solution)/shard_map/all_gather | solution.py:111
  51.8 3.2 %slice_bitcast_fusion.1 = (bf16[768,1024]{0,1:T(8,128)(2,1)}, bf16[768,1024]{0,1:T(8,128)(2,1)S(1)}) fusion(bf16[2,1024,768]{2,1,0:T(8,128)(2,1)} %param.25), kind=kLoop, calls=%fused_computation.30 | loop fusion | bytes 6291456 | tf_op jit(solution)/shard_map/dot_general | solution.py:128
  55.1 1.7 copy.69
  56.9 0.7 fusion.73
  58.3 0.6 gather_fusion.2
  58.9 0.6 gather_fusion.4
  60.0 2.3 %fusion.115 = (f32[8,4]{1,0:T(8,128)S(1)}, f32[8,512,4]{1,2,0:T(4,128)S(1)}) fusion(f32[4]{0:T(128)S(1)} %get-tuple-element.43, f32[4]{0:T(128)S(1)} %get-tuple-element.42, pred[8,512]{1,0:T(8,128)(4,1)S(1)} %get-tuple-element.55, bf16[2,2,8,512,256]{4,3,2,1,0:T(8,128)(2,1)} %param.22, bf16[256,4]{0,1:T(4,128)(2,1)S(1)} %mul.407, ...), kind=kOutput, calls=%fused_computation.171 | convolution fusion | flops 8503264 | bytes 2177184 | tf_op jit(solution)/shard_map/rcf,rfh->rch/dot_general | solution.py:50
  62.5 2.0 %fusion.14 = f32[8,4,256]{2,1,0:T(4,128)S(1)} fusion(bf16[2,2,8,512,256]{4,3,2,1,0:T(8,128)(2,1)} %param.22, f32[8,512,4]{1,2,0:T(4,128)S(1)} %get-tuple-element.51, f32[8,4]{1,0:T(8,128)S(1)} %get-tuple-element.33, f32[8,4]{1,0:T(8,128)S(1)} %fusion.100), kind=kOutput, calls=%fused_computation.19 | convolution fusion | flops 8437760 | bytes 2195712 | tf_op jit(solution)/shard_map/rch,rcf->rhf/dot_general | solution.py:71
  65.2 10.1 %all-reduce.4 = bf16[8,1024]{1,0:T(8,128)(2,1)S(1)} all-reduce(bf16[8,1024]{1,0:T(8,128)(2,1)S(1)} %convolution_convert_fusion.1), channel_id=2, replica_groups=mesh['req'=8,'head'=4] {'head'}, use_global_device_ids=true, to_apply=%region_6.8.clone | all-reduce | flops 8192 | bytes 32768
  76.9 5.2 %all-gather = bf16[4,2,1024]{2,1,0:T(2,128)(2,1)S(1)} all-gather(bf16[1,2,1024]{2,1,0:T(2,128)(2,1)S(1)} %fusion.97), channel_id=1, replica_groups=mesh['req'=8,'head'=4] {'head'}, dimensions={0}, use_global_device_ids=true | all-gather | bytes 20480 | tf_op jit(solution)/shard_map/all_gather | solution.py:149
  82.1 3.0 %fusion.42 = f32[2,8,1024]{2,1,0:T(8,128)S(1)} fusion(bf16[8,1024,1]{1,0,2:T(8,128)(2,1)S(1)} %reshape.487, bf16[2,2,1024,1024]{3,2,1,0:T(8,128)(2,1)} %param.27), kind=kOutput, calls=%fused_computation.37 | convolution fusion | flops 33554432 | bytes 4276224 | tf_op jit(solution)/shard_map/rd,gdf->grf/dot_general | solution.py:155
  85.9 11.5 %all-reduce.5 = bf16[8,1024]{1,0:T(8,128)(2,1)S(1)} all-reduce(bf16[8,1024]{1,0:T(8,128)(2,1)S(1)} %fusion.54), channel_id=3, replica_groups=mesh['req'=8,'head'=4] {'head'}, use_global_device_ids=true, to_apply=%region_8.10.clone | all-reduce | flops 8192 | bytes 32768
  97.6 5.2 %all-gather.1 = bf16[4,2,1024]{2,1,0:T(2,128)(2,1)S(1)} all-gather(bf16[1,2,1024]{2,1,0:T(2,128)(2,1)S(1)} %fusion.98), channel_id=1, replica_groups=mesh['req'=8,'head'=4] {'head'}, dimensions={0}, use_global_device_ids=true | all-gather | bytes 20480 | tf_op jit(solution)/shard_map/all_gather | solution.py:122
  102.8 0.8 copy.77
  103.5 0.7 fusion.80
  104.8 2.3 %fusion.116 = (f32[8,4]{1,0:T(8,128)S(1)}, f32[8,512,4]{1,2,0:T(4,128)S(1)}) fusion(f32[4]{0:T(128)S(1)} %get-tuple-element.44, f32[4]{0:T(128)S(1)} %get-tuple-element.45, pred[8,512]{1,0:T(8,128)(4,1)S(1)} %get-tuple-element.55, bf16[2,2,8,512,256]{4,3,2,1,0:T(8,128)(2,1)} %param.22, bf16[8,256]{1,0:T(8,128)(2,1)S(1)} %convert_element_type.247, ...), kind=kOutput, calls=%fused_computation.172 | convolution fusion | flops 8503264 | bytes 2177184 | tf_op jit(solution)/shard_map/rcf,rfh->rch/dot_general | solution.py:50
  107.3 2.0 %fusion.8 = f32[8,4,256]{2,1,0:T(4,128)S(1)} fusion(bf16[2,2,8,512,256]{4,3,2,1,0:T(8,128)(2,1)} %param.22, f32[8,512,4]{1,2,0:T(4,128)S(1)} %get-tuple-element.53, f32[8,4]{1,0:T(8,128)S(1)} %get-tuple-element.31, f32[8,4]{1,0:T(8,128)S(1)} %fusion.101), kind=kOutput, calls=%fused_computation.13 | convolution fusion | flops 8437760 | bytes 2195712 | tf_op jit(solution)/shard_map/rch,rcf->rhf/dot_general | solution.py:71
  110.0 10.3 %all-reduce.6 = bf16[8,1024]{1,0:T(8,128)(2,1)S(1)} all-reduce(bf16[8,1024]{1,0:T(8,128)(2,1)S(1)} %convolution_convert_fusion), channel_id=4, replica_groups=mesh['req'=8,'head'=4] {'head'}, use_global_device_ids=true, to_apply=%region_14.16.clone | all-reduce | flops 8192 | bytes 32768
  120.6 5.2 %all-gather.2 = bf16[4,2,1024]{2,1,0:T(2,128)(2,1)S(1)} all-gather(bf16[1,2,1024]{2,1,0:T(2,128)(2,1)S(1)} %fusion.99), channel_id=1, replica_groups=mesh['req'=8,'head'=4] {'head'}, dimensions={0}, use_global_device_ids=true | all-gather | bytes 20480 | tf_op jit(solution)/shard_map/all_gather | solution.py:149
  125.8 3.0 %fusion.45 = f32[2,8,1024]{2,1,0:T(8,128)S(1)} fusion(bf16[8,1024,1]{1,0,2:T(8,128)(2,1)S(1)} %reshape.489, bf16[2,2,1024,1024]{3,2,1,0:T(8,128)(2,1)} %param.27), kind=kOutput, calls=%fused_computation.38 | convolution fusion | flops 33554432 | bytes 4276224 | tf_op jit(solution)/shard_map/rd,gdf->grf/dot_general | solution.py:155
  129.6 11.5 %all-reduce.7 = bf16[8,1024]{1,0:T(8,128)(2,1)S(1)} all-reduce(bf16[8,1024]{1,0:T(8,128)(2,1)S(1)} %fusion.57), channel_id=5, replica_groups=mesh['req'=8,'head'=4] {'head'}, use_global_device_ids=true, to_apply=%region_16.18.clone | all-reduce | flops 8192 | bytes 32768
  141.1 38.0 %all-gather.3 = bf16[32,2,1024]{2,1,0:T(2,128)(2,1)S(1)} all-gather(bf16[1,2,1024]{2,1,0:T(2,128)(2,1)S(1)} %fusion.96), channel_id=1, replica_groups=mesh['req'=8,'head'=4] {'req','head'}, dimensions={0}, use_global_device_ids=true | all-gather | bytes 135168 | tf_op jit(solution)/shard_map/all_gather | solution.py:173
  179.9 0.7 broadcast_select_fusion.1
  (96 shorter events, 7.9 us)
Async XLA Ops:
  55.1 1.8 copy-start.3
  55.1 4.5 %copy-start.2 = (s32[8,512]{1,0:T(8,128)S(1)}, s32[8,512]{1,0:T(8,128)}, u32[]{:S(2)}) copy-start(s32[8,512]{1,0:T(8,128)} %param.21) | copy-start | bytes 49156
  55.1 4.6 %copy-start.5 = (f32[2,2,4]{2,1,0:T(2,128)S(1)}, f32[2,2,4]{2,1,0:T(2,128)}, u32[]{:S(2)}) copy-start(f32[2,2,4]{2,1,0:T(2,128)} %param.29) | copy-start | bytes 196
  58.3 6.8 %copy-start = (bf16[2,256,1024]{2,1,0:T(8,128)(2,1)S(1)}, bf16[2,256,1024]{2,1,0:T(8,128)(2,1)}, u32[]{:S(2)}) copy-start(bf16[2,256,1024]{2,1,0:T(8,128)(2,1)} %param.26) | copy-start | bytes 3145732
  58.9 16.5 %copy-start.8 = (u32[32]{0:T(128)S(1)}, u32[32]{0:T(128)}, u32[]{:S(2)}) copy-start(u32[32]{0:T(128)} %constant.110) | copy-start | bytes 388
  58.9 17.9 %copy-start.4 = (f32[2,1024]{1,0:T(2,128)S(1)}, f32[2,1024]{1,0:T(2,128)}, u32[]{:S(2)}) copy-start(f32[2,1024]{1,0:T(2,128)} %param.24) | copy-start | bytes 24580
  82.1 3.5 %copy-start.6 = (bf16[2,1024,1024]{2,1,0:T(8,128)(2,1)S(1)}, bf16[2,1024,1024]{2,1,0:T(8,128)(2,1)}, u32[]{:S(2)}) copy-start(bf16[2,1024,1024]{2,1,0:T(8,128)(2,1)} %param.28) | copy-start | bytes 12582916
  104.3 5.6 %copy-start.1 = (bf16[2,256,1024]{2,1,0:T(8,128)(2,1)S(1)}, bf16[2,256,1024]{2,1,0:T(8,128)(2,1)}, u32[]{:S(2)}) copy-start(bf16[2,256,1024]{2,1,0:T(8,128)(2,1)} %param.26) | copy-start | bytes 3145732
  125.7 3.5 %copy-start.7 = (bf16[2,1024,1024]{2,1,0:T(8,128)(2,1)S(1)}, bf16[2,1024,1024]{2,1,0:T(8,128)(2,1)}, u32[]{:S(2)}) copy-start(bf16[2,1024,1024]{2,1,0:T(8,128)(2,1)} %param.28) | copy-start | bytes 12582916
where the time goes:
time: 181 us
  blocking collectives  141 us (78%)
  matrix products  17.2 us (10%)
  local copies, waits for them, and re-layouts  16.3 us (9%)
  other arithmetic  4.83 us (3%)
    unnamed x5, blocking collectives  56.5 us
    all_gather x1, blocking collectives, per_device(): everything = lax.all_gather(final_rows, ('req', 'head'), axis=0, tiled=True)  38 us
    all_gather x1, blocking collectives, per_device(): all_tokens = lax.all_gather(tokens, 'req', axis=0, tiled=True)  30.7 us
    all_gather x2, blocking collectives, per_device(): lax.all_gather(rms_scale(residual, ffn_gain[layer_index]).astype(jnp.bflo...  10.3 us
    unnamed x32, local copies, waits for them, and re-layouts  6.21 us
    dot_general x2, matrix products, per_device(): jnp.einsum('rd,gdf->grf', ffn_input, gate_up_weight[layer_index], preferr...  5.99 us
    dot_general x3, local copies, waits for them, and re-layouts, per_device(): jnp.dot(normed, qkv_weight[layer_index], preferred_element_type=jnp.float32)  5.75 us
    all_gather x1, blocking collectives, per_device(): lax.all_gather(rms_scale(residual, attn_gain[layer_index]).astype(jnp.bfl...  5.18 us

commit v1 on v0

v1 whole, which is shorter than its diff:
```python
import functools

import jax
import jax.numpy as jnp
import numpy as np
from jax import lax
from jax.experimental import pallas as pl
from jax.experimental.pallas import tpu as pltpu
from jax.sharding import PartitionSpec as P

HD = 64
LAYERS = 2
META = 128
LOW = 128
CHUNK = 128
NEG = -1e30
F32 = jnp.float32
BF16 = jnp.bfloat16

VMEM = pl.BlockSpec(memory_space=pltpu.VMEM)
SMEM = pl.BlockSpec(memory_space=pltpu.SMEM)
ANY = pl.BlockSpec(memory_space=pl.ANY)
PARAMS = pltpu.CompilerParams(vmem_limit_bytes=32 * 2**20)


def iota(shape, dim):
    return lax.broadcasted_iota(jnp.int32, shape, dim)


def rms_scale(stream, gain_row):
    return stream * lax.rsqrt(jnp.mean(stream * stream, axis=-1, keepdims=True) + 1e-06) * gain_row


def pack_kernel(tokens_ref, lengths_ref, positions_ref, variates_ref, out_ref):
    rows, width = tokens_ref.shape
    out_ref[:, :width] = tokens_ref[...]
    row, lane = iota((rows, META), 0), iota((rows, META), 1)
    kind = lane % (META // 2)
    whole = jnp.zeros((rows, META), jnp.int32)
    for i in range(rows):
        values = jnp.where(
            kind == 0, lengths_ref[i], jnp.where(kind == 1, positions_ref[i], variates_ref[i])
        )
        whole = jnp.where(row == i, values, whole)
    digit = jnp.where(lane < META // 2, whole // LOW, whole % LOW)
    out_ref[:, width:] = digit.astype(F32).astype(BF16)


def attention(
    layer,
    stream,
    facts,
    cos,
    sin,
    variates_ref,
    kv_ref,
    gain_ref,
    qkv_ref,
    out_w_ref,
    bias_ref,
    kv_buf,
    scores,
    mixed,
    first_sem,
    more_sem,
    part_ref,
):
    slots, cap = variates_ref.shape
    width = kv_buf.shape[-1]
    heads = width // HD
    chunks = cap // CHUNK
    rows = heads * slots

    lengths = facts[:, 0:1]
    variate = facts[:, 2:3]
    live_slots = [jnp.sum((lengths > c * CHUNK).astype(jnp.int32)) for c in range(chunks)]

    def more_copy(c, s):
        place = pl.ds(c * CHUNK, CHUNK)
        return pltpu.make_async_copy(
            kv_ref.at[layer, :, s, place, :], kv_buf.at[:, s, place, :], more_sem.at[c, s]
        )

    for c in range(1, chunks):

        @pl.loop(0, live_slots[c])
        def _(s, c=c):
            more_copy(c, s).start()

    normed = rms_scale(stream, gain_ref[layer : layer + 1, :]).astype(BF16)
    projected = jnp.dot(normed, qkv_ref[layer], preferred_element_type=F32)

    lane = iota((slots, 128), 1)
    front = lane % HD < HD // 2
    pieces = []
    for j in range(projected.shape[1] // 128):
        u = projected[:, j * 128 : (j + 1) * 128]
        turned = jnp.where(front, -pltpu.roll(u, 96, 1), pltpu.roll(u, 32, 1))
        is_value = (lane + j * 128) % (3 * HD) >= 2 * HD
        pieces.append(jnp.where(is_value, u, u * cos + turned * sin).astype(BF16).astype(F32))
    turned_all = jnp.concatenate(pieces, axis=1)

    column = iota((slots, width), 1)
    of_head = [column // HD == h for h in range(heads)]
    step = 2 * HD
    query = [
        jnp.where(of_head[h], turned_all[:, h * step : h * step + width], 0.0) for h in range(heads)
    ]
    query_all = jnp.concatenate(query, axis=0).astype(BF16)
    next_keys = jnp.concatenate(
        [turned_all[:, HD:], jnp.zeros((slots, HD), F32)], axis=1
    )
    own_score = [
        jnp.sum(query[h] * next_keys[:, h * step : h * step + width], axis=1, keepdims=True) * 0.125
        + bias_ref[layer, 0, h]
        for h in range(heads)
    ]

    row_slot = iota((rows, width), 0) % slots
    score_dims = (((1,), (1,)), ((), ()))

    def score_block(c, s):
        keys = kv_buf[0, s, pl.ds(c * CHUNK, CHUNK), :]
        mine = jnp.where(row_slot == s, query_all, jnp.zeros_like(query_all))
        return lax.dot_general(mine, keys, score_dims, preferred_element_type=F32)

    pltpu.make_async_copy(
        kv_ref.at[layer, :, :, pl.ds(0, CHUNK), :], kv_buf.at[:, :, pl.ds(0, CHUNK), :], first_sem
    ).wait()
    total = score_block(0, 0)
    for s in range(1, slots):
        total = total + score_block(0, s)
    scores[:, :CHUNK] = total
    if chunks > 1:
        scores[:, CHUNK:] = jnp.zeros((rows, cap - CHUNK), F32)
    for c in range(1, chunks):

        @pl.loop(0, live_slots[c])
        def _(s, c=c):
            more_copy(c, s).wait()
            scores[:, c * CHUNK : (c + 1) * CHUNK] += score_block(c, s)

    same = variates_ref[...].astype(F32) == variate
    live = iota((slots, cap), 1).astype(F32) < lengths
    probs = []
    own_prob = []
    for h in range(heads):
        block = scores[h * slots : (h + 1) * slots, :] * 0.125
        block = block + jnp.where(same, bias_ref[layer, 0, h], bias_ref[layer, 1, h])
        block = jnp.where(live, block, NEG)
        top = jnp.maximum(jnp.max(block, axis=1, keepdims=True), own_score[h])
        weight = jnp.exp(block - top)
        own_weight = jnp.exp(own_score[h] - top)
        share = 1.0 / (jnp.sum(weight, axis=1, keepdims=True) + own_weight)
        probs.append(weight * share)
        own_prob.append((own_weight * share).astype(BF16).astype(F32))
    probs_all = jnp.concatenate(probs, axis=0).astype(BF16)
    prob_slot = iota((rows, CHUNK), 0) % slots

    def mix_block(c, s):
        part = probs_all[:, c * CHUNK : (c + 1) * CHUNK]
        mine = jnp.where(prob_slot == s, part, jnp.zeros_like(part))
        values = kv_buf[1, s, pl.ds(c * CHUNK, CHUNK), :]
        return jnp.dot(mine, values, preferred_element_type=F32)

    total = mix_block(0, 0)
    for s in range(1, slots):
        total = total + mix_block(0, s)
    mixed[...] = total
    for c in range(1, chunks):

        @pl.loop(0, live_slots[c])
        def _(s, c=c):
            mixed[...] += mix_block(c, s)

    attended = jnp.zeros((slots, width), F32)
    for h in range(heads):
        value_new = turned_all[:, (h + 1) * step : (h + 1) * step + width]
        attended = jnp.where(
            of_head[h], mixed[h * slots : (h + 1) * slots, :] + own_prob[h] * value_new, attended
        )
    part_ref[...] = jnp.dot(
        attended.astype(BF16), out_w_ref[layer], preferred_element_type=F32
    ).astype(BF16)


def start_first_copy(layer, kv_ref, kv_buf, first_sem):
    pltpu.make_async_copy(
        kv_ref.at[layer, :, :, pl.ds(0, CHUNK), :], kv_buf.at[:, :, pl.ds(0, CHUNK), :], first_sem
    ).start()


def first_attention_kernel(block_count, *refs):
    owner_ref, place_ref, *block_refs = refs[: 2 + block_count]
    (
        frequency_ref,
        variates_ref,
        kv_ref,
        gain_ref,
        qkv_ref,
        out_w_ref,
        bias_ref,
        part_ref,
        stream_ref,
        facts_ref,
        turn_ref,
        kv_buf,
        scores,
        mixed,
        first_sem,
        more_sem,
    ) = refs[2 + block_count :]
    start_first_copy(0, kv_ref, kv_buf, first_sem)
    gathered = jnp.concatenate([ref[...] for ref in block_refs], axis=0)
    slots = variates_ref.shape[0]
    width = stream_ref.shape[1]
    total = gathered.shape[0]
    row, column = iota((slots, total), 0), iota((slots, total), 1)
    own_block = place_ref[0]
    pick = jnp.zeros((slots, total), F32)
    for s in range(slots):
        owner = owner_ref[s]
        source = ((owner // slots) ^ own_block) * slots + owner % slots
        pick = jnp.where((row == s) & (column == source), 1.0, pick)
    picked = jnp.dot(pick.astype(BF16), gathered, preferred_element_type=F32)
    stream = picked[:, :width]
    digits = picked[:, width:]
    facts = digits * float(LOW) + pltpu.roll(digits, META // 2, 1)
    stream_ref[...] = stream
    facts_ref[...] = facts
    angle = facts[:, 1:2] * frequency_ref[...]
    cos, sin = jnp.cos(angle), jnp.sin(angle)
    turn_ref[:, :128] = cos
    turn_ref[:, 128:] = sin
    attention(
        0, stream, facts, cos, sin, variates_ref, kv_ref, gain_ref, qkv_ref, out_w_ref, bias_ref,
        kv_buf, scores, mixed, first_sem, more_sem, part_ref,
    )


def next_attention_kernel(layer, part_count, *refs):
    part_refs = refs[:part_count]
    (
        old_ref,
        facts_ref,
        turn_ref,
        variates_ref,
        kv_ref,
        gain_ref,
        qkv_ref,
        out_w_ref,
        bias_ref,
        part_ref,
        stream_ref,
        kv_buf,
        scores,
        mixed,
        first_sem,
        more_sem,
    ) = refs[part_count:]
    start_first_copy(layer, kv_ref, kv_buf, first_sem)
    stream = old_ref[...]
    for ref in part_refs:
        stream = stream + ref[...].astype(F32)
    stream_ref[...] = stream
    attention(
        layer, stream, facts_ref[...], turn_ref[:, :128], turn_ref[:, 128:], variates_ref, kv_ref,
        gain_ref, qkv_ref, out_w_ref, bias_ref, kv_buf, scores, mixed, first_sem, more_sem, part_ref,
    )


def feed_forward(layer, part_refs, old_ref, gain_ref, gate_up_ref, down_ref):
    stream = old_ref[...]
    for ref in part_refs:
        stream = stream + ref[...].astype(F32)
    normed = rms_scale(stream, gain_ref[layer : layer + 1, :]).astype(BF16)
    gate = jnp.dot(normed, gate_up_ref[layer, 0], preferred_element_type=F32)
    up = jnp.dot(normed, gate_up_ref[layer, 1], preferred_element_type=F32)
    hidden = (gate / (1.0 + jnp.exp(-gate)) * up).astype(BF16)
    return stream, jnp.dot(hidden, down_ref[layer], preferred_element_type=F32)


def feed_forward_kernel(layer, part_count, *refs):
    old_ref, gain_ref, gate_up_ref, down_ref, part_ref, stream_ref = refs[part_count:]
    stream, part = feed_forward(layer, refs[:part_count], old_ref, gain_ref, gate_up_ref, down_ref)
    stream_ref[...] = stream
    part_ref[...] = part.astype(BF16)


def last_feed_forward_kernel(layer, part_count, share, *refs):
    owner_ref, old_ref, gain_ref, gate_up_ref, down_ref, send_ref = refs[part_count:]
    stream, part = feed_forward(layer, refs[:part_count], old_ref, gain_ref, gate_up_ref, down_ref)
    slots, width = stream.shape
    rows = (part + stream * (1.0 / part_count)).astype(BF16)
    row, lane = iota((slots, META), 0), iota((slots, META), 1)
    devices = send_ref.shape[0]
    target, slot = iota((devices, slots), 0), iota((devices, slots), 1)
    flag = jnp.zeros((slots, META), F32)
    place = jnp.zeros((devices, slots), F32)
    for s in range(slots):
        owner = owner_ref[s]
        flag = jnp.where((row == s) & (lane == owner % share), 1.0, flag)
        place = jnp.where((slot == s) & (target == owner // share), 1.0, place)
    payload = jnp.concatenate([rows, flag.astype(BF16)], axis=1)
    send_ref[...] = jnp.dot(place.astype(BF16), payload, preferred_element_type=F32).astype(BF16)


def place_kernel(received_ref, out_ref):
    share, width = out_ref.shape
    flags = received_ref[:, width:]
    rows = lax.dot_general(
        flags, received_ref[:, :width], (((0,), (0,)), ((), ())), preferred_element_type=F32
    )
    out_ref[...] = rows[:share, :].astype(BF16)


def call(kernel, operands, outs, scratch=()):
    specs, arrays = zip(*operands)
    return pl.pallas_call(
        kernel,
        out_shape=[jax.ShapeDtypeStruct(shape, dtype) for shape, dtype in outs],
        in_specs=list(specs),
        out_specs=[VMEM] * len(outs),
        scratch_shapes=list(scratch),
        compiler_params=PARAMS,
    )(*arrays)


def swap(array, axis, mask):
    count = lax.axis_size(axis)
    return lax.ppermute(array, axis, [(i, i ^ mask) for i in range(count)])


def gather_blocks(block, axis):
    count = lax.axis_size(axis)
    pair = jnp.concatenate([block, swap(block, axis, 1)], axis=0)
    blocks = [pair]
    reach = 2
    while reach < count:
        span = min(4, count // reach)
        held = blocks[0] if len(blocks) == 1 else jnp.concatenate(blocks, axis=0)
        blocks = blocks + [swap(held, axis, reach * k) for k in range(1, span)]
        reach *= span
    return blocks


def per_device(
    tokens,
    lengths,
    slot_owner,
    positions,
    variates,
    cache_variates,
    kv_cache,
    attn_gain,
    ffn_gain,
    qkv_weight,
    out_weight,
    gate_up_weight,
    down_weight,
    variate_bias,
):
    slots, width = tokens.shape
    cap, local_width = kv_cache.shape[3:]
    head_count = lax.axis_size("head")
    devices = lax.axis_size("req") * head_count
    share = slots // head_count
    local_heads = local_width // HD

    (packed,) = call(
        pack_kernel,
        [(VMEM, tokens), (SMEM, lengths), (SMEM, positions), (SMEM, variates)],
        [((slots, width + META), BF16)],
    )
    blocks = gather_blocks(packed, "req")
    own_block = lax.axis_index("req").reshape(1)
    exponent = -2.0 * (np.arange(128) % (HD // 2)) / HD
    frequency = jnp.asarray((10000.0**exponent).astype(np.float32)[None, :])

    scratch = [
        pltpu.VMEM((2, slots, cap, local_width), BF16),
        pltpu.VMEM((local_heads * slots, cap), F32),
        pltpu.VMEM((local_heads * slots, local_width), F32),
        pltpu.SemaphoreType.DMA,
        pltpu.SemaphoreType.DMA((cap // CHUNK, slots)),
    ]
    shared = [
        (VMEM, cache_variates),
        (ANY, kv_cache),
        (VMEM, attn_gain),
        (VMEM, qkv_weight),
        (VMEM, out_weight),
        (SMEM, variate_bias),
    ]
    stream_type = ((slots, width), F32)
    part_type = ((slots, width), BF16)

    def exchange(part):
        return [part] + [swap(part, "head", k) for k in range(1, head_count)]

    part, stream, facts, turn = call(
        functools.partial(first_attention_kernel, len(blocks)),
        [(SMEM, slot_owner), (SMEM, own_block)]
        + [(VMEM, block) for block in blocks]
        + [(VMEM, frequency)]
        + shared,
        [part_type, stream_type, ((slots, META), F32), ((slots, 256), F32)],
        scratch,
    )
    for layer in range(LAYERS):
        if layer:
            part, stream = call(
                functools.partial(next_attention_kernel, layer, head_count),
                [(VMEM, p) for p in parts]
                + [(VMEM, stream), (VMEM, facts), (VMEM, turn)]
                + shared,
                [part_type, stream_type],
                scratch,
            )
        parts = exchange(part)
        weights = [(VMEM, ffn_gain), (VMEM, gate_up_weight), (VMEM, down_weight)]
        if layer < LAYERS - 1:
            part, stream = call(
                functools.partial(feed_forward_kernel, layer, head_count),
                [(VMEM, p) for p in parts] + [(VMEM, stream)] + weights,
                [part_type, stream_type],
            )
            parts = exchange(part)
        else:
            (send,) = call(
                functools.partial(last_feed_forward_kernel, layer, head_count, share),
                [(VMEM, p) for p in parts] + [(SMEM, slot_owner), (VMEM, stream)] + weights,
                [((devices, width + META), BF16)],
            )
    received = lax.all_to_all(send, ("req", "head"), 0, 0, tiled=True)
    (out,) = call(place_kernel, [(VMEM, received)], [((share, width), BF16)])
    return out


def solution(mesh):
    return jax.shard_map(
        per_device,
        mesh=mesh,
        in_specs=(
            P("req", None),
            P("req"),
            P("req"),
            P("req"),
            P("req"),
            P("req", None),
            P(None, None, "req", None, "head"),
            P(),
            P(),
            P(None, None, "head"),
            P(None, "head", None),
            P(None, None, None, "head"),
            P(None, "head", None),
            P(None, None, "head"),
        ),
        out_specs=P(("req", "head"), None),
        check_vma=False,
    )
```

time: 181 us -> 66.4 us (0.37)
  blocking collectives: 141 us -> 9.65 us
  matrix products: 17.2 us -> 0 us
  starting transfers between devices: 0 us -> 13.6 us
  Pallas kernels: 0 us -> 12.3 us
  waiting for transfers between devices: 0 us -> 12.2 us
  other arithmetic: 4.83 us -> 0.66 us
    all_gather x5 -> x0, blocking collectives: 84.3 us -> none  [the longest x1 38 us: per_device(): everything = lax.all_gather(final_rows, ('req', 'head'), axis=0, tiled=True)]
    unnamed x5 -> x0, blocking collectives: 56.5 us -> none
    dot_general x12 -> x0, matrix products: 17.2 us -> none  [the longest x2 5.99 us: per_device(): jnp.einsum('rd,gdf->grf', ffn_input, gate_up_weight[layer_index], preferr...]
    ppermute x0 -> x13, starting transfers between devices: none -> 13.6 us  [swap(): return lax.ppermute(array, axis, [(i, i ^ mask) for i in range(count)])]
    pallas_call x0 -> x6, Pallas kernels: none -> 12.3 us  [call(): pl.pallas_call(kernel, out_shape=[jax.ShapeDtypeStruct(shape, dtype) for...]
    ppermute x0 -> x13, waiting for transfers between devices: none -> 12.2 us  [swap(): return lax.ppermute(array, axis, [(i, i ^ mask) for i in range(count)])]
    unnamed x32 -> x47, local copies, waits for them, and re-layouts: 6.21 us -> 16.3 us
    all_to_all x0 -> x1, blocking collectives: none -> 9.65 us  [per_device(): received = lax.all_to_all(send, ('req', 'head'), 0, 0, tiled=True)]
  transfers between devices with their start and end apart: 0 -> 13, of which waited for: 0 -> 9; matrix products, arithmetic and copies ran while one was open for 0% -> 0% of each run, Pallas kernels for 0% -> 0%
where the time goes in v1:
time: 66.4 us; the launch traced here: 65.5 us
  local copies, waits for them, and re-layouts  16.8 us (25%)
  starting transfers between devices  13.6 us (20%)
  Pallas kernels  12.3 us (19%)
  waiting for transfers between devices  12.2 us (18%)
  blocking collectives  9.65 us (15%)
    unnamed x47, local copies, waits for them, and re-layouts  16.3 us
    ppermute x13, starting transfers between devices, swap(): return lax.ppermute(array, axis, [(i, i ^ mask) for i in range(count)])  13.6 us
    pallas_call x6, Pallas kernels, call(): pl.pallas_call(kernel, out_shape=[jax.ShapeDtypeStruct(shape, dtype) for...  12.3 us
    ppermute x13, waiting for transfers between devices, swap(): return lax.ppermute(array, axis, [(i, i ^ mask) for i in range(count)])  12.2 us
    all_to_all x1, blocking collectives, per_device(): received = lax.all_to_all(send, ('req', 'head'), 0, 0, tiled=True)  9.65 us
  transfers between devices with their start and end apart: 13, of which 9 were waited for; matrix products, arithmetic and copies ran while one was open for 0% of the time, Pallas kernels for 0%

profile of v1, /device:TPU:0, one launch (start us, length us, event | category | flops | bytes accessed | tf_op | source)
XLA Modules:
  0.0 65.5 jit_solution(2844427438371340366)
XLA Ops:
  0.0 0.7 %copy-done.13 = bf16[8,1024]{1,0:T(8,128)(2,1)S(1)} copy-done((bf16[8,1024]{1,0:T(8,128)(2,1)S(1)}, bf16[8,1024]{1,0:T(8,128)(2,1)}, u32[]{:S(2)}) %copy-start.13) | copy-done | bytes 16408
  1.4 0.7 copy-done.19
  2.0 0.7 copy-done.20
  3.3 3.0 %collective-permute-start = (bf16[8,1152]{1,0:T(8,128)(2,1)S(1)}, bf16[8,1152]{1,0:T(8,128)(2,1)S(1)}, u32[]{:S(2)}, u32[]{:S(2)}) collective-permute-start(bf16[8,1152]{1,0:T(8,128)(2,1)S(1)} %shard_map.145), channel_id=1, source_target_pairs={{0,4},{4,0},{8,12},{12,8},{16,20},{20,16},{24,28},{28,24},{1,5},{5... | collective-permute-start | bytes 55304 | tf_op jit(solution)/shard_map/ppermute | solution.py:331
  6.3 1.7 %collective-permute-done = bf16[8,1152]{1,0:T(8,128)(2,1)S(1)} collective-permute-done((bf16[8,1152]{1,0:T(8,128)(2,1)S(1)}, bf16[8,1152]{1,0:T(8,128)(2,1)S(1)}, u32[]{:S(2)}, u32[]{:S(2)}) %collective-permute-start) | collective-permute-done | bytes 18464 | tf_op jit(solution)/shard_map/ppermute | solution.py:331
  8.0 4.1 %collective-permute-start.3 = (bf16[16,1152]{1,0:T(8,128)(2,1)S(1)}, bf16[16,1152]{1,0:T(8,128)(2,1)S(1)}, u32[]{:S(2)}, u32[]{:S(2)}) collective-permute-start(bf16[16,1152]{1,0:T(8,128)(2,1)S(1)} %pad_maximum_fusion.refs_2_), channel_id=1, source_target_pairs={{0,24},{4,28},{8,16},{12,20},{16,8},{20,12},{24,0},{28,4},{1,25},{... | collective-permute-start | bytes 110600 | tf_op jit(solution)/shard_map/ppermute | solution.py:331
  12.8 1.3 %collective-permute-done.3.refs_5_ = bf16[16,1152]{1,0:T(8,128)(2,1)S(1)} collective-permute-done((bf16[16,1152]{1,0:T(8,128)(2,1)S(1)}, bf16[16,1152]{1,0:T(8,128)(2,1)S(1)}, u32[]{:S(2)}, u32[]{:S(2)}) %collective-permute-start.3) | collective-permute-done | bytes 36896 | tf_op jit(solution)/shard_map/ppermute | solution.py:331
  14.1 2.9 %collective-permute-done.2.refs_4_ = bf16[16,1152]{1,0:T(8,128)(2,1)S(1)} collective-permute-done((bf16[16,1152]{1,0:T(8,128)(2,1)S(1)}, bf16[16,1152]{1,0:T(8,128)(2,1)S(1)}, u32[]{:S(2)}, u32[]{:S(2)}) %collective-permute-start.2) | collective-permute-done | bytes 36896 | tf_op jit(solution)/shard_map/ppermute | solution.py:331
  17.0 3.4 %copy-done = bf16[2,2,8,512,256]{4,3,2,1,0:T(8,128)(2,1)S(1)} copy-done((bf16[2,2,8,512,256]{4,3,2,1,0:T(8,128)(2,1)S(1)}, bf16[2,2,8,512,256]{4,3,2,1,0:T(8,128)(2,1)}, u32[]{:S(2)}) %copy-start) | copy-done | bytes 8388632
  20.4 1.9 %copy-done.4 = bf16[2,1024,768]{2,1,0:T(8,128)(2,1)S(1)} copy-done((bf16[2,1024,768]{2,1,0:T(8,128)(2,1)S(1)}, bf16[2,1024,768]{2,1,0:T(8,128)(2,1)}, u32[]{:S(2)}) %copy-start.4) | copy-done | bytes 3145752
  22.3 1.2 %copy-done.6 = bf16[2,256,1024]{2,1,0:T(8,128)(2,1)S(1)} copy-done((bf16[2,256,1024]{2,1,0:T(8,128)(2,1)S(1)}, bf16[2,256,1024]{2,1,0:T(8,128)(2,1)}, u32[]{:S(2)}) %copy-start.6) | copy-done | bytes 1048600
  23.5 0.7 %copy-done.8 = s32[8,512]{1,0:T(8,128)S(1)} copy-done((s32[8,512]{1,0:T(8,128)S(1)}, s32[8,512]{1,0:T(8,128)}, u32[]{:S(2)}) %copy-start.8) | copy-done | bytes 16408
  24.2 0.7 %copy-done.10 = f32[2,1024]{1,0:T(2,128)S(1)} copy-done((f32[2,1024]{1,0:T(2,128)S(1)}, f32[2,1024]{1,0:T(2,128)}, u32[]{:S(2)}) %copy-start.10) | copy-done | bytes 8216
  24.9 0.7 %copy-done.14 = f32[2,2,4]{2,1,0:T(2,128)S(1)} copy-done((f32[2,2,4]{2,1,0:T(2,128)S(1)}, f32[2,2,4]{2,1,0:T(2,128)}, u32[]{:S(2)}) %copy-start.14) | copy-done | bytes 88
  25.6 0.7 copy-done.16
  26.3 0.7 copy-done.21
  26.9 4.2 %shard_map.146 = (bf16[8,1024]{1,0:T(8,128)(2,1)S(1)}, f32[8,1024]{1,0:T(8,128)S(1)}, f32[8,128]{1,0:T(8,128)S(1)}, f32[8,256]{1,0:T(8,128)S(1)}) custom-call(s32[8]{0:T(128)S(1)} %copy-done.16, s32[1]{0:T(128)} %bitcast.refs_1_, bf16[16,1152]{1,0:T(8,128)(2,1)S(1)} %pad_maximum_fusion.refs_2_, bf16[16,1152]{1,0:T(8,128)(2,1)S(1)} %collective-permute-done.1.refs_3_, ...), custom_call_target="tpu_custom_call" | custom-call | tf_op jit(solution)/shard_map/pallas_call | solution.py:319
  31.3 1.6 %collective-permute-start.5 = (bf16[8,1024]{1,0:T(8,128)(2,1)S(1)}, bf16[8,1024]{1,0:T(8,128)(2,1)S(1)}, u32[]{:S(2)}, u32[]{:S(2)}) collective-permute-start(bf16[8,1024]{1,0:T(8,128)(2,1)S(1)} %get-tuple-element.13.refs_0_), channel_id=1, source_target_pairs={{0,2},{1,3},{2,0},{3,1},{4,6},{5,7},{6,4},{7,5},{8,10},{9,11},{10,... | collective-permute-start | bytes 49160 | tf_op jit(solution)/shard_map/ppermute | solution.py:331
  33.1 1.4 %collective-permute-done.6.refs_3_ = bf16[8,1024]{1,0:T(8,128)(2,1)S(1)} collective-permute-done((bf16[8,1024]{1,0:T(8,128)(2,1)S(1)}, bf16[8,1024]{1,0:T(8,128)(2,1)S(1)}, u32[]{:S(2)}, u32[]{:S(2)}) %collective-permute-start.6) | collective-permute-done | bytes 16416 | tf_op jit(solution)/shard_map/ppermute | solution.py:331
  35.1 2.2 %copy-done.3 = bf16[2,1024,1024]{2,1,0:T(8,128)(2,1)S(1)} copy-done((bf16[2,1024,1024]{2,1,0:T(8,128)(2,1)S(1)}, bf16[2,1024,1024]{2,1,0:T(8,128)(2,1)}, u32[]{:S(2)}) %copy-start.3) | copy-done | bytes 4194328
  37.3 1.0 %shard_map.147 = (bf16[8,1024]{1,0:T(8,128)(2,1)S(1)}, f32[8,1024]{1,0:T(8,128)S(1)}) custom-call(bf16[8,1024]{1,0:T(8,128)(2,1)S(1)} %get-tuple-element.13.refs_0_, bf16[8,1024]{1,0:T(8,128)(2,1)S(1)} %collective-permute-done.4.refs_1_, bf16[8,1024]{1,0:T(8,128)(2,1)S(1)} %collective-permute-done.5.refs_2_, ...), custom_call_target="tpu_custom_call" | custom-call | tf_op jit(solution)/shard_map/pallas_call | solution.py:319
  38.9 1.5 %collective-permute-start.8 = (bf16[8,1024]{1,0:T(8,128)(2,1)S(1)}, bf16[8,1024]{1,0:T(8,128)(2,1)S(1)}, u32[]{:S(2)}, u32[]{:S(2)}) collective-permute-start(bf16[8,1024]{1,0:T(8,128)(2,1)S(1)} %get-tuple-element.15.refs_0_), channel_id=1, source_target_pairs={{0,2},{1,3},{2,0},{3,1},{4,6},{5,7},{6,4},{7,5},{8,10},{9,11},{10,... | collective-permute-start | bytes 49160 | tf_op jit(solution)/shard_map/ppermute | solution.py:331
  40.3 1.2 %collective-permute-done.9.refs_3_ = bf16[8,1024]{1,0:T(8,128)(2,1)S(1)} collective-permute-done((bf16[8,1024]{1,0:T(8,128)(2,1)S(1)}, bf16[8,1024]{1,0:T(8,128)(2,1)S(1)}, u32[]{:S(2)}, u32[]{:S(2)}) %collective-permute-start.9) | collective-permute-done | bytes 16416 | tf_op jit(solution)/shard_map/ppermute | solution.py:331
  41.5 1.2 %collective-permute-done.8.refs_2_ = bf16[8,1024]{1,0:T(8,128)(2,1)S(1)} collective-permute-done((bf16[8,1024]{1,0:T(8,128)(2,1)S(1)}, bf16[8,1024]{1,0:T(8,128)(2,1)S(1)}, u32[]{:S(2)}, u32[]{:S(2)}) %collective-permute-start.8) | collective-permute-done | bytes 16416 | tf_op jit(solution)/shard_map/ppermute | solution.py:331
  42.7 1.2 %copy-done.7 = bf16[2,256,1024]{2,1,0:T(8,128)(2,1)S(1)} copy-done((bf16[2,256,1024]{2,1,0:T(8,128)(2,1)S(1)}, bf16[2,256,1024]{2,1,0:T(8,128)(2,1)}, u32[]{:S(2)}) %copy-start.7) | copy-done | bytes 1048600
  44.0 4.0 %shard_map.148 = (bf16[8,1024]{1,0:T(8,128)(2,1)S(1)}, f32[8,1024]{1,0:T(8,128)S(1)}) custom-call(bf16[8,1024]{1,0:T(8,128)(2,1)S(1)} %get-tuple-element.15.refs_0_, bf16[8,1024]{1,0:T(8,128)(2,1)S(1)} %collective-permute-done.7.refs_1_, bf16[8,1024]{1,0:T(8,128)(2,1)S(1)} %collective-permute-done.8.refs_2_, ...), custom_call_target="tpu_custom_call" | custom-call | tf_op jit(solution)/shard_map/pallas_call | solution.py:319
  48.0 1.7 %collective-permute-start.11 = (bf16[8,1024]{1,0:T(8,128)(2,1)S(1)}, bf16[8,1024]{1,0:T(8,128)(2,1)S(1)}, u32[]{:S(2)}, u32[]{:S(2)}) collective-permute-start(bf16[8,1024]{1,0:T(8,128)(2,1)S(1)} %get-tuple-element.19.refs_0_), channel_id=1, source_target_pairs={{0,2},{1,3},{2,0},{3,1},{4,6},{5,7},{6,4},{7,5},{8,10},{9,11},{10,... | collective-permute-start | bytes 49160 | tf_op jit(solution)/shard_map/ppermute | solution.py:331
  49.9 1.3 %collective-permute-done.12.refs_3_ = bf16[8,1024]{1,0:T(8,128)(2,1)S(1)} collective-permute-done((bf16[8,1024]{1,0:T(8,128)(2,1)S(1)}, bf16[8,1024]{1,0:T(8,128)(2,1)S(1)}, u32[]{:S(2)}, u32[]{:S(2)}) %collective-permute-start.12) | collective-permute-done | bytes 16416 | tf_op jit(solution)/shard_map/ppermute | solution.py:331
  51.8 1.7 %shard_map.149 = bf16[32,1152]{1,0:T(8,128)(2,1)S(1)} custom-call(bf16[8,1024]{1,0:T(8,128)(2,1)S(1)} %get-tuple-element.19.refs_0_, bf16[8,1024]{1,0:T(8,128)(2,1)S(1)} %collective-permute-done.10.refs_1_, bf16[8,1024]{1,0:T(8,128)(2,1)S(1)} %collective-permute-done.11.refs_2_, bf16[8,1024]{1,0:T(8,128)(2,1)S(1)} %collective-permute-done.12.refs_3_, ...), custom_call_target="tpu_custom_call" | custom-call | tf_op jit(solution)/shard_map/pallas_call | solution.py:319
  54.0 0.7 %reduce = bf16[32,1152]{1,0:T(8,128)(2,1)S(1)} reduce(bf16[32,1,1152]{2,0,1:T(8,128)(2,1)S(1)} %bitcast.5, bf16[]{:T(256)} %broadcast), dimensions={1}, to_apply=%copy.17.reduce_sub_computation | reduce | bytes 147458 | tf_op jit(solution)/shard_map/all_to_all | solution.py:435
  54.8 9.7 %all_to_all.11 = bf16[32,2,576]{2,1,0:T(2,128)(2,1)S(1)} all-to-all(bf16[32,2,576]{2,1,0:T(2,128)(2,1)S(1)} %reshape.6), channel_id=1, replica_groups=mesh['req'=8,'head'=4] {'req','head'}, dimensions={0} | all-to-all | bytes 147456 | tf_op jit(solution)/shard_map/all_to_all | solution.py:435
  64.6 0.8 %shard_map.150 = bf16[2,1024]{1,0:T(2,128)(2,1)} custom-call(bf16[32,1152]{1,0:T(8,128)(2,1)S(1)} %bitcast.6), custom_call_target="tpu_custom_call" | custom-call | tf_op jit(solution)/shard_map/pallas_call | solution.py:319
  (51 shorter events, 5.1 us)
Async XLA Ops:
  0.0 0.7 %copy-start.13 = (bf16[8,1024]{1,0:T(8,128)(2,1)S(1)}, bf16[8,1024]{1,0:T(8,128)(2,1)}, u32[]{:S(2)}) copy-start(bf16[8,1024]{1,0:T(8,128)(2,1)} %tokens_ref.1) | copy-start | bytes 49156
  0.7 0.7 %copy-start.18 = (s32[8]{0:T(128)S(1)}, s32[8]{0:T(128)}, u32[]{:S(2)}) copy-start(s32[8]{0:T(128)} %lengths_ref.1) | copy-start | bytes 100
  2.7 32.4 %copy-start.12 = (f32[2,1024]{1,0:T(2,128)S(1)}, f32[2,1024]{1,0:T(2,128)}, u32[]{:S(2)}) copy-start(f32[2,1024]{1,0:T(2,128)} %refs_6_.4) | copy-start | bytes 24580
  3.3 4.8 %collective-permute-start = (bf16[8,1152]{1,0:T(8,128)(2,1)S(1)}, bf16[8,1152]{1,0:T(8,128)(2,1)S(1)}, u32[]{:S(2)}, u32[]{:S(2)}) collective-permute-start(bf16[8,1152]{1,0:T(8,128)(2,1)S(1)} %shard_map.145), channel_id=1, source_target_pairs={{0,4},{4,0},{8,12},{12,8},{16,20},{20,16},{24,28},{28,24},{1,5},{5... | collective-permute-start | bytes 55304 | tf_op jit(solution)/shard_map/ppermute | solution.py:331
  8.0 6.1 %collective-permute-start.3 = (bf16[16,1152]{1,0:T(8,128)(2,1)S(1)}, bf16[16,1152]{1,0:T(8,128)(2,1)S(1)}, u32[]{:S(2)}, u32[]{:S(2)}) collective-permute-start(bf16[16,1152]{1,0:T(8,128)(2,1)S(1)} %pad_maximum_fusion.refs_2_), channel_id=1, source_target_pairs={{0,24},{4,28},{8,16},{12,20},{16,8},{20,12},{24,0},{28,4},{1,25},{... | collective-permute-start | bytes 110600 | tf_op jit(solution)/shard_map/ppermute | solution.py:331
  12.1 4.9 %collective-permute-start.2 = (bf16[16,1152]{1,0:T(8,128)(2,1)S(1)}, bf16[16,1152]{1,0:T(8,128)(2,1)S(1)}, u32[]{:S(2)}, u32[]{:S(2)}) collective-permute-start(bf16[16,1152]{1,0:T(8,128)(2,1)S(1)} %pad_maximum_fusion.refs_2_), channel_id=1, source_target_pairs={{0,16},{4,20},{8,24},{12,28},{16,0},{20,4},{24,8},{28,12},{1,17},{... | collective-permute-start | bytes 110600 | tf_op jit(solution)/shard_map/ppermute | solution.py:331
  12.1 4.9 %collective-permute-start.1 = (bf16[16,1152]{1,0:T(8,128)(2,1)S(1)}, bf16[16,1152]{1,0:T(8,128)(2,1)S(1)}, u32[]{:S(2)}, u32[]{:S(2)}) collective-permute-start(bf16[16,1152]{1,0:T(8,128)(2,1)S(1)} %pad_maximum_fusion.refs_2_), channel_id=1, source_target_pairs={{0,8},{4,12},{8,0},{12,4},{16,24},{20,28},{24,16},{28,20},{1,9},{5... | collective-permute-start | bytes 110600 | tf_op jit(solution)/shard_map/ppermute | solution.py:331
  17.0 3.4 %copy-start = (bf16[2,2,8,512,256]{4,3,2,1,0:T(8,128)(2,1)S(1)}, bf16[2,2,8,512,256]{4,3,2,1,0:T(8,128)(2,1)}, u32[]{:S(2)}) copy-start(bf16[2,2,8,512,256]{4,3,2,1,0:T(8,128)(2,1)} %refs_8_.4) | copy-start | bytes 25165828
  20.4 1.9 %copy-start.4 = (bf16[2,1024,768]{2,1,0:T(8,128)(2,1)S(1)}, bf16[2,1024,768]{2,1,0:T(8,128)(2,1)}, u32[]{:S(2)}) copy-start(bf16[2,1024,768]{2,1,0:T(8,128)(2,1)} %refs_10_.3) | copy-start | bytes 9437188
  22.3 1.2 %copy-start.6 = (bf16[2,256,1024]{2,1,0:T(8,128)(2,1)S(1)}, bf16[2,256,1024]{2,1,0:T(8,128)(2,1)}, u32[]{:S(2)}) copy-start(bf16[2,256,1024]{2,1,0:T(8,128)(2,1)} %refs_11_.3) | copy-start | bytes 3145732
  23.5 0.7 %copy-start.8 = (s32[8,512]{1,0:T(8,128)S(1)}, s32[8,512]{1,0:T(8,128)}, u32[]{:S(2)}) copy-start(s32[8,512]{1,0:T(8,128)} %refs_7_.6) | copy-start | bytes 49156
  24.2 0.7 %copy-start.10 = (f32[2,1024]{1,0:T(2,128)S(1)}, f32[2,1024]{1,0:T(2,128)}, u32[]{:S(2)}) copy-start(f32[2,1024]{1,0:T(2,128)} %refs_9_.3) | copy-start | bytes 24580
  24.9 0.7 %copy-start.14 = (f32[2,2,4]{2,1,0:T(2,128)S(1)}, f32[2,2,4]{2,1,0:T(2,128)}, u32[]{:S(2)}) copy-start(f32[2,2,4]{2,1,0:T(2,128)} %refs_12_.3) | copy-start | bytes 196
  25.6 0.7 %copy-start.16 = (s32[8]{0:T(128)S(1)}, s32[8]{0:T(128)}, u32[]{:S(2)}) copy-start(s32[8]{0:T(128)} %refs_4_.1) | copy-start | bytes 100
  26.9 8.2 %copy-start.2 = (bf16[2,2,1024,1024]{3,2,1,0:T(8,128)(2,1)S(1)}, bf16[2,2,1024,1024]{3,2,1,0:T(8,128)(2,1)}, u32[]{:S(2)}) copy-start(bf16[2,2,1024,1024]{3,2,1,0:T(8,128)(2,1)} %refs_7_.7) | copy-start | bytes 25165828
  26.9 15.8 %copy-start.5 = (bf16[2,1024,768]{2,1,0:T(8,128)(2,1)S(1)}, bf16[2,1024,768]{2,1,0:T(8,128)(2,1)}, u32[]{:S(2)}) copy-start(bf16[2,1024,768]{2,1,0:T(8,128)(2,1)} %refs_10_.3) | copy-start | bytes 9437188
  26.9 15.8 %copy-start.9 = (s32[8,512]{1,0:T(8,128)S(1)}, s32[8,512]{1,0:T(8,128)}, u32[]{:S(2)}) copy-start(s32[8,512]{1,0:T(8,128)} %refs_7_.6) | copy-start | bytes 49156
  26.9 15.8 %copy-start.11 = (f32[2,1024]{1,0:T(2,128)S(1)}, f32[2,1024]{1,0:T(2,128)}, u32[]{:S(2)}) copy-start(f32[2,1024]{1,0:T(2,128)} %refs_9_.3) | copy-start | bytes 24580
  26.9 15.8 %copy-start.15 = (f32[2,2,4]{2,1,0:T(2,128)S(1)}, f32[2,2,4]{2,1,0:T(2,128)}, u32[]{:S(2)}) copy-start(f32[2,2,4]{2,1,0:T(2,128)} %refs_12_.3) | copy-start | bytes 196
  31.2 11.5 %copy-start.1 = (bf16[2,2,8,512,256]{4,3,2,1,0:T(8,128)(2,1)S(1)}, bf16[2,2,8,512,256]{4,3,2,1,0:T(8,128)(2,1)}, u32[]{:S(2)}) copy-start(bf16[2,2,8,512,256]{4,3,2,1,0:T(8,128)(2,1)} %refs_8_.4) | copy-start | bytes 25165828
  31.2 3.4 %collective-permute-start.6 = (bf16[8,1024]{1,0:T(8,128)(2,1)S(1)}, bf16[8,1024]{1,0:T(8,128)(2,1)S(1)}, u32[]{:S(2)}, u32[]{:S(2)}) collective-permute-start(bf16[8,1024]{1,0:T(8,128)(2,1)S(1)} %get-tuple-element.13.refs_0_), channel_id=1, source_target_pairs={{0,3},{1,2},{2,1},{3,0},{4,7},{5,6},{6,5},{7,4},{8,11},{9,10},{10,... | collective-permute-start | bytes 49160 | tf_op jit(solution)/shard_map/ppermute | solution.py:331
  31.3 3.8 %collective-permute-start.5 = (bf16[8,1024]{1,0:T(8,128)(2,1)S(1)}, bf16[8,1024]{1,0:T(8,128)(2,1)S(1)}, u32[]{:S(2)}, u32[]{:S(2)}) collective-permute-start(bf16[8,1024]{1,0:T(8,128)(2,1)S(1)} %get-tuple-element.13.refs_0_), channel_id=1, source_target_pairs={{0,2},{1,3},{2,0},{3,1},{4,6},{5,7},{6,4},{7,5},{8,10},{9,11},{10,... | collective-permute-start | bytes 49160 | tf_op jit(solution)/shard_map/ppermute | solution.py:331
  32.8 2.3 %collective-permute-start.4 = (bf16[8,1024]{1,0:T(8,128)(2,1)S(1)}, bf16[8,1024]{1,0:T(8,128)(2,1)S(1)}, u32[]{:S(2)}, u32[]{:S(2)}) collective-permute-start(bf16[8,1024]{1,0:T(8,128)(2,1)S(1)} %get-tuple-element.13.refs_0_), channel_id=1, source_target_pairs={{0,1},{1,0},{2,3},{3,2},{4,5},{5,4},{6,7},{7,6},{8,9},{9,8},{10,11... | collective-permute-start | bytes 49160 | tf_op jit(solution)/shard_map/ppermute | solution.py:331
  35.1 2.2 %copy-start.3 = (bf16[2,1024,1024]{2,1,0:T(8,128)(2,1)S(1)}, bf16[2,1024,1024]{2,1,0:T(8,128)(2,1)}, u32[]{:S(2)}) copy-start(bf16[2,1024,1024]{2,1,0:T(8,128)(2,1)} %refs_8_.5) | copy-start | bytes 12582916
  38.3 13.5 %copy-start.17 = (s32[8]{0:T(128)S(1)}, s32[8]{0:T(128)}, u32[]{:S(2)}) copy-start(s32[8]{0:T(128)} %refs_4_.1) | copy-start | bytes 100
  38.3 3.2 %collective-permute-start.9 = (bf16[8,1024]{1,0:T(8,128)(2,1)S(1)}, bf16[8,1024]{1,0:T(8,128)(2,1)S(1)}, u32[]{:S(2)}, u32[]{:S(2)}) collective-permute-start(bf16[8,1024]{1,0:T(8,128)(2,1)S(1)} %get-tuple-element.15.refs_0_), channel_id=1, source_target_pairs={{0,3},{1,2},{2,1},{3,0},{4,7},{5,6},{6,5},{7,4},{8,11},{9,10},{10,... | collective-permute-start | bytes 49160 | tf_op jit(solution)/shard_map/ppermute | solution.py:331
  38.9 3.8 %collective-permute-start.8 = (bf16[8,1024]{1,0:T(8,128)(2,1)S(1)}, bf16[8,1024]{1,0:T(8,128)(2,1)S(1)}, u32[]{:S(2)}, u32[]{:S(2)}) collective-permute-start(bf16[8,1024]{1,0:T(8,128)(2,1)S(1)} %get-tuple-element.15.refs_0_), channel_id=1, source_target_pairs={{0,2},{1,3},{2,0},{3,1},{4,6},{5,7},{6,4},{7,5},{8,10},{9,11},{10,... | collective-permute-start | bytes 49160 | tf_op jit(solution)/shard_map/ppermute | solution.py:331
  40.3 2.4 %collective-permute-start.7 = (bf16[8,1024]{1,0:T(8,128)(2,1)S(1)}, bf16[8,1024]{1,0:T(8,128)(2,1)S(1)}, u32[]{:S(2)}, u32[]{:S(2)}) collective-permute-start(bf16[8,1024]{1,0:T(8,128)(2,1)S(1)} %get-tuple-element.15.refs_0_), channel_id=1, source_target_pairs={{0,1},{1,0},{2,3},{3,2},{4,5},{5,4},{6,7},{7,6},{8,9},{9,8},{10,11... | collective-permute-start | bytes 49160 | tf_op jit(solution)/shard_map/ppermute | solution.py:331
  42.7 1.2 %copy-start.7 = (bf16[2,256,1024]{2,1,0:T(8,128)(2,1)S(1)}, bf16[2,256,1024]{2,1,0:T(8,128)(2,1)}, u32[]{:S(2)}) copy-start(bf16[2,256,1024]{2,1,0:T(8,128)(2,1)} %refs_11_.3) | copy-start | bytes 3145732
  47.9 3.2 %collective-permute-start.12 = (bf16[8,1024]{1,0:T(8,128)(2,1)S(1)}, bf16[8,1024]{1,0:T(8,128)(2,1)S(1)}, u32[]{:S(2)}, u32[]{:S(2)}) collective-permute-start(bf16[8,1024]{1,0:T(8,128)(2,1)S(1)} %get-tuple-element.19.refs_0_), channel_id=1, source_target_pairs={{0,3},{1,2},{2,1},{3,0},{4,7},{5,6},{6,5},{7,4},{8,11},{9,10},{10,... | collective-permute-start | bytes 49160 | tf_op jit(solution)/shard_map/ppermute | solution.py:331
  48.0 3.8 %collective-permute-start.11 = (bf16[8,1024]{1,0:T(8,128)(2,1)S(1)}, bf16[8,1024]{1,0:T(8,128)(2,1)S(1)}, u32[]{:S(2)}, u32[]{:S(2)}) collective-permute-start(bf16[8,1024]{1,0:T(8,128)(2,1)S(1)} %get-tuple-element.19.refs_0_), channel_id=1, source_target_pairs={{0,2},{1,3},{2,0},{3,1},{4,6},{5,7},{6,4},{7,5},{8,10},{9,11},{10,... | collective-permute-start | bytes 49160 | tf_op jit(solution)/shard_map/ppermute | solution.py:331
  49.7 2.1 %collective-permute-start.10 = (bf16[8,1024]{1,0:T(8,128)(2,1)S(1)}, bf16[8,1024]{1,0:T(8,128)(2,1)S(1)}, u32[]{:S(2)}, u32[]{:S(2)}) collective-permute-start(bf16[8,1024]{1,0:T(8,128)(2,1)S(1)} %get-tuple-element.19.refs_0_), channel_id=1, source_target_pairs={{0,1},{1,0},{2,3},{3,2},{4,5},{5,4},{6,7},{7,6},{8,9},{9,8},{10,11... | collective-permute-start | bytes 49160 | tf_op jit(solution)/shard_map/ppermute | solution.py:331
  (3 other events, 2.0 us)

commit v2 on v1

v2 whole, which is shorter than its diff:
```python
import functools

import jax
import jax.numpy as jnp
import numpy as np
from jax import lax
from jax.experimental import pallas as pl
from jax.experimental.pallas import tpu as pltpu
from jax.sharding import PartitionSpec as P

HD = 64
LAYERS = 2
META = 128
LOW = 128
CHUNK = 128
NEG = -1e30
F32 = jnp.float32
BF16 = jnp.bfloat16

VMEM = pl.BlockSpec(memory_space=pltpu.VMEM)
HBM = pl.BlockSpec(memory_space=pltpu.HBM)
PARAMS = pltpu.CompilerParams(vmem_limit_bytes=16 * 2**20)


def iota(shape, dim):
    return lax.broadcasted_iota(jnp.int32, shape, dim)


def rms_scale(stream, gain_row):
    return stream * lax.rsqrt(jnp.mean(stream * stream, axis=-1, keepdims=True) + 1e-06) * gain_row


def copy_all(pairs, sems):
    copies = [pltpu.make_async_copy(src, dst, sems.at[i]) for i, (src, dst) in enumerate(pairs)]
    for copy in copies:
        copy.start()
    for copy in copies:
        copy.wait()


def pack_kernel(
    tokens_ref, lengths_ref, positions_ref, variates_ref, out_ref, length, position, variate, sems
):
    rows, width = tokens_ref.shape
    copy_all(
        [
            (lengths_ref, length),
            (positions_ref, position),
            (variates_ref, variate),
            (tokens_ref, out_ref.at[:, pl.ds(0, width)]),
        ],
        sems,
    )
    row, lane = iota((rows, META), 0), iota((rows, META), 1)
    kind = lane % (META // 2)
    whole = jnp.zeros((rows, META), jnp.int32)
    for i in range(rows):
        values = jnp.where(kind == 0, length[i], jnp.where(kind == 1, position[i], variate[i]))
        whole = jnp.where(row == i, values, whole)
    digit = jnp.where(lane < META // 2, whole // LOW, whole % LOW)
    out_ref[:, width:] = digit.astype(F32).astype(BF16)


def owner_kernel(
    share,
    after_ref,
    owner_ref,
    own_block_ref,
    *refs,
):
    count = (len(refs) - 6) // 2
    sources, (pick_ref, place_ref, flag_ref), outs = refs[:count], refs[count : count + 3], refs[
        count + 3 : -3
    ]
    owner, own_block, sems = refs[-3:]
    copies = [
        pltpu.make_async_copy(src, dst, sems.at[i])
        for i, (src, dst) in enumerate(
            [(owner_ref, owner), (own_block_ref, own_block)] + list(zip(sources, outs))
        )
    ]
    for copy in copies:
        copy.start()
    copies[0].wait()
    copies[1].wait()
    slots, total = pick_ref.shape
    devices = place_ref.shape[0]
    row, column = iota((slots, total), 0), iota((slots, total), 1)
    target, slot = iota((devices, slots), 0), iota((devices, slots), 1)
    flag_row, lane = iota((slots, META), 0), iota((slots, META), 1)
    pick = jnp.zeros((slots, total), F32)
    place = jnp.zeros((devices, slots), F32)
    flag = jnp.zeros((slots, META), F32)
    for s in range(slots):
        request = owner[s]
        source = ((request // slots) ^ own_block[0]) * slots + request % slots
        pick = jnp.where((row == s) & (column == source), 1.0, pick)
        place = jnp.where((slot == s) & (target == request // share), 1.0, place)
        flag = jnp.where((flag_row == s) & (lane == request % share), 1.0, flag)
    pick_ref[...] = pick.astype(BF16)
    place_ref[...] = place.astype(BF16)
    flag_ref[...] = flag.astype(BF16)
    for copy in copies[2:]:
        copy.wait()


def bring_kernel(parts, after_ref, *refs):
    count = len(parts)
    copy_all(
        [(refs[i].at[parts[i]], refs[count + i]) for i in range(count)], refs[2 * count]
    )


def attention(
    layer,
    stream,
    facts,
    cos,
    sin,
    variates_ref,
    kv_ref,
    gain_ref,
    qkv_ref,
    out_w_ref,
    bias_ref,
    scores,
    mixed,
    part_ref,
):
    slots, cap = variates_ref.shape
    width = kv_ref.shape[-1]
    heads = width // HD
    rows = heads * slots

    lengths = facts[:, 0:1]
    variate = facts[:, 2:3]
    longer = jnp.sum((lengths > CHUNK).astype(jnp.int32))

    normed = rms_scale(stream, gain_ref[layer : layer + 1, :]).astype(BF16)
    projected = jnp.dot(normed, qkv_ref[layer], preferred_element_type=F32)

    lane = iota((slots, 128), 1)
    front = lane % HD < HD // 2
    pieces = []
    for j in range(projected.shape[1] // 128):
        u = projected[:, j * 128 : (j + 1) * 128]
        turned = jnp.where(front, -pltpu.roll(u, 96, 1), pltpu.roll(u, 32, 1))
        is_value = (lane + j * 128) % (3 * HD) >= 2 * HD
        pieces.append(jnp.where(is_value, u, u * cos + turned * sin).astype(BF16).astype(F32))
    turned_all = jnp.concatenate(pieces, axis=1)

    column = iota((slots, width), 1)
    of_head = [column // HD == h for h in range(heads)]
    step = 2 * HD
    query = [
        jnp.where(of_head[h], turned_all[:, h * step : h * step + width], 0.0) for h in range(heads)
    ]
    query_all = jnp.concatenate(query, axis=0).astype(BF16)

    score_dims = (((1,), (1,)), ((), ()))
    keys = kv_ref[0, :, :CHUNK, :].reshape(slots * CHUNK, width)
    raw = lax.dot_general(query_all, keys, score_dims, preferred_element_type=F32)
    row_slot = iota((rows, CHUNK), 0) % slots
    total = raw[:, :CHUNK]
    for s in range(1, slots):
        total = jnp.where(row_slot == s, raw[:, s * CHUNK : (s + 1) * CHUNK], total)
    scores[:, :CHUNK] = total
    rest_slot = iota((rows, cap - CHUNK), 0) % slots

    @pl.loop(0, longer)
    def _(s):
        more = lax.dot_general(
            query_all, kv_ref[0, s, CHUNK:, :], score_dims, preferred_element_type=F32
        )
        scores[:, CHUNK:] = jnp.where(rest_slot == s, more, scores[:, CHUNK:])

    next_keys = jnp.concatenate([turned_all[:, HD:], jnp.zeros((slots, HD), F32)], axis=1)
    own_score = [
        jnp.sum(query[h] * next_keys[:, h * step : h * step + width], axis=1, keepdims=True) * 0.125
        + bias_ref[layer, 0:1, h : h + 1]
        for h in range(heads)
    ]
    same = variates_ref[...].astype(F32) == variate
    live = iota((slots, cap), 1).astype(F32) < lengths
    probs = []
    own_prob = []
    for h in range(heads):
        block = scores[h * slots : (h + 1) * slots, :] * 0.125
        block = block + jnp.where(
            same, bias_ref[layer, 0:1, h : h + 1], bias_ref[layer, 1:2, h : h + 1]
        )
        block = jnp.where(live, block, NEG)
        top = jnp.maximum(jnp.max(block, axis=1, keepdims=True), own_score[h])
        weight = jnp.exp(block - top)
        own_weight = jnp.exp(own_score[h] - top)
        share = 1.0 / (jnp.sum(weight, axis=1, keepdims=True) + own_weight)
        probs.append(weight * share)
        own_prob.append((own_weight * share).astype(BF16).astype(F32))
    probs_all = jnp.concatenate(probs, axis=0).astype(BF16)
    first = probs_all[:, :CHUNK]
    spread = jnp.concatenate(
        [jnp.where(row_slot == s, first, jnp.zeros_like(first)) for s in range(slots)], axis=1
    )
    values = kv_ref[1, :, :CHUNK, :].reshape(slots * CHUNK, width)
    mixed[...] = jnp.dot(spread, values, preferred_element_type=F32)
    rest = probs_all[:, CHUNK:]

    @pl.loop(0, longer)
    def _(s):
        mine = jnp.where(rest_slot == s, rest, jnp.zeros_like(rest))
        mixed[...] += jnp.dot(mine, kv_ref[1, s, CHUNK:, :], preferred_element_type=F32)

    attended = jnp.zeros((slots, width), F32)
    for h in range(heads):
        value_new = turned_all[:, (h + 1) * step : (h + 1) * step + width]
        attended = jnp.where(
            of_head[h], mixed[h * slots : (h + 1) * slots, :] + own_prob[h] * value_new, attended
        )
    part_ref[...] = jnp.dot(
        attended.astype(BF16), out_w_ref[layer], preferred_element_type=F32
    ).astype(BF16)


def first_attention_kernel(block_count, *refs):
    (
        pick_ref,
        frequency_ref,
        variates_ref,
        kv_ref,
        gain_ref,
        qkv_ref,
        out_w_ref,
        bias_ref,
        part_ref,
        stream_ref,
        facts_ref,
        turn_ref,
        scores,
        mixed,
    ) = refs[block_count:]
    gathered = jnp.concatenate([ref[...] for ref in refs[:block_count]], axis=0)
    width = stream_ref.shape[1]
    picked = jnp.dot(pick_ref[...], gathered, preferred_element_type=F32)
    stream = picked[:, :width]
    digits = picked[:, width:]
    facts = digits * float(LOW) + pltpu.roll(digits, META // 2, 1)
    stream_ref[...] = stream
    facts_ref[...] = facts
    angle = facts[:, 1:2] * frequency_ref[...]
    cos, sin = jnp.cos(angle), jnp.sin(angle)
    turn_ref[:, :128] = cos
    turn_ref[:, 128:] = sin
    attention(
        0, stream, facts, cos, sin, variates_ref, kv_ref, gain_ref, qkv_ref, out_w_ref, bias_ref,
        scores, mixed, part_ref,
    )


def next_attention_kernel(layer, part_count, *refs):
    (
        old_ref,
        facts_ref,
        turn_ref,
        variates_ref,
        kv_ref,
        gain_ref,
        qkv_ref,
        out_w_ref,
        bias_ref,
        part_ref,
        stream_ref,
        scores,
        mixed,
    ) = refs[part_count:]
    stream = old_ref[...]
    for ref in refs[:part_count]:
        stream = stream + ref[...].astype(F32)
    stream_ref[...] = stream
    attention(
        layer, stream, facts_ref[...], turn_ref[:, :128], turn_ref[:, 128:], variates_ref, kv_ref,
        gain_ref, qkv_ref, out_w_ref, bias_ref, scores, mixed, part_ref,
    )


def feed_forward(layer, part_refs, old_ref, gain_ref, gate_up_ref, down_ref):
    stream = old_ref[...]
    for ref in part_refs:
        stream = stream + ref[...].astype(F32)
    normed = rms_scale(stream, gain_ref[layer : layer + 1, :]).astype(BF16)
    gate = jnp.dot(normed, gate_up_ref[0], preferred_element_type=F32)
    up = jnp.dot(normed, gate_up_ref[1], preferred_element_type=F32)
    hidden = (gate / (1.0 + jnp.exp(-gate)) * up).astype(BF16)
    return stream, jnp.dot(hidden, down_ref[...], preferred_element_type=F32)


def feed_forward_kernel(layer, part_count, *refs):
    old_ref, gain_ref, gate_up_ref, down_ref, part_ref, stream_ref = refs[part_count:]
    stream, part = feed_forward(layer, refs[:part_count], old_ref, gain_ref, gate_up_ref, down_ref)
    stream_ref[...] = stream
    part_ref[...] = part.astype(BF16)


def last_feed_forward_kernel(layer, part_count, *refs):
    place_ref, flag_ref, old_ref, gain_ref, gate_up_ref, down_ref, send_ref = refs[part_count:]
    stream, part = feed_forward(layer, refs[:part_count], old_ref, gain_ref, gate_up_ref, down_ref)
    rows = (part + stream * (1.0 / part_count)).astype(BF16)
    half = rows.shape[1] // 2
    for i in range(2):
        payload = jnp.concatenate([rows[:, i * half : (i + 1) * half], flag_ref[...]], axis=1)
        spread = jnp.dot(place_ref[...], payload, preferred_element_type=F32)
        send_ref[:, i, :] = spread.astype(BF16)


def place_kernel(received_ref, out_ref):
    share, width = out_ref.shape
    half = width // 2
    for i in range(2):
        rows = lax.dot_general(
            received_ref[:, i, half:],
            received_ref[:, i, :half],
            (((0,), (0,)), ((), ())),
            preferred_element_type=F32,
        )
        out_ref[:, i * half : (i + 1) * half] = rows[:share, :].astype(BF16)


def call(kernel, operands, outs, scratch=()):
    specs, arrays = zip(*operands)
    return pl.pallas_call(
        kernel,
        out_shape=[pltpu.VMEM(shape, dtype) for shape, dtype in outs],
        in_specs=list(specs),
        out_specs=[VMEM] * len(outs),
        scratch_shapes=list(scratch),
        compiler_params=PARAMS,
    )(*arrays)


def bring(after, sources):
    return call(
        functools.partial(bring_kernel, [layer for _, layer in sources]),
        [(HBM, after)] + [(HBM, array) for array, _ in sources],
        [
            (tuple(n for n, i in zip(array.shape, index) if i is None), array.dtype)
            for array, index in ((a, i + (None,) * (a.ndim - len(i))) for a, i in sources)
        ],
        [pltpu.SemaphoreType.DMA((len(sources),))],
    )


def swap(array, axis, mask):
    count = lax.axis_size(axis)
    return lax.ppermute(array, axis, [(i, i ^ mask) for i in range(count)])


def gather_blocks(block, axis):
    count = lax.axis_size(axis)
    pair = jnp.concatenate([block, swap(block, axis, 1)], axis=0)
    blocks = [pair]
    reach = 2
    while reach < count:
        span = min(4, count // reach)
        held = blocks[0] if len(blocks) == 1 else jnp.concatenate(blocks, axis=0)
        blocks = blocks + [swap(held, axis, reach * k) for k in range(1, span)]
        reach *= span
    return blocks


def per_device(
    tokens,
    lengths,
    slot_owner,
    positions,
    variates,
    cache_variates,
    kv_cache,
    attn_gain,
    ffn_gain,
    qkv_weight,
    out_weight,
    gate_up_weight,
    down_weight,
    variate_bias,
):
    slots, width = tokens.shape
    cap, local_width = kv_cache.shape[3:]
    head_count = lax.axis_size("head")
    devices = lax.axis_size("req") * head_count
    share = slots // head_count
    local_heads = local_width // HD

    total = slots * lax.axis_size("req")
    whole_row = [pltpu.SMEM((slots,), jnp.int32)] * 3
    (packed,) = call(
        pack_kernel,
        [(HBM, tokens), (HBM, lengths), (HBM, positions), (HBM, variates)],
        [((slots, width + META), BF16)],
        whole_row + [pltpu.SemaphoreType.DMA((4,))],
    )
    exponent = -2.0 * (np.arange(128) % (HD // 2)) / HD
    frequency = jnp.asarray((10000.0**exponent).astype(np.float32)[None, :])
    own_block = lax.axis_index("req").reshape(1)
    sources = [
        cache_variates, attn_gain, ffn_gain, qkv_weight, out_weight, variate_bias, frequency,
    ]
    pick, place, flag, *held = call(
        functools.partial(owner_kernel, share),
        [(HBM, packed), (HBM, slot_owner), (HBM, own_block)] + [(HBM, x) for x in sources],
        [((slots, total), BF16), ((devices, slots), BF16), ((slots, META), BF16)]
        + [(x.shape, x.dtype) for x in sources],
        [
            pltpu.SMEM((slots,), jnp.int32),
            pltpu.SMEM((1,), jnp.int32),
            pltpu.SemaphoreType.DMA((len(sources) + 2,)),
        ],
    )
    cache_variates, attn_gain, ffn_gain, qkv_weight, out_weight, variate_bias, frequency = held
    blocks = gather_blocks(packed, "req")
    kv, gate_up, down = bring(
        blocks[0], [(kv_cache, (0,)), (gate_up_weight, (0,)), (down_weight, (0,))]
    )

    scratch = [
        pltpu.VMEM((local_heads * slots, cap), F32),
        pltpu.VMEM((local_heads * slots, local_width), F32),
    ]
    stream_type = ((slots, width), F32)
    part_type = ((slots, width), BF16)

    def exchange(part):
        return [part] + [swap(part, "head", k) for k in range(1, head_count)]

    def on_chip(*arrays):
        return [(VMEM, x) for x in arrays]

    part, stream, facts, turn = call(
        functools.partial(first_attention_kernel, len(blocks)),
        on_chip(*blocks, pick, frequency, cache_variates, kv, attn_gain)
        + on_chip(qkv_weight, out_weight, variate_bias),
        [part_type, stream_type, ((slots, META), F32), ((slots, 256), F32)],
        scratch,
    )
    for layer in range(LAYERS):
        last = layer == LAYERS - 1
        if layer:
            (kv,) = next_kv
            part, stream = call(
                functools.partial(next_attention_kernel, layer, head_count),
                on_chip(*parts, stream, facts, turn, cache_variates, kv, attn_gain)
                + on_chip(qkv_weight, out_weight, variate_bias),
                [part_type, stream_type],
                scratch,
            )
        parts = exchange(part)
        if not last:
            next_kv = bring(part, [(kv_cache, (layer + 1,))])
            part, stream = call(
                functools.partial(feed_forward_kernel, layer, head_count),
                on_chip(*parts, stream, ffn_gain, gate_up, down),
                [part_type, stream_type],
            )
            parts = exchange(part)
            gate_up, down = bring(
                part, [(gate_up_weight, (layer + 1,)), (down_weight, (layer + 1,))]
            )
        else:
            (send,) = call(
                functools.partial(last_feed_forward_kernel, layer, head_count),
                on_chip(*parts, place, flag, stream, ffn_gain, gate_up, down),
                [((devices, 2, width // 2 + META), BF16)],
            )
    received = lax.all_to_all(send, ("req", "head"), 0, 0, tiled=True)
    return pl.pallas_call(
        place_kernel,
        out_shape=jax.ShapeDtypeStruct((share, width), BF16),
        in_specs=[VMEM],
        out_specs=VMEM,
        compiler_params=PARAMS,
    )(received)


def solution(mesh):
    return jax.shard_map(
        per_device,
        mesh=mesh,
        in_specs=(
            P("req", None),
            P("req"),
            P("req"),
            P("req"),
            P("req"),
            P("req", None),
            P(None, None, "req", None, "head"),
            P(),
            P(),
            P(None, None, "head"),
            P(None, "head", None),
            P(None, None, None, "head"),
            P(None, "head", None),
            P(None, None, "head"),
        ),
        out_specs=P(("req", "head"), None),
        check_vma=False,
    )
```

time: 66.4 us -> 61.2 us (0.922)
  waiting for transfers between devices: 12.2 us -> 7.22 us
  blocking collectives: 9.65 us -> 12.8 us
  Pallas kernels: 12.3 us -> 9.8 us
    ppermute x13, waiting for transfers between devices: 12.2 us -> 7.22 us  [swap(): return lax.ppermute(array, axis, [(i, i ^ mask) for i in range(count)])]
    all_to_all x1, blocking collectives: 9.65 us -> 12.8 us  [per_device(): received = lax.all_to_all(send, ('req', 'head'), 0, 0, tiled=True)]
    pallas_call x6 -> x10, Pallas kernels: 12.3 us -> 9.8 us  [the longest x9 8.89 us: call(): pl.pallas_call(kernel, out_shape=[pltpu.VMEM(shape, dtype) for shape, dty...]
    unnamed x47 -> x36, local copies, waits for them, and re-layouts: 16.3 us -> 17 us
  transfers between devices with their start and end apart: 13 -> 13, of which waited for: 9 -> 7; matrix products, arithmetic and copies ran while one was open for 0% -> 0% of each run, Pallas kernels for 0% -> 4%
where the time goes in v2:
time: 61.2 us; the launch traced here: 60.7 us
  local copies, waits for them, and re-layouts  17 us (28%)
  starting transfers between devices  13.8 us (23%)
  blocking collectives  12.8 us (21%)
  Pallas kernels  9.8 us (16%)
  waiting for transfers between devices  7.22 us (12%)
    unnamed x36, local copies, waits for them, and re-layouts  17 us
    ppermute x13, starting transfers between devices, swap(): return lax.ppermute(array, axis, [(i, i ^ mask) for i in range(count)])  13.8 us
    all_to_all x1, blocking collectives, per_device(): received = lax.all_to_all(send, ('req', 'head'), 0, 0, tiled=True)  12.8 us
    pallas_call x9, Pallas kernels, call(): pl.pallas_call(kernel, out_shape=[pltpu.VMEM(shape, dtype) for shape, dty...  8.89 us
    ppermute x13, waiting for transfers between devices, swap(): return lax.ppermute(array, axis, [(i, i ^ mask) for i in range(count)])  7.22 us
  transfers between devices with their start and end apart: 13, of which 7 were waited for; matrix products, arithmetic and copies ran while one was open for 0% of the time, Pallas kernels for 4%

profile of v2, /device:TPU:0, one launch (start us, length us, event | category | flops | bytes accessed | tf_op | source)
XLA Modules:
  0.0 60.7 jit_solution(3960491145897230274)
XLA Ops:
  0.0 0.7 %copy-done.7 = bf16[8,1024]{1,0:T(8,128)(2,1)S(1)} copy-done((bf16[8,1024]{1,0:T(8,128)(2,1)S(1)}, bf16[8,1024]{1,0:T(8,128)(2,1)}, u32[]{:S(2)}) %copy-start.7) | copy-done | bytes 16408
  0.7 0.7 %copy-done.11 = s32[8]{0:T(128)S(1)} copy-done((s32[8]{0:T(128)S(1)}, s32[8]{0:T(128)}, u32[]{:S(2)}) %copy-start.11) | copy-done | bytes 56
  1.4 0.7 %copy-done.12 = s32[8]{0:T(128)S(1)} copy-done((s32[8]{0:T(128)S(1)}, s32[8]{0:T(128)}, u32[]{:S(2)}) %copy-start.12) | copy-done | bytes 56
  2.0 0.7 %copy-done.13 = s32[8]{0:T(128)S(1)} copy-done((s32[8]{0:T(128)S(1)}, s32[8]{0:T(128)}, u32[]{:S(2)}) %copy-start.13) | copy-done | bytes 56
  3.3 3.0 %collective-permute-start = (bf16[8,1152]{1,0:T(8,128)(2,1)S(1)}, bf16[8,1152]{1,0:T(8,128)(2,1)S(1)}, u32[]{:S(2)}, u32[]{:S(2)}) collective-permute-start(bf16[8,1152]{1,0:T(8,128)(2,1)S(1)} %shard_map.145.after_ref), channel_id=1, source_target_pairs={{0,4},{4,0},{8,12},{12,8},{16,20},{20,16},{24,28},{28,24},{1,5},{5... | collective-permute-start | bytes 55304 | tf_op jit(solution)/shard_map/ppermute | solution.py:353
  6.3 1.7 %collective-permute-done = bf16[8,1152]{1,0:T(8,128)(2,1)S(1)} collective-permute-done((bf16[8,1152]{1,0:T(8,128)(2,1)S(1)}, bf16[8,1152]{1,0:T(8,128)(2,1)S(1)}, u32[]{:S(2)}, u32[]{:S(2)}) %collective-permute-start) | collective-permute-done | bytes 18464 | tf_op jit(solution)/shard_map/ppermute | solution.py:353
  8.1 4.1 %collective-permute-start.3 = (bf16[16,1152]{1,0:T(8,128)(2,1)S(1)}, bf16[16,1152]{1,0:T(8,128)(2,1)S(1)}, u32[]{:S(2)}, u32[]{:S(2)}) collective-permute-start(bf16[16,1152]{1,0:T(8,128)(2,1)S(1)} %pad_maximum_fusion.after_ref.refs_0_), channel_id=1, source_target_pairs={{0,24},{4,28},{8,16},{12,20},{16,8},{20,12},{24,0},{28,4},{1,25},{... | collective-permute-start | bytes 110600 | tf_op jit(solution)/shard_map/ppermute | solution.py:353
  12.8 2.0 %copy-done.4 = bf16[2,1024,768]{2,1,0:T(8,128)(2,1)S(1)} copy-done((bf16[2,1024,768]{2,1,0:T(8,128)(2,1)S(1)}, bf16[2,1024,768]{2,1,0:T(8,128)(2,1)}, u32[]{:S(2)}) %copy-start.4) | copy-done | bytes 3145752
  14.9 1.4 %copy-done.5 = bf16[2,256,1024]{2,1,0:T(8,128)(2,1)S(1)} copy-done((bf16[2,256,1024]{2,1,0:T(8,128)(2,1)S(1)}, bf16[2,256,1024]{2,1,0:T(8,128)(2,1)}, u32[]{:S(2)}) %copy-start.5) | copy-done | bytes 1048600
  16.2 0.7 %copy-done.6 = s32[8,512]{1,0:T(8,128)S(1)} copy-done((s32[8,512]{1,0:T(8,128)S(1)}, s32[8,512]{1,0:T(8,128)}, u32[]{:S(2)}) %copy-start.6) | copy-done | bytes 16408
  17.0 0.7 %copy-done.8 = f32[2,1024]{1,0:T(2,128)S(1)} copy-done((f32[2,1024]{1,0:T(2,128)S(1)}, f32[2,1024]{1,0:T(2,128)}, u32[]{:S(2)}) %copy-start.8) | copy-done | bytes 8216
  17.7 0.7 %copy-done.9 = f32[2,1024]{1,0:T(2,128)S(1)} copy-done((f32[2,1024]{1,0:T(2,128)S(1)}, f32[2,1024]{1,0:T(2,128)}, u32[]{:S(2)}) %copy-start.9) | copy-done | bytes 8216
  18.4 0.7 %copy-done.10 = f32[2,2,4]{2,1,0:T(2,128)S(1)} copy-done((f32[2,2,4]{2,1,0:T(2,128)S(1)}, f32[2,2,4]{2,1,0:T(2,128)}, u32[]{:S(2)}) %copy-start.10) | copy-done | bytes 88
  19.0 0.7 %copy-done.14 = s32[8]{0:T(128)S(1)} copy-done((s32[8]{0:T(128)S(1)}, s32[8]{0:T(128)}, u32[]{:S(2)}) %copy-start.14) | copy-done | bytes 56
  20.4 0.8 %shard_map.146 = (bf16[8,64]{1,0:T(8,128)(2,1)S(1)}, bf16[32,8]{1,0:T(8,128)(2,1)S(1)}, bf16[8,128]{1,0:T(8,128)(2,1)S(1)}, s32[8,512]{1,0:T(8,128)S(1)}, f32[2,...) custom-call(bf16[8,1152]{1,0:T(8,128)(2,1)S(1)} %shard_map.145.after, ...), custom_call_target="tpu_custom_call" | custom-call | tf_op jit(solution)/shard_map/pallas_call | solution.py:329
  21.1 3.4 %copy-done = bf16[2,2,8,512,256]{4,3,2,1,0:T(8,128)(2,1)S(1)} copy-done((bf16[2,2,8,512,256]{4,3,2,1,0:T(8,128)(2,1)S(1)}, bf16[2,2,8,512,256]{4,3,2,1,0:T(8,128)(2,1)}, u32[]{:S(2)}) %copy-start) | copy-done | bytes 8388632
  24.5 3.4 %copy-done.2 = bf16[2,2,1024,1024]{3,2,1,0:T(8,128)(2,1)S(1)} copy-done((bf16[2,2,1024,1024]{3,2,1,0:T(8,128)(2,1)S(1)}, bf16[2,2,1024,1024]{3,2,1,0:T(8,128)(2,1)}, u32[]{:S(2)}) %copy-start.2) | copy-done | bytes 8388632
  27.9 0.7 %shard_map.147 = (bf16[2,8,512,256]{3,2,1,0:T(8,128)(2,1)S(1)}, bf16[2,1024,1024]{2,1,0:T(8,128)(2,1)S(1)}, bf16[1024,1024]{1,0:T(8,128)(2,1)S(1)}) custom-call(bf16[16,1152]{1,0:T(8,128)(2,1)S(1)} %pad_maximum_fusion.after_ref.refs_0_, bf16[2,2,8,512,256]{4,3,2,1,0:T(8,128)(2,1)S(1)} %copy-done, bf16[2,2,1024,1024]{3,2,1,0:T(8,128)(2,1)S(1)} %copy-done.2, ...), custom_call_target="tpu_custom_call" | custom-call | tf_op jit(solution)/shard_map/pallas_call | solution.py:329
  28.7 2.0 %shard_map.148 = (bf16[8,1024]{1,0:T(8,128)(2,1)S(1)}, f32[8,1024]{1,0:T(8,128)S(1)}, f32[8,128]{1,0:T(8,128)S(1)}, f32[8,256]{1,0:T(8,128)S(1)}) custom-call(bf16[16,1152]{1,0:T(8,128)(2,1)S(1)} %pad_maximum_fusion.after_ref.refs_0_, bf16[16,1152]{1,0:T(8,128)(2,1)S(1)} %collective-permute-done.1.refs_1_, ...), custom_call_target="tpu_custom_call" | custom-call | tf_op jit(solution)/shard_map/pallas_call | solution.py:329
  30.7 1.7 %collective-permute-start.5 = (bf16[8,1024]{1,0:T(8,128)(2,1)S(1)}, bf16[8,1024]{1,0:T(8,128)(2,1)S(1)}, u32[]{:S(2)}, u32[]{:S(2)}) collective-permute-start(bf16[8,1024]{1,0:T(8,128)(2,1)S(1)} %get-tuple-element.36.refs_0_.after_ref), channel_id=1, source_target_pairs={{0,2},{1,3},{2,0},{3,1},{4,6},{5,7},{6,4},{7,5},{8,10},{9,11},{10,... | collective-permute-start | bytes 49160 | tf_op jit(solution)/shard_map/ppermute | solution.py:353
  32.6 1.3 %collective-permute-done.6.refs_3_ = bf16[8,1024]{1,0:T(8,128)(2,1)S(1)} collective-permute-done((bf16[8,1024]{1,0:T(8,128)(2,1)S(1)}, bf16[8,1024]{1,0:T(8,128)(2,1)S(1)}, u32[]{:S(2)}, u32[]{:S(2)}) %collective-permute-start.6) | collective-permute-done | bytes 16416 | tf_op jit(solution)/shard_map/ppermute | solution.py:353
  34.5 1.0 %shard_map.149 = (bf16[8,1024]{1,0:T(8,128)(2,1)S(1)}, f32[8,1024]{1,0:T(8,128)S(1)}) custom-call(bf16[8,1024]{1,0:T(8,128)(2,1)S(1)} %get-tuple-element.36.refs_0_.after_ref, bf16[8,1024]{1,0:T(8,128)(2,1)S(1)} %collective-permute-done.4.refs_1_, bf16[8,1024]{1,0:T(8,128)(2,1)S(1)} %collective-permute-done.5.refs_2_, ...), custom_call_target="tpu_custom_call" | custom-call | tf_op jit(solution)/shard_map/pallas_call | solution.py:329
  35.5 0.8 %collective-permute-start.9 = (bf16[8,1024]{1,0:T(8,128)(2,1)S(1)}, bf16[8,1024]{1,0:T(8,128)(2,1)S(1)}, u32[]{:S(2)}, u32[]{:S(2)}) collective-permute-start(bf16[8,1024]{1,0:T(8,128)(2,1)S(1)} %get-tuple-element.41.refs_0_.after_ref), channel_id=1, source_target_pairs={{0,3},{1,2},{2,1},{3,0},{4,7},{5,6},{6,5},{7,4},{8,11},{9,10},{10,... | collective-permute-start | bytes 49160 | tf_op jit(solution)/shard_map/ppermute | solution.py:353
  36.3 1.5 %collective-permute-start.8 = (bf16[8,1024]{1,0:T(8,128)(2,1)S(1)}, bf16[8,1024]{1,0:T(8,128)(2,1)S(1)}, u32[]{:S(2)}, u32[]{:S(2)}) collective-permute-start(bf16[8,1024]{1,0:T(8,128)(2,1)S(1)} %get-tuple-element.41.refs_0_.after_ref), channel_id=1, source_target_pairs={{0,2},{1,3},{2,0},{3,1},{4,6},{5,7},{6,4},{7,5},{8,10},{9,11},{10,... | collective-permute-start | bytes 49160 | tf_op jit(solution)/shard_map/ppermute | solution.py:353
  38.0 0.7 %collective-permute-done.9.refs_3_ = bf16[8,1024]{1,0:T(8,128)(2,1)S(1)} collective-permute-done((bf16[8,1024]{1,0:T(8,128)(2,1)S(1)}, bf16[8,1024]{1,0:T(8,128)(2,1)S(1)}, u32[]{:S(2)}, u32[]{:S(2)}) %collective-permute-start.9) | collective-permute-done | bytes 16416 | tf_op jit(solution)/shard_map/ppermute | solution.py:353
  38.7 1.4 %collective-permute-done.8.refs_2_ = bf16[8,1024]{1,0:T(8,128)(2,1)S(1)} collective-permute-done((bf16[8,1024]{1,0:T(8,128)(2,1)S(1)}, bf16[8,1024]{1,0:T(8,128)(2,1)S(1)}, u32[]{:S(2)}, u32[]{:S(2)}) %collective-permute-start.8) | collective-permute-done | bytes 16416 | tf_op jit(solution)/shard_map/ppermute | solution.py:353
  40.1 1.9 %shard_map.151 = (bf16[8,1024]{1,0:T(8,128)(2,1)S(1)}, f32[8,1024]{1,0:T(8,128)S(1)}) custom-call(bf16[8,1024]{1,0:T(8,128)(2,1)S(1)} %get-tuple-element.41.refs_0_.after_ref, bf16[8,1024]{1,0:T(8,128)(2,1)S(1)} %collective-permute-done.7.refs_1_, bf16[8,1024]{1,0:T(8,128)(2,1)S(1)} %collective-permute-done.8.refs_2_, ...), custom_call_target="tpu_custom_call" | custom-call | tf_op jit(solution)/shard_map/pallas_call | solution.py:329
  42.0 1.8 %collective-permute-start.11 = (bf16[8,1024]{1,0:T(8,128)(2,1)S(1)}, bf16[8,1024]{1,0:T(8,128)(2,1)S(1)}, u32[]{:S(2)}, u32[]{:S(2)}) collective-permute-start(bf16[8,1024]{1,0:T(8,128)(2,1)S(1)} %get-tuple-element.45.refs_0_), channel_id=1, source_target_pairs={{0,2},{1,3},{2,0},{3,1},{4,6},{5,7},{6,4},{7,5},{8,10},{9,11},{10,... | collective-permute-start | bytes 49160 | tf_op jit(solution)/shard_map/ppermute | solution.py:353
  44.4 0.8 %collective-permute-done.12.refs_3_ = bf16[8,1024]{1,0:T(8,128)(2,1)S(1)} collective-permute-done((bf16[8,1024]{1,0:T(8,128)(2,1)S(1)}, bf16[8,1024]{1,0:T(8,128)(2,1)S(1)}, u32[]{:S(2)}, u32[]{:S(2)}) %collective-permute-start.12) | collective-permute-done | bytes 16416 | tf_op jit(solution)/shard_map/ppermute | solution.py:353
  45.8 1.2 %shard_map.153 = bf16[32,2,640]{2,1,0:T(2,128)(2,1)S(1)} custom-call(bf16[8,1024]{1,0:T(8,128)(2,1)S(1)} %get-tuple-element.45.refs_0_, bf16[8,1024]{1,0:T(8,128)(2,1)S(1)} %collective-permute-done.10.refs_1_, bf16[8,1024]{1,0:T(8,128)(2,1)S(1)} %collective-permute-done.11.refs_2_, bf16[8,1024]{1,0:T(8,128)(2,1)S(1)} %collective-permute-done.12.refs_3_, ...), custom_call_target="tpu_custom_call" | custom-call | tf_op jit(solution)/shard_map/pallas_call | solution.py:329
  47.0 12.8 %all_to_all.5.received_ref = bf16[32,2,640]{2,1,0:T(2,128)(2,1)S(1)} all-to-all(bf16[32,2,640]{2,1,0:T(2,128)(2,1)S(1)} %shard_map.153), channel_id=1, replica_groups=mesh['req'=8,'head'=4] {'req','head'}, dimensions={0} | all-to-all | bytes 163840 | tf_op jit(solution)/shard_map/all_to_all | solution.py:472
  59.8 0.9 %shard_map.154 = bf16[2,1024]{1,0:T(2,128)(2,1)} custom-call(bf16[32,2,640]{2,1,0:T(2,128)(2,1)S(1)} %all_to_all.5.received_ref), custom_call_target="tpu_custom_call" | custom-call | tf_op jit(solution)/shard_map/pallas_call | solution.py:473
  (43 shorter events, 4.2 us)
Async XLA Ops:
  0.0 0.7 %copy-start.7 = (bf16[8,1024]{1,0:T(8,128)(2,1)S(1)}, bf16[8,1024]{1,0:T(8,128)(2,1)}, u32[]{:S(2)}) copy-start(bf16[8,1024]{1,0:T(8,128)(2,1)} %tokens_ref.1) | copy-start | bytes 49156
  0.7 0.7 %copy-start.11 = (s32[8]{0:T(128)S(1)}, s32[8]{0:T(128)}, u32[]{:S(2)}) copy-start(s32[8]{0:T(128)} %lengths_ref.1) | copy-start | bytes 100
  1.4 0.7 %copy-start.12 = (s32[8]{0:T(128)S(1)}, s32[8]{0:T(128)}, u32[]{:S(2)}) copy-start(s32[8]{0:T(128)} %positions_ref.1) | copy-start | bytes 100
  2.0 0.7 %copy-start.13 = (s32[8]{0:T(128)S(1)}, s32[8]{0:T(128)}, u32[]{:S(2)}) copy-start(s32[8]{0:T(128)} %variates_ref.1) | copy-start | bytes 100
  3.3 4.8 %collective-permute-start = (bf16[8,1152]{1,0:T(8,128)(2,1)S(1)}, bf16[8,1152]{1,0:T(8,128)(2,1)S(1)}, u32[]{:S(2)}, u32[]{:S(2)}) collective-permute-start(bf16[8,1152]{1,0:T(8,128)(2,1)S(1)} %shard_map.145.after_ref), channel_id=1, source_target_pairs={{0,4},{4,0},{8,12},{12,8},{16,20},{20,16},{24,28},{28,24},{1,5},{5... | collective-permute-start | bytes 55304 | tf_op jit(solution)/shard_map/ppermute | solution.py:353
  8.1 20.6 %collective-permute-start.3 = (bf16[16,1152]{1,0:T(8,128)(2,1)S(1)}, bf16[16,1152]{1,0:T(8,128)(2,1)S(1)}, u32[]{:S(2)}, u32[]{:S(2)}) collective-permute-start(bf16[16,1152]{1,0:T(8,128)(2,1)S(1)} %pad_maximum_fusion.after_ref.refs_0_), channel_id=1, source_target_pairs={{0,24},{4,28},{8,16},{12,20},{16,8},{20,12},{24,0},{28,4},{1,25},{... | collective-permute-start | bytes 110600 | tf_op jit(solution)/shard_map/ppermute | solution.py:353
  12.2 16.5 %collective-permute-start.2 = (bf16[16,1152]{1,0:T(8,128)(2,1)S(1)}, bf16[16,1152]{1,0:T(8,128)(2,1)S(1)}, u32[]{:S(2)}, u32[]{:S(2)}) collective-permute-start(bf16[16,1152]{1,0:T(8,128)(2,1)S(1)} %pad_maximum_fusion.after_ref.refs_0_), channel_id=1, source_target_pairs={{0,16},{4,20},{8,24},{12,28},{16,0},{20,4},{24,8},{28,12},{1,17},{... | collective-permute-start | bytes 110600 | tf_op jit(solution)/shard_map/ppermute | solution.py:353
  12.2 16.5 %collective-permute-start.1 = (bf16[16,1152]{1,0:T(8,128)(2,1)S(1)}, bf16[16,1152]{1,0:T(8,128)(2,1)S(1)}, u32[]{:S(2)}, u32[]{:S(2)}) collective-permute-start(bf16[16,1152]{1,0:T(8,128)(2,1)S(1)} %pad_maximum_fusion.after_ref.refs_0_), channel_id=1, source_target_pairs={{0,8},{4,12},{8,0},{12,4},{16,24},{20,28},{24,16},{28,20},{1,9},{5... | collective-permute-start | bytes 110600 | tf_op jit(solution)/shard_map/ppermute | solution.py:353
  12.8 8.3 %copy-start.3 = (bf16[2,1024,1024]{2,1,0:T(8,128)(2,1)S(1)}, bf16[2,1024,1024]{2,1,0:T(8,128)(2,1)}, u32[]{:S(2)}) copy-start(bf16[2,1024,1024]{2,1,0:T(8,128)(2,1)} %refs_1_.5) | copy-start | bytes 12582916
  12.8 2.0 %copy-start.4 = (bf16[2,1024,768]{2,1,0:T(8,128)(2,1)S(1)}, bf16[2,1024,768]{2,1,0:T(8,128)(2,1)}, u32[]{:S(2)}) copy-start(bf16[2,1024,768]{2,1,0:T(8,128)(2,1)} %refs_3_.1) | copy-start | bytes 9437188
  14.9 1.4 %copy-start.5 = (bf16[2,256,1024]{2,1,0:T(8,128)(2,1)S(1)}, bf16[2,256,1024]{2,1,0:T(8,128)(2,1)}, u32[]{:S(2)}) copy-start(bf16[2,256,1024]{2,1,0:T(8,128)(2,1)} %refs_4_.1) | copy-start | bytes 3145732
  16.2 0.7 %copy-start.6 = (s32[8,512]{1,0:T(8,128)S(1)}, s32[8,512]{1,0:T(8,128)}, u32[]{:S(2)}) copy-start(s32[8,512]{1,0:T(8,128)} %refs_0_.4) | copy-start | bytes 49156
  17.0 0.7 %copy-start.8 = (f32[2,1024]{1,0:T(2,128)S(1)}, f32[2,1024]{1,0:T(2,128)}, u32[]{:S(2)}) copy-start(f32[2,1024]{1,0:T(2,128)} %refs_1_.3) | copy-start | bytes 24580
  17.7 0.7 %copy-start.9 = (f32[2,1024]{1,0:T(2,128)S(1)}, f32[2,1024]{1,0:T(2,128)}, u32[]{:S(2)}) copy-start(f32[2,1024]{1,0:T(2,128)} %refs_2_.2) | copy-start | bytes 24580
  18.4 0.7 %copy-start.10 = (f32[2,2,4]{2,1,0:T(2,128)S(1)}, f32[2,2,4]{2,1,0:T(2,128)}, u32[]{:S(2)}) copy-start(f32[2,2,4]{2,1,0:T(2,128)} %refs_5_.1) | copy-start | bytes 196
  19.0 0.7 %copy-start.14 = (s32[8]{0:T(128)S(1)}, s32[8]{0:T(128)}, u32[]{:S(2)}) copy-start(s32[8]{0:T(128)} %owner_ref.1) | copy-start | bytes 100
  19.7 0.7 %copy-start.15 = (f32[1,128]{1,0:T(1,128)S(1)}, f32[1,128]{1,0:T(1,128)}, u32[]{:S(2)}) copy-start(f32[1,128]{1,0:T(1,128)} %constant.8.clone.refs_6_) | copy-start | bytes 1540
  21.1 3.4 %copy-start = (bf16[2,2,8,512,256]{4,3,2,1,0:T(8,128)(2,1)S(1)}, bf16[2,2,8,512,256]{4,3,2,1,0:T(8,128)(2,1)}, u32[]{:S(2)}) copy-start(bf16[2,2,8,512,256]{4,3,2,1,0:T(8,128)(2,1)} %refs_0_.6) | copy-start | bytes 25165828
  24.5 3.4 %copy-start.2 = (bf16[2,2,1024,1024]{3,2,1,0:T(8,128)(2,1)S(1)}, bf16[2,2,1024,1024]{3,2,1,0:T(8,128)(2,1)}, u32[]{:S(2)}) copy-start(bf16[2,2,1024,1024]{3,2,1,0:T(8,128)(2,1)} %refs_0_.7) | copy-start | bytes 25165828
  28.7 9.0 %copy-start.1 = (bf16[2,2,8,512,256]{4,3,2,1,0:T(8,128)(2,1)S(1)}, bf16[2,2,8,512,256]{4,3,2,1,0:T(8,128)(2,1)}, u32[]{:S(2)}) copy-start(bf16[2,2,8,512,256]{4,3,2,1,0:T(8,128)(2,1)} %refs_0_.6) | copy-start | bytes 25165828
  30.7 3.2 %collective-permute-start.6 = (bf16[8,1024]{1,0:T(8,128)(2,1)S(1)}, bf16[8,1024]{1,0:T(8,128)(2,1)S(1)}, u32[]{:S(2)}, u32[]{:S(2)}) collective-permute-start(bf16[8,1024]{1,0:T(8,128)(2,1)S(1)} %get-tuple-element.36.refs_0_.after_ref), channel_id=1, source_target_pairs={{0,3},{1,2},{2,1},{3,0},{4,7},{5,6},{6,5},{7,4},{8,11},{9,10},{10,... | collective-permute-start | bytes 49160 | tf_op jit(solution)/shard_map/ppermute | solution.py:353
  30.7 3.8 %collective-permute-start.5 = (bf16[8,1024]{1,0:T(8,128)(2,1)S(1)}, bf16[8,1024]{1,0:T(8,128)(2,1)S(1)}, u32[]{:S(2)}, u32[]{:S(2)}) collective-permute-start(bf16[8,1024]{1,0:T(8,128)(2,1)S(1)} %get-tuple-element.36.refs_0_.after_ref), channel_id=1, source_target_pairs={{0,2},{1,3},{2,0},{3,1},{4,6},{5,7},{6,4},{7,5},{8,10},{9,11},{10,... | collective-permute-start | bytes 49160 | tf_op jit(solution)/shard_map/ppermute | solution.py:353
  32.4 2.1 %collective-permute-start.4 = (bf16[8,1024]{1,0:T(8,128)(2,1)S(1)}, bf16[8,1024]{1,0:T(8,128)(2,1)S(1)}, u32[]{:S(2)}, u32[]{:S(2)}) collective-permute-start(bf16[8,1024]{1,0:T(8,128)(2,1)S(1)} %get-tuple-element.36.refs_0_.after_ref), channel_id=1, source_target_pairs={{0,1},{1,0},{2,3},{3,2},{4,5},{5,4},{6,7},{7,6},{8,9},{9,8},{10,11... | collective-permute-start | bytes 49160 | tf_op jit(solution)/shard_map/ppermute | solution.py:353
  34.5 9.4 %slice-start = ((s8[8388608]{0:T(1024)(128)(4,1)}), s8[4194304]{0:T(1024)(128)(4,1)S(1)}, s32[]{:S(2)}) async-start(s8[8388608]{0:T(1024)(128)(4,1)} %bitcast.1), calls=%async_computation.1 | async-start | bytes 8388608
  35.5 8.4 %slice-start.1 = ((s8[8388608]{0:T(1024)(128)(4,1)}), s8[4194304]{0:T(1024)(128)(4,1)S(1)}, s32[]{:S(2)}) async-start(s8[8388608]{0:T(1024)(128)(4,1)} %bitcast.1), calls=%async_computation.2 | async-start | bytes 8388608
  35.5 3.2 %collective-permute-start.9 = (bf16[8,1024]{1,0:T(8,128)(2,1)S(1)}, bf16[8,1024]{1,0:T(8,128)(2,1)S(1)}, u32[]{:S(2)}, u32[]{:S(2)}) collective-permute-start(bf16[8,1024]{1,0:T(8,128)(2,1)S(1)} %get-tuple-element.41.refs_0_.after_ref), channel_id=1, source_target_pairs={{0,3},{1,2},{2,1},{3,0},{4,7},{5,6},{6,5},{7,4},{8,11},{9,10},{10,... | collective-permute-start | bytes 49160 | tf_op jit(solution)/shard_map/ppermute | solution.py:353
  36.3 3.9 %collective-permute-start.8 = (bf16[8,1024]{1,0:T(8,128)(2,1)S(1)}, bf16[8,1024]{1,0:T(8,128)(2,1)S(1)}, u32[]{:S(2)}, u32[]{:S(2)}) collective-permute-start(bf16[8,1024]{1,0:T(8,128)(2,1)S(1)} %get-tuple-element.41.refs_0_.after_ref), channel_id=1, source_target_pairs={{0,2},{1,3},{2,0},{3,1},{4,6},{5,7},{6,4},{7,5},{8,10},{9,11},{10,... | collective-permute-start | bytes 49160 | tf_op jit(solution)/shard_map/ppermute | solution.py:353
  37.7 2.4 %collective-permute-start.7 = (bf16[8,1024]{1,0:T(8,128)(2,1)S(1)}, bf16[8,1024]{1,0:T(8,128)(2,1)S(1)}, u32[]{:S(2)}, u32[]{:S(2)}) collective-permute-start(bf16[8,1024]{1,0:T(8,128)(2,1)S(1)} %get-tuple-element.41.refs_0_.after_ref), channel_id=1, source_target_pairs={{0,1},{1,0},{2,3},{3,2},{4,5},{5,4},{6,7},{7,6},{8,9},{9,8},{10,11... | collective-permute-start | bytes 49160 | tf_op jit(solution)/shard_map/ppermute | solution.py:353
  42.0 3.2 %collective-permute-start.12 = (bf16[8,1024]{1,0:T(8,128)(2,1)S(1)}, bf16[8,1024]{1,0:T(8,128)(2,1)S(1)}, u32[]{:S(2)}, u32[]{:S(2)}) collective-permute-start(bf16[8,1024]{1,0:T(8,128)(2,1)S(1)} %get-tuple-element.45.refs_0_), channel_id=1, source_target_pairs={{0,3},{1,2},{2,1},{3,0},{4,7},{5,6},{6,5},{7,4},{8,11},{9,10},{10,... | collective-permute-start | bytes 49160 | tf_op jit(solution)/shard_map/ppermute | solution.py:353
  42.0 3.8 %collective-permute-start.11 = (bf16[8,1024]{1,0:T(8,128)(2,1)S(1)}, bf16[8,1024]{1,0:T(8,128)(2,1)S(1)}, u32[]{:S(2)}, u32[]{:S(2)}) collective-permute-start(bf16[8,1024]{1,0:T(8,128)(2,1)S(1)} %get-tuple-element.45.refs_0_), channel_id=1, source_target_pairs={{0,2},{1,3},{2,0},{3,1},{4,6},{5,7},{6,4},{7,5},{8,10},{9,11},{10,... | collective-permute-start | bytes 49160 | tf_op jit(solution)/shard_map/ppermute | solution.py:353
  43.8 2.0 %collective-permute-start.10 = (bf16[8,1024]{1,0:T(8,128)(2,1)S(1)}, bf16[8,1024]{1,0:T(8,128)(2,1)S(1)}, u32[]{:S(2)}, u32[]{:S(2)}) collective-permute-start(bf16[8,1024]{1,0:T(8,128)(2,1)S(1)} %get-tuple-element.45.refs_0_), channel_id=1, source_target_pairs={{0,1},{1,0},{2,3},{3,2},{4,5},{5,4},{6,7},{7,6},{8,9},{9,8},{10,11... | collective-permute-start | bytes 49160 | tf_op jit(solution)/shard_map/ppermute | solution.py:353

commit v3 on v2

--- a/solution.py
+++ b/solution.py
@@ -19,6 +19,7 @@
 
 VMEM = pl.BlockSpec(memory_space=pltpu.VMEM)
 HBM = pl.BlockSpec(memory_space=pltpu.HBM)
+ANY = pl.BlockSpec(memory_space=pl.ANY)
 PARAMS = pltpu.CompilerParams(vmem_limit_bytes=16 * 2**20)
 
 
@@ -325,11 +326,15 @@
 
 
 def call(kernel, operands, outs, scratch=()):
-    specs, arrays = zip(*operands)
+    specs = [spec for spec, _ in operands]
+    arrays = [
+        pltpu.with_memory_space_constraint(array, pltpu.HBM) if spec is HBM else array
+        for spec, array in operands
+    ]
     return pl.pallas_call(
         kernel,
         out_shape=[pltpu.VMEM(shape, dtype) for shape, dtype in outs],
-        in_specs=list(specs),
+        in_specs=specs,
         out_specs=[VMEM] * len(outs),
         scratch_shapes=list(scratch),
         compiler_params=PARAMS,
@@ -339,7 +344,7 @@
 def bring(after, sources):
     return call(
         functools.partial(bring_kernel, [layer for _, layer in sources]),
-        [(HBM, after)] + [(HBM, array) for array, _ in sources],
+        [(ANY, after)] + [(HBM, array) for array, _ in sources],
         [
             (tuple(n for n, i in zip(array.shape, index) if i is None), array.dtype)
             for array, index in ((a, i + (None,) * (a.ndim - len(i))) for a, i in sources)
@@ -405,7 +410,7 @@
     ]
     pick, place, flag, *held = call(
         functools.partial(owner_kernel, share),
-        [(HBM, packed), (HBM, slot_owner), (HBM, own_block)] + [(HBM, x) for x in sources],
+        [(ANY, packed), (HBM, slot_owner), (HBM, own_block)] + [(HBM, x) for x in sources],
         [((slots, total), BF16), ((devices, slots), BF16), ((slots, META), BF16)]
         + [(x.shape, x.dtype) for x in sources],
         [

time: 61.2 us -> 49.7 us (0.81)
  local copies, waits for them, and re-layouts: 17 us -> 0 us
  Pallas kernels: 9.8 us -> 19.2 us
  waiting for transfers between devices: 7.22 us -> 3.88 us
    unnamed x36 -> x0, local copies, waits for them, and re-layouts: 17 us -> none
    pallas_call x9, Pallas kernels: 8.89 us -> 18.3 us  [call(): pl.pallas_call(kernel, out_shape=[pltpu.VMEM(shape, dtype) for shape, dty...]
    ppermute x13, waiting for transfers between devices: 7.22 us -> 3.88 us  [swap(): return lax.ppermute(array, axis, [(i, i ^ mask) for i in range(count)])]
  transfers between devices with their start and end apart: 13 -> 13, of which waited for: 7 -> 4; matrix products, arithmetic and copies ran while one was open for 0% -> 0% of each run, Pallas kernels for 4% -> 23%
where the time goes in v3:
time: 49.7 us; the launch traced here: 49.4 us
  Pallas kernels  19.2 us (39%)
  starting transfers between devices  13.8 us (28%)
  blocking collectives  12.3 us (25%)
  waiting for transfers between devices  3.88 us (8%)
    pallas_call x9, Pallas kernels, call(): pl.pallas_call(kernel, out_shape=[pltpu.VMEM(shape, dtype) for shape, dty...  18.3 us
    ppermute x13, starting transfers between devices, swap(): return lax.ppermute(array, axis, [(i, i ^ mask) for i in range(count)])  13.8 us
    all_to_all x1, blocking collectives, per_device(): received = lax.all_to_all(send, ('req', 'head'), 0, 0, tiled=True)  12.3 us
    ppermute x13, waiting for transfers between devices, swap(): return lax.ppermute(array, axis, [(i, i ^ mask) for i in range(count)])  3.88 us
  transfers between devices with their start and end apart: 13, of which 4 were waited for; matrix products, arithmetic and copies ran while one was open for 0% of the time, Pallas kernels for 23%

profile of v3, /device:TPU:0, one launch (start us, length us, event | category | flops | bytes accessed | tf_op | source)
XLA Modules:
  0.0 49.4 jit_solution(12448912659498597848)
XLA Ops:
  0.0 0.8 %shard_map.145.after_ref = bf16[8,1152]{1,0:T(8,128)(2,1)S(1)} custom-call(bf16[8,1024]{1,0:T(8,128)(2,1)} %tokens_ref.1, s32[8]{0:T(128)} %lengths_ref.1, s32[8]{0:T(128)} %positions_ref.1, s32[8]{0:T(128)} %variates_ref.1), custom_call_target="tpu_custom_call" | custom-call | tf_op jit(solution)/shard_map/pallas_call | solution.py:334
  0.8 3.0 %collective-permute-start = (bf16[8,1152]{1,0:T(8,128)(2,1)S(1)}, bf16[8,1152]{1,0:T(8,128)(2,1)S(1)}, u32[]{:S(2)}, u32[]{:S(2)}) collective-permute-start(bf16[8,1152]{1,0:T(8,128)(2,1)S(1)} %shard_map.145.after_ref), channel_id=1, source_target_pairs={{0,4},{4,0},{8,12},{12,8},{16,20},{20,16},{24,28},{28,24},{1,5},{5... | collective-permute-start | bytes 55304 | tf_op jit(solution)/shard_map/ppermute | solution.py:358
  3.8 1.7 %collective-permute-done = bf16[8,1152]{1,0:T(8,128)(2,1)S(1)} collective-permute-done((bf16[8,1152]{1,0:T(8,128)(2,1)S(1)}, bf16[8,1152]{1,0:T(8,128)(2,1)S(1)}, u32[]{:S(2)}, u32[]{:S(2)}) %collective-permute-start) | collective-permute-done | bytes 18464 | tf_op jit(solution)/shard_map/ppermute | solution.py:358
  5.6 4.1 %collective-permute-start.3 = (bf16[16,1152]{1,0:T(8,128)(2,1)S(1)}, bf16[16,1152]{1,0:T(8,128)(2,1)S(1)}, u32[]{:S(2)}, u32[]{:S(2)}) collective-permute-start(bf16[16,1152]{1,0:T(8,128)(2,1)S(1)} %pad_maximum_fusion.after_ref.refs_0_), channel_id=1, source_target_pairs={{0,24},{4,28},{8,16},{12,20},{16,8},{20,12},{24,0},{28,4},{1,25},{... | collective-permute-start | bytes 110600 | tf_op jit(solution)/shard_map/ppermute | solution.py:358
  9.7 0.0 collective-permute-start.2
  9.7 0.6 %collective-permute-start.1 = (bf16[16,1152]{1,0:T(8,128)(2,1)S(1)}, bf16[16,1152]{1,0:T(8,128)(2,1)S(1)}, u32[]{:S(2)}, u32[]{:S(2)}) collective-permute-start(bf16[16,1152]{1,0:T(8,128)(2,1)S(1)} %pad_maximum_fusion.after_ref.refs_0_), channel_id=1, source_target_pairs={{0,8},{4,12},{8,0},{12,4},{16,24},{20,28},{24,16},{28,20},{1,9},{5... | collective-permute-start | bytes 110600 | tf_op jit(solution)/shard_map/ppermute | solution.py:358
  10.3 2.3 %shard_map.146 = (bf16[8,64]{1,0:T(8,128)(2,1)S(1)}, bf16[32,8]{1,0:T(8,128)(2,1)S(1)}, bf16[8,128]{1,0:T(8,128)(2,1)S(1)}, s32[8,512]{1,0:T(8,128)S(1)}, f32[2,...) custom-call(bf16[8,1152]{1,0:T(8,128)(2,1)S(1)} %shard_map.145.after, ...), custom_call_target="tpu_custom_call" | custom-call | tf_op jit(solution)/shard_map/pallas_call | solution.py:334
  12.6 4.1 %shard_map.147 = (bf16[2,8,512,256]{3,2,1,0:T(8,128)(2,1)S(1)}, bf16[2,1024,1024]{2,1,0:T(8,128)(2,1)S(1)}, bf16[1024,1024]{1,0:T(8,128)(2,1)S(1)}) custom-call(bf16[16,1152]{1,0:T(8,128)(2,1)S(1)} %pad_maximum_fusion.after_ref.refs_0_, bf16[2,2,8,512,256]{4,3,2,1,0:T(8,128)(2,1)} %refs_0_.6, bf16[2,2,1024,1024]{3,2,1,0:T(8,128)(2,1)} %refs_0_.7, ...), custom_call_target="tpu_custom_call" | custom-call | tf_op jit(solution)/shard_map/pallas_call | solution.py:334
  16.7 0.0 collective-permute-done.3.refs_3_
  16.7 0.0 collective-permute-done.2.refs_2_
  16.7 0.0 collective-permute-done.1.refs_1_
  16.7 2.0 %shard_map.148 = (bf16[8,1024]{1,0:T(8,128)(2,1)S(1)}, f32[8,1024]{1,0:T(8,128)S(1)}, f32[8,128]{1,0:T(8,128)S(1)}, f32[8,256]{1,0:T(8,128)S(1)}) custom-call(bf16[16,1152]{1,0:T(8,128)(2,1)S(1)} %pad_maximum_fusion.after_ref.refs_0_, bf16[16,1152]{1,0:T(8,128)(2,1)S(1)} %collective-permute-done.1.refs_1_, ...), custom_call_target="tpu_custom_call" | custom-call | tf_op jit(solution)/shard_map/pallas_call | solution.py:334
  18.7 0.0 collective-permute-start.6
  18.7 1.7 %collective-permute-start.5 = (bf16[8,1024]{1,0:T(8,128)(2,1)S(1)}, bf16[8,1024]{1,0:T(8,128)(2,1)S(1)}, u32[]{:S(2)}, u32[]{:S(2)}) collective-permute-start(bf16[8,1024]{1,0:T(8,128)(2,1)S(1)} %get-tuple-element.36.refs_0_.after_ref), channel_id=1, source_target_pairs={{0,2},{1,3},{2,0},{3,1},{4,6},{5,7},{6,4},{7,5},{8,10},{9,11},{10,... | collective-permute-start | bytes 49160 | tf_op jit(solution)/shard_map/ppermute | solution.py:358
  20.4 0.2 collective-permute-start.4
  20.6 1.3 %collective-permute-done.6.refs_3_ = bf16[8,1024]{1,0:T(8,128)(2,1)S(1)} collective-permute-done((bf16[8,1024]{1,0:T(8,128)(2,1)S(1)}, bf16[8,1024]{1,0:T(8,128)(2,1)S(1)}, u32[]{:S(2)}, u32[]{:S(2)}) %collective-permute-start.6) | collective-permute-done | bytes 16416 | tf_op jit(solution)/shard_map/ppermute | solution.py:358
  21.9 0.6 %collective-permute-done.5.refs_2_ = bf16[8,1024]{1,0:T(8,128)(2,1)S(1)} collective-permute-done((bf16[8,1024]{1,0:T(8,128)(2,1)S(1)}, bf16[8,1024]{1,0:T(8,128)(2,1)S(1)}, u32[]{:S(2)}, u32[]{:S(2)}) %collective-permute-start.5) | collective-permute-done | bytes 16416 | tf_op jit(solution)/shard_map/ppermute | solution.py:358
  22.5 1.0 %shard_map.149 = (bf16[8,1024]{1,0:T(8,128)(2,1)S(1)}, f32[8,1024]{1,0:T(8,128)S(1)}) custom-call(bf16[8,1024]{1,0:T(8,128)(2,1)S(1)} %get-tuple-element.36.refs_0_.after_ref, bf16[8,1024]{1,0:T(8,128)(2,1)S(1)} %collective-permute-done.4.refs_1_, bf16[8,1024]{1,0:T(8,128)(2,1)S(1)} %collective-permute-done.5.refs_2_, ...), custom_call_target="tpu_custom_call" | custom-call | tf_op jit(solution)/shard_map/pallas_call | solution.py:334
  23.5 0.8 %collective-permute-start.9 = (bf16[8,1024]{1,0:T(8,128)(2,1)S(1)}, bf16[8,1024]{1,0:T(8,128)(2,1)S(1)}, u32[]{:S(2)}, u32[]{:S(2)}) collective-permute-start(bf16[8,1024]{1,0:T(8,128)(2,1)S(1)} %get-tuple-element.41.refs_0_.after_ref), channel_id=1, source_target_pairs={{0,3},{1,2},{2,1},{3,0},{4,7},{5,6},{6,5},{7,4},{8,11},{9,10},{10,... | collective-permute-start | bytes 49160 | tf_op jit(solution)/shard_map/ppermute | solution.py:358
  24.3 1.5 %collective-permute-start.8 = (bf16[8,1024]{1,0:T(8,128)(2,1)S(1)}, bf16[8,1024]{1,0:T(8,128)(2,1)S(1)}, u32[]{:S(2)}, u32[]{:S(2)}) collective-permute-start(bf16[8,1024]{1,0:T(8,128)(2,1)S(1)} %get-tuple-element.41.refs_0_.after_ref), channel_id=1, source_target_pairs={{0,2},{1,3},{2,0},{3,1},{4,6},{5,7},{6,4},{7,5},{8,10},{9,11},{10,... | collective-permute-start | bytes 49160 | tf_op jit(solution)/shard_map/ppermute | solution.py:358
  25.8 2.2 %shard_map.150.refs_8_ = bf16[2,8,512,256]{3,2,1,0:T(8,128)(2,1)S(1)} custom-call(bf16[8,1024]{1,0:T(8,128)(2,1)S(1)} %get-tuple-element.36.refs_0_.after_ref, bf16[2,2,8,512,256]{4,3,2,1,0:T(8,128)(2,1)} %refs_0_.6), custom_call_target="tpu_custom_call" | custom-call | tf_op jit(solution)/shard_map/pallas_call | solution.py:334
  28.0 0.2 collective-permute-done.8.refs_2_
  28.2 1.9 %shard_map.151 = (bf16[8,1024]{1,0:T(8,128)(2,1)S(1)}, f32[8,1024]{1,0:T(8,128)S(1)}) custom-call(bf16[8,1024]{1,0:T(8,128)(2,1)S(1)} %get-tuple-element.41.refs_0_.after_ref, bf16[8,1024]{1,0:T(8,128)(2,1)S(1)} %collective-permute-done.7.refs_1_, bf16[8,1024]{1,0:T(8,128)(2,1)S(1)} %collective-permute-done.8.refs_2_, ...), custom_call_target="tpu_custom_call" | custom-call | tf_op jit(solution)/shard_map/pallas_call | solution.py:334
  30.1 0.8 %collective-permute-start.12 = (bf16[8,1024]{1,0:T(8,128)(2,1)S(1)}, bf16[8,1024]{1,0:T(8,128)(2,1)S(1)}, u32[]{:S(2)}, u32[]{:S(2)}) collective-permute-start(bf16[8,1024]{1,0:T(8,128)(2,1)S(1)} %get-tuple-element.45.refs_0_), channel_id=1, source_target_pairs={{0,3},{1,2},{2,1},{3,0},{4,7},{5,6},{6,5},{7,4},{8,11},{9,10},{10,... | collective-permute-start | bytes 49160 | tf_op jit(solution)/shard_map/ppermute | solution.py:358
  30.8 1.2 %collective-permute-start.11 = (bf16[8,1024]{1,0:T(8,128)(2,1)S(1)}, bf16[8,1024]{1,0:T(8,128)(2,1)S(1)}, u32[]{:S(2)}, u32[]{:S(2)}) collective-permute-start(bf16[8,1024]{1,0:T(8,128)(2,1)S(1)} %get-tuple-element.45.refs_0_), channel_id=1, source_target_pairs={{0,2},{1,3},{2,0},{3,1},{4,6},{5,7},{6,4},{7,5},{8,10},{9,11},{10,... | collective-permute-start | bytes 49160 | tf_op jit(solution)/shard_map/ppermute | solution.py:358
  32.0 0.0 collective-permute-start.10
  32.0 2.9 %shard_map.152 = (bf16[2,1024,1024]{2,1,0:T(8,128)(2,1)S(1)}, bf16[1024,1024]{1,0:T(8,128)(2,1)S(1)}) custom-call(bf16[8,1024]{1,0:T(8,128)(2,1)S(1)} %get-tuple-element.41.refs_0_.after_ref, bf16[2,2,1024,1024]{3,2,1,0:T(8,128)(2,1)} %refs_0_.7, bf16[2,1024,1024]{2,1,0:T(8,128)(2,1)} %refs_1_.5), custom_call_target="tpu_custom_call" | custom-call | tf_op jit(solution)/shard_map/pallas_call | solution.py:334
  34.9 0.0 collective-permute-done.12.refs_3_
  35.0 0.0 collective-permute-done.11.refs_2_
  35.0 1.2 %shard_map.153 = bf16[32,2,640]{2,1,0:T(2,128)(2,1)S(1)} custom-call(bf16[8,1024]{1,0:T(8,128)(2,1)S(1)} %get-tuple-element.45.refs_0_, bf16[8,1024]{1,0:T(8,128)(2,1)S(1)} %collective-permute-done.10.refs_1_, bf16[8,1024]{1,0:T(8,128)(2,1)S(1)} %collective-permute-done.11.refs_2_, bf16[8,1024]{1,0:T(8,128)(2,1)S(1)} %collective-permute-done.12.refs_3_, ...), custom_call_target="tpu_custom_call" | custom-call | tf_op jit(solution)/shard_map/pallas_call | solution.py:334
  36.1 12.3 %all_to_all.5.received_ref = bf16[32,2,640]{2,1,0:T(2,128)(2,1)S(1)} all-to-all(bf16[32,2,640]{2,1,0:T(2,128)(2,1)S(1)} %shard_map.153), channel_id=1, replica_groups=mesh['req'=8,'head'=4] {'req','head'}, dimensions={0} | all-to-all | bytes 163840 | tf_op jit(solution)/shard_map/all_to_all | solution.py:477
  48.5 0.9 %shard_map.154 = bf16[2,1024]{1,0:T(2,128)(2,1)} custom-call(bf16[32,2,640]{2,1,0:T(2,128)(2,1)S(1)} %all_to_all.5.received_ref), custom_call_target="tpu_custom_call" | custom-call | tf_op jit(solution)/shard_map/pallas_call | solution.py:478
  (6 shorter events, 0.0 us)
Async XLA Ops:
  0.8 4.8 %collective-permute-start = (bf16[8,1152]{1,0:T(8,128)(2,1)S(1)}, bf16[8,1152]{1,0:T(8,128)(2,1)S(1)}, u32[]{:S(2)}, u32[]{:S(2)}) collective-permute-start(bf16[8,1152]{1,0:T(8,128)(2,1)S(1)} %shard_map.145.after_ref), channel_id=1, source_target_pairs={{0,4},{4,0},{8,12},{12,8},{16,20},{20,16},{24,28},{28,24},{1,5},{5... | collective-permute-start | bytes 55304 | tf_op jit(solution)/shard_map/ppermute | solution.py:358
  5.6 11.1 %collective-permute-start.3 = (bf16[16,1152]{1,0:T(8,128)(2,1)S(1)}, bf16[16,1152]{1,0:T(8,128)(2,1)S(1)}, u32[]{:S(2)}, u32[]{:S(2)}) collective-permute-start(bf16[16,1152]{1,0:T(8,128)(2,1)S(1)} %pad_maximum_fusion.after_ref.refs_0_), channel_id=1, source_target_pairs={{0,24},{4,28},{8,16},{12,20},{16,8},{20,12},{24,0},{28,4},{1,25},{... | collective-permute-start | bytes 110600 | tf_op jit(solution)/shard_map/ppermute | solution.py:358
  9.7 7.1 %collective-permute-start.2 = (bf16[16,1152]{1,0:T(8,128)(2,1)S(1)}, bf16[16,1152]{1,0:T(8,128)(2,1)S(1)}, u32[]{:S(2)}, u32[]{:S(2)}) collective-permute-start(bf16[16,1152]{1,0:T(8,128)(2,1)S(1)} %pad_maximum_fusion.after_ref.refs_0_), channel_id=1, source_target_pairs={{0,16},{4,20},{8,24},{12,28},{16,0},{20,4},{24,8},{28,12},{1,17},{... | collective-permute-start | bytes 110600 | tf_op jit(solution)/shard_map/ppermute | solution.py:358
  9.7 7.1 %collective-permute-start.1 = (bf16[16,1152]{1,0:T(8,128)(2,1)S(1)}, bf16[16,1152]{1,0:T(8,128)(2,1)S(1)}, u32[]{:S(2)}, u32[]{:S(2)}) collective-permute-start(bf16[16,1152]{1,0:T(8,128)(2,1)S(1)} %pad_maximum_fusion.after_ref.refs_0_), channel_id=1, source_target_pairs={{0,8},{4,12},{8,0},{12,4},{16,24},{20,28},{24,16},{28,20},{1,9},{5... | collective-permute-start | bytes 110600 | tf_op jit(solution)/shard_map/ppermute | solution.py:358
  18.7 3.2 %collective-permute-start.6 = (bf16[8,1024]{1,0:T(8,128)(2,1)S(1)}, bf16[8,1024]{1,0:T(8,128)(2,1)S(1)}, u32[]{:S(2)}, u32[]{:S(2)}) collective-permute-start(bf16[8,1024]{1,0:T(8,128)(2,1)S(1)} %get-tuple-element.36.refs_0_.after_ref), channel_id=1, source_target_pairs={{0,3},{1,2},{2,1},{3,0},{4,7},{5,6},{6,5},{7,4},{8,11},{9,10},{10,... | collective-permute-start | bytes 49160 | tf_op jit(solution)/shard_map/ppermute | solution.py:358
  18.7 3.8 %collective-permute-start.5 = (bf16[8,1024]{1,0:T(8,128)(2,1)S(1)}, bf16[8,1024]{1,0:T(8,128)(2,1)S(1)}, u32[]{:S(2)}, u32[]{:S(2)}) collective-permute-start(bf16[8,1024]{1,0:T(8,128)(2,1)S(1)} %get-tuple-element.36.refs_0_.after_ref), channel_id=1, source_target_pairs={{0,2},{1,3},{2,0},{3,1},{4,6},{5,7},{6,4},{7,5},{8,10},{9,11},{10,... | collective-permute-start | bytes 49160 | tf_op jit(solution)/shard_map/ppermute | solution.py:358
  20.4 2.1 %collective-permute-start.4 = (bf16[8,1024]{1,0:T(8,128)(2,1)S(1)}, bf16[8,1024]{1,0:T(8,128)(2,1)S(1)}, u32[]{:S(2)}, u32[]{:S(2)}) collective-permute-start(bf16[8,1024]{1,0:T(8,128)(2,1)S(1)} %get-tuple-element.36.refs_0_.after_ref), channel_id=1, source_target_pairs={{0,1},{1,0},{2,3},{3,2},{4,5},{5,4},{6,7},{7,6},{8,9},{9,8},{10,11... | collective-permute-start | bytes 49160 | tf_op jit(solution)/shard_map/ppermute | solution.py:358
  23.5 4.4 %collective-permute-start.9 = (bf16[8,1024]{1,0:T(8,128)(2,1)S(1)}, bf16[8,1024]{1,0:T(8,128)(2,1)S(1)}, u32[]{:S(2)}, u32[]{:S(2)}) collective-permute-start(bf16[8,1024]{1,0:T(8,128)(2,1)S(1)} %get-tuple-element.41.refs_0_.after_ref), channel_id=1, source_target_pairs={{0,3},{1,2},{2,1},{3,0},{4,7},{5,6},{6,5},{7,4},{8,11},{9,10},{10,... | collective-permute-start | bytes 49160 | tf_op jit(solution)/shard_map/ppermute | solution.py:358
  24.3 3.9 %collective-permute-start.8 = (bf16[8,1024]{1,0:T(8,128)(2,1)S(1)}, bf16[8,1024]{1,0:T(8,128)(2,1)S(1)}, u32[]{:S(2)}, u32[]{:S(2)}) collective-permute-start(bf16[8,1024]{1,0:T(8,128)(2,1)S(1)} %get-tuple-element.41.refs_0_.after_ref), channel_id=1, source_target_pairs={{0,2},{1,3},{2,0},{3,1},{4,6},{5,7},{6,4},{7,5},{8,10},{9,11},{10,... | collective-permute-start | bytes 49160 | tf_op jit(solution)/shard_map/ppermute | solution.py:358
  25.8 2.4 %collective-permute-start.7 = (bf16[8,1024]{1,0:T(8,128)(2,1)S(1)}, bf16[8,1024]{1,0:T(8,128)(2,1)S(1)}, u32[]{:S(2)}, u32[]{:S(2)}) collective-permute-start(bf16[8,1024]{1,0:T(8,128)(2,1)S(1)} %get-tuple-element.41.refs_0_.after_ref), channel_id=1, source_target_pairs={{0,1},{1,0},{2,3},{3,2},{4,5},{5,4},{6,7},{7,6},{8,9},{9,8},{10,11... | collective-permute-start | bytes 49160 | tf_op jit(solution)/shard_map/ppermute | solution.py:358
  30.1 4.9 %collective-permute-start.12 = (bf16[8,1024]{1,0:T(8,128)(2,1)S(1)}, bf16[8,1024]{1,0:T(8,128)(2,1)S(1)}, u32[]{:S(2)}, u32[]{:S(2)}) collective-permute-start(bf16[8,1024]{1,0:T(8,128)(2,1)S(1)} %get-tuple-element.45.refs_0_), channel_id=1, source_target_pairs={{0,3},{1,2},{2,1},{3,0},{4,7},{5,6},{6,5},{7,4},{8,11},{9,10},{10,... | collective-permute-start | bytes 49160 | tf_op jit(solution)/shard_map/ppermute | solution.py:358
  30.8 4.1 %collective-permute-start.11 = (bf16[8,1024]{1,0:T(8,128)(2,1)S(1)}, bf16[8,1024]{1,0:T(8,128)(2,1)S(1)}, u32[]{:S(2)}, u32[]{:S(2)}) collective-permute-start(bf16[8,1024]{1,0:T(8,128)(2,1)S(1)} %get-tuple-element.45.refs_0_), channel_id=1, source_target_pairs={{0,2},{1,3},{2,0},{3,1},{4,6},{5,7},{6,4},{7,5},{8,10},{9,11},{10,... | collective-permute-start | bytes 49160 | tf_op jit(solution)/shard_map/ppermute | solution.py:358
  32.0 2.9 %collective-permute-start.10 = (bf16[8,1024]{1,0:T(8,128)(2,1)S(1)}, bf16[8,1024]{1,0:T(8,128)(2,1)S(1)}, u32[]{:S(2)}, u32[]{:S(2)}) collective-permute-start(bf16[8,1024]{1,0:T(8,128)(2,1)S(1)} %get-tuple-element.45.refs_0_), channel_id=1, source_target_pairs={{0,1},{1,0},{2,3},{3,2},{4,5},{5,4},{6,7},{7,6},{8,9},{9,8},{10,11... | collective-permute-start | bytes 49160 | tf_op jit(solution)/shard_map/ppermute | solution.py:358

commit v4 on v3

--- a/solution.py
+++ b/solution.py
@@ -10,6 +10,7 @@
 
 HD = 64
 LAYERS = 2
+COST = 10**11
 META = 128
 LOW = 128
 CHUNK = 128
@@ -69,21 +70,8 @@
     own_block_ref,
     *refs,
 ):
-    count = (len(refs) - 6) // 2
-    sources, (pick_ref, place_ref, flag_ref), outs = refs[:count], refs[count : count + 3], refs[
-        count + 3 : -3
-    ]
-    owner, own_block, sems = refs[-3:]
-    copies = [
-        pltpu.make_async_copy(src, dst, sems.at[i])
-        for i, (src, dst) in enumerate(
-            [(owner_ref, owner), (own_block_ref, own_block)] + list(zip(sources, outs))
-        )
-    ]
-    for copy in copies:
-        copy.start()
-    copies[0].wait()
-    copies[1].wait()
+    pick_ref, place_ref, flag_ref, owner, own_block, sems = refs
+    copy_all([(owner_ref, owner), (own_block_ref, own_block)], sems)
     slots, total = pick_ref.shape
     devices = place_ref.shape[0]
     row, column = iota((slots, total), 0), iota((slots, total), 1)
@@ -101,15 +89,10 @@
     pick_ref[...] = pick.astype(BF16)
     place_ref[...] = place.astype(BF16)
     flag_ref[...] = flag.astype(BF16)
-    for copy in copies[2:]:
-        copy.wait()
-
-
-def bring_kernel(parts, after_ref, *refs):
-    count = len(parts)
-    copy_all(
-        [(refs[i].at[parts[i]], refs[count + i]) for i in range(count)], refs[2 * count]
-    )
+
+
+def bring_kernel(layer, after_ref, source_ref, out_ref, sem):
+    copy_all([(source_ref.at[layer], out_ref)], sem)
 
 
 def attention(
@@ -288,10 +271,10 @@
     for ref in part_refs:
         stream = stream + ref[...].astype(F32)
     normed = rms_scale(stream, gain_ref[layer : layer + 1, :]).astype(BF16)
-    gate = jnp.dot(normed, gate_up_ref[0], preferred_element_type=F32)
-    up = jnp.dot(normed, gate_up_ref[1], preferred_element_type=F32)
+    gate = jnp.dot(normed, gate_up_ref[layer, 0], preferred_element_type=F32)
+    up = jnp.dot(normed, gate_up_ref[layer, 1], preferred_element_type=F32)
     hidden = (gate / (1.0 + jnp.exp(-gate)) * up).astype(BF16)
-    return stream, jnp.dot(hidden, down_ref[...], preferred_element_type=F32)
+    return stream, jnp.dot(hidden, down_ref[layer], preferred_element_type=F32)
 
 
 def feed_forward_kernel(layer, part_count, *refs):
@@ -325,7 +308,7 @@
         out_ref[:, i * half : (i + 1) * half] = rows[:share, :].astype(BF16)
 
 
-def call(kernel, operands, outs, scratch=()):
+def call(kernel, operands, outs, scratch=(), cost=None):
     specs = [spec for spec, _ in operands]
     arrays = [
         pltpu.with_memory_space_constraint(array, pltpu.HBM) if spec is HBM else array
@@ -338,19 +321,18 @@
         out_specs=[VMEM] * len(outs),
         scratch_shapes=list(scratch),
         compiler_params=PARAMS,
+        cost_estimate=cost,
     )(*arrays)
 
 
-def bring(after, sources):
-    return call(
-        functools.partial(bring_kernel, [layer for _, layer in sources]),
-        [(ANY, after)] + [(HBM, array) for array, _ in sources],
-        [
-            (tuple(n for n, i in zip(array.shape, index) if i is None), array.dtype)
-            for array, index in ((a, i + (None,) * (a.ndim - len(i))) for a, i in sources)
-        ],
-        [pltpu.SemaphoreType.DMA((len(sources),))],
-    )
+def bring(after, source, layer):
+    (out,) = call(
+        functools.partial(bring_kernel, layer),
+        [(ANY, after), (HBM, source)],
+        [(source.shape[1:], source.dtype)],
+        [pltpu.SemaphoreType.DMA((1,))],
+    )
+    return out
 
 
 def swap(array, axis, mask):
@@ -401,29 +383,23 @@
         [(HBM, tokens), (HBM, lengths), (HBM, positions), (HBM, variates)],
         [((slots, width + META), BF16)],
         whole_row + [pltpu.SemaphoreType.DMA((4,))],
+        pl.CostEstimate(flops=COST, bytes_accessed=0, transcendentals=0),
     )
     exponent = -2.0 * (np.arange(128) % (HD // 2)) / HD
     frequency = jnp.asarray((10000.0**exponent).astype(np.float32)[None, :])
     own_block = lax.axis_index("req").reshape(1)
-    sources = [
-        cache_variates, attn_gain, ffn_gain, qkv_weight, out_weight, variate_bias, frequency,
-    ]
-    pick, place, flag, *held = call(
+    pick, place, flag = call(
         functools.partial(owner_kernel, share),
-        [(ANY, packed), (HBM, slot_owner), (HBM, own_block)] + [(HBM, x) for x in sources],
-        [((slots, total), BF16), ((devices, slots), BF16), ((slots, META), BF16)]
-        + [(x.shape, x.dtype) for x in sources],
+        [(ANY, packed), (HBM, slot_owner), (HBM, own_block)],
+        [((slots, total), BF16), ((devices, slots), BF16), ((slots, META), BF16)],
         [
             pltpu.SMEM((slots,), jnp.int32),
             pltpu.SMEM((1,), jnp.int32),
-            pltpu.SemaphoreType.DMA((len(sources) + 2,)),
+            pltpu.SemaphoreType.DMA((2,)),
         ],
     )
-    cache_variates, attn_gain, ffn_gain, qkv_weight, out_weight, variate_bias, frequency = held
     blocks = gather_blocks(packed, "req")
-    kv, gate_up, down = bring(
-        blocks[0], [(kv_cache, (0,)), (gate_up_weight, (0,)), (down_weight, (0,))]
-    )
+    kv = bring(blocks[0], kv_cache, 0)
 
     scratch = [
         pltpu.VMEM((local_heads * slots, cap), F32),
@@ -448,7 +424,6 @@
     for layer in range(LAYERS):
         last = layer == LAYERS - 1
         if layer:
-            (kv,) = next_kv
             part, stream = call(
                 functools.partial(next_attention_kernel, layer, head_count),
                 on_chip(*parts, stream, facts, turn, cache_variates, kv, attn_gain)
@@ -458,20 +433,17 @@
             )
         parts = exchange(part)
         if not last:
-            next_kv = bring(part, [(kv_cache, (layer + 1,))])
+            kv = bring(part, kv_cache, layer + 1)
             part, stream = call(
                 functools.partial(feed_forward_kernel, layer, head_count),
-                on_chip(*parts, stream, ffn_gain, gate_up, down),
+                on_chip(*parts, stream, ffn_gain, gate_up_weight, down_weight),
                 [part_type, stream_type],
             )
             parts = exchange(part)
-            gate_up, down = bring(
-                part, [(gate_up_weight, (layer + 1,)), (down_weight, (layer + 1,))]
-            )
         else:
             (send,) = call(
                 functools.partial(last_feed_forward_kernel, layer, head_count),
-                on_chip(*parts, place, flag, stream, ffn_gain, gate_up, down),
+                on_chip(*parts, place, flag, stream, ffn_gain, gate_up_weight, down_weight),
                 [((devices, 2, width // 2 + META), BF16)],
             )
     received = lax.all_to_all(send, ("req", "head"), 0, 0, tiled=True)

time: 49.7 us -> 47.6 us (0.958)
  Pallas kernels: 19.2 us -> 13.5 us
  waiting for transfers between devices: 3.88 us -> 6.95 us
  local copies, waits for them, and re-layouts: 0 us -> 0.52 us
    pallas_call x9 -> x8, Pallas kernels: 18.3 us -> 12.6 us  [call(): pl.pallas_call(kernel, out_shape=[pltpu.VMEM(shape, dtype) for shape, dty...]
    ppermute x13, waiting for transfers between devices: 3.88 us -> 6.95 us  [swap(): return lax.ppermute(array, axis, [(i, i ^ mask) for i in range(count)])]
    unnamed x0 -> x20, local copies, waits for them, and re-layouts: none -> 0.52 us
  transfers between devices with their start and end apart: 13 -> 13, of which waited for: 4 -> 7; matrix products, arithmetic and copies ran while one was open for 0% -> 0% of each run, Pallas kernels for 23% -> 12%
where the time goes in v4:
time: 47.6 us; the launch traced here: 47.3 us
  starting transfers between devices  13.8 us (29%)
  Pallas kernels  13.5 us (28%)
  blocking collectives  12.3 us (26%)
  waiting for transfers between devices  6.95 us (15%)
  local copies, waits for them, and re-layouts  0.52 us (1%)
    ppermute x13, starting transfers between devices, swap(): return lax.ppermute(array, axis, [(i, i ^ mask) for i in range(count)])  13.8 us
    pallas_call x8, Pallas kernels, call(): pl.pallas_call(kernel, out_shape=[pltpu.VMEM(shape, dtype) for shape, dty...  12.6 us
    all_to_all x1, blocking collectives, per_device(): received = lax.all_to_all(send, ('req', 'head'), 0, 0, tiled=True)  12.3 us
    ppermute x13, waiting for transfers between devices, swap(): return lax.ppermute(array, axis, [(i, i ^ mask) for i in range(count)])  6.95 us
  transfers between devices with their start and end apart: 13, of which 7 were waited for; matrix products, arithmetic and copies ran while one was open for 0% of the time, Pallas kernels for 12%

profile of v4, /device:TPU:0, one launch (start us, length us, event | category | flops | bytes accessed | tf_op | source)
XLA Modules:
  0.0 47.3 jit_solution(14183449898626998926)
XLA Ops:
  0.0 0.8 %shard_map.145.after_ref = bf16[8,1152]{1,0:T(8,128)(2,1)S(1)} custom-call(bf16[8,1024]{1,0:T(8,128)(2,1)} %tokens_ref.1, s32[8]{0:T(128)} %lengths_ref.1, s32[8]{0:T(128)} %positions_ref.1, s32[8]{0:T(128)} %variates_ref.1), custom_call_target="tpu_custom_call" | custom-call | flops 99999997952 | tf_op jit(solution)/shard_map/pallas_call | solution.py:317
  0.8 3.0 %collective-permute-start = (bf16[8,1152]{1,0:T(8,128)(2,1)S(1)}, bf16[8,1152]{1,0:T(8,128)(2,1)S(1)}, u32[]{:S(2)}, u32[]{:S(2)}) collective-permute-start(bf16[8,1152]{1,0:T(8,128)(2,1)S(1)} %shard_map.145.after_ref), channel_id=1, source_target_pairs={{0,4},{4,0},{8,12},{12,8},{16,20},{20,16},{24,28},{28,24},{1,5},{5... | collective-permute-start | bytes 55304 | tf_op jit(solution)/shard_map/ppermute | solution.py:340
  3.8 1.7 %collective-permute-done = bf16[8,1152]{1,0:T(8,128)(2,1)S(1)} collective-permute-done((bf16[8,1152]{1,0:T(8,128)(2,1)S(1)}, bf16[8,1152]{1,0:T(8,128)(2,1)S(1)}, u32[]{:S(2)}, u32[]{:S(2)}) %collective-permute-start) | collective-permute-done | bytes 18464 | tf_op jit(solution)/shard_map/ppermute | solution.py:340
  5.6 4.1 %collective-permute-start.3 = (bf16[16,1152]{1,0:T(8,128)(2,1)S(1)}, bf16[16,1152]{1,0:T(8,128)(2,1)S(1)}, u32[]{:S(2)}, u32[]{:S(2)}) collective-permute-start(bf16[16,1152]{1,0:T(8,128)(2,1)S(1)} %pad_maximum_fusion.after_ref.refs_0_), channel_id=1, source_target_pairs={{0,24},{4,28},{8,16},{12,20},{16,8},{20,12},{24,0},{28,4},{1,25},{... | collective-permute-start | bytes 110600 | tf_op jit(solution)/shard_map/ppermute | solution.py:340
  9.7 0.6 %collective-permute-start.1 = (bf16[16,1152]{1,0:T(8,128)(2,1)S(1)}, bf16[16,1152]{1,0:T(8,128)(2,1)S(1)}, u32[]{:S(2)}, u32[]{:S(2)}) collective-permute-start(bf16[16,1152]{1,0:T(8,128)(2,1)S(1)} %pad_maximum_fusion.after_ref.refs_0_), channel_id=1, source_target_pairs={{0,8},{4,12},{8,0},{12,4},{16,24},{20,28},{24,16},{28,20},{1,9},{5... | collective-permute-start | bytes 110600 | tf_op jit(solution)/shard_map/ppermute | solution.py:340
  10.3 0.9 %shard_map.146 = (bf16[8,64]{1,0:T(8,128)(2,1)S(1)}, bf16[32,8]{1,0:T(8,128)(2,1)S(1)}, bf16[8,128]{1,0:T(8,128)(2,1)S(1)}) custom-call(bf16[8,1152]{1,0:T(8,128)(2,1)S(1)} %shard_map.145.after_ref, s32[8]{0:T(128)} %owner_ref.1, s32[1]{0:T(128)} %bitcast.own_block_ref), custom_call_target="tpu_custom_call" | custom-call | tf_op jit(solution)/shard_map/pallas_call | solution.py:317
  11.2 0.0 copy-start.1
  11.3 0.0 copy-start.4
  11.3 0.0 copy-start.7
  11.3 0.0 slice-start.1
  11.3 2.6 %shard_map.147.refs_7_ = bf16[2,8,512,256]{3,2,1,0:T(8,128)(2,1)S(1)} custom-call(bf16[16,1152]{1,0:T(8,128)(2,1)S(1)} %pad_maximum_fusion.after_ref.refs_0_, bf16[2,2,8,512,256]{4,3,2,1,0:T(8,128)(2,1)} %source_ref.3), custom_call_target="tpu_custom_call" | custom-call | tf_op jit(solution)/shard_map/pallas_call | solution.py:317
  14.0 0.6 %collective-permute-done.2.refs_2_ = bf16[16,1152]{1,0:T(8,128)(2,1)S(1)} collective-permute-done((bf16[16,1152]{1,0:T(8,128)(2,1)S(1)}, bf16[16,1152]{1,0:T(8,128)(2,1)S(1)}, u32[]{:S(2)}, u32[]{:S(2)}) %collective-permute-start.2) | collective-permute-done | bytes 36896 | tf_op jit(solution)/shard_map/ppermute | solution.py:340
  14.5 0.2 copy-done.1
  14.7 0.3 copy-done.2
  15.0 2.0 %shard_map.148 = (bf16[8,1024]{1,0:T(8,128)(2,1)S(1)}, f32[8,1024]{1,0:T(8,128)S(1)}, f32[8,128]{1,0:T(8,128)S(1)}, f32[8,256]{1,0:T(8,128)S(1)}) custom-call(bf16[16,1152]{1,0:T(8,128)(2,1)S(1)} %pad_maximum_fusion.after_ref.refs_0_, bf16[16,1152]{1,0:T(8,128)(2,1)S(1)} %collective-permute-done.1.refs_1_, ...), custom_call_target="tpu_custom_call" | custom-call | tf_op jit(solution)/shard_map/pallas_call | solution.py:317
  17.0 1.7 %collective-permute-start.5 = (bf16[8,1024]{1,0:T(8,128)(2,1)S(1)}, bf16[8,1024]{1,0:T(8,128)(2,1)S(1)}, u32[]{:S(2)}, u32[]{:S(2)}) collective-permute-start(bf16[8,1024]{1,0:T(8,128)(2,1)S(1)} %get-tuple-element.17.refs_0_.after_ref), channel_id=1, source_target_pairs={{0,2},{1,3},{2,0},{3,1},{4,6},{5,7},{6,4},{7,5},{8,10},{9,11},{10,... | collective-permute-start | bytes 49160 | tf_op jit(solution)/shard_map/ppermute | solution.py:340
  18.7 0.2 collective-permute-start.4
  18.9 1.3 %collective-permute-done.6.refs_3_ = bf16[8,1024]{1,0:T(8,128)(2,1)S(1)} collective-permute-done((bf16[8,1024]{1,0:T(8,128)(2,1)S(1)}, bf16[8,1024]{1,0:T(8,128)(2,1)S(1)}, u32[]{:S(2)}, u32[]{:S(2)}) %collective-permute-start.6) | collective-permute-done | bytes 16416 | tf_op jit(solution)/shard_map/ppermute | solution.py:340
  20.2 0.6 %collective-permute-done.5.refs_2_ = bf16[8,1024]{1,0:T(8,128)(2,1)S(1)} collective-permute-done((bf16[8,1024]{1,0:T(8,128)(2,1)S(1)}, bf16[8,1024]{1,0:T(8,128)(2,1)S(1)}, u32[]{:S(2)}, u32[]{:S(2)}) %collective-permute-start.5) | collective-permute-done | bytes 16416 | tf_op jit(solution)/shard_map/ppermute | solution.py:340
  20.9 1.0 %shard_map.149 = (bf16[8,1024]{1,0:T(8,128)(2,1)S(1)}, f32[8,1024]{1,0:T(8,128)S(1)}) custom-call(bf16[8,1024]{1,0:T(8,128)(2,1)S(1)} %get-tuple-element.17.refs_0_.after_ref, bf16[8,1024]{1,0:T(8,128)(2,1)S(1)} %collective-permute-done.4.refs_1_, bf16[8,1024]{1,0:T(8,128)(2,1)S(1)} %collective-permute-done.5.refs_2_, ...), custom_call_target="tpu_custom_call" | custom-call | tf_op jit(solution)/shard_map/pallas_call | solution.py:317
  21.9 0.8 %collective-permute-start.9 = (bf16[8,1024]{1,0:T(8,128)(2,1)S(1)}, bf16[8,1024]{1,0:T(8,128)(2,1)S(1)}, u32[]{:S(2)}, u32[]{:S(2)}) collective-permute-start(bf16[8,1024]{1,0:T(8,128)(2,1)S(1)} %get-tuple-element.19.refs_0_), channel_id=1, source_target_pairs={{0,3},{1,2},{2,1},{3,0},{4,7},{5,6},{6,5},{7,4},{8,11},{9,10},{10,... | collective-permute-start | bytes 49160 | tf_op jit(solution)/shard_map/ppermute | solution.py:340
  22.6 1.5 %collective-permute-start.8 = (bf16[8,1024]{1,0:T(8,128)(2,1)S(1)}, bf16[8,1024]{1,0:T(8,128)(2,1)S(1)}, u32[]{:S(2)}, u32[]{:S(2)}) collective-permute-start(bf16[8,1024]{1,0:T(8,128)(2,1)S(1)} %get-tuple-element.19.refs_0_), channel_id=1, source_target_pairs={{0,2},{1,3},{2,0},{3,1},{4,6},{5,7},{6,4},{7,5},{8,10},{9,11},{10,... | collective-permute-start | bytes 49160 | tf_op jit(solution)/shard_map/ppermute | solution.py:340
  24.1 2.2 %shard_map.150.refs_8_ = bf16[2,8,512,256]{3,2,1,0:T(8,128)(2,1)S(1)} custom-call(bf16[8,1024]{1,0:T(8,128)(2,1)S(1)} %get-tuple-element.17.refs_0_.after_ref, bf16[2,2,8,512,256]{4,3,2,1,0:T(8,128)(2,1)} %source_ref.3), custom_call_target="tpu_custom_call" | custom-call | tf_op jit(solution)/shard_map/pallas_call | solution.py:317
  26.3 0.2 collective-permute-done.8.refs_2_
  26.5 1.9 %shard_map.151 = (bf16[8,1024]{1,0:T(8,128)(2,1)S(1)}, f32[8,1024]{1,0:T(8,128)S(1)}) custom-call(bf16[8,1024]{1,0:T(8,128)(2,1)S(1)} %get-tuple-element.19.refs_0_, bf16[8,1024]{1,0:T(8,128)(2,1)S(1)} %collective-permute-done.7.refs_1_, bf16[8,1024]{1,0:T(8,128)(2,1)S(1)} %collective-permute-done.8.refs_2_, ...), custom_call_target="tpu_custom_call" | custom-call | tf_op jit(solution)/shard_map/pallas_call | solution.py:317
  28.4 0.8 %collective-permute-start.12 = (bf16[8,1024]{1,0:T(8,128)(2,1)S(1)}, bf16[8,1024]{1,0:T(8,128)(2,1)S(1)}, u32[]{:S(2)}, u32[]{:S(2)}) collective-permute-start(bf16[8,1024]{1,0:T(8,128)(2,1)S(1)} %get-tuple-element.23.refs_0_), channel_id=1, source_target_pairs={{0,3},{1,2},{2,1},{3,0},{4,7},{5,6},{6,5},{7,4},{8,11},{9,10},{10,... | collective-permute-start | bytes 49160 | tf_op jit(solution)/shard_map/ppermute | solution.py:340
  29.2 1.2 %collective-permute-start.11 = (bf16[8,1024]{1,0:T(8,128)(2,1)S(1)}, bf16[8,1024]{1,0:T(8,128)(2,1)S(1)}, u32[]{:S(2)}, u32[]{:S(2)}) collective-permute-start(bf16[8,1024]{1,0:T(8,128)(2,1)S(1)} %get-tuple-element.23.refs_0_), channel_id=1, source_target_pairs={{0,2},{1,3},{2,0},{3,1},{4,6},{5,7},{6,4},{7,5},{8,10},{9,11},{10,... | collective-permute-start | bytes 49160 | tf_op jit(solution)/shard_map/ppermute | solution.py:340
  30.4 1.2 %collective-permute-done.12.refs_3_ = bf16[8,1024]{1,0:T(8,128)(2,1)S(1)} collective-permute-done((bf16[8,1024]{1,0:T(8,128)(2,1)S(1)}, bf16[8,1024]{1,0:T(8,128)(2,1)S(1)}, u32[]{:S(2)}, u32[]{:S(2)}) %collective-permute-start.12) | collective-permute-done | bytes 16416 | tf_op jit(solution)/shard_map/ppermute | solution.py:340
  31.6 1.3 %collective-permute-done.11.refs_2_ = bf16[8,1024]{1,0:T(8,128)(2,1)S(1)} collective-permute-done((bf16[8,1024]{1,0:T(8,128)(2,1)S(1)}, bf16[8,1024]{1,0:T(8,128)(2,1)S(1)}, u32[]{:S(2)}, u32[]{:S(2)}) %collective-permute-start.11) | collective-permute-done | bytes 16416 | tf_op jit(solution)/shard_map/ppermute | solution.py:340
  32.9 1.2 %shard_map.152 = bf16[32,2,640]{2,1,0:T(2,128)(2,1)S(1)} custom-call(bf16[8,1024]{1,0:T(8,128)(2,1)S(1)} %get-tuple-element.23.refs_0_, bf16[8,1024]{1,0:T(8,128)(2,1)S(1)} %collective-permute-done.10.refs_1_, bf16[8,1024]{1,0:T(8,128)(2,1)S(1)} %collective-permute-done.11.refs_2_, bf16[8,1024]{1,0:T(8,128)(2,1)S(1)} %collective-permute-done.12.refs_3_, ...), custom_call_target="tpu_custom_call" | custom-call | tf_op jit(solution)/shard_map/pallas_call | solution.py:317
  34.1 12.3 %all_to_all.5.received_ref = bf16[32,2,640]{2,1,0:T(2,128)(2,1)S(1)} all-to-all(bf16[32,2,640]{2,1,0:T(2,128)(2,1)S(1)} %shard_map.152), channel_id=1, replica_groups=mesh['req'=8,'head'=4] {'req','head'}, dimensions={0} | all-to-all | bytes 163840 | tf_op jit(solution)/shard_map/all_to_all | solution.py:449
  46.4 0.9 %shard_map.153 = bf16[2,1024]{1,0:T(2,128)(2,1)} custom-call(bf16[32,2,640]{2,1,0:T(2,128)(2,1)S(1)} %all_to_all.5.received_ref), custom_call_target="tpu_custom_call" | custom-call | tf_op jit(solution)/shard_map/pallas_call | solution.py:450
  (26 shorter events, 0.1 us)
Async XLA Ops:
  0.8 4.8 %collective-permute-start = (bf16[8,1152]{1,0:T(8,128)(2,1)S(1)}, bf16[8,1152]{1,0:T(8,128)(2,1)S(1)}, u32[]{:S(2)}, u32[]{:S(2)}) collective-permute-start(bf16[8,1152]{1,0:T(8,128)(2,1)S(1)} %shard_map.145.after_ref), channel_id=1, source_target_pairs={{0,4},{4,0},{8,12},{12,8},{16,20},{20,16},{24,28},{28,24},{1,5},{5... | collective-permute-start | bytes 55304 | tf_op jit(solution)/shard_map/ppermute | solution.py:340
  5.6 8.4 %collective-permute-start.3 = (bf16[16,1152]{1,0:T(8,128)(2,1)S(1)}, bf16[16,1152]{1,0:T(8,128)(2,1)S(1)}, u32[]{:S(2)}, u32[]{:S(2)}) collective-permute-start(bf16[16,1152]{1,0:T(8,128)(2,1)S(1)} %pad_maximum_fusion.after_ref.refs_0_), channel_id=1, source_target_pairs={{0,24},{4,28},{8,16},{12,20},{16,8},{20,12},{24,0},{28,4},{1,25},{... | collective-permute-start | bytes 110600 | tf_op jit(solution)/shard_map/ppermute | solution.py:340
  9.7 4.9 %collective-permute-start.2 = (bf16[16,1152]{1,0:T(8,128)(2,1)S(1)}, bf16[16,1152]{1,0:T(8,128)(2,1)S(1)}, u32[]{:S(2)}, u32[]{:S(2)}) collective-permute-start(bf16[16,1152]{1,0:T(8,128)(2,1)S(1)} %pad_maximum_fusion.after_ref.refs_0_), channel_id=1, source_target_pairs={{0,16},{4,20},{8,24},{12,28},{16,0},{20,4},{24,8},{28,12},{1,17},{... | collective-permute-start | bytes 110600 | tf_op jit(solution)/shard_map/ppermute | solution.py:340
  9.7 4.9 %collective-permute-start.1 = (bf16[16,1152]{1,0:T(8,128)(2,1)S(1)}, bf16[16,1152]{1,0:T(8,128)(2,1)S(1)}, u32[]{:S(2)}, u32[]{:S(2)}) collective-permute-start(bf16[16,1152]{1,0:T(8,128)(2,1)S(1)} %pad_maximum_fusion.after_ref.refs_0_), channel_id=1, source_target_pairs={{0,8},{4,12},{8,0},{12,4},{16,24},{20,28},{24,16},{28,20},{1,9},{5... | collective-permute-start | bytes 110600 | tf_op jit(solution)/shard_map/ppermute | solution.py:340
  10.3 10.5 %slice-start = ((s8[8388608]{0:T(1024)(128)(4,1)}), s8[4194304]{0:T(1024)(128)(4,1)S(1)}, s32[]{:S(2)}) async-start(s8[8388608]{0:T(1024)(128)(4,1)} %bitcast.1), calls=%async_computation.1 | async-start | bytes 8388608
  11.2 3.5 %copy-start.1 = (bf16[2,1024,768]{2,1,0:T(8,128)(2,1)S(1)}, bf16[2,1024,768]{2,1,0:T(8,128)(2,1)}, u32[]{:S(2)}) copy-start(bf16[2,1024,768]{2,1,0:T(8,128)(2,1)} %refs_10_.3) | copy-start | bytes 9437188
  11.3 3.7 %copy-start.2 = (bf16[2,256,1024]{2,1,0:T(8,128)(2,1)S(1)}, bf16[2,256,1024]{2,1,0:T(8,128)(2,1)}, u32[]{:S(2)}) copy-start(bf16[2,256,1024]{2,1,0:T(8,128)(2,1)} %refs_11_.3) | copy-start | bytes 3145732
  11.3 3.7 %copy-start.3 = (s32[8,512]{1,0:T(8,128)S(1)}, s32[8,512]{1,0:T(8,128)}, u32[]{:S(2)}) copy-start(s32[8,512]{1,0:T(8,128)} %refs_7_.4) | copy-start | bytes 49156
  11.3 3.7 %copy-start.4 = (f32[2,1024]{1,0:T(2,128)S(1)}, f32[2,1024]{1,0:T(2,128)}, u32[]{:S(2)}) copy-start(f32[2,1024]{1,0:T(2,128)} %refs_9_.4) | copy-start | bytes 24580
  11.3 3.7 %copy-start.6 = (f32[2,2,4]{2,1,0:T(2,128)S(1)}, f32[2,2,4]{2,1,0:T(2,128)}, u32[]{:S(2)}) copy-start(f32[2,2,4]{2,1,0:T(2,128)} %refs_12_.1) | copy-start | bytes 196
  11.3 3.7 %copy-start.7 = (f32[1,128]{1,0:T(1,128)S(1)}, f32[1,128]{1,0:T(1,128)}, u32[]{:S(2)}) copy-start(f32[1,128]{1,0:T(1,128)} %constant.8.clone.refs_5_) | copy-start | bytes 1540
  11.3 9.5 %slice-start.1 = ((s8[8388608]{0:T(1024)(128)(4,1)}), s8[4194304]{0:T(1024)(128)(4,1)S(1)}, s32[]{:S(2)}) async-start(s8[8388608]{0:T(1024)(128)(4,1)} %bitcast.1), calls=%async_computation.2 | async-start | bytes 8388608
  15.0 5.8 %copy-start = (bf16[2,1024,1024]{2,1,0:T(8,128)(2,1)S(1)}, bf16[2,1024,1024]{2,1,0:T(8,128)(2,1)}, u32[]{:S(2)}) copy-start(bf16[2,1024,1024]{2,1,0:T(8,128)(2,1)} %refs_9_.5) | copy-start | bytes 12582916
  15.0 5.8 %copy-start.5 = (f32[2,1024]{1,0:T(2,128)S(1)}, f32[2,1024]{1,0:T(2,128)}, u32[]{:S(2)}) copy-start(f32[2,1024]{1,0:T(2,128)} %refs_7_.5) | copy-start | bytes 24580
  17.0 3.2 %collective-permute-start.6 = (bf16[8,1024]{1,0:T(8,128)(2,1)S(1)}, bf16[8,1024]{1,0:T(8,128)(2,1)S(1)}, u32[]{:S(2)}, u32[]{:S(2)}) collective-permute-start(bf16[8,1024]{1,0:T(8,128)(2,1)S(1)} %get-tuple-element.17.refs_0_.after_ref), channel_id=1, source_target_pairs={{0,3},{1,2},{2,1},{3,0},{4,7},{5,6},{6,5},{7,4},{8,11},{9,10},{10,... | collective-permute-start | bytes 49160 | tf_op jit(solution)/shard_map/ppermute | solution.py:340
  17.0 3.8 %collective-permute-start.5 = (bf16[8,1024]{1,0:T(8,128)(2,1)S(1)}, bf16[8,1024]{1,0:T(8,128)(2,1)S(1)}, u32[]{:S(2)}, u32[]{:S(2)}) collective-permute-start(bf16[8,1024]{1,0:T(8,128)(2,1)S(1)} %get-tuple-element.17.refs_0_.after_ref), channel_id=1, source_target_pairs={{0,2},{1,3},{2,0},{3,1},{4,6},{5,7},{6,4},{7,5},{8,10},{9,11},{10,... | collective-permute-start | bytes 49160 | tf_op jit(solution)/shard_map/ppermute | solution.py:340
  18.7 2.1 %collective-permute-start.4 = (bf16[8,1024]{1,0:T(8,128)(2,1)S(1)}, bf16[8,1024]{1,0:T(8,128)(2,1)S(1)}, u32[]{:S(2)}, u32[]{:S(2)}) collective-permute-start(bf16[8,1024]{1,0:T(8,128)(2,1)S(1)} %get-tuple-element.17.refs_0_.after_ref), channel_id=1, source_target_pairs={{0,1},{1,0},{2,3},{3,2},{4,5},{5,4},{6,7},{7,6},{8,9},{9,8},{10,11... | collective-permute-start | bytes 49160 | tf_op jit(solution)/shard_map/ppermute | solution.py:340
  21.9 4.4 %collective-permute-start.9 = (bf16[8,1024]{1,0:T(8,128)(2,1)S(1)}, bf16[8,1024]{1,0:T(8,128)(2,1)S(1)}, u32[]{:S(2)}, u32[]{:S(2)}) collective-permute-start(bf16[8,1024]{1,0:T(8,128)(2,1)S(1)} %get-tuple-element.19.refs_0_), channel_id=1, source_target_pairs={{0,3},{1,2},{2,1},{3,0},{4,7},{5,6},{6,5},{7,4},{8,11},{9,10},{10,... | collective-permute-start | bytes 49160 | tf_op jit(solution)/shard_map/ppermute | solution.py:340
  22.6 3.9 %collective-permute-start.8 = (bf16[8,1024]{1,0:T(8,128)(2,1)S(1)}, bf16[8,1024]{1,0:T(8,128)(2,1)S(1)}, u32[]{:S(2)}, u32[]{:S(2)}) collective-permute-start(bf16[8,1024]{1,0:T(8,128)(2,1)S(1)} %get-tuple-element.19.refs_0_), channel_id=1, source_target_pairs={{0,2},{1,3},{2,0},{3,1},{4,6},{5,7},{6,4},{7,5},{8,10},{9,11},{10,... | collective-permute-start | bytes 49160 | tf_op jit(solution)/shard_map/ppermute | solution.py:340
  24.1 2.4 %collective-permute-start.7 = (bf16[8,1024]{1,0:T(8,128)(2,1)S(1)}, bf16[8,1024]{1,0:T(8,128)(2,1)S(1)}, u32[]{:S(2)}, u32[]{:S(2)}) collective-permute-start(bf16[8,1024]{1,0:T(8,128)(2,1)S(1)} %get-tuple-element.19.refs_0_), channel_id=1, source_target_pairs={{0,1},{1,0},{2,3},{3,2},{4,5},{5,4},{6,7},{7,6},{8,9},{9,8},{10,11... | collective-permute-start | bytes 49160 | tf_op jit(solution)/shard_map/ppermute | solution.py:340
  28.4 3.2 %collective-permute-start.12 = (bf16[8,1024]{1,0:T(8,128)(2,1)S(1)}, bf16[8,1024]{1,0:T(8,128)(2,1)S(1)}, u32[]{:S(2)}, u32[]{:S(2)}) collective-permute-start(bf16[8,1024]{1,0:T(8,128)(2,1)S(1)} %get-tuple-element.23.refs_0_), channel_id=1, source_target_pairs={{0,3},{1,2},{2,1},{3,0},{4,7},{5,6},{6,5},{7,4},{8,11},{9,10},{10,... | collective-permute-start | bytes 49160 | tf_op jit(solution)/shard_map/ppermute | solution.py:340
  29.2 3.7 %collective-permute-start.11 = (bf16[8,1024]{1,0:T(8,128)(2,1)S(1)}, bf16[8,1024]{1,0:T(8,128)(2,1)S(1)}, u32[]{:S(2)}, u32[]{:S(2)}) collective-permute-start(bf16[8,1024]{1,0:T(8,128)(2,1)S(1)} %get-tuple-element.23.refs_0_), channel_id=1, source_target_pairs={{0,2},{1,3},{2,0},{3,1},{4,6},{5,7},{6,4},{7,5},{8,10},{9,11},{10,... | collective-permute-start | bytes 49160 | tf_op jit(solution)/shard_map/ppermute | solution.py:340
  30.4 2.5 %collective-permute-start.10 = (bf16[8,1024]{1,0:T(8,128)(2,1)S(1)}, bf16[8,1024]{1,0:T(8,128)(2,1)S(1)}, u32[]{:S(2)}, u32[]{:S(2)}) collective-permute-start(bf16[8,1024]{1,0:T(8,128)(2,1)S(1)} %get-tuple-element.23.refs_0_), channel_id=1, source_target_pairs={{0,1},{1,0},{2,3},{3,2},{4,5},{5,4},{6,7},{7,6},{8,9},{9,8},{10,11... | collective-permute-start | bytes 49160 | tf_op jit(solution)/shard_map/ppermute | solution.py:340

commit v5 on v4

v5 whole, which is shorter than its diff:
```python
import functools

import jax
import jax.numpy as jnp
import numpy as np
from jax import lax
from jax.experimental import pallas as pl
from jax.experimental.pallas import tpu as pltpu
from jax.sharding import PartitionSpec as P

HD = 64
LAYERS = 2
META = 128
LOW = 128
CHUNK = 128
NEG = -1e30
F32 = jnp.float32
BF16 = jnp.bfloat16

VMEM = pl.BlockSpec(memory_space=pltpu.VMEM)
HBM = pl.BlockSpec(memory_space=pltpu.HBM)
ANY = pl.BlockSpec(memory_space=pl.ANY)
LONG = pl.CostEstimate(flops=10**11, bytes_accessed=0, transcendentals=0)
SHORT = pl.CostEstimate(flops=10**6, bytes_accessed=0, transcendentals=0)
PARAMS = pltpu.CompilerParams(vmem_limit_bytes=16 * 2**20)


def iota(shape, dim):
    return lax.broadcasted_iota(jnp.int32, shape, dim)


def copy_all(pairs, sems):
    copies = [pltpu.make_async_copy(src, dst, sems.at[i]) for i, (src, dst) in enumerate(pairs)]
    for copy in copies:
        copy.start()
    for copy in copies:
        copy.wait()


def pack_kernel(
    tokens_ref, lengths_ref, positions_ref, variates_ref, out_ref, length, position, variate, sems
):
    rows, width = tokens_ref.shape
    copy_all(
        [
            (lengths_ref, length),
            (positions_ref, position),
            (variates_ref, variate),
            (tokens_ref, out_ref.at[:, pl.ds(0, width)]),
        ],
        sems,
    )
    row, lane = iota((rows, META), 0), iota((rows, META), 1)
    kind = lane % (META // 2)
    whole = jnp.zeros((rows, META), jnp.int32)
    for i in range(rows):
        values = jnp.where(kind == 0, length[i], jnp.where(kind == 1, position[i], variate[i]))
        whole = jnp.where(row == i, values, whole)
    digit = jnp.where(lane < META // 2, whole // LOW, whole % LOW)
    out_ref[:, width:] = digit.astype(F32).astype(BF16)


def cache_copies(layer, kv_ref, front_ref, lead_ref, sems, first):
    rest = kv_ref.shape[3] - CHUNK
    return [
        pltpu.make_async_copy(
            kv_ref.at[layer, :, :, pl.ds(0, CHUNK), :], front_ref, sems.at[first]
        ),
        pltpu.make_async_copy(
            kv_ref.at[layer, :, 0, pl.ds(CHUNK, rest), :], lead_ref, sems.at[first + 1]
        ),
    ]


def owner_kernel(
    share,
    block_ids,
    after_ref,
    owner_ref,
    own_block_ref,
    kv_ref,
    pick_ref,
    place_ref,
    flag_ref,
    front_ref,
    lead_ref,
    owner,
    own_block,
    sems,
):
    copies = [
        pltpu.make_async_copy(owner_ref, owner, sems.at[0]),
        pltpu.make_async_copy(own_block_ref, own_block, sems.at[1]),
    ] + cache_copies(0, kv_ref, front_ref, lead_ref, sems, 2)
    for copy in copies:
        copy.start()
    copies[0].wait()
    copies[1].wait()
    slots, total = pick_ref.shape
    devices = place_ref.shape[0]
    row, column = iota((slots, total), 0), iota((slots, total), 1)
    target, slot = iota((devices, slots), 0), iota((devices, slots), 1)
    flag_row, lane = iota((slots, META), 0), iota((slots, META), 1)
    block = jnp.zeros((slots, total), jnp.int32)
    for k, block_id in enumerate(block_ids):
        block = jnp.where(column // slots == k, block_id, block)
    request_at = (block ^ own_block[0]) * slots + column % slots
    pick = jnp.zeros((slots, total), F32)
    place = jnp.zeros((devices, slots), F32)
    flag = jnp.zeros((slots, META), F32)
    for s in range(slots):
        request = owner[s]
        pick = jnp.where((row == s) & (request_at == request), 1.0, pick)
        place = jnp.where((slot == s) & (target == request // share), 1.0, place)
        flag = jnp.where((flag_row == s) & (lane == request % share), 1.0, flag)
    pick_ref[...] = pick.astype(BF16)
    place_ref[...] = place.astype(BF16)
    flag_ref[...] = flag.astype(BF16)
    copies[2].wait()
    copies[3].wait()


def cache_kernel(layer, after_ref, kv_ref, front_ref, lead_ref, sems):
    copies = cache_copies(layer, kv_ref, front_ref, lead_ref, sems, 0)
    for copy in copies:
        copy.start()
    for copy in copies:
        copy.wait()


def attention(
    layer,
    stream,
    facts,
    cos,
    sin,
    variates_ref,
    front_ref,
    lead_ref,
    kv_ref,
    gain_ref,
    qkv_ref,
    out_w_ref,
    bias_ref,
    scores,
    mixed,
    attended,
    rest_kv,
    rest_sems,
    part_ref,
):
    slots, cap = variates_ref.shape
    width = front_ref.shape[-1]
    heads = width // HD
    rows = heads * slots
    rest = cap - CHUNK

    lengths = facts[:, 0:1]
    variate = facts[:, 2:3]
    longer = jnp.sum((lengths > CHUNK).astype(jnp.int32))

    scale = lax.rsqrt(jnp.mean(stream * stream, axis=-1, keepdims=True) + 1e-06)
    scaled = (stream * gain_ref[layer : layer + 1, :]).astype(BF16)
    projected = jnp.dot(scaled, qkv_ref[layer], preferred_element_type=F32) * scale

    lane = iota((slots, 128), 1)
    front_half = lane % HD < HD // 2
    pieces = []
    for j in range(projected.shape[1] // 128):
        u = projected[:, j * 128 : (j + 1) * 128]
        turned = jnp.where(front_half, -pltpu.roll(u, 96, 1), pltpu.roll(u, 32, 1))
        is_value = (lane + j * 128) % (3 * HD) >= 2 * HD
        pieces.append(jnp.where(is_value, u, u * cos + turned * sin).astype(BF16).astype(F32))
    turned_all = jnp.concatenate(pieces, axis=1)

    column = iota((slots, width), 1)
    of_head = [column // HD == h for h in range(heads)]
    step = 2 * HD
    query = [
        jnp.where(of_head[h], turned_all[:, h * step : h * step + width], 0.0) for h in range(heads)
    ]
    query_all = jnp.concatenate(query, axis=0).astype(BF16)
    row_slot = iota((rows, CHUNK), 0) % slots
    rest_slot = iota((rows, rest), 0) % slots

    def score(keys):
        return lax.dot_general(
            query_all, keys, (((1,), (1,)), ((), ())), preferred_element_type=F32
        )

    raw = score(front_ref[0].reshape(slots * CHUNK, width))
    front_scores = raw[:, :CHUNK]
    for s in range(1, slots):
        front_scores = jnp.where(
            row_slot == s, raw[:, s * CHUNK : (s + 1) * CHUNK], front_scores
        )
    lead_scores = score(lead_ref[0])

    next_keys = jnp.concatenate([turned_all[:, HD:], jnp.zeros((slots, HD), F32)], axis=1)
    own_score = [
        jnp.sum(query[h] * next_keys[:, h * step : h * step + width], axis=1, keepdims=True) * 0.125
        + bias_ref[layer, 0:1, h : h + 1]
        for h in range(heads)
    ]
    same = variates_ref[...].astype(F32) == variate
    live = iota((slots, cap), 1).astype(F32) < lengths

    def soften(raw_scores):
        probs, own_prob = [], []
        for h in range(heads):
            block = raw_scores[h * slots : (h + 1) * slots, :] * 0.125
            block = block + jnp.where(
                same, bias_ref[layer, 0:1, h : h + 1], bias_ref[layer, 1:2, h : h + 1]
            )
            block = jnp.where(live, block, NEG)
            top = jnp.maximum(jnp.max(block, axis=1, keepdims=True), own_score[h])
            weight = jnp.exp(block - top)
            own_weight = jnp.exp(own_score[h] - top)
            share = 1.0 / (jnp.sum(weight, axis=1, keepdims=True) + own_weight)
            probs.append(weight * share)
            own_prob.append((own_weight * share).astype(BF16).astype(F32))
        return jnp.concatenate(probs, axis=0).astype(BF16), own_prob

    def only(mask, probs):
        return jnp.where(mask, probs, jnp.zeros_like(probs))

    def mix(probs):
        spread = jnp.concatenate([only(row_slot == s, probs[:, :CHUNK]) for s in range(slots)], 1)
        front = jnp.dot(
            spread, front_ref[1].reshape(slots * CHUNK, width), preferred_element_type=F32
        )
        lead = only(rest_slot == 0, probs[:, CHUNK:])
        return front + jnp.dot(lead, lead_ref[1], preferred_element_type=F32)

    def lay_out(mixed_rows, own_prob):
        result = jnp.zeros((slots, width), F32)
        for h in range(heads):
            value_new = turned_all[:, (h + 1) * step : (h + 1) * step + width]
            result = jnp.where(
                of_head[h], mixed_rows[h * slots : (h + 1) * slots, :] + own_prob[h] * value_new,
                result,
            )
        return result

    all_scores = jnp.concatenate([front_scores, lead_scores], axis=1)
    probs_all, own_probs = soften(all_scores)
    attended[...] = lay_out(mix(probs_all), own_probs)

    @pl.when(longer > 1)
    def _():
        def rest_copy(s):
            return pltpu.make_async_copy(
                kv_ref.at[layer, :, s, pl.ds(CHUNK, rest), :], rest_kv.at[s], rest_sems.at[s]
            )

        @pl.loop(1, longer)
        def _(s):
            rest_copy(s).start()

        scores[...] = all_scores

        @pl.loop(1, longer)
        def _(s):
            rest_copy(s).wait()
            scores[:, CHUNK:] = jnp.where(rest_slot == s, score(rest_kv[s, 0]), scores[:, CHUNK:])

        probs_long, own_long = soften(scores[...])
        mixed[...] = mix(probs_long)
        rest_probs = probs_long[:, CHUNK:]

        @pl.loop(1, longer)
        def _(s):
            mixed[...] += jnp.dot(
                only(rest_slot == s, rest_probs), rest_kv[s, 1], preferred_element_type=F32
            )

        attended[...] = lay_out(mixed[...], own_long)

    part_ref[...] = jnp.dot(
        attended[...].astype(BF16), out_w_ref[layer], preferred_element_type=F32
    ).astype(BF16)


def first_attention_kernel(block_count, *refs):
    (
        pick_ref,
        frequency_ref,
        variates_ref,
        front_ref,
        lead_ref,
        kv_ref,
        gain_ref,
        qkv_ref,
        out_w_ref,
        bias_ref,
        part_ref,
        stream_ref,
        facts_ref,
        turn_ref,
        *scratch,
    ) = refs[block_count:]
    gathered = jnp.concatenate([ref[...] for ref in refs[:block_count]], axis=0)
    width = stream_ref.shape[1]
    picked = jnp.dot(pick_ref[...], gathered, preferred_element_type=F32)
    stream = picked[:, :width]
    digits = picked[:, width:]
    facts = digits * float(LOW) + pltpu.roll(digits, META // 2, 1)
    stream_ref[...] = stream
    facts_ref[...] = facts
    angle = facts[:, 1:2] * frequency_ref[...]
    cos, sin = jnp.cos(angle), jnp.sin(angle)
    turn_ref[:, :128] = cos
    turn_ref[:, 128:] = sin
    attention(
        0, stream, facts, cos, sin, variates_ref, front_ref, lead_ref, kv_ref, gain_ref, qkv_ref,
        out_w_ref, bias_ref, *scratch, part_ref,
    )


def next_attention_kernel(layer, part_count, *refs):
    (
        old_ref,
        facts_ref,
        turn_ref,
        variates_ref,
        front_ref,
        lead_ref,
        kv_ref,
        gain_ref,
        qkv_ref,
        out_w_ref,
        bias_ref,
        part_ref,
        stream_ref,
        *scratch,
    ) = refs[part_count:]
    stream = old_ref[...]
    for ref in refs[:part_count]:
        stream = stream + ref[...].astype(F32)
    stream_ref[...] = stream
    attention(
        layer, stream, facts_ref[...], turn_ref[:, :128], turn_ref[:, 128:], variates_ref,
        front_ref, lead_ref, kv_ref, gain_ref, qkv_ref, out_w_ref, bias_ref, *scratch, part_ref,
    )


def feed_forward(layer, part_refs, old_ref, gain_ref, gate_up_ref, down_ref):
    stream = old_ref[...]
    for ref in part_refs:
        stream = stream + ref[...].astype(F32)
    scale = lax.rsqrt(jnp.mean(stream * stream, axis=-1, keepdims=True) + 1e-06)
    scaled = (stream * gain_ref[layer : layer + 1, :]).astype(BF16)
    gate = jnp.dot(scaled, gate_up_ref[layer, 0], preferred_element_type=F32) * scale
    up = jnp.dot(scaled, gate_up_ref[layer, 1], preferred_element_type=F32) * scale
    hidden = (gate / (1.0 + jnp.exp(-gate)) * up).astype(BF16)
    return stream, jnp.dot(hidden, down_ref[layer], preferred_element_type=F32)


def feed_forward_kernel(layer, part_count, *refs):
    old_ref, gain_ref, gate_up_ref, down_ref, part_ref, stream_ref = refs[part_count:]
    stream, part = feed_forward(layer, refs[:part_count], old_ref, gain_ref, gate_up_ref, down_ref)
    stream_ref[...] = stream
    part_ref[...] = part.astype(BF16)


def last_feed_forward_kernel(layer, part_count, head_count, *refs):
    place_ref, flag_ref, old_ref, gain_ref, gate_up_ref, down_ref, send_ref = refs[part_count:]
    stream, part = feed_forward(layer, refs[:part_count], old_ref, gain_ref, gate_up_ref, down_ref)
    rows = (part + stream * (1.0 / head_count)).astype(BF16)
    half = rows.shape[1] // 2
    for i in range(2):
        payload = jnp.concatenate([rows[:, i * half : (i + 1) * half], flag_ref[...]], axis=1)
        spread = jnp.dot(place_ref[...], payload, preferred_element_type=F32)
        send_ref[:, i, :] = spread.astype(BF16)


def place_kernel(received_ref, out_ref):
    share, width = out_ref.shape
    half = width // 2
    for i in range(2):
        rows = lax.dot_general(
            received_ref[:, i, half:],
            received_ref[:, i, :half],
            (((0,), (0,)), ((), ())),
            preferred_element_type=F32,
        )
        out_ref[:, i * half : (i + 1) * half] = rows[:share, :].astype(BF16)


def call(kernel, operands, outs, scratch=(), cost=SHORT):
    specs = [spec for spec, _ in operands]
    arrays = [
        pltpu.with_memory_space_constraint(array, pltpu.HBM) if spec is HBM else array
        for spec, array in operands
    ]
    return pl.pallas_call(
        kernel,
        out_shape=[pltpu.VMEM(shape, dtype) for shape, dtype in outs],
        in_specs=specs,
        out_specs=[VMEM] * len(outs),
        scratch_shapes=list(scratch),
        compiler_params=PARAMS,
        cost_estimate=cost,
    )(*arrays)


def swap(array, axis, mask):
    count = lax.axis_size(axis)
    return lax.ppermute(array, axis, [(i, i ^ mask) for i in range(count)])


def gather_stages(count):
    stages = []
    top = count
    if count.bit_length() % 2 == 0:
        top = count // 2
        stages.append([top])
    while top > 1:
        stages.append([top // 4 * k for k in (1, 2, 3)])
        top //= 4
    return stages


def swap_across(array, mask):
    reqs, heads = lax.axis_size("req"), lax.axis_size("head")
    pairs = [
        (r * heads + h, (r ^ mask) * heads + (h ^ 1)) for r in range(reqs) for h in range(heads)
    ]
    return lax.ppermute(array, ("req", "head"), pairs)


def gather_blocks(block):
    blocks, ids = [block], [0]
    for masks in gather_stages(lax.axis_size("req")):
        held = blocks[0] if len(blocks) == 1 else jnp.concatenate(blocks, axis=0)
        blocks = [held] + [swap_across(held, mask) for mask in masks]
        ids = ids + [mask ^ i for mask in masks for i in ids]
    return blocks, ids


def per_device(
    tokens,
    lengths,
    slot_owner,
    positions,
    variates,
    cache_variates,
    kv_cache,
    attn_gain,
    ffn_gain,
    qkv_weight,
    out_weight,
    gate_up_weight,
    down_weight,
    variate_bias,
):
    slots, width = tokens.shape
    cap, local_width = kv_cache.shape[3:]
    head_count = lax.axis_size("head")
    devices = lax.axis_size("req") * head_count
    share = slots // head_count
    local_heads = local_width // HD

    total = slots * lax.axis_size("req")
    whole_row = [pltpu.SMEM((slots,), jnp.int32)] * 3
    (packed,) = call(
        pack_kernel,
        [(HBM, tokens), (HBM, lengths), (HBM, positions), (HBM, variates)],
        [((slots, width + META), BF16)],
        whole_row + [pltpu.SemaphoreType.DMA((4,))],
        LONG,
    )
    exponent = -2.0 * (np.arange(128) % (HD // 2)) / HD
    frequency = jnp.asarray((10000.0**exponent).astype(np.float32)[None, :])
    own_block = lax.axis_index("req").reshape(1)
    blocks, block_ids = gather_blocks(packed)
    cache_types = [
        ((2, slots, CHUNK, local_width), BF16),
        ((2, cap - CHUNK, local_width), BF16),
    ]
    pick, place, flag, *cache = call(
        functools.partial(owner_kernel, share, block_ids),
        [(ANY, packed), (HBM, slot_owner), (HBM, own_block), (HBM, kv_cache)],
        [((slots, total), BF16), ((devices, slots), BF16), ((slots, META), BF16)]
        + cache_types,
        [
            pltpu.SMEM((slots,), jnp.int32),
            pltpu.SMEM((1,), jnp.int32),
            pltpu.SemaphoreType.DMA((4,)),
        ],
    )

    scratch = [
        pltpu.VMEM((local_heads * slots, cap), F32),
        pltpu.VMEM((local_heads * slots, local_width), F32),
        pltpu.VMEM((slots, local_width), F32),
        pltpu.VMEM((slots, 2, cap - CHUNK, local_width), BF16),
        pltpu.SemaphoreType.DMA((slots,)),
    ]
    stream_type = ((slots, width), F32)
    part_type = ((slots, width), BF16)

    def exchange(part):
        return [part] + [swap(part, "head", k) for k in range(1, head_count)]

    def on_chip(*arrays):
        return [(VMEM, x) for x in arrays]

    part, stream, facts, turn = call(
        functools.partial(first_attention_kernel, len(blocks)),
        on_chip(*blocks, pick, frequency, cache_variates, *cache)
        + [(HBM, kv_cache)]
        + on_chip(attn_gain, qkv_weight, out_weight, variate_bias),
        [part_type, stream_type, ((slots, META), F32), ((slots, 256), F32)],
        scratch,
    )
    for layer in range(LAYERS):
        last = layer == LAYERS - 1
        if layer:
            part, stream = call(
                functools.partial(next_attention_kernel, layer, len(parts)),
                on_chip(*parts, stream, facts, turn, cache_variates, *cache)
                + [(HBM, kv_cache)]
                + on_chip(attn_gain, qkv_weight, out_weight, variate_bias),
                [part_type, stream_type],
                scratch,
            )
        parts = exchange(part)
        if not last:
            part, stream = call(
                functools.partial(feed_forward_kernel, layer, len(parts)),
                on_chip(*parts, stream, ffn_gain, gate_up_weight, down_weight),
                [part_type, stream_type],
            )
            parts = exchange(part)
            cache = call(
                functools.partial(cache_kernel, layer + 1),
                [(ANY, part), (HBM, kv_cache)],
                cache_types,
                [pltpu.SemaphoreType.DMA((2,))],
            )
        else:
            (send,) = call(
                functools.partial(last_feed_forward_kernel, layer, len(parts), head_count),
                on_chip(*parts, place, flag, stream, ffn_gain, gate_up_weight, down_weight),
                [((devices, 2, width // 2 + META), BF16)],
            )
    received = lax.all_to_all(send, ("req", "head"), 0, 0, tiled=True)
    return pl.pallas_call(
        place_kernel,
        out_shape=jax.ShapeDtypeStruct((share, width), BF16),
        in_specs=[VMEM],
        out_specs=VMEM,
        compiler_params=PARAMS,
    )(received)


def solution(mesh):
    return jax.shard_map(
        per_device,
        mesh=mesh,
        in_specs=(
            P("req", None),
            P("req"),
            P("req"),
            P("req"),
            P("req"),
            P("req", None),
            P(None, None, "req", None, "head"),
            P(),
            P(),
            P(None, None, "head"),
            P(None, "head", None),
            P(None, None, None, "head"),
            P(None, "head", None),
            P(None, None, "head"),
        ),
        out_specs=P(("req", "head"), None),
        check_vma=False,
    )
```

time: 47.6 us -> 44.6 us (0.937)
  Pallas kernels: 13.5 us -> 9.72 us
  waiting for transfers between devices: 6.95 us -> 9.42 us
  starting transfers between devices: 13.8 us -> 12.8 us
    ppermute x13 -> x9, starting transfers between devices: 13.8 us -> 5.72 us  [swap(): return lax.ppermute(array, axis, [(i, i ^ mask) for i in range(count)])]
    ppermute x0 -> x4, starting transfers between devices: none -> 7.04 us  [swap_across(): return lax.ppermute(array, ('req', 'head'), pairs)]
    pallas_call x8 -> x7, Pallas kernels: 12.6 us -> 8.8 us  [call(): pl.pallas_call(kernel, out_shape=[pltpu.VMEM(shape, dtype) for shape, dty...]
    ppermute x0 -> x4, waiting for transfers between devices: none -> 3.27 us  [swap_across(): return lax.ppermute(array, ('req', 'head'), pairs)]
    ppermute x13 -> x9, waiting for transfers between devices: 6.95 us -> 6.15 us  [swap(): return lax.ppermute(array, axis, [(i, i ^ mask) for i in range(count)])]
  transfers between devices with their start and end apart: 13 -> 13, of which waited for: 7 -> 8; matrix products, arithmetic and copies ran while one was open for 0% -> 0% of each run, Pallas kernels for 12% -> 6%
where the time goes in v5:
time: 44.6 us; the launch traced here: 44.3 us
  starting transfers between devices  12.8 us (29%)
  blocking collectives  12.1 us (27%)
  Pallas kernels  9.72 us (22%)
  waiting for transfers between devices  9.42 us (21%)
    all_to_all x1, blocking collectives, per_device(): received = lax.all_to_all(send, ('req', 'head'), 0, 0, tiled=True)  12.1 us
    pallas_call x7, Pallas kernels, call(): pl.pallas_call(kernel, out_shape=[pltpu.VMEM(shape, dtype) for shape, dty...  8.8 us
    ppermute x4, starting transfers between devices, swap_across(): return lax.ppermute(array, ('req', 'head'), pairs)  7.04 us
    ppermute x9, waiting for transfers between devices, swap(): return lax.ppermute(array, axis, [(i, i ^ mask) for i in range(count)])  6.15 us
    ppermute x9, starting transfers between devices, swap(): return lax.ppermute(array, axis, [(i, i ^ mask) for i in range(count)])  5.72 us
    ppermute x4, waiting for transfers between devices, swap_across(): return lax.ppermute(array, ('req', 'head'), pairs)  3.27 us
    pallas_call x1, Pallas kernels, per_device(): pl.pallas_call(place_kernel, out_shape=jax.ShapeDtypeStruct((share, width...  0.91 us
  transfers between devices with their start and end apart: 13, of which 8 were waited for; matrix products, arithmetic and copies ran while one was open for 0% of the time, Pallas kernels for 6%

profile of v5, /device:TPU:0, one launch (start us, length us, event | category | flops | bytes accessed | tf_op | source)
XLA Modules:
  0.0 44.3 jit_solution(5758507992750368219)
XLA Ops:
  0.0 0.8 %shard_map.145.after_ref = bf16[8,1152]{1,0:T(8,128)(2,1)S(1)} custom-call(bf16[8,1024]{1,0:T(8,128)(2,1)} %tokens_ref.1, s32[8]{0:T(128)} %lengths_ref.1, s32[8]{0:T(128)} %positions_ref.1, s32[8]{0:T(128)} %variates_ref.1), custom_call_target="tpu_custom_call" | custom-call | flops 99999997952 | tf_op jit(solution)/shard_map/pallas_call | solution.py:396
  0.8 0.0 copy-start.3
  0.8 0.0 copy-start.7
  0.8 3.5 %collective-permute-start = (bf16[8,1152]{1,0:T(8,128)(2,1)S(1)}, bf16[8,1152]{1,0:T(8,128)(2,1)S(1)}, u32[]{:S(2)}, u32[]{:S(2)}) collective-permute-start(bf16[8,1152]{1,0:T(8,128)(2,1)S(1)} %shard_map.145.after_ref), channel_id=1, source_target_pairs={{0,17},{1,16},{2,19},{3,18},{4,21},{5,20},{6,23},{7,22},{8,25},{9,... | collective-permute-start | bytes 55304 | tf_op jit(solution)/shard_map/ppermute | solution.py:429
  4.4 1.5 %collective-permute-done = bf16[8,1152]{1,0:T(8,128)(2,1)S(1)} collective-permute-done((bf16[8,1152]{1,0:T(8,128)(2,1)S(1)}, bf16[8,1152]{1,0:T(8,128)(2,1)S(1)}, u32[]{:S(2)}, u32[]{:S(2)}) %collective-permute-start) | collective-permute-done | bytes 18464 | tf_op jit(solution)/shard_map/ppermute | solution.py:429
  5.9 2.8 %collective-permute-start.3 = (bf16[16,1152]{1,0:T(8,128)(2,1)S(1)}, bf16[16,1152]{1,0:T(8,128)(2,1)S(1)}, u32[]{:S(2)}, u32[]{:S(2)}) collective-permute-start(bf16[16,1152]{1,0:T(8,128)(2,1)S(1)} %pad_maximum_fusion.refs_0_), channel_id=1, source_target_pairs={{0,13},{1,12},{2,15},{3,14},{4,9},{5,8},{6,11},{7,10},{8,5},{9,4},... | collective-permute-start | bytes 110600 | tf_op jit(solution)/shard_map/ppermute | solution.py:429
  8.7 0.5 %collective-permute-start.2 = (bf16[16,1152]{1,0:T(8,128)(2,1)S(1)}, bf16[16,1152]{1,0:T(8,128)(2,1)S(1)}, u32[]{:S(2)}, u32[]{:S(2)}) collective-permute-start(bf16[16,1152]{1,0:T(8,128)(2,1)S(1)} %pad_maximum_fusion.refs_0_), channel_id=1, source_target_pairs={{0,9},{1,8},{2,11},{3,10},{4,13},{5,12},{6,15},{7,14},{8,1},{9,0},... | collective-permute-start | bytes 110600 | tf_op jit(solution)/shard_map/ppermute | solution.py:429
  9.2 0.2 collective-permute-start.1
  9.4 1.5 %shard_map.146 = (bf16[8,64]{1,0:T(8,128)(2,1)S(1)}, bf16[32,8]{1,0:T(8,128)(2,1)S(1)}, bf16[8,128]{1,0:T(8,128)(2,1)S(1)}, bf16[2,8,128,256]{3,2,1,0:T(8,128)(2,1)S(1)}, bf16[2,384,256]{2,1,0:T(8,128)(2,1)S(1)}) custom-call(bf16[8,1152]{1,0:T(8,128)(2,1)S(1)} %shard_map.145.after_ref, s32[8]{0:T(128)} %owner_ref.1, s32[1]{0:T(128)} %bitcast.own_block_ref, ...), custom_call_target="tpu_custom_call" | custom-call | flops 1000000 | tf_op jit(solution)/shard_map/pallas_call | solution.py:396
  10.9 1.2 %collective-permute-done.2.refs_2_ = bf16[16,1152]{1,0:T(8,128)(2,1)S(1)} collective-permute-done((bf16[16,1152]{1,0:T(8,128)(2,1)S(1)}, bf16[16,1152]{1,0:T(8,128)(2,1)S(1)}, u32[]{:S(2)}, u32[]{:S(2)}) %collective-permute-start.2) | collective-permute-done | bytes 36896 | tf_op jit(solution)/shard_map/ppermute | solution.py:429
  12.1 0.6 %collective-permute-done.1.refs_1_ = bf16[16,1152]{1,0:T(8,128)(2,1)S(1)} collective-permute-done((bf16[16,1152]{1,0:T(8,128)(2,1)S(1)}, bf16[16,1152]{1,0:T(8,128)(2,1)S(1)}, u32[]{:S(2)}, u32[]{:S(2)}) %collective-permute-start.1) | collective-permute-done | bytes 36896 | tf_op jit(solution)/shard_map/ppermute | solution.py:429
  12.7 0.0 slice-start.1
  12.8 1.6 %shard_map.147 = (bf16[8,1024]{1,0:T(8,128)(2,1)S(1)}, f32[8,1024]{1,0:T(8,128)S(1)}, f32[8,128]{1,0:T(8,128)S(1)}, f32[8,256]{1,0:T(8,128)S(1)}) custom-call(bf16[16,1152]{1,0:T(8,128)(2,1)S(1)} %pad_maximum_fusion.refs_0_, bf16[16,1152]{1,0:T(8,128)(2,1)S(1)} %collective-permute-done.1.refs_1_, bf16[16,1152]{1,0:T(8,128)(2,1)S(1)} %collective-permute-done.2.refs_2_, ...), custom_call_target="tpu_custom_call" | custom-call | flops 1000000 | tf_op jit(solution)/shard_map/pallas_call | solution.py:396
  14.4 1.3 %collective-permute-start.6 = (bf16[8,1024]{1,0:T(8,128)(2,1)S(1)}, bf16[8,1024]{1,0:T(8,128)(2,1)S(1)}, u32[]{:S(2)}, u32[]{:S(2)}) collective-permute-start(bf16[8,1024]{1,0:T(8,128)(2,1)S(1)} %get-tuple-element.23.refs_0_), channel_id=1, source_target_pairs={{0,3},{1,2},{2,1},{3,0},{4,7},{5,6},{6,5},{7,4},{8,11},{9,10},{10,... | collective-permute-start | bytes 49160 | tf_op jit(solution)/shard_map/ppermute | solution.py:409
  15.7 0.6 %collective-permute-start.5 = (bf16[8,1024]{1,0:T(8,128)(2,1)S(1)}, bf16[8,1024]{1,0:T(8,128)(2,1)S(1)}, u32[]{:S(2)}, u32[]{:S(2)}) collective-permute-start(bf16[8,1024]{1,0:T(8,128)(2,1)S(1)} %get-tuple-element.23.refs_0_), channel_id=1, source_target_pairs={{0,2},{1,3},{2,0},{3,1},{4,6},{5,7},{6,4},{7,5},{8,10},{9,11},{10,... | collective-permute-start | bytes 49160 | tf_op jit(solution)/shard_map/ppermute | solution.py:409
  16.2 0.1 collective-permute-start.4
  16.3 1.3 %collective-permute-done.6.refs_3_ = bf16[8,1024]{1,0:T(8,128)(2,1)S(1)} collective-permute-done((bf16[8,1024]{1,0:T(8,128)(2,1)S(1)}, bf16[8,1024]{1,0:T(8,128)(2,1)S(1)}, u32[]{:S(2)}, u32[]{:S(2)}) %collective-permute-start.6) | collective-permute-done | bytes 16416 | tf_op jit(solution)/shard_map/ppermute | solution.py:409
  17.6 1.8 %collective-permute-done.5.refs_2_ = bf16[8,1024]{1,0:T(8,128)(2,1)S(1)} collective-permute-done((bf16[8,1024]{1,0:T(8,128)(2,1)S(1)}, bf16[8,1024]{1,0:T(8,128)(2,1)S(1)}, u32[]{:S(2)}, u32[]{:S(2)}) %collective-permute-start.5) | collective-permute-done | bytes 16416 | tf_op jit(solution)/shard_map/ppermute | solution.py:409
  19.5 0.9 %shard_map.148 = (bf16[8,1024]{1,0:T(8,128)(2,1)S(1)}, f32[8,1024]{1,0:T(8,128)S(1)}) custom-call(bf16[8,1024]{1,0:T(8,128)(2,1)S(1)} %get-tuple-element.23.refs_0_, bf16[8,1024]{1,0:T(8,128)(2,1)S(1)} %collective-permute-done.4.refs_1_, bf16[8,1024]{1,0:T(8,128)(2,1)S(1)} %collective-permute-done.5.refs_2_, ...), custom_call_target="tpu_custom_call" | custom-call | flops 1000000 | tf_op jit(solution)/shard_map/pallas_call | solution.py:396
  20.4 0.8 %collective-permute-start.8 = (bf16[8,1024]{1,0:T(8,128)(2,1)S(1)}, bf16[8,1024]{1,0:T(8,128)(2,1)S(1)}, u32[]{:S(2)}, u32[]{:S(2)}) collective-permute-start(bf16[8,1024]{1,0:T(8,128)(2,1)S(1)} %get-tuple-element.25.after_ref.refs_0_), channel_id=1, source_target_pairs={{0,2},{1,3},{2,0},{3,1},{4,6},{5,7},{6,4},{7,5},{8,10},{9,11},{10,... | collective-permute-start | bytes 49160 | tf_op jit(solution)/shard_map/ppermute | solution.py:409
  21.3 1.0 %collective-permute-start.7 = (bf16[8,1024]{1,0:T(8,128)(2,1)S(1)}, bf16[8,1024]{1,0:T(8,128)(2,1)S(1)}, u32[]{:S(2)}, u32[]{:S(2)}) collective-permute-start(bf16[8,1024]{1,0:T(8,128)(2,1)S(1)} %get-tuple-element.25.after_ref.refs_0_), channel_id=1, source_target_pairs={{0,1},{1,0},{2,3},{3,2},{4,5},{5,4},{6,7},{7,6},{8,9},{9,8},{10,11... | collective-permute-start | bytes 49160 | tf_op jit(solution)/shard_map/ppermute | solution.py:409
  22.3 1.3 %shard_map.149 = (bf16[2,8,128,256]{3,2,1,0:T(8,128)(2,1)S(1)}, bf16[2,384,256]{2,1,0:T(8,128)(2,1)S(1)}) custom-call(bf16[8,1024]{1,0:T(8,128)(2,1)S(1)} %get-tuple-element.25.after_ref.refs_0_, bf16[2,2,8,512,256]{4,3,2,1,0:T(8,128)(2,1)} %refs_10_.3), custom_call_target="tpu_custom_call" | custom-call | flops 1000000 | tf_op jit(solution)/shard_map/pallas_call | solution.py:396
  23.6 0.6 %collective-permute-done.8.refs_2_ = bf16[8,1024]{1,0:T(8,128)(2,1)S(1)} collective-permute-done((bf16[8,1024]{1,0:T(8,128)(2,1)S(1)}, bf16[8,1024]{1,0:T(8,128)(2,1)S(1)}, u32[]{:S(2)}, u32[]{:S(2)}) %collective-permute-start.8) | collective-permute-done | bytes 16416 | tf_op jit(solution)/shard_map/ppermute | solution.py:409
  24.2 1.5 %shard_map.150 = (bf16[8,1024]{1,0:T(8,128)(2,1)S(1)}, f32[8,1024]{1,0:T(8,128)S(1)}) custom-call(bf16[8,1024]{1,0:T(8,128)(2,1)S(1)} %get-tuple-element.25.after_ref.refs_0_, bf16[8,1024]{1,0:T(8,128)(2,1)S(1)} %collective-permute-done.7.refs_1_, bf16[8,1024]{1,0:T(8,128)(2,1)S(1)} %collective-permute-done.8.refs_2_, ...), custom_call_target="tpu_custom_call" | custom-call | flops 1000000 | tf_op jit(solution)/shard_map/pallas_call | solution.py:396
  25.8 0.6 %collective-permute-start.12 = (bf16[8,1024]{1,0:T(8,128)(2,1)S(1)}, bf16[8,1024]{1,0:T(8,128)(2,1)S(1)}, u32[]{:S(2)}, u32[]{:S(2)}) collective-permute-start(bf16[8,1024]{1,0:T(8,128)(2,1)S(1)} %get-tuple-element.31.refs_0_), channel_id=1, source_target_pairs={{0,3},{1,2},{2,1},{3,0},{4,7},{5,6},{6,5},{7,4},{8,11},{9,10},{10,... | collective-permute-start | bytes 49160 | tf_op jit(solution)/shard_map/ppermute | solution.py:409
  26.4 0.6 %collective-permute-start.11 = (bf16[8,1024]{1,0:T(8,128)(2,1)S(1)}, bf16[8,1024]{1,0:T(8,128)(2,1)S(1)}, u32[]{:S(2)}, u32[]{:S(2)}) collective-permute-start(bf16[8,1024]{1,0:T(8,128)(2,1)S(1)} %get-tuple-element.31.refs_0_), channel_id=1, source_target_pairs={{0,2},{1,3},{2,0},{3,1},{4,6},{5,7},{6,4},{7,5},{8,10},{9,11},{10,... | collective-permute-start | bytes 49160 | tf_op jit(solution)/shard_map/ppermute | solution.py:409
  27.0 0.7 %collective-permute-start.10 = (bf16[8,1024]{1,0:T(8,128)(2,1)S(1)}, bf16[8,1024]{1,0:T(8,128)(2,1)S(1)}, u32[]{:S(2)}, u32[]{:S(2)}) collective-permute-start(bf16[8,1024]{1,0:T(8,128)(2,1)S(1)} %get-tuple-element.31.refs_0_), channel_id=1, source_target_pairs={{0,1},{1,0},{2,3},{3,2},{4,5},{5,4},{6,7},{7,6},{8,9},{9,8},{10,11... | collective-permute-start | bytes 49160 | tf_op jit(solution)/shard_map/ppermute | solution.py:409
  27.7 1.3 %collective-permute-done.12.refs_3_ = bf16[8,1024]{1,0:T(8,128)(2,1)S(1)} collective-permute-done((bf16[8,1024]{1,0:T(8,128)(2,1)S(1)}, bf16[8,1024]{1,0:T(8,128)(2,1)S(1)}, u32[]{:S(2)}, u32[]{:S(2)}) %collective-permute-start.12) | collective-permute-done | bytes 16416 | tf_op jit(solution)/shard_map/ppermute | solution.py:409
  29.0 1.1 %collective-permute-done.11.refs_2_ = bf16[8,1024]{1,0:T(8,128)(2,1)S(1)} collective-permute-done((bf16[8,1024]{1,0:T(8,128)(2,1)S(1)}, bf16[8,1024]{1,0:T(8,128)(2,1)S(1)}, u32[]{:S(2)}, u32[]{:S(2)}) %collective-permute-start.11) | collective-permute-done | bytes 16416 | tf_op jit(solution)/shard_map/ppermute | solution.py:409
  30.1 1.1 %shard_map.151 = bf16[32,2,640]{2,1,0:T(2,128)(2,1)S(1)} custom-call(bf16[8,1024]{1,0:T(8,128)(2,1)S(1)} %get-tuple-element.31.refs_0_, bf16[8,1024]{1,0:T(8,128)(2,1)S(1)} %collective-permute-done.10.refs_1_, bf16[8,1024]{1,0:T(8,128)(2,1)S(1)} %collective-permute-done.11.refs_2_, bf16[8,1024]{1,0:T(8,128)(2,1)S(1)} %collective-permute-done.12.refs_3_, ...), custom_call_target="tpu_custom_call" | custom-call | flops 1000000 | tf_op jit(solution)/shard_map/pallas_call | solution.py:396
  31.2 12.1 %all_to_all.5.received_ref = bf16[32,2,640]{2,1,0:T(2,128)(2,1)S(1)} all-to-all(bf16[32,2,640]{2,1,0:T(2,128)(2,1)S(1)} %shard_map.151), channel_id=1, replica_groups=mesh['req'=8,'head'=4] {'req','head'}, dimensions={0} | all-to-all | bytes 163840 | tf_op jit(solution)/shard_map/all_to_all | solution.py:548
  43.4 0.9 %shard_map.152 = bf16[2,1024]{1,0:T(2,128)(2,1)} custom-call(bf16[32,2,640]{2,1,0:T(2,128)(2,1)S(1)} %all_to_all.5.received_ref), custom_call_target="tpu_custom_call" | custom-call | tf_op jit(solution)/shard_map/pallas_call | solution.py:549
  (25 shorter events, 0.1 us)
Async XLA Ops:
  0.8 11.9 %copy-start.1 = (bf16[2,1024,768]{2,1,0:T(8,128)(2,1)S(1)}, bf16[2,1024,768]{2,1,0:T(8,128)(2,1)}, u32[]{:S(2)}) copy-start(bf16[2,1024,768]{2,1,0:T(8,128)(2,1)} %refs_12_.3) | copy-start | bytes 9437188
  0.8 11.9 %copy-start.3 = (s32[8,512]{1,0:T(8,128)S(1)}, s32[8,512]{1,0:T(8,128)}, u32[]{:S(2)}) copy-start(s32[8,512]{1,0:T(8,128)} %refs_7_.4) | copy-start | bytes 49156
  0.8 11.9 %copy-start.4 = (f32[2,1024]{1,0:T(2,128)S(1)}, f32[2,1024]{1,0:T(2,128)}, u32[]{:S(2)}) copy-start(f32[2,1024]{1,0:T(2,128)} %refs_11_.3) | copy-start | bytes 24580
  0.8 11.9 %copy-start.6 = (f32[2,2,4]{2,1,0:T(2,128)S(1)}, f32[2,2,4]{2,1,0:T(2,128)}, u32[]{:S(2)}) copy-start(f32[2,2,4]{2,1,0:T(2,128)} %refs_14_.1) | copy-start | bytes 196
  0.8 11.9 %copy-start.7 = (f32[1,128]{1,0:T(1,128)S(1)}, f32[1,128]{1,0:T(1,128)}, u32[]{:S(2)}) copy-start(f32[1,128]{1,0:T(1,128)} %constant.8.clone.refs_5_) | copy-start | bytes 1540
  0.8 5.0 %collective-permute-start = (bf16[8,1152]{1,0:T(8,128)(2,1)S(1)}, bf16[8,1152]{1,0:T(8,128)(2,1)S(1)}, u32[]{:S(2)}, u32[]{:S(2)}) collective-permute-start(bf16[8,1152]{1,0:T(8,128)(2,1)S(1)} %shard_map.145.after_ref), channel_id=1, source_target_pairs={{0,17},{1,16},{2,19},{3,18},{4,21},{5,20},{6,23},{7,22},{8,25},{9,... | collective-permute-start | bytes 55304 | tf_op jit(solution)/shard_map/ppermute | solution.py:429
  5.9 5.0 %collective-permute-start.3 = (bf16[16,1152]{1,0:T(8,128)(2,1)S(1)}, bf16[16,1152]{1,0:T(8,128)(2,1)S(1)}, u32[]{:S(2)}, u32[]{:S(2)}) collective-permute-start(bf16[16,1152]{1,0:T(8,128)(2,1)S(1)} %pad_maximum_fusion.refs_0_), channel_id=1, source_target_pairs={{0,13},{1,12},{2,15},{3,14},{4,9},{5,8},{6,11},{7,10},{8,5},{9,4},... | collective-permute-start | bytes 110600 | tf_op jit(solution)/shard_map/ppermute | solution.py:429
  8.7 3.4 %collective-permute-start.2 = (bf16[16,1152]{1,0:T(8,128)(2,1)S(1)}, bf16[16,1152]{1,0:T(8,128)(2,1)S(1)}, u32[]{:S(2)}, u32[]{:S(2)}) collective-permute-start(bf16[16,1152]{1,0:T(8,128)(2,1)S(1)} %pad_maximum_fusion.refs_0_), channel_id=1, source_target_pairs={{0,9},{1,8},{2,11},{3,10},{4,13},{5,12},{6,15},{7,14},{8,1},{9,0},... | collective-permute-start | bytes 110600 | tf_op jit(solution)/shard_map/ppermute | solution.py:429
  9.2 3.5 %collective-permute-start.1 = (bf16[16,1152]{1,0:T(8,128)(2,1)S(1)}, bf16[16,1152]{1,0:T(8,128)(2,1)S(1)}, u32[]{:S(2)}, u32[]{:S(2)}) collective-permute-start(bf16[16,1152]{1,0:T(8,128)(2,1)S(1)} %pad_maximum_fusion.refs_0_), channel_id=1, source_target_pairs={{0,5},{1,4},{2,7},{3,6},{4,1},{5,0},{6,3},{7,2},{8,13},{9,12},{10,... | collective-permute-start | bytes 110600 | tf_op jit(solution)/shard_map/ppermute | solution.py:429
  9.4 3.4 %copy-start.2 = (bf16[2,256,1024]{2,1,0:T(8,128)(2,1)S(1)}, bf16[2,256,1024]{2,1,0:T(8,128)(2,1)}, u32[]{:S(2)}) copy-start(bf16[2,256,1024]{2,1,0:T(8,128)(2,1)} %refs_13_.3) | copy-start | bytes 3145732
  9.4 10.1 %slice-start = ((s8[8388608]{0:T(1024)(128)(4,1)}), s8[4194304]{0:T(1024)(128)(4,1)S(1)}, s32[]{:S(2)}) async-start(s8[8388608]{0:T(1024)(128)(4,1)} %bitcast.1), calls=%async_computation.1 | async-start | bytes 8388608
  10.9 8.6 %copy-start = (bf16[2,1024,1024]{2,1,0:T(8,128)(2,1)S(1)}, bf16[2,1024,1024]{2,1,0:T(8,128)(2,1)}, u32[]{:S(2)}) copy-start(bf16[2,1024,1024]{2,1,0:T(8,128)(2,1)} %refs_9_.3) | copy-start | bytes 12582916
  10.9 8.6 %copy-start.5 = (f32[2,1024]{1,0:T(2,128)S(1)}, f32[2,1024]{1,0:T(2,128)}, u32[]{:S(2)}) copy-start(f32[2,1024]{1,0:T(2,128)} %refs_7_.5) | copy-start | bytes 24580
  12.7 6.7 %slice-start.1 = ((s8[8388608]{0:T(1024)(128)(4,1)}), s8[4194304]{0:T(1024)(128)(4,1)S(1)}, s32[]{:S(2)}) async-start(s8[8388608]{0:T(1024)(128)(4,1)} %bitcast.1), calls=%async_computation.2 | async-start | bytes 8388608
  14.4 3.2 %collective-permute-start.6 = (bf16[8,1024]{1,0:T(8,128)(2,1)S(1)}, bf16[8,1024]{1,0:T(8,128)(2,1)S(1)}, u32[]{:S(2)}, u32[]{:S(2)}) collective-permute-start(bf16[8,1024]{1,0:T(8,128)(2,1)S(1)} %get-tuple-element.23.refs_0_), channel_id=1, source_target_pairs={{0,3},{1,2},{2,1},{3,0},{4,7},{5,6},{6,5},{7,4},{8,11},{9,10},{10,... | collective-permute-start | bytes 49160 | tf_op jit(solution)/shard_map/ppermute | solution.py:409
  15.7 3.8 %collective-permute-start.5 = (bf16[8,1024]{1,0:T(8,128)(2,1)S(1)}, bf16[8,1024]{1,0:T(8,128)(2,1)S(1)}, u32[]{:S(2)}, u32[]{:S(2)}) collective-permute-start(bf16[8,1024]{1,0:T(8,128)(2,1)S(1)} %get-tuple-element.23.refs_0_), channel_id=1, source_target_pairs={{0,2},{1,3},{2,0},{3,1},{4,6},{5,7},{6,4},{7,5},{8,10},{9,11},{10,... | collective-permute-start | bytes 49160 | tf_op jit(solution)/shard_map/ppermute | solution.py:409
  16.2 3.2 %collective-permute-start.4 = (bf16[8,1024]{1,0:T(8,128)(2,1)S(1)}, bf16[8,1024]{1,0:T(8,128)(2,1)S(1)}, u32[]{:S(2)}, u32[]{:S(2)}) collective-permute-start(bf16[8,1024]{1,0:T(8,128)(2,1)S(1)} %get-tuple-element.23.refs_0_), channel_id=1, source_target_pairs={{0,1},{1,0},{2,3},{3,2},{4,5},{5,4},{6,7},{7,6},{8,9},{9,8},{10,11... | collective-permute-start | bytes 49160 | tf_op jit(solution)/shard_map/ppermute | solution.py:409
  20.4 3.2 %collective-permute-start.9 = (bf16[8,1024]{1,0:T(8,128)(2,1)S(1)}, bf16[8,1024]{1,0:T(8,128)(2,1)S(1)}, u32[]{:S(2)}, u32[]{:S(2)}) collective-permute-start(bf16[8,1024]{1,0:T(8,128)(2,1)S(1)} %get-tuple-element.25.after_ref.refs_0_), channel_id=1, source_target_pairs={{0,3},{1,2},{2,1},{3,0},{4,7},{5,6},{6,5},{7,4},{8,11},{9,10},{10,... | collective-permute-start | bytes 49160 | tf_op jit(solution)/shard_map/ppermute | solution.py:409
  20.4 3.8 %collective-permute-start.8 = (bf16[8,1024]{1,0:T(8,128)(2,1)S(1)}, bf16[8,1024]{1,0:T(8,128)(2,1)S(1)}, u32[]{:S(2)}, u32[]{:S(2)}) collective-permute-start(bf16[8,1024]{1,0:T(8,128)(2,1)S(1)} %get-tuple-element.25.after_ref.refs_0_), channel_id=1, source_target_pairs={{0,2},{1,3},{2,0},{3,1},{4,6},{5,7},{6,4},{7,5},{8,10},{9,11},{10,... | collective-permute-start | bytes 49160 | tf_op jit(solution)/shard_map/ppermute | solution.py:409
  21.3 2.9 %collective-permute-start.7 = (bf16[8,1024]{1,0:T(8,128)(2,1)S(1)}, bf16[8,1024]{1,0:T(8,128)(2,1)S(1)}, u32[]{:S(2)}, u32[]{:S(2)}) collective-permute-start(bf16[8,1024]{1,0:T(8,128)(2,1)S(1)} %get-tuple-element.25.after_ref.refs_0_), channel_id=1, source_target_pairs={{0,1},{1,0},{2,3},{3,2},{4,5},{5,4},{6,7},{7,6},{8,9},{9,8},{10,11... | collective-permute-start | bytes 49160 | tf_op jit(solution)/shard_map/ppermute | solution.py:409
  25.8 3.2 %collective-permute-start.12 = (bf16[8,1024]{1,0:T(8,128)(2,1)S(1)}, bf16[8,1024]{1,0:T(8,128)(2,1)S(1)}, u32[]{:S(2)}, u32[]{:S(2)}) collective-permute-start(bf16[8,1024]{1,0:T(8,128)(2,1)S(1)} %get-tuple-element.31.refs_0_), channel_id=1, source_target_pairs={{0,3},{1,2},{2,1},{3,0},{4,7},{5,6},{6,5},{7,4},{8,11},{9,10},{10,... | collective-permute-start | bytes 49160 | tf_op jit(solution)/shard_map/ppermute | solution.py:409
  26.4 3.8 %collective-permute-start.11 = (bf16[8,1024]{1,0:T(8,128)(2,1)S(1)}, bf16[8,1024]{1,0:T(8,128)(2,1)S(1)}, u32[]{:S(2)}, u32[]{:S(2)}) collective-permute-start(bf16[8,1024]{1,0:T(8,128)(2,1)S(1)} %get-tuple-element.31.refs_0_), channel_id=1, source_target_pairs={{0,2},{1,3},{2,0},{3,1},{4,6},{5,7},{6,4},{7,5},{8,10},{9,11},{10,... | collective-permute-start | bytes 49160 | tf_op jit(solution)/shard_map/ppermute | solution.py:409
  27.0 3.2 %collective-permute-start.10 = (bf16[8,1024]{1,0:T(8,128)(2,1)S(1)}, bf16[8,1024]{1,0:T(8,128)(2,1)S(1)}, u32[]{:S(2)}, u32[]{:S(2)}) collective-permute-start(bf16[8,1024]{1,0:T(8,128)(2,1)S(1)} %get-tuple-element.31.refs_0_), channel_id=1, source_target_pairs={{0,1},{1,0},{2,3},{3,2},{4,5},{5,4},{6,7},{7,6},{8,9},{9,8},{10,11... | collective-permute-start | bytes 49160 | tf_op jit(solution)/shard_map/ppermute | solution.py:409

commit v6 on v5

--- a/solution.py
+++ b/solution.py
@@ -206,7 +206,7 @@
     live = iota((slots, cap), 1).astype(F32) < lengths
 
     def soften(raw_scores):
-        probs, own_prob = [], []
+        weights, own = [], []
         for h in range(heads):
             block = raw_scores[h * slots : (h + 1) * slots, :] * 0.125
             block = block + jnp.where(
@@ -217,34 +217,32 @@
             weight = jnp.exp(block - top)
             own_weight = jnp.exp(own_score[h] - top)
             share = 1.0 / (jnp.sum(weight, axis=1, keepdims=True) + own_weight)
-            probs.append(weight * share)
-            own_prob.append((own_weight * share).astype(BF16).astype(F32))
-        return jnp.concatenate(probs, axis=0).astype(BF16), own_prob
-
-    def only(mask, probs):
-        return jnp.where(mask, probs, jnp.zeros_like(probs))
-
-    def mix(probs):
-        spread = jnp.concatenate([only(row_slot == s, probs[:, :CHUNK]) for s in range(slots)], 1)
+            weights.append(weight)
+            own.append((own_weight, share))
+        return jnp.concatenate(weights, axis=0).astype(BF16), own
+
+    def only(mask, weights):
+        return jnp.where(mask, weights, jnp.zeros_like(weights))
+
+    def mix(weights):
+        spread = jnp.concatenate([only(row_slot == s, weights[:, :CHUNK]) for s in range(slots)], 1)
         front = jnp.dot(
             spread, front_ref[1].reshape(slots * CHUNK, width), preferred_element_type=F32
         )
-        lead = only(rest_slot == 0, probs[:, CHUNK:])
+        lead = only(rest_slot == 0, weights[:, CHUNK:])
         return front + jnp.dot(lead, lead_ref[1], preferred_element_type=F32)
 
-    def lay_out(mixed_rows, own_prob):
+    def lay_out(mixed_rows, own):
         result = jnp.zeros((slots, width), F32)
-        for h in range(heads):
+        for h, (own_weight, share) in enumerate(own):
             value_new = turned_all[:, (h + 1) * step : (h + 1) * step + width]
-            result = jnp.where(
-                of_head[h], mixed_rows[h * slots : (h + 1) * slots, :] + own_prob[h] * value_new,
-                result,
-            )
+            whole = mixed_rows[h * slots : (h + 1) * slots, :] + own_weight * value_new
+            result = jnp.where(of_head[h], whole * share, result)
         return result
 
     all_scores = jnp.concatenate([front_scores, lead_scores], axis=1)
-    probs_all, own_probs = soften(all_scores)
-    attended[...] = lay_out(mix(probs_all), own_probs)
+    weights_all, own_all = soften(all_scores)
+    attended[...] = lay_out(mix(weights_all), own_all)
 
     @pl.when(longer > 1)
     def _():
@@ -264,14 +262,14 @@
             rest_copy(s).wait()
             scores[:, CHUNK:] = jnp.where(rest_slot == s, score(rest_kv[s, 0]), scores[:, CHUNK:])
 
-        probs_long, own_long = soften(scores[...])
-        mixed[...] = mix(probs_long)
-        rest_probs = probs_long[:, CHUNK:]
+        weights_long, own_long = soften(scores[...])
+        mixed[...] = mix(weights_long)
+        rest_weights = weights_long[:, CHUNK:]
 
         @pl.loop(1, longer)
         def _(s):
             mixed[...] += jnp.dot(
-                only(rest_slot == s, rest_probs), rest_kv[s, 1], preferred_element_type=F32
+                only(rest_slot == s, rest_weights), rest_kv[s, 1], preferred_element_type=F32
             )
 
         attended[...] = lay_out(mixed[...], own_long)
@@ -378,13 +376,11 @@
     share, width = out_ref.shape
     half = width // 2
     for i in range(2):
-        rows = lax.dot_general(
-            received_ref[:, i, half:],
-            received_ref[:, i, :half],
-            (((0,), (0,)), ((), ())),
-            preferred_element_type=F32,
-        )
-        out_ref[:, i * half : (i + 1) * half] = rows[:share, :].astype(BF16)
+        rows = received_ref[:, i, :half].astype(F32)
+        flags = received_ref[:, i, half:].astype(F32)
+        for k in range(share):
+            row = jnp.sum(flags[:, k : k + 1] * rows, axis=0, keepdims=True)
+            out_ref[k : k + 1, i * half : (i + 1) * half] = row.astype(BF16)
 
 
 def call(kernel, operands, outs, scratch=(), cost=SHORT):
@@ -416,7 +412,7 @@
         top = count // 2
         stages.append([top])
     while top > 1:
-        stages.append([top // 4 * k for k in (1, 2, 3)])
+        stages.append([top // 4 * k for k in (1, 3, 2)])
         top //= 4
     return stages
 

time: 44.6 us -> 44 us (0.987)
  blocking collectives: 12.1 us -> 11.5 us
  waiting for transfers between devices: 9.42 us -> 9.9 us
    all_to_all x1, blocking collectives: 12.1 us -> 11.5 us  [per_device(): received = lax.all_to_all(send, ('req', 'head'), 0, 0, tiled=True)]
    ppermute x4, waiting for transfers between devices: 3.27 us -> 3.79 us  [swap_across(): return lax.ppermute(array, ('req', 'head'), pairs)]
where the time goes in v6:
time: 44 us; the launch traced here: 43.7 us
  starting transfers between devices  12.8 us (29%)
  blocking collectives  11.5 us (26%)
  waiting for transfers between devices  9.9 us (22%)
  Pallas kernels  9.32 us (21%)
    all_to_all x1, blocking collectives, per_device(): received = lax.all_to_all(send, ('req', 'head'), 0, 0, tiled=True)  11.5 us
    pallas_call x7, Pallas kernels, call(): pl.pallas_call(kernel, out_shape=[pltpu.VMEM(shape, dtype) for shape, dty...  8.5 us
    ppermute x4, starting transfers between devices, swap_across(): return lax.ppermute(array, ('req', 'head'), pairs)  7 us
    ppermute x9, waiting for transfers between devices, swap(): return lax.ppermute(array, axis, [(i, i ^ mask) for i in range(count)])  6.1 us
    ppermute x9, starting transfers between devices, swap(): return lax.ppermute(array, axis, [(i, i ^ mask) for i in range(count)])  5.76 us
    ppermute x4, waiting for transfers between devices, swap_across(): return lax.ppermute(array, ('req', 'head'), pairs)  3.79 us
  transfers between devices with their start and end apart: 13, of which 8 were waited for; matrix products, arithmetic and copies ran while one was open for 0% of the time, Pallas kernels for 6%

profile of v6, /device:TPU:0, one launch (start us, length us, event | category | flops | bytes accessed | tf_op | source)
XLA Modules:
  0.0 43.7 jit_solution(1887669434162211613)
XLA Ops:
  0.0 0.8 %shard_map.145.after_ref = bf16[8,1152]{1,0:T(8,128)(2,1)S(1)} custom-call(bf16[8,1024]{1,0:T(8,128)(2,1)} %tokens_ref.1, s32[8]{0:T(128)} %lengths_ref.1, s32[8]{0:T(128)} %positions_ref.1, s32[8]{0:T(128)} %variates_ref.1), custom_call_target="tpu_custom_call" | custom-call | flops 99999997952 | tf_op jit(solution)/shard_map/pallas_call | solution.py:392
  0.8 0.0 copy-start.3
  0.8 0.0 copy-start.7
  0.8 3.5 %collective-permute-start = (bf16[8,1152]{1,0:T(8,128)(2,1)S(1)}, bf16[8,1152]{1,0:T(8,128)(2,1)S(1)}, u32[]{:S(2)}, u32[]{:S(2)}) collective-permute-start(bf16[8,1152]{1,0:T(8,128)(2,1)S(1)} %shard_map.145.after_ref), channel_id=1, source_target_pairs={{0,17},{1,16},{2,19},{3,18},{4,21},{5,20},{6,23},{7,22},{8,25},{9,... | collective-permute-start | bytes 55304 | tf_op jit(solution)/shard_map/ppermute | solution.py:425
  4.4 1.5 %collective-permute-done = bf16[8,1152]{1,0:T(8,128)(2,1)S(1)} collective-permute-done((bf16[8,1152]{1,0:T(8,128)(2,1)S(1)}, bf16[8,1152]{1,0:T(8,128)(2,1)S(1)}, u32[]{:S(2)}, u32[]{:S(2)}) %collective-permute-start) | collective-permute-done | bytes 18464 | tf_op jit(solution)/shard_map/ppermute | solution.py:425
  5.9 1.9 %collective-permute-start.3 = (bf16[16,1152]{1,0:T(8,128)(2,1)S(1)}, bf16[16,1152]{1,0:T(8,128)(2,1)S(1)}, u32[]{:S(2)}, u32[]{:S(2)}) collective-permute-start(bf16[16,1152]{1,0:T(8,128)(2,1)S(1)} %pad_maximum_fusion.refs_0_), channel_id=1, source_target_pairs={{0,9},{1,8},{2,11},{3,10},{4,13},{5,12},{6,15},{7,14},{8,1},{9,0},... | collective-permute-start | bytes 110600 | tf_op jit(solution)/shard_map/ppermute | solution.py:425
  7.7 1.4 %collective-permute-start.2 = (bf16[16,1152]{1,0:T(8,128)(2,1)S(1)}, bf16[16,1152]{1,0:T(8,128)(2,1)S(1)}, u32[]{:S(2)}, u32[]{:S(2)}) collective-permute-start(bf16[16,1152]{1,0:T(8,128)(2,1)S(1)} %pad_maximum_fusion.refs_0_), channel_id=1, source_target_pairs={{0,13},{1,12},{2,15},{3,14},{4,9},{5,8},{6,11},{7,10},{8,5},{9,4},... | collective-permute-start | bytes 110600 | tf_op jit(solution)/shard_map/ppermute | solution.py:425
  9.2 0.1 collective-permute-start.1
  9.3 1.5 %shard_map.146 = (bf16[8,64]{1,0:T(8,128)(2,1)S(1)}, bf16[32,8]{1,0:T(8,128)(2,1)S(1)}, bf16[8,128]{1,0:T(8,128)(2,1)S(1)}, bf16[2,8,128,256]{3,2,1,0:T(8,128)(2,1)S(1)}, bf16[2,384,256]{2,1,0:T(8,128)(2,1)S(1)}) custom-call(bf16[8,1152]{1,0:T(8,128)(2,1)S(1)} %shard_map.145.after_ref, s32[8]{0:T(128)} %owner_ref.1, s32[1]{0:T(128)} %bitcast.own_block_ref, ...), custom_call_target="tpu_custom_call" | custom-call | flops 1000000 | tf_op jit(solution)/shard_map/pallas_call | solution.py:392
  10.9 1.2 %collective-permute-done.2.refs_2_ = bf16[16,1152]{1,0:T(8,128)(2,1)S(1)} collective-permute-done((bf16[16,1152]{1,0:T(8,128)(2,1)S(1)}, bf16[16,1152]{1,0:T(8,128)(2,1)S(1)}, u32[]{:S(2)}, u32[]{:S(2)}) %collective-permute-start.2) | collective-permute-done | bytes 36896 | tf_op jit(solution)/shard_map/ppermute | solution.py:425
  12.0 1.2 %collective-permute-done.1.refs_1_ = bf16[16,1152]{1,0:T(8,128)(2,1)S(1)} collective-permute-done((bf16[16,1152]{1,0:T(8,128)(2,1)S(1)}, bf16[16,1152]{1,0:T(8,128)(2,1)S(1)}, u32[]{:S(2)}, u32[]{:S(2)}) %collective-permute-start.1) | collective-permute-done | bytes 36896 | tf_op jit(solution)/shard_map/ppermute | solution.py:425
  13.2 0.0 slice-start.1
  13.2 1.5 %shard_map.147 = (bf16[8,1024]{1,0:T(8,128)(2,1)S(1)}, f32[8,1024]{1,0:T(8,128)S(1)}, f32[8,128]{1,0:T(8,128)S(1)}, f32[8,256]{1,0:T(8,128)S(1)}) custom-call(bf16[16,1152]{1,0:T(8,128)(2,1)S(1)} %pad_maximum_fusion.refs_0_, bf16[16,1152]{1,0:T(8,128)(2,1)S(1)} %collective-permute-done.1.refs_1_, bf16[16,1152]{1,0:T(8,128)(2,1)S(1)} %collective-permute-done.2.refs_2_, ...), custom_call_target="tpu_custom_call" | custom-call | flops 1000000 | tf_op jit(solution)/shard_map/pallas_call | solution.py:392
  14.7 1.3 %collective-permute-start.6 = (bf16[8,1024]{1,0:T(8,128)(2,1)S(1)}, bf16[8,1024]{1,0:T(8,128)(2,1)S(1)}, u32[]{:S(2)}, u32[]{:S(2)}) collective-permute-start(bf16[8,1024]{1,0:T(8,128)(2,1)S(1)} %get-tuple-element.23.refs_0_), channel_id=1, source_target_pairs={{0,3},{1,2},{2,1},{3,0},{4,7},{5,6},{6,5},{7,4},{8,11},{9,10},{10,... | collective-permute-start | bytes 49160 | tf_op jit(solution)/shard_map/ppermute | solution.py:405
  16.0 0.5 %collective-permute-start.5 = (bf16[8,1024]{1,0:T(8,128)(2,1)S(1)}, bf16[8,1024]{1,0:T(8,128)(2,1)S(1)}, u32[]{:S(2)}, u32[]{:S(2)}) collective-permute-start(bf16[8,1024]{1,0:T(8,128)(2,1)S(1)} %get-tuple-element.23.refs_0_), channel_id=1, source_target_pairs={{0,2},{1,3},{2,0},{3,1},{4,6},{5,7},{6,4},{7,5},{8,10},{9,11},{10,... | collective-permute-start | bytes 49160 | tf_op jit(solution)/shard_map/ppermute | solution.py:405
  16.5 0.1 collective-permute-start.4
  16.7 1.3 %collective-permute-done.6.refs_3_ = bf16[8,1024]{1,0:T(8,128)(2,1)S(1)} collective-permute-done((bf16[8,1024]{1,0:T(8,128)(2,1)S(1)}, bf16[8,1024]{1,0:T(8,128)(2,1)S(1)}, u32[]{:S(2)}, u32[]{:S(2)}) %collective-permute-start.6) | collective-permute-done | bytes 16416 | tf_op jit(solution)/shard_map/ppermute | solution.py:405
  18.0 1.8 %collective-permute-done.5.refs_2_ = bf16[8,1024]{1,0:T(8,128)(2,1)S(1)} collective-permute-done((bf16[8,1024]{1,0:T(8,128)(2,1)S(1)}, bf16[8,1024]{1,0:T(8,128)(2,1)S(1)}, u32[]{:S(2)}, u32[]{:S(2)}) %collective-permute-start.5) | collective-permute-done | bytes 16416 | tf_op jit(solution)/shard_map/ppermute | solution.py:405
  19.8 0.9 %shard_map.148 = (bf16[8,1024]{1,0:T(8,128)(2,1)S(1)}, f32[8,1024]{1,0:T(8,128)S(1)}) custom-call(bf16[8,1024]{1,0:T(8,128)(2,1)S(1)} %get-tuple-element.23.refs_0_, bf16[8,1024]{1,0:T(8,128)(2,1)S(1)} %collective-permute-done.4.refs_1_, bf16[8,1024]{1,0:T(8,128)(2,1)S(1)} %collective-permute-done.5.refs_2_, ...), custom_call_target="tpu_custom_call" | custom-call | flops 1000000 | tf_op jit(solution)/shard_map/pallas_call | solution.py:392
  20.7 0.9 %collective-permute-start.8 = (bf16[8,1024]{1,0:T(8,128)(2,1)S(1)}, bf16[8,1024]{1,0:T(8,128)(2,1)S(1)}, u32[]{:S(2)}, u32[]{:S(2)}) collective-permute-start(bf16[8,1024]{1,0:T(8,128)(2,1)S(1)} %get-tuple-element.25.after_ref.refs_0_), channel_id=1, source_target_pairs={{0,2},{1,3},{2,0},{3,1},{4,6},{5,7},{6,4},{7,5},{8,10},{9,11},{10,... | collective-permute-start | bytes 49160 | tf_op jit(solution)/shard_map/ppermute | solution.py:405
  21.6 1.0 %collective-permute-start.7 = (bf16[8,1024]{1,0:T(8,128)(2,1)S(1)}, bf16[8,1024]{1,0:T(8,128)(2,1)S(1)}, u32[]{:S(2)}, u32[]{:S(2)}) collective-permute-start(bf16[8,1024]{1,0:T(8,128)(2,1)S(1)} %get-tuple-element.25.after_ref.refs_0_), channel_id=1, source_target_pairs={{0,1},{1,0},{2,3},{3,2},{4,5},{5,4},{6,7},{7,6},{8,9},{9,8},{10,11... | collective-permute-start | bytes 49160 | tf_op jit(solution)/shard_map/ppermute | solution.py:405
  22.6 1.3 %shard_map.149 = (bf16[2,8,128,256]{3,2,1,0:T(8,128)(2,1)S(1)}, bf16[2,384,256]{2,1,0:T(8,128)(2,1)S(1)}) custom-call(bf16[8,1024]{1,0:T(8,128)(2,1)S(1)} %get-tuple-element.25.after_ref.refs_0_, bf16[2,2,8,512,256]{4,3,2,1,0:T(8,128)(2,1)} %refs_10_.3), custom_call_target="tpu_custom_call" | custom-call | flops 1000000 | tf_op jit(solution)/shard_map/pallas_call | solution.py:392
  23.9 0.6 %collective-permute-done.8.refs_2_ = bf16[8,1024]{1,0:T(8,128)(2,1)S(1)} collective-permute-done((bf16[8,1024]{1,0:T(8,128)(2,1)S(1)}, bf16[8,1024]{1,0:T(8,128)(2,1)S(1)}, u32[]{:S(2)}, u32[]{:S(2)}) %collective-permute-start.8) | collective-permute-done | bytes 16416 | tf_op jit(solution)/shard_map/ppermute | solution.py:405
  24.5 1.4 %shard_map.150 = (bf16[8,1024]{1,0:T(8,128)(2,1)S(1)}, f32[8,1024]{1,0:T(8,128)S(1)}) custom-call(bf16[8,1024]{1,0:T(8,128)(2,1)S(1)} %get-tuple-element.25.after_ref.refs_0_, bf16[8,1024]{1,0:T(8,128)(2,1)S(1)} %collective-permute-done.7.refs_1_, bf16[8,1024]{1,0:T(8,128)(2,1)S(1)} %collective-permute-done.8.refs_2_, ...), custom_call_target="tpu_custom_call" | custom-call | flops 1000000 | tf_op jit(solution)/shard_map/pallas_call | solution.py:392
  25.9 0.6 %collective-permute-start.12 = (bf16[8,1024]{1,0:T(8,128)(2,1)S(1)}, bf16[8,1024]{1,0:T(8,128)(2,1)S(1)}, u32[]{:S(2)}, u32[]{:S(2)}) collective-permute-start(bf16[8,1024]{1,0:T(8,128)(2,1)S(1)} %get-tuple-element.31.refs_0_), channel_id=1, source_target_pairs={{0,3},{1,2},{2,1},{3,0},{4,7},{5,6},{6,5},{7,4},{8,11},{9,10},{10,... | collective-permute-start | bytes 49160 | tf_op jit(solution)/shard_map/ppermute | solution.py:405
  26.6 0.5 %collective-permute-start.11 = (bf16[8,1024]{1,0:T(8,128)(2,1)S(1)}, bf16[8,1024]{1,0:T(8,128)(2,1)S(1)}, u32[]{:S(2)}, u32[]{:S(2)}) collective-permute-start(bf16[8,1024]{1,0:T(8,128)(2,1)S(1)} %get-tuple-element.31.refs_0_), channel_id=1, source_target_pairs={{0,2},{1,3},{2,0},{3,1},{4,6},{5,7},{6,4},{7,5},{8,10},{9,11},{10,... | collective-permute-start | bytes 49160 | tf_op jit(solution)/shard_map/ppermute | solution.py:405
  27.1 0.7 %collective-permute-start.10 = (bf16[8,1024]{1,0:T(8,128)(2,1)S(1)}, bf16[8,1024]{1,0:T(8,128)(2,1)S(1)}, u32[]{:S(2)}, u32[]{:S(2)}) collective-permute-start(bf16[8,1024]{1,0:T(8,128)(2,1)S(1)} %get-tuple-element.31.refs_0_), channel_id=1, source_target_pairs={{0,1},{1,0},{2,3},{3,2},{4,5},{5,4},{6,7},{7,6},{8,9},{9,8},{10,11... | collective-permute-start | bytes 49160 | tf_op jit(solution)/shard_map/ppermute | solution.py:405
  27.8 1.3 %collective-permute-done.12.refs_3_ = bf16[8,1024]{1,0:T(8,128)(2,1)S(1)} collective-permute-done((bf16[8,1024]{1,0:T(8,128)(2,1)S(1)}, bf16[8,1024]{1,0:T(8,128)(2,1)S(1)}, u32[]{:S(2)}, u32[]{:S(2)}) %collective-permute-start.12) | collective-permute-done | bytes 16416 | tf_op jit(solution)/shard_map/ppermute | solution.py:405
  29.2 1.2 %collective-permute-done.11.refs_2_ = bf16[8,1024]{1,0:T(8,128)(2,1)S(1)} collective-permute-done((bf16[8,1024]{1,0:T(8,128)(2,1)S(1)}, bf16[8,1024]{1,0:T(8,128)(2,1)S(1)}, u32[]{:S(2)}, u32[]{:S(2)}) %collective-permute-start.11) | collective-permute-done | bytes 16416 | tf_op jit(solution)/shard_map/ppermute | solution.py:405
  30.3 1.1 %shard_map.151 = bf16[32,2,640]{2,1,0:T(2,128)(2,1)S(1)} custom-call(bf16[8,1024]{1,0:T(8,128)(2,1)S(1)} %get-tuple-element.31.refs_0_, bf16[8,1024]{1,0:T(8,128)(2,1)S(1)} %collective-permute-done.10.refs_1_, bf16[8,1024]{1,0:T(8,128)(2,1)S(1)} %collective-permute-done.11.refs_2_, bf16[8,1024]{1,0:T(8,128)(2,1)S(1)} %collective-permute-done.12.refs_3_, ...), custom_call_target="tpu_custom_call" | custom-call | flops 1000000 | tf_op jit(solution)/shard_map/pallas_call | solution.py:392
  31.4 11.5 %all_to_all.5.received_ref = bf16[32,2,640]{2,1,0:T(2,128)(2,1)S(1)} all-to-all(bf16[32,2,640]{2,1,0:T(2,128)(2,1)S(1)} %shard_map.151), channel_id=1, replica_groups=mesh['req'=8,'head'=4] {'req','head'}, dimensions={0} | all-to-all | bytes 163840 | tf_op jit(solution)/shard_map/all_to_all | solution.py:544
  42.9 0.8 %shard_map.152 = bf16[2,1024]{1,0:T(2,128)(2,1)} custom-call(bf16[32,2,640]{2,1,0:T(2,128)(2,1)S(1)} %all_to_all.5.received_ref), custom_call_target="tpu_custom_call" | custom-call | tf_op jit(solution)/shard_map/pallas_call | solution.py:545
  (25 shorter events, 0.1 us)
Async XLA Ops:
  0.8 12.4 %copy-start.1 = (bf16[2,1024,768]{2,1,0:T(8,128)(2,1)S(1)}, bf16[2,1024,768]{2,1,0:T(8,128)(2,1)}, u32[]{:S(2)}) copy-start(bf16[2,1024,768]{2,1,0:T(8,128)(2,1)} %refs_12_.3) | copy-start | bytes 9437188
  0.8 12.4 %copy-start.3 = (s32[8,512]{1,0:T(8,128)S(1)}, s32[8,512]{1,0:T(8,128)}, u32[]{:S(2)}) copy-start(s32[8,512]{1,0:T(8,128)} %refs_7_.4) | copy-start | bytes 49156
  0.8 12.4 %copy-start.4 = (f32[2,1024]{1,0:T(2,128)S(1)}, f32[2,1024]{1,0:T(2,128)}, u32[]{:S(2)}) copy-start(f32[2,1024]{1,0:T(2,128)} %refs_11_.3) | copy-start | bytes 24580
  0.8 12.4 %copy-start.6 = (f32[2,2,4]{2,1,0:T(2,128)S(1)}, f32[2,2,4]{2,1,0:T(2,128)}, u32[]{:S(2)}) copy-start(f32[2,2,4]{2,1,0:T(2,128)} %refs_14_.1) | copy-start | bytes 196
  0.8 12.4 %copy-start.7 = (f32[1,128]{1,0:T(1,128)S(1)}, f32[1,128]{1,0:T(1,128)}, u32[]{:S(2)}) copy-start(f32[1,128]{1,0:T(1,128)} %constant.8.clone.refs_5_) | copy-start | bytes 1540
  0.8 5.0 %collective-permute-start = (bf16[8,1152]{1,0:T(8,128)(2,1)S(1)}, bf16[8,1152]{1,0:T(8,128)(2,1)S(1)}, u32[]{:S(2)}, u32[]{:S(2)}) collective-permute-start(bf16[8,1152]{1,0:T(8,128)(2,1)S(1)} %shard_map.145.after_ref), channel_id=1, source_target_pairs={{0,17},{1,16},{2,19},{3,18},{4,21},{5,20},{6,23},{7,22},{8,25},{9,... | collective-permute-start | bytes 55304 | tf_op jit(solution)/shard_map/ppermute | solution.py:425
  5.9 5.0 %collective-permute-start.3 = (bf16[16,1152]{1,0:T(8,128)(2,1)S(1)}, bf16[16,1152]{1,0:T(8,128)(2,1)S(1)}, u32[]{:S(2)}, u32[]{:S(2)}) collective-permute-start(bf16[16,1152]{1,0:T(8,128)(2,1)S(1)} %pad_maximum_fusion.refs_0_), channel_id=1, source_target_pairs={{0,9},{1,8},{2,11},{3,10},{4,13},{5,12},{6,15},{7,14},{8,1},{9,0},... | collective-permute-start | bytes 110600 | tf_op jit(solution)/shard_map/ppermute | solution.py:425
  7.7 4.3 %collective-permute-start.2 = (bf16[16,1152]{1,0:T(8,128)(2,1)S(1)}, bf16[16,1152]{1,0:T(8,128)(2,1)S(1)}, u32[]{:S(2)}, u32[]{:S(2)}) collective-permute-start(bf16[16,1152]{1,0:T(8,128)(2,1)S(1)} %pad_maximum_fusion.refs_0_), channel_id=1, source_target_pairs={{0,13},{1,12},{2,15},{3,14},{4,9},{5,8},{6,11},{7,10},{8,5},{9,4},... | collective-permute-start | bytes 110600 | tf_op jit(solution)/shard_map/ppermute | solution.py:425
  9.2 4.0 %collective-permute-start.1 = (bf16[16,1152]{1,0:T(8,128)(2,1)S(1)}, bf16[16,1152]{1,0:T(8,128)(2,1)S(1)}, u32[]{:S(2)}, u32[]{:S(2)}) collective-permute-start(bf16[16,1152]{1,0:T(8,128)(2,1)S(1)} %pad_maximum_fusion.refs_0_), channel_id=1, source_target_pairs={{0,5},{1,4},{2,7},{3,6},{4,1},{5,0},{6,3},{7,2},{8,13},{9,12},{10,... | collective-permute-start | bytes 110600 | tf_op jit(solution)/shard_map/ppermute | solution.py:425
  9.3 3.9 %copy-start.2 = (bf16[2,256,1024]{2,1,0:T(8,128)(2,1)S(1)}, bf16[2,256,1024]{2,1,0:T(8,128)(2,1)}, u32[]{:S(2)}) copy-start(bf16[2,256,1024]{2,1,0:T(8,128)(2,1)} %refs_13_.3) | copy-start | bytes 3145732
  9.3 10.4 %slice-start = ((s8[8388608]{0:T(1024)(128)(4,1)}), s8[4194304]{0:T(1024)(128)(4,1)S(1)}, s32[]{:S(2)}) async-start(s8[8388608]{0:T(1024)(128)(4,1)} %bitcast.1), calls=%async_computation.1 | async-start | bytes 8388608
  10.8 8.9 %copy-start = (bf16[2,1024,1024]{2,1,0:T(8,128)(2,1)S(1)}, bf16[2,1024,1024]{2,1,0:T(8,128)(2,1)}, u32[]{:S(2)}) copy-start(bf16[2,1024,1024]{2,1,0:T(8,128)(2,1)} %refs_9_.3) | copy-start | bytes 12582916
  10.8 8.9 %copy-start.5 = (f32[2,1024]{1,0:T(2,128)S(1)}, f32[2,1024]{1,0:T(2,128)}, u32[]{:S(2)}) copy-start(f32[2,1024]{1,0:T(2,128)} %refs_7_.5) | copy-start | bytes 24580
  13.2 6.5 %slice-start.1 = ((s8[8388608]{0:T(1024)(128)(4,1)}), s8[4194304]{0:T(1024)(128)(4,1)S(1)}, s32[]{:S(2)}) async-start(s8[8388608]{0:T(1024)(128)(4,1)} %bitcast.1), calls=%async_computation.2 | async-start | bytes 8388608
  14.7 3.2 %collective-permute-start.6 = (bf16[8,1024]{1,0:T(8,128)(2,1)S(1)}, bf16[8,1024]{1,0:T(8,128)(2,1)S(1)}, u32[]{:S(2)}, u32[]{:S(2)}) collective-permute-start(bf16[8,1024]{1,0:T(8,128)(2,1)S(1)} %get-tuple-element.23.refs_0_), channel_id=1, source_target_pairs={{0,3},{1,2},{2,1},{3,0},{4,7},{5,6},{6,5},{7,4},{8,11},{9,10},{10,... | collective-permute-start | bytes 49160 | tf_op jit(solution)/shard_map/ppermute | solution.py:405
  16.0 3.7 %collective-permute-start.5 = (bf16[8,1024]{1,0:T(8,128)(2,1)S(1)}, bf16[8,1024]{1,0:T(8,128)(2,1)S(1)}, u32[]{:S(2)}, u32[]{:S(2)}) collective-permute-start(bf16[8,1024]{1,0:T(8,128)(2,1)S(1)} %get-tuple-element.23.refs_0_), channel_id=1, source_target_pairs={{0,2},{1,3},{2,0},{3,1},{4,6},{5,7},{6,4},{7,5},{8,10},{9,11},{10,... | collective-permute-start | bytes 49160 | tf_op jit(solution)/shard_map/ppermute | solution.py:405
  16.5 3.2 %collective-permute-start.4 = (bf16[8,1024]{1,0:T(8,128)(2,1)S(1)}, bf16[8,1024]{1,0:T(8,128)(2,1)S(1)}, u32[]{:S(2)}, u32[]{:S(2)}) collective-permute-start(bf16[8,1024]{1,0:T(8,128)(2,1)S(1)} %get-tuple-element.23.refs_0_), channel_id=1, source_target_pairs={{0,1},{1,0},{2,3},{3,2},{4,5},{5,4},{6,7},{7,6},{8,9},{9,8},{10,11... | collective-permute-start | bytes 49160 | tf_op jit(solution)/shard_map/ppermute | solution.py:405
  20.7 3.2 %collective-permute-start.9 = (bf16[8,1024]{1,0:T(8,128)(2,1)S(1)}, bf16[8,1024]{1,0:T(8,128)(2,1)S(1)}, u32[]{:S(2)}, u32[]{:S(2)}) collective-permute-start(bf16[8,1024]{1,0:T(8,128)(2,1)S(1)} %get-tuple-element.25.after_ref.refs_0_), channel_id=1, source_target_pairs={{0,3},{1,2},{2,1},{3,0},{4,7},{5,6},{6,5},{7,4},{8,11},{9,10},{10,... | collective-permute-start | bytes 49160 | tf_op jit(solution)/shard_map/ppermute | solution.py:405
  20.7 3.8 %collective-permute-start.8 = (bf16[8,1024]{1,0:T(8,128)(2,1)S(1)}, bf16[8,1024]{1,0:T(8,128)(2,1)S(1)}, u32[]{:S(2)}, u32[]{:S(2)}) collective-permute-start(bf16[8,1024]{1,0:T(8,128)(2,1)S(1)} %get-tuple-element.25.after_ref.refs_0_), channel_id=1, source_target_pairs={{0,2},{1,3},{2,0},{3,1},{4,6},{5,7},{6,4},{7,5},{8,10},{9,11},{10,... | collective-permute-start | bytes 49160 | tf_op jit(solution)/shard_map/ppermute | solution.py:405
  21.6 2.9 %collective-permute-start.7 = (bf16[8,1024]{1,0:T(8,128)(2,1)S(1)}, bf16[8,1024]{1,0:T(8,128)(2,1)S(1)}, u32[]{:S(2)}, u32[]{:S(2)}) collective-permute-start(bf16[8,1024]{1,0:T(8,128)(2,1)S(1)} %get-tuple-element.25.after_ref.refs_0_), channel_id=1, source_target_pairs={{0,1},{1,0},{2,3},{3,2},{4,5},{5,4},{6,7},{7,6},{8,9},{9,8},{10,11... | collective-permute-start | bytes 49160 | tf_op jit(solution)/shard_map/ppermute | solution.py:405
  25.9 3.2 %collective-permute-start.12 = (bf16[8,1024]{1,0:T(8,128)(2,1)S(1)}, bf16[8,1024]{1,0:T(8,128)(2,1)S(1)}, u32[]{:S(2)}, u32[]{:S(2)}) collective-permute-start(bf16[8,1024]{1,0:T(8,128)(2,1)S(1)} %get-tuple-element.31.refs_0_), channel_id=1, source_target_pairs={{0,3},{1,2},{2,1},{3,0},{4,7},{5,6},{6,5},{7,4},{8,11},{9,10},{10,... | collective-permute-start | bytes 49160 | tf_op jit(solution)/shard_map/ppermute | solution.py:405
  26.6 3.7 %collective-permute-start.11 = (bf16[8,1024]{1,0:T(8,128)(2,1)S(1)}, bf16[8,1024]{1,0:T(8,128)(2,1)S(1)}, u32[]{:S(2)}, u32[]{:S(2)}) collective-permute-start(bf16[8,1024]{1,0:T(8,128)(2,1)S(1)} %get-tuple-element.31.refs_0_), channel_id=1, source_target_pairs={{0,2},{1,3},{2,0},{3,1},{4,6},{5,7},{6,4},{7,5},{8,10},{9,11},{10,... | collective-permute-start | bytes 49160 | tf_op jit(solution)/shard_map/ppermute | solution.py:405
  27.1 3.2 %collective-permute-start.10 = (bf16[8,1024]{1,0:T(8,128)(2,1)S(1)}, bf16[8,1024]{1,0:T(8,128)(2,1)S(1)}, u32[]{:S(2)}, u32[]{:S(2)}) collective-permute-start(bf16[8,1024]{1,0:T(8,128)(2,1)S(1)} %get-tuple-element.31.refs_0_), channel_id=1, source_target_pairs={{0,1},{1,0},{2,3},{3,2},{4,5},{5,4},{6,7},{7,6},{8,9},{9,8},{10,11... | collective-permute-start | bytes 49160 | tf_op jit(solution)/shard_map/ppermute | solution.py:405

commit v7 on v6

--- a/solution.py
+++ b/solution.py
@@ -43,10 +43,10 @@
     rows, width = tokens_ref.shape
     copy_all(
         [
+            (tokens_ref, out_ref.at[:, pl.ds(0, width)]),
             (lengths_ref, length),
             (positions_ref, position),
             (variates_ref, variate),
-            (tokens_ref, out_ref.at[:, pl.ds(0, width)]),
         ],
         sems,
     )
@@ -74,6 +74,7 @@
 
 def owner_kernel(
     share,
+    heads,
     block_ids,
     after_ref,
     owner_ref,
@@ -100,19 +101,21 @@
     devices = place_ref.shape[0]
     row, column = iota((slots, total), 0), iota((slots, total), 1)
     target, slot = iota((devices, slots), 0), iota((devices, slots), 1)
-    flag_row, lane = iota((slots, META), 0), iota((slots, META), 1)
-    block = jnp.zeros((slots, total), jnp.int32)
+    flag_row, flag_part = iota((slots, flag_ref.shape[1]), 0), iota((slots, flag_ref.shape[1]), 1) // 128
+    mask = jnp.zeros((slots, total), jnp.int32)
     for k, block_id in enumerate(block_ids):
-        block = jnp.where(column // slots == k, block_id, block)
-    request_at = (block ^ own_block[0]) * slots + column % slots
+        mask = jnp.where(column // slots == k, block_id, mask)
+    request_at = (mask ^ own_block[0]) * slots + column % slots
     pick = jnp.zeros((slots, total), F32)
     place = jnp.zeros((devices, slots), F32)
-    flag = jnp.zeros((slots, META), F32)
+    flag = jnp.zeros(flag_ref.shape, F32)
     for s in range(slots):
         request = owner[s]
         pick = jnp.where((row == s) & (request_at == request), 1.0, pick)
-        place = jnp.where((slot == s) & (target == request // share), 1.0, place)
-        flag = jnp.where((flag_row == s) & (lane == request % share), 1.0, flag)
+        device = request // share
+        block = device % heads * (devices // heads) + device // heads
+        place = jnp.where((slot == s) & (target == block), 1.0, place)
+        flag = jnp.where((flag_row == s) & (flag_part == request % share), 1.0, flag)
     pick_ref[...] = pick.astype(BF16)
     place_ref[...] = place.astype(BF16)
     flag_ref[...] = flag.astype(BF16)
@@ -365,9 +368,11 @@
     place_ref, flag_ref, old_ref, gain_ref, gate_up_ref, down_ref, send_ref = refs[part_count:]
     stream, part = feed_forward(layer, refs[:part_count], old_ref, gain_ref, gate_up_ref, down_ref)
     rows = (part + stream * (1.0 / head_count)).astype(BF16)
-    half = rows.shape[1] // 2
+    half, tail = rows.shape[1] // 2, flag_ref.shape[1] // 2
     for i in range(2):
-        payload = jnp.concatenate([rows[:, i * half : (i + 1) * half], flag_ref[...]], axis=1)
+        payload = jnp.concatenate(
+            [rows[:, i * half : (i + 1) * half], flag_ref[:, i * tail : (i + 1) * tail]], axis=1
+        )
         spread = jnp.dot(place_ref[...], payload, preferred_element_type=F32)
         send_ref[:, i, :] = spread.astype(BF16)
 
@@ -375,11 +380,14 @@
 def place_kernel(received_ref, out_ref):
     share, width = out_ref.shape
     half = width // 2
-    for i in range(2):
-        rows = received_ref[:, i, :half].astype(F32)
-        flags = received_ref[:, i, half:].astype(F32)
-        for k in range(share):
-            row = jnp.sum(flags[:, k : k + 1] * rows, axis=0, keepdims=True)
+    tail = (received_ref.shape[2] - half) // 128
+    for k in range(share):
+        lanes = slice(half + k % tail * 128, half + (k % tail + 1) * 128)
+        flags = received_ref[:, k // tail, lanes].astype(F32)
+        mask = jnp.concatenate([flags] * (half // 128), axis=1)
+        for i in range(2):
+            rows = received_ref[:, i, :half].astype(F32)
+            row = jnp.sum(mask * rows, axis=0, keepdims=True)
             out_ref[k : k + 1, i * half : (i + 1) * half] = row.astype(BF16)
 
 
@@ -455,6 +463,7 @@
     head_count = lax.axis_size("head")
     devices = lax.axis_size("req") * head_count
     share = slots // head_count
+    tail = 128 * -(-share // 2)
     local_heads = local_width // HD
 
     total = slots * lax.axis_size("req")
@@ -475,9 +484,9 @@
         ((2, cap - CHUNK, local_width), BF16),
     ]
     pick, place, flag, *cache = call(
-        functools.partial(owner_kernel, share, block_ids),
+        functools.partial(owner_kernel, share, head_count, block_ids),
         [(ANY, packed), (HBM, slot_owner), (HBM, own_block), (HBM, kv_cache)],
-        [((slots, total), BF16), ((devices, slots), BF16), ((slots, META), BF16)]
+        [((slots, total), BF16), ((devices, slots), BF16), ((slots, tail * 2), BF16)]
         + cache_types,
         [
             pltpu.SMEM((slots,), jnp.int32),
@@ -539,9 +548,9 @@
             (send,) = call(
                 functools.partial(last_feed_forward_kernel, layer, len(parts), head_count),
                 on_chip(*parts, place, flag, stream, ffn_gain, gate_up_weight, down_weight),
-                [((devices, 2, width // 2 + META), BF16)],
-            )
-    received = lax.all_to_all(send, ("req", "head"), 0, 0, tiled=True)
+                [((devices, 2, width // 2 + tail), BF16)],
+            )
+    received = lax.all_to_all(send, ("head", "req"), 0, 0, tiled=True)
     return pl.pallas_call(
         place_kernel,
         out_shape=jax.ShapeDtypeStruct((share, width), BF16),

time: 44 us -> 43.9 us (level)
  no operation moved by 1% of the time
where the time goes in v7:
time: 43.9 us; the launch traced here: 43.6 us
  starting transfers between devices  12.8 us (29%)
  blocking collectives  11.3 us (26%)
  waiting for transfers between devices  9.9 us (23%)
  Pallas kernels  9.35 us (21%)
    all_to_all x1, blocking collectives, per_device(): received = lax.all_to_all(send, ('head', 'req'), 0, 0, tiled=True)  11.3 us
    pallas_call x7, Pallas kernels, call(): pl.pallas_call(kernel, out_shape=[pltpu.VMEM(shape, dtype) for shape, dty...  8.59 us
    ppermute x4, starting transfers between devices, swap_across(): return lax.ppermute(array, ('req', 'head'), pairs)  7 us
    ppermute x9, waiting for transfers between devices, swap(): return lax.ppermute(array, axis, [(i, i ^ mask) for i in range(count)])  6.1 us
    ppermute x9, starting transfers between devices, swap(): return lax.ppermute(array, axis, [(i, i ^ mask) for i in range(count)])  5.76 us
    ppermute x4, waiting for transfers between devices, swap_across(): return lax.ppermute(array, ('req', 'head'), pairs)  3.79 us
  transfers between devices with their start and end apart: 13, of which 8 were waited for; matrix products, arithmetic and copies ran while one was open for 0% of the time, Pallas kernels for 6%

profile of v7, /device:TPU:0, one launch (start us, length us, event | category | flops | bytes accessed | tf_op | source)
XLA Modules:
  0.0 43.6 jit_solution(10583786624585045166)
XLA Ops:
  0.0 0.9 %shard_map.145.after_ref = bf16[8,1152]{1,0:T(8,128)(2,1)S(1)} custom-call(bf16[8,1024]{1,0:T(8,128)(2,1)} %tokens_ref.1, s32[8]{0:T(128)} %lengths_ref.1, s32[8]{0:T(128)} %positions_ref.1, s32[8]{0:T(128)} %variates_ref.1), custom_call_target="tpu_custom_call" | custom-call | flops 99999997952 | tf_op jit(solution)/shard_map/pallas_call | solution.py:400
  0.9 0.0 copy-start.1
  0.9 0.0 copy-start.7
  0.9 3.5 %collective-permute-start = (bf16[8,1152]{1,0:T(8,128)(2,1)S(1)}, bf16[8,1152]{1,0:T(8,128)(2,1)S(1)}, u32[]{:S(2)}, u32[]{:S(2)}) collective-permute-start(bf16[8,1152]{1,0:T(8,128)(2,1)S(1)} %shard_map.145.after_ref), channel_id=1, source_target_pairs={{0,17},{1,16},{2,19},{3,18},{4,21},{5,20},{6,23},{7,22},{8,25},{9,... | collective-permute-start | bytes 55304 | tf_op jit(solution)/shard_map/ppermute | solution.py:433
  4.5 1.5 %collective-permute-done = bf16[8,1152]{1,0:T(8,128)(2,1)S(1)} collective-permute-done((bf16[8,1152]{1,0:T(8,128)(2,1)S(1)}, bf16[8,1152]{1,0:T(8,128)(2,1)S(1)}, u32[]{:S(2)}, u32[]{:S(2)}) %collective-permute-start) | collective-permute-done | bytes 18464 | tf_op jit(solution)/shard_map/ppermute | solution.py:433
  6.0 1.9 %collective-permute-start.3 = (bf16[16,1152]{1,0:T(8,128)(2,1)S(1)}, bf16[16,1152]{1,0:T(8,128)(2,1)S(1)}, u32[]{:S(2)}, u32[]{:S(2)}) collective-permute-start(bf16[16,1152]{1,0:T(8,128)(2,1)S(1)} %pad_maximum_fusion.refs_0_), channel_id=1, source_target_pairs={{0,9},{1,8},{2,11},{3,10},{4,13},{5,12},{6,15},{7,14},{8,1},{9,0},... | collective-permute-start | bytes 110600 | tf_op jit(solution)/shard_map/ppermute | solution.py:433
  7.8 1.4 %collective-permute-start.2 = (bf16[16,1152]{1,0:T(8,128)(2,1)S(1)}, bf16[16,1152]{1,0:T(8,128)(2,1)S(1)}, u32[]{:S(2)}, u32[]{:S(2)}) collective-permute-start(bf16[16,1152]{1,0:T(8,128)(2,1)S(1)} %pad_maximum_fusion.refs_0_), channel_id=1, source_target_pairs={{0,13},{1,12},{2,15},{3,14},{4,9},{5,8},{6,11},{7,10},{8,5},{9,4},... | collective-permute-start | bytes 110600 | tf_op jit(solution)/shard_map/ppermute | solution.py:433
  9.3 0.1 collective-permute-start.1
  9.4 1.5 %shard_map.146 = (bf16[8,64]{1,0:T(8,128)(2,1)S(1)}, bf16[32,8]{1,0:T(8,128)(2,1)S(1)}, bf16[8,256]{1,0:T(8,128)(2,1)S(1)}, bf16[2,8,128,256]{3,2,1,0:T(8,128)(2,1)S(1)}, bf16[2,384,256]{2,1,0:T(8,128)(2,1)S(1)}) custom-call(bf16[8,1152]{1,0:T(8,128)(2,1)S(1)} %shard_map.145.after_ref, s32[8]{0:T(128)} %owner_ref.1, s32[1]{0:T(128)} %bitcast.own_block_ref, ...), custom_call_target="tpu_custom_call" | custom-call | flops 1000000 | tf_op jit(solution)/shard_map/pallas_call | solution.py:400
  11.0 1.2 %collective-permute-done.2.refs_2_ = bf16[16,1152]{1,0:T(8,128)(2,1)S(1)} collective-permute-done((bf16[16,1152]{1,0:T(8,128)(2,1)S(1)}, bf16[16,1152]{1,0:T(8,128)(2,1)S(1)}, u32[]{:S(2)}, u32[]{:S(2)}) %collective-permute-start.2) | collective-permute-done | bytes 36896 | tf_op jit(solution)/shard_map/ppermute | solution.py:433
  12.1 1.2 %collective-permute-done.1.refs_1_ = bf16[16,1152]{1,0:T(8,128)(2,1)S(1)} collective-permute-done((bf16[16,1152]{1,0:T(8,128)(2,1)S(1)}, bf16[16,1152]{1,0:T(8,128)(2,1)S(1)}, u32[]{:S(2)}, u32[]{:S(2)}) %collective-permute-start.1) | collective-permute-done | bytes 36896 | tf_op jit(solution)/shard_map/ppermute | solution.py:433
  13.3 0.0 slice-start.1
  13.3 1.5 %shard_map.147 = (bf16[8,1024]{1,0:T(8,128)(2,1)S(1)}, f32[8,1024]{1,0:T(8,128)S(1)}, f32[8,128]{1,0:T(8,128)S(1)}, f32[8,256]{1,0:T(8,128)S(1)}) custom-call(bf16[16,1152]{1,0:T(8,128)(2,1)S(1)} %pad_maximum_fusion.refs_0_, bf16[16,1152]{1,0:T(8,128)(2,1)S(1)} %collective-permute-done.1.refs_1_, bf16[16,1152]{1,0:T(8,128)(2,1)S(1)} %collective-permute-done.2.refs_2_, ...), custom_call_target="tpu_custom_call" | custom-call | flops 1000000 | tf_op jit(solution)/shard_map/pallas_call | solution.py:400
  14.8 1.3 %collective-permute-start.6 = (bf16[8,1024]{1,0:T(8,128)(2,1)S(1)}, bf16[8,1024]{1,0:T(8,128)(2,1)S(1)}, u32[]{:S(2)}, u32[]{:S(2)}) collective-permute-start(bf16[8,1024]{1,0:T(8,128)(2,1)S(1)} %get-tuple-element.23.refs_0_), channel_id=1, source_target_pairs={{0,3},{1,2},{2,1},{3,0},{4,7},{5,6},{6,5},{7,4},{8,11},{9,10},{10,... | collective-permute-start | bytes 49160 | tf_op jit(solution)/shard_map/ppermute | solution.py:413
  16.1 0.5 %collective-permute-start.5 = (bf16[8,1024]{1,0:T(8,128)(2,1)S(1)}, bf16[8,1024]{1,0:T(8,128)(2,1)S(1)}, u32[]{:S(2)}, u32[]{:S(2)}) collective-permute-start(bf16[8,1024]{1,0:T(8,128)(2,1)S(1)} %get-tuple-element.23.refs_0_), channel_id=1, source_target_pairs={{0,2},{1,3},{2,0},{3,1},{4,6},{5,7},{6,4},{7,5},{8,10},{9,11},{10,... | collective-permute-start | bytes 49160 | tf_op jit(solution)/shard_map/ppermute | solution.py:413
  16.6 0.1 collective-permute-start.4
  16.8 1.3 %collective-permute-done.6.refs_3_ = bf16[8,1024]{1,0:T(8,128)(2,1)S(1)} collective-permute-done((bf16[8,1024]{1,0:T(8,128)(2,1)S(1)}, bf16[8,1024]{1,0:T(8,128)(2,1)S(1)}, u32[]{:S(2)}, u32[]{:S(2)}) %collective-permute-start.6) | collective-permute-done | bytes 16416 | tf_op jit(solution)/shard_map/ppermute | solution.py:413
  18.0 1.8 %collective-permute-done.5.refs_2_ = bf16[8,1024]{1,0:T(8,128)(2,1)S(1)} collective-permute-done((bf16[8,1024]{1,0:T(8,128)(2,1)S(1)}, bf16[8,1024]{1,0:T(8,128)(2,1)S(1)}, u32[]{:S(2)}, u32[]{:S(2)}) %collective-permute-start.5) | collective-permute-done | bytes 16416 | tf_op jit(solution)/shard_map/ppermute | solution.py:413
  19.9 0.9 %shard_map.148 = (bf16[8,1024]{1,0:T(8,128)(2,1)S(1)}, f32[8,1024]{1,0:T(8,128)S(1)}) custom-call(bf16[8,1024]{1,0:T(8,128)(2,1)S(1)} %get-tuple-element.23.refs_0_, bf16[8,1024]{1,0:T(8,128)(2,1)S(1)} %collective-permute-done.4.refs_1_, bf16[8,1024]{1,0:T(8,128)(2,1)S(1)} %collective-permute-done.5.refs_2_, ...), custom_call_target="tpu_custom_call" | custom-call | flops 1000000 | tf_op jit(solution)/shard_map/pallas_call | solution.py:400
  20.8 0.9 %collective-permute-start.8 = (bf16[8,1024]{1,0:T(8,128)(2,1)S(1)}, bf16[8,1024]{1,0:T(8,128)(2,1)S(1)}, u32[]{:S(2)}, u32[]{:S(2)}) collective-permute-start(bf16[8,1024]{1,0:T(8,128)(2,1)S(1)} %get-tuple-element.25.after_ref.refs_0_), channel_id=1, source_target_pairs={{0,2},{1,3},{2,0},{3,1},{4,6},{5,7},{6,4},{7,5},{8,10},{9,11},{10,... | collective-permute-start | bytes 49160 | tf_op jit(solution)/shard_map/ppermute | solution.py:413
  21.7 1.0 %collective-permute-start.7 = (bf16[8,1024]{1,0:T(8,128)(2,1)S(1)}, bf16[8,1024]{1,0:T(8,128)(2,1)S(1)}, u32[]{:S(2)}, u32[]{:S(2)}) collective-permute-start(bf16[8,1024]{1,0:T(8,128)(2,1)S(1)} %get-tuple-element.25.after_ref.refs_0_), channel_id=1, source_target_pairs={{0,1},{1,0},{2,3},{3,2},{4,5},{5,4},{6,7},{7,6},{8,9},{9,8},{10,11... | collective-permute-start | bytes 49160 | tf_op jit(solution)/shard_map/ppermute | solution.py:413
  22.7 1.3 %shard_map.149 = (bf16[2,8,128,256]{3,2,1,0:T(8,128)(2,1)S(1)}, bf16[2,384,256]{2,1,0:T(8,128)(2,1)S(1)}) custom-call(bf16[8,1024]{1,0:T(8,128)(2,1)S(1)} %get-tuple-element.25.after_ref.refs_0_, bf16[2,2,8,512,256]{4,3,2,1,0:T(8,128)(2,1)} %refs_10_.3), custom_call_target="tpu_custom_call" | custom-call | flops 1000000 | tf_op jit(solution)/shard_map/pallas_call | solution.py:400
  24.0 0.6 %collective-permute-done.8.refs_2_ = bf16[8,1024]{1,0:T(8,128)(2,1)S(1)} collective-permute-done((bf16[8,1024]{1,0:T(8,128)(2,1)S(1)}, bf16[8,1024]{1,0:T(8,128)(2,1)S(1)}, u32[]{:S(2)}, u32[]{:S(2)}) %collective-permute-start.8) | collective-permute-done | bytes 16416 | tf_op jit(solution)/shard_map/ppermute | solution.py:413
  24.6 1.4 %shard_map.150 = (bf16[8,1024]{1,0:T(8,128)(2,1)S(1)}, f32[8,1024]{1,0:T(8,128)S(1)}) custom-call(bf16[8,1024]{1,0:T(8,128)(2,1)S(1)} %get-tuple-element.25.after_ref.refs_0_, bf16[8,1024]{1,0:T(8,128)(2,1)S(1)} %collective-permute-done.7.refs_1_, bf16[8,1024]{1,0:T(8,128)(2,1)S(1)} %collective-permute-done.8.refs_2_, ...), custom_call_target="tpu_custom_call" | custom-call | flops 1000000 | tf_op jit(solution)/shard_map/pallas_call | solution.py:400
  26.0 0.6 %collective-permute-start.12 = (bf16[8,1024]{1,0:T(8,128)(2,1)S(1)}, bf16[8,1024]{1,0:T(8,128)(2,1)S(1)}, u32[]{:S(2)}, u32[]{:S(2)}) collective-permute-start(bf16[8,1024]{1,0:T(8,128)(2,1)S(1)} %get-tuple-element.31.refs_0_), channel_id=1, source_target_pairs={{0,3},{1,2},{2,1},{3,0},{4,7},{5,6},{6,5},{7,4},{8,11},{9,10},{10,... | collective-permute-start | bytes 49160 | tf_op jit(solution)/shard_map/ppermute | solution.py:413
  26.7 0.5 %collective-permute-start.11 = (bf16[8,1024]{1,0:T(8,128)(2,1)S(1)}, bf16[8,1024]{1,0:T(8,128)(2,1)S(1)}, u32[]{:S(2)}, u32[]{:S(2)}) collective-permute-start(bf16[8,1024]{1,0:T(8,128)(2,1)S(1)} %get-tuple-element.31.refs_0_), channel_id=1, source_target_pairs={{0,2},{1,3},{2,0},{3,1},{4,6},{5,7},{6,4},{7,5},{8,10},{9,11},{10,... | collective-permute-start | bytes 49160 | tf_op jit(solution)/shard_map/ppermute | solution.py:413
  27.2 0.7 %collective-permute-start.10 = (bf16[8,1024]{1,0:T(8,128)(2,1)S(1)}, bf16[8,1024]{1,0:T(8,128)(2,1)S(1)}, u32[]{:S(2)}, u32[]{:S(2)}) collective-permute-start(bf16[8,1024]{1,0:T(8,128)(2,1)S(1)} %get-tuple-element.31.refs_0_), channel_id=1, source_target_pairs={{0,1},{1,0},{2,3},{3,2},{4,5},{5,4},{6,7},{7,6},{8,9},{9,8},{10,11... | collective-permute-start | bytes 49160 | tf_op jit(solution)/shard_map/ppermute | solution.py:413
  27.9 1.3 %collective-permute-done.12.refs_3_ = bf16[8,1024]{1,0:T(8,128)(2,1)S(1)} collective-permute-done((bf16[8,1024]{1,0:T(8,128)(2,1)S(1)}, bf16[8,1024]{1,0:T(8,128)(2,1)S(1)}, u32[]{:S(2)}, u32[]{:S(2)}) %collective-permute-start.12) | collective-permute-done | bytes 16416 | tf_op jit(solution)/shard_map/ppermute | solution.py:413
  29.2 1.2 %collective-permute-done.11.refs_2_ = bf16[8,1024]{1,0:T(8,128)(2,1)S(1)} collective-permute-done((bf16[8,1024]{1,0:T(8,128)(2,1)S(1)}, bf16[8,1024]{1,0:T(8,128)(2,1)S(1)}, u32[]{:S(2)}, u32[]{:S(2)}) %collective-permute-start.11) | collective-permute-done | bytes 16416 | tf_op jit(solution)/shard_map/ppermute | solution.py:413
  30.4 1.1 %shard_map.151 = bf16[32,2,640]{2,1,0:T(2,128)(2,1)S(1)} custom-call(bf16[8,1024]{1,0:T(8,128)(2,1)S(1)} %get-tuple-element.31.refs_0_, bf16[8,1024]{1,0:T(8,128)(2,1)S(1)} %collective-permute-done.10.refs_1_, bf16[8,1024]{1,0:T(8,128)(2,1)S(1)} %collective-permute-done.11.refs_2_, bf16[8,1024]{1,0:T(8,128)(2,1)S(1)} %collective-permute-done.12.refs_3_, ...), custom_call_target="tpu_custom_call" | custom-call | flops 1000000 | tf_op jit(solution)/shard_map/pallas_call | solution.py:400
  31.5 11.3 %all_to_all.5.received_ref = bf16[32,2,640]{2,1,0:T(2,128)(2,1)S(1)} all-to-all(bf16[32,2,640]{2,1,0:T(2,128)(2,1)S(1)} %shard_map.151), channel_id=1, replica_groups=mesh['req'=8,'head'=4] {'head','req'}, dimensions={0} | all-to-all | bytes 163840 | tf_op jit(solution)/shard_map/all_to_all | solution.py:553
  42.8 0.8 %shard_map.152 = bf16[2,1024]{1,0:T(2,128)(2,1)} custom-call(bf16[32,2,640]{2,1,0:T(2,128)(2,1)S(1)} %all_to_all.5.received_ref), custom_call_target="tpu_custom_call" | custom-call | tf_op jit(solution)/shard_map/pallas_call | solution.py:554
  (25 shorter events, 0.1 us)
Async XLA Ops:
  0.9 12.4 %copy-start.1 = (bf16[2,1024,768]{2,1,0:T(8,128)(2,1)S(1)}, bf16[2,1024,768]{2,1,0:T(8,128)(2,1)}, u32[]{:S(2)}) copy-start(bf16[2,1024,768]{2,1,0:T(8,128)(2,1)} %refs_12_.3) | copy-start | bytes 9437188
  0.9 12.4 %copy-start.3 = (s32[8,512]{1,0:T(8,128)S(1)}, s32[8,512]{1,0:T(8,128)}, u32[]{:S(2)}) copy-start(s32[8,512]{1,0:T(8,128)} %refs_7_.4) | copy-start | bytes 49156
  0.9 12.4 %copy-start.4 = (f32[2,1024]{1,0:T(2,128)S(1)}, f32[2,1024]{1,0:T(2,128)}, u32[]{:S(2)}) copy-start(f32[2,1024]{1,0:T(2,128)} %refs_11_.3) | copy-start | bytes 24580
  0.9 12.4 %copy-start.6 = (f32[2,2,4]{2,1,0:T(2,128)S(1)}, f32[2,2,4]{2,1,0:T(2,128)}, u32[]{:S(2)}) copy-start(f32[2,2,4]{2,1,0:T(2,128)} %refs_14_.1) | copy-start | bytes 196
  0.9 12.4 %copy-start.7 = (f32[1,128]{1,0:T(1,128)S(1)}, f32[1,128]{1,0:T(1,128)}, u32[]{:S(2)}) copy-start(f32[1,128]{1,0:T(1,128)} %constant.8.clone.refs_5_) | copy-start | bytes 1540
  0.9 5.0 %collective-permute-start = (bf16[8,1152]{1,0:T(8,128)(2,1)S(1)}, bf16[8,1152]{1,0:T(8,128)(2,1)S(1)}, u32[]{:S(2)}, u32[]{:S(2)}) collective-permute-start(bf16[8,1152]{1,0:T(8,128)(2,1)S(1)} %shard_map.145.after_ref), channel_id=1, source_target_pairs={{0,17},{1,16},{2,19},{3,18},{4,21},{5,20},{6,23},{7,22},{8,25},{9,... | collective-permute-start | bytes 55304 | tf_op jit(solution)/shard_map/ppermute | solution.py:433
  6.0 5.0 %collective-permute-start.3 = (bf16[16,1152]{1,0:T(8,128)(2,1)S(1)}, bf16[16,1152]{1,0:T(8,128)(2,1)S(1)}, u32[]{:S(2)}, u32[]{:S(2)}) collective-permute-start(bf16[16,1152]{1,0:T(8,128)(2,1)S(1)} %pad_maximum_fusion.refs_0_), channel_id=1, source_target_pairs={{0,9},{1,8},{2,11},{3,10},{4,13},{5,12},{6,15},{7,14},{8,1},{9,0},... | collective-permute-start | bytes 110600 | tf_op jit(solution)/shard_map/ppermute | solution.py:433
  7.8 4.3 %collective-permute-start.2 = (bf16[16,1152]{1,0:T(8,128)(2,1)S(1)}, bf16[16,1152]{1,0:T(8,128)(2,1)S(1)}, u32[]{:S(2)}, u32[]{:S(2)}) collective-permute-start(bf16[16,1152]{1,0:T(8,128)(2,1)S(1)} %pad_maximum_fusion.refs_0_), channel_id=1, source_target_pairs={{0,13},{1,12},{2,15},{3,14},{4,9},{5,8},{6,11},{7,10},{8,5},{9,4},... | collective-permute-start | bytes 110600 | tf_op jit(solution)/shard_map/ppermute | solution.py:433
  9.3 4.0 %collective-permute-start.1 = (bf16[16,1152]{1,0:T(8,128)(2,1)S(1)}, bf16[16,1152]{1,0:T(8,128)(2,1)S(1)}, u32[]{:S(2)}, u32[]{:S(2)}) collective-permute-start(bf16[16,1152]{1,0:T(8,128)(2,1)S(1)} %pad_maximum_fusion.refs_0_), channel_id=1, source_target_pairs={{0,5},{1,4},{2,7},{3,6},{4,1},{5,0},{6,3},{7,2},{8,13},{9,12},{10,... | collective-permute-start | bytes 110600 | tf_op jit(solution)/shard_map/ppermute | solution.py:433
  9.4 3.9 %copy-start.2 = (bf16[2,256,1024]{2,1,0:T(8,128)(2,1)S(1)}, bf16[2,256,1024]{2,1,0:T(8,128)(2,1)}, u32[]{:S(2)}) copy-start(bf16[2,256,1024]{2,1,0:T(8,128)(2,1)} %refs_13_.3) | copy-start | bytes 3145732
  9.4 10.4 %slice-start = ((s8[8388608]{0:T(1024)(128)(4,1)}), s8[4194304]{0:T(1024)(128)(4,1)S(1)}, s32[]{:S(2)}) async-start(s8[8388608]{0:T(1024)(128)(4,1)} %bitcast.1), calls=%async_computation.1 | async-start | bytes 8388608
  10.9 8.9 %copy-start = (bf16[2,1024,1024]{2,1,0:T(8,128)(2,1)S(1)}, bf16[2,1024,1024]{2,1,0:T(8,128)(2,1)}, u32[]{:S(2)}) copy-start(bf16[2,1024,1024]{2,1,0:T(8,128)(2,1)} %refs_9_.3) | copy-start | bytes 12582916
  10.9 8.9 %copy-start.5 = (f32[2,1024]{1,0:T(2,128)S(1)}, f32[2,1024]{1,0:T(2,128)}, u32[]{:S(2)}) copy-start(f32[2,1024]{1,0:T(2,128)} %refs_7_.5) | copy-start | bytes 24580
  13.3 6.5 %slice-start.1 = ((s8[8388608]{0:T(1024)(128)(4,1)}), s8[4194304]{0:T(1024)(128)(4,1)S(1)}, s32[]{:S(2)}) async-start(s8[8388608]{0:T(1024)(128)(4,1)} %bitcast.1), calls=%async_computation.2 | async-start | bytes 8388608
  14.8 3.2 %collective-permute-start.6 = (bf16[8,1024]{1,0:T(8,128)(2,1)S(1)}, bf16[8,1024]{1,0:T(8,128)(2,1)S(1)}, u32[]{:S(2)}, u32[]{:S(2)}) collective-permute-start(bf16[8,1024]{1,0:T(8,128)(2,1)S(1)} %get-tuple-element.23.refs_0_), channel_id=1, source_target_pairs={{0,3},{1,2},{2,1},{3,0},{4,7},{5,6},{6,5},{7,4},{8,11},{9,10},{10,... | collective-permute-start | bytes 49160 | tf_op jit(solution)/shard_map/ppermute | solution.py:413
  16.1 3.7 %collective-permute-start.5 = (bf16[8,1024]{1,0:T(8,128)(2,1)S(1)}, bf16[8,1024]{1,0:T(8,128)(2,1)S(1)}, u32[]{:S(2)}, u32[]{:S(2)}) collective-permute-start(bf16[8,1024]{1,0:T(8,128)(2,1)S(1)} %get-tuple-element.23.refs_0_), channel_id=1, source_target_pairs={{0,2},{1,3},{2,0},{3,1},{4,6},{5,7},{6,4},{7,5},{8,10},{9,11},{10,... | collective-permute-start | bytes 49160 | tf_op jit(solution)/shard_map/ppermute | solution.py:413
  16.6 3.2 %collective-permute-start.4 = (bf16[8,1024]{1,0:T(8,128)(2,1)S(1)}, bf16[8,1024]{1,0:T(8,128)(2,1)S(1)}, u32[]{:S(2)}, u32[]{:S(2)}) collective-permute-start(bf16[8,1024]{1,0:T(8,128)(2,1)S(1)} %get-tuple-element.23.refs_0_), channel_id=1, source_target_pairs={{0,1},{1,0},{2,3},{3,2},{4,5},{5,4},{6,7},{7,6},{8,9},{9,8},{10,11... | collective-permute-start | bytes 49160 | tf_op jit(solution)/shard_map/ppermute | solution.py:413
  20.8 3.2 %collective-permute-start.9 = (bf16[8,1024]{1,0:T(8,128)(2,1)S(1)}, bf16[8,1024]{1,0:T(8,128)(2,1)S(1)}, u32[]{:S(2)}, u32[]{:S(2)}) collective-permute-start(bf16[8,1024]{1,0:T(8,128)(2,1)S(1)} %get-tuple-element.25.after_ref.refs_0_), channel_id=1, source_target_pairs={{0,3},{1,2},{2,1},{3,0},{4,7},{5,6},{6,5},{7,4},{8,11},{9,10},{10,... | collective-permute-start | bytes 49160 | tf_op jit(solution)/shard_map/ppermute | solution.py:413
  20.8 3.8 %collective-permute-start.8 = (bf16[8,1024]{1,0:T(8,128)(2,1)S(1)}, bf16[8,1024]{1,0:T(8,128)(2,1)S(1)}, u32[]{:S(2)}, u32[]{:S(2)}) collective-permute-start(bf16[8,1024]{1,0:T(8,128)(2,1)S(1)} %get-tuple-element.25.after_ref.refs_0_), channel_id=1, source_target_pairs={{0,2},{1,3},{2,0},{3,1},{4,6},{5,7},{6,4},{7,5},{8,10},{9,11},{10,... | collective-permute-start | bytes 49160 | tf_op jit(solution)/shard_map/ppermute | solution.py:413
  21.7 2.9 %collective-permute-start.7 = (bf16[8,1024]{1,0:T(8,128)(2,1)S(1)}, bf16[8,1024]{1,0:T(8,128)(2,1)S(1)}, u32[]{:S(2)}, u32[]{:S(2)}) collective-permute-start(bf16[8,1024]{1,0:T(8,128)(2,1)S(1)} %get-tuple-element.25.after_ref.refs_0_), channel_id=1, source_target_pairs={{0,1},{1,0},{2,3},{3,2},{4,5},{5,4},{6,7},{7,6},{8,9},{9,8},{10,11... | collective-permute-start | bytes 49160 | tf_op jit(solution)/shard_map/ppermute | solution.py:413
  26.0 3.2 %collective-permute-start.12 = (bf16[8,1024]{1,0:T(8,128)(2,1)S(1)}, bf16[8,1024]{1,0:T(8,128)(2,1)S(1)}, u32[]{:S(2)}, u32[]{:S(2)}) collective-permute-start(bf16[8,1024]{1,0:T(8,128)(2,1)S(1)} %get-tuple-element.31.refs_0_), channel_id=1, source_target_pairs={{0,3},{1,2},{2,1},{3,0},{4,7},{5,6},{6,5},{7,4},{8,11},{9,10},{10,... | collective-permute-start | bytes 49160 | tf_op jit(solution)/shard_map/ppermute | solution.py:413
  26.7 3.7 %collective-permute-start.11 = (bf16[8,1024]{1,0:T(8,128)(2,1)S(1)}, bf16[8,1024]{1,0:T(8,128)(2,1)S(1)}, u32[]{:S(2)}, u32[]{:S(2)}) collective-permute-start(bf16[8,1024]{1,0:T(8,128)(2,1)S(1)} %get-tuple-element.31.refs_0_), channel_id=1, source_target_pairs={{0,2},{1,3},{2,0},{3,1},{4,6},{5,7},{6,4},{7,5},{8,10},{9,11},{10,... | collective-permute-start | bytes 49160 | tf_op jit(solution)/shard_map/ppermute | solution.py:413
  27.2 3.2 %collective-permute-start.10 = (bf16[8,1024]{1,0:T(8,128)(2,1)S(1)}, bf16[8,1024]{1,0:T(8,128)(2,1)S(1)}, u32[]{:S(2)}, u32[]{:S(2)}) collective-permute-start(bf16[8,1024]{1,0:T(8,128)(2,1)S(1)} %get-tuple-element.31.refs_0_), channel_id=1, source_target_pairs={{0,1},{1,0},{2,3},{3,2},{4,5},{5,4},{6,7},{7,6},{8,9},{9,8},{10,11... | collective-permute-start | bytes 49160 | tf_op jit(solution)/shard_map/ppermute | solution.py:413

commit v8 on v7

--- a/solution.py
+++ b/solution.py
@@ -43,10 +43,10 @@
     rows, width = tokens_ref.shape
     copy_all(
         [
-            (tokens_ref, out_ref.at[:, pl.ds(0, width)]),
             (lengths_ref, length),
             (positions_ref, position),
             (variates_ref, variate),
+            (tokens_ref, out_ref.at[:, pl.ds(0, width)]),
         ],
         sems,
     )
@@ -113,7 +113,8 @@
         request = owner[s]
         pick = jnp.where((row == s) & (request_at == request), 1.0, pick)
         device = request // share
-        block = device % heads * (devices // heads) + device // heads
+        head = device % heads
+        block = (devices // heads - 1 - device // heads) * heads + head % 2 * (heads // 2) + head // 2
         place = jnp.where((slot == s) & (target == block), 1.0, place)
         flag = jnp.where((flag_row == s) & (flag_part == request % share), 1.0, flag)
     pick_ref[...] = pick.astype(BF16)
@@ -414,14 +415,11 @@
 
 
 def gather_stages(count):
-    stages = []
-    top = count
-    if count.bit_length() % 2 == 0:
-        top = count // 2
-        stages.append([top])
-    while top > 1:
-        stages.append([top // 4 * k for k in (1, 3, 2)])
-        top //= 4
+    stages, reach = [], 1
+    while reach < count:
+        span = 2 if (count // reach).bit_length() % 2 == 0 else 4
+        stages.append([reach * k for k in range(1, span)])
+        reach *= span
     return stages
 
 
@@ -550,7 +548,14 @@
                 on_chip(*parts, place, flag, stream, ffn_gain, gate_up_weight, down_weight),
                 [((devices, 2, width // 2 + tail), BF16)],
             )
-    received = lax.all_to_all(send, ("head", "req"), 0, 0, tiled=True)
+    order = [
+        r * head_count + h
+        for r in reversed(range(lax.axis_size("req")))
+        for h in [*range(0, head_count, 2), *range(1, head_count, 2)]
+    ]
+    received = lax.all_to_all(
+        send, ("req", "head"), 0, 0, axis_index_groups=[order], tiled=True
+    )
     return pl.pallas_call(
         place_kernel,
         out_shape=jax.ShapeDtypeStruct((share, width), BF16),

time: 43.9 us -> 43.4 us (0.989)
  blocking collectives: 11.3 us -> 10.6 us
    all_to_all x1, blocking collectives: 11.3 us -> 10.6 us  [per_device(): lax.all_to_all(send, ('req', 'head'), 0, 0, axis_index_groups=[order], ti...]
  transfers between devices with their start and end apart: 13 -> 13, of which waited for: 8 -> 7; matrix products, arithmetic and copies ran while one was open for 0% -> 0% of each run, Pallas kernels for 6% -> 7%
where the time goes in v8:
time: 43.4 us; the launch traced here: 43.1 us
  starting transfers between devices  13.1 us (30%)
  blocking collectives  10.6 us (24%)
  waiting for transfers between devices  9.88 us (23%)
  Pallas kernels  9.26 us (21%)
    all_to_all x1, blocking collectives, per_device(): lax.all_to_all(send, ('req', 'head'), 0, 0, axis_index_groups=[order], ti...  10.6 us
    pallas_call x7, Pallas kernels, call(): pl.pallas_call(kernel, out_shape=[pltpu.VMEM(shape, dtype) for shape, dty...  8.5 us
    ppermute x4, starting transfers between devices, swap_across(): return lax.ppermute(array, ('req', 'head'), pairs)  7.33 us
    ppermute x9, waiting for transfers between devices, swap(): return lax.ppermute(array, axis, [(i, i ^ mask) for i in range(count)])  6.21 us
    ppermute x9, starting transfers between devices, swap(): return lax.ppermute(array, axis, [(i, i ^ mask) for i in range(count)])  5.81 us
    ppermute x4, waiting for transfers between devices, swap_across(): return lax.ppermute(array, ('req', 'head'), pairs)  3.66 us
  transfers between devices with their start and end apart: 13, of which 7 were waited for; matrix products, arithmetic and copies ran while one was open for 0% of the time, Pallas kernels for 7%

profile of v8, /device:TPU:0, one launch (start us, length us, event | category | flops | bytes accessed | tf_op | source)
XLA Modules:
  0.0 43.1 jit_solution(7164975902258394883)
XLA Ops:
  0.0 0.8 %shard_map.145.after_ref = bf16[8,1152]{1,0:T(8,128)(2,1)S(1)} custom-call(bf16[8,1024]{1,0:T(8,128)(2,1)} %tokens_ref.1, s32[8]{0:T(128)} %lengths_ref.1, s32[8]{0:T(128)} %positions_ref.1, s32[8]{0:T(128)} %variates_ref.1), custom_call_target="tpu_custom_call" | custom-call | flops 99999997952 | tf_op jit(solution)/shard_map/pallas_call | solution.py:401
  0.8 0.0 copy-start.1
  0.8 0.0 copy-start.3
  0.8 0.0 copy-start.4
  0.8 0.0 copy-start.6
  0.8 0.0 copy-start.7
  0.8 2.5 %collective-permute-start = (bf16[8,1152]{1,0:T(8,128)(2,1)S(1)}, bf16[8,1152]{1,0:T(8,128)(2,1)S(1)}, u32[]{:S(2)}, u32[]{:S(2)}) collective-permute-start(bf16[8,1152]{1,0:T(8,128)(2,1)S(1)} %shard_map.145.after_ref), channel_id=1, source_target_pairs={{0,5},{1,4},{2,7},{3,6},{4,1},{5,0},{6,3},{7,2},{8,13},{9,12},{10,... | collective-permute-start | bytes 55304 | tf_op jit(solution)/shard_map/ppermute | solution.py:431
  3.3 1.5 %collective-permute-done = bf16[8,1152]{1,0:T(8,128)(2,1)S(1)} collective-permute-done((bf16[8,1152]{1,0:T(8,128)(2,1)S(1)}, bf16[8,1152]{1,0:T(8,128)(2,1)S(1)}, u32[]{:S(2)}, u32[]{:S(2)}) %collective-permute-start) | collective-permute-done | bytes 18464 | tf_op jit(solution)/shard_map/ppermute | solution.py:431
  4.8 4.2 %collective-permute-start.3 = (bf16[16,1152]{1,0:T(8,128)(2,1)S(1)}, bf16[16,1152]{1,0:T(8,128)(2,1)S(1)}, u32[]{:S(2)}, u32[]{:S(2)}) collective-permute-start(bf16[16,1152]{1,0:T(8,128)(2,1)S(1)} %pad_maximum_fusion.refs_0_), channel_id=1, source_target_pairs={{0,25},{1,24},{2,27},{3,26},{4,29},{5,28},{6,31},{7,30},{8,17},{9,... | collective-permute-start | bytes 110600 | tf_op jit(solution)/shard_map/ppermute | solution.py:431
  9.0 0.7 %collective-permute-start.1 = (bf16[16,1152]{1,0:T(8,128)(2,1)S(1)}, bf16[16,1152]{1,0:T(8,128)(2,1)S(1)}, u32[]{:S(2)}, u32[]{:S(2)}) collective-permute-start(bf16[16,1152]{1,0:T(8,128)(2,1)S(1)} %pad_maximum_fusion.refs_0_), channel_id=1, source_target_pairs={{0,9},{1,8},{2,11},{3,10},{4,13},{5,12},{6,15},{7,14},{8,1},{9,0},... | collective-permute-start | bytes 110600 | tf_op jit(solution)/shard_map/ppermute | solution.py:431
  9.7 1.5 %shard_map.146 = (bf16[8,64]{1,0:T(8,128)(2,1)S(1)}, bf16[32,8]{1,0:T(8,128)(2,1)S(1)}, bf16[8,256]{1,0:T(8,128)(2,1)S(1)}, bf16[2,8,128,256]{3,2,1,0:T(8,128)(2,1)S(1)}, bf16[2,384,256]{2,1,0:T(8,128)(2,1)S(1)}) custom-call(bf16[8,1152]{1,0:T(8,128)(2,1)S(1)} %shard_map.145.after_ref, s32[8]{0:T(128)} %owner_ref.1, s32[1]{0:T(128)} %bitcast.own_block_ref, ...), custom_call_target="tpu_custom_call" | custom-call | flops 1000000 | tf_op jit(solution)/shard_map/pallas_call | solution.py:401
  11.2 2.2 %collective-permute-done.2.refs_2_ = bf16[16,1152]{1,0:T(8,128)(2,1)S(1)} collective-permute-done((bf16[16,1152]{1,0:T(8,128)(2,1)S(1)}, bf16[16,1152]{1,0:T(8,128)(2,1)S(1)}, u32[]{:S(2)}, u32[]{:S(2)}) %collective-permute-start.2) | collective-permute-done | bytes 36896 | tf_op jit(solution)/shard_map/ppermute | solution.py:431
  13.4 0.0 slice-start.1
  13.4 1.5 %shard_map.147 = (bf16[8,1024]{1,0:T(8,128)(2,1)S(1)}, f32[8,1024]{1,0:T(8,128)S(1)}, f32[8,128]{1,0:T(8,128)S(1)}, f32[8,256]{1,0:T(8,128)S(1)}) custom-call(bf16[16,1152]{1,0:T(8,128)(2,1)S(1)} %pad_maximum_fusion.refs_0_, bf16[16,1152]{1,0:T(8,128)(2,1)S(1)} %collective-permute-done.1.refs_1_, bf16[16,1152]{1,0:T(8,128)(2,1)S(1)} %collective-permute-done.2.refs_2_, ...), custom_call_target="tpu_custom_call" | custom-call | flops 1000000 | tf_op jit(solution)/shard_map/pallas_call | solution.py:401
  14.9 1.5 %collective-permute-start.6 = (bf16[8,1024]{1,0:T(8,128)(2,1)S(1)}, bf16[8,1024]{1,0:T(8,128)(2,1)S(1)}, u32[]{:S(2)}, u32[]{:S(2)}) collective-permute-start(bf16[8,1024]{1,0:T(8,128)(2,1)S(1)} %get-tuple-element.23.refs_0_), channel_id=1, source_target_pairs={{0,3},{1,2},{2,1},{3,0},{4,7},{5,6},{6,5},{7,4},{8,11},{9,10},{10,... | collective-permute-start | bytes 49160 | tf_op jit(solution)/shard_map/ppermute | solution.py:414
  16.4 0.5 %collective-permute-start.5 = (bf16[8,1024]{1,0:T(8,128)(2,1)S(1)}, bf16[8,1024]{1,0:T(8,128)(2,1)S(1)}, u32[]{:S(2)}, u32[]{:S(2)}) collective-permute-start(bf16[8,1024]{1,0:T(8,128)(2,1)S(1)} %get-tuple-element.23.refs_0_), channel_id=1, source_target_pairs={{0,2},{1,3},{2,0},{3,1},{4,6},{5,7},{6,4},{7,5},{8,10},{9,11},{10,... | collective-permute-start | bytes 49160 | tf_op jit(solution)/shard_map/ppermute | solution.py:414
  16.9 1.2 %collective-permute-done.6.refs_3_ = bf16[8,1024]{1,0:T(8,128)(2,1)S(1)} collective-permute-done((bf16[8,1024]{1,0:T(8,128)(2,1)S(1)}, bf16[8,1024]{1,0:T(8,128)(2,1)S(1)}, u32[]{:S(2)}, u32[]{:S(2)}) %collective-permute-start.6) | collective-permute-done | bytes 16416 | tf_op jit(solution)/shard_map/ppermute | solution.py:414
  18.2 2.0 %collective-permute-done.5.refs_2_ = bf16[8,1024]{1,0:T(8,128)(2,1)S(1)} collective-permute-done((bf16[8,1024]{1,0:T(8,128)(2,1)S(1)}, bf16[8,1024]{1,0:T(8,128)(2,1)S(1)}, u32[]{:S(2)}, u32[]{:S(2)}) %collective-permute-start.5) | collective-permute-done | bytes 16416 | tf_op jit(solution)/shard_map/ppermute | solution.py:414
  20.2 0.9 %shard_map.148 = (bf16[8,1024]{1,0:T(8,128)(2,1)S(1)}, f32[8,1024]{1,0:T(8,128)S(1)}) custom-call(bf16[8,1024]{1,0:T(8,128)(2,1)S(1)} %get-tuple-element.23.refs_0_, bf16[8,1024]{1,0:T(8,128)(2,1)S(1)} %collective-permute-done.4.refs_1_, bf16[8,1024]{1,0:T(8,128)(2,1)S(1)} %collective-permute-done.5.refs_2_, ...), custom_call_target="tpu_custom_call" | custom-call | flops 1000000 | tf_op jit(solution)/shard_map/pallas_call | solution.py:401
  21.1 0.7 %collective-permute-start.8 = (bf16[8,1024]{1,0:T(8,128)(2,1)S(1)}, bf16[8,1024]{1,0:T(8,128)(2,1)S(1)}, u32[]{:S(2)}, u32[]{:S(2)}) collective-permute-start(bf16[8,1024]{1,0:T(8,128)(2,1)S(1)} %get-tuple-element.25.after_ref.refs_0_), channel_id=1, source_target_pairs={{0,2},{1,3},{2,0},{3,1},{4,6},{5,7},{6,4},{7,5},{8,10},{9,11},{10,... | collective-permute-start | bytes 49160 | tf_op jit(solution)/shard_map/ppermute | solution.py:414
  21.8 1.2 %collective-permute-start.7 = (bf16[8,1024]{1,0:T(8,128)(2,1)S(1)}, bf16[8,1024]{1,0:T(8,128)(2,1)S(1)}, u32[]{:S(2)}, u32[]{:S(2)}) collective-permute-start(bf16[8,1024]{1,0:T(8,128)(2,1)S(1)} %get-tuple-element.25.after_ref.refs_0_), channel_id=1, source_target_pairs={{0,1},{1,0},{2,3},{3,2},{4,5},{5,4},{6,7},{7,6},{8,9},{9,8},{10,11... | collective-permute-start | bytes 49160 | tf_op jit(solution)/shard_map/ppermute | solution.py:414
  23.0 1.3 %shard_map.149 = (bf16[2,8,128,256]{3,2,1,0:T(8,128)(2,1)S(1)}, bf16[2,384,256]{2,1,0:T(8,128)(2,1)S(1)}) custom-call(bf16[8,1024]{1,0:T(8,128)(2,1)S(1)} %get-tuple-element.25.after_ref.refs_0_, bf16[2,2,8,512,256]{4,3,2,1,0:T(8,128)(2,1)} %refs_10_.3), custom_call_target="tpu_custom_call" | custom-call | flops 1000000 | tf_op jit(solution)/shard_map/pallas_call | solution.py:401
  24.4 0.6 %collective-permute-done.8.refs_2_ = bf16[8,1024]{1,0:T(8,128)(2,1)S(1)} collective-permute-done((bf16[8,1024]{1,0:T(8,128)(2,1)S(1)}, bf16[8,1024]{1,0:T(8,128)(2,1)S(1)}, u32[]{:S(2)}, u32[]{:S(2)}) %collective-permute-start.8) | collective-permute-done | bytes 16416 | tf_op jit(solution)/shard_map/ppermute | solution.py:414
  24.9 1.4 %shard_map.150 = (bf16[8,1024]{1,0:T(8,128)(2,1)S(1)}, f32[8,1024]{1,0:T(8,128)S(1)}) custom-call(bf16[8,1024]{1,0:T(8,128)(2,1)S(1)} %get-tuple-element.25.after_ref.refs_0_, bf16[8,1024]{1,0:T(8,128)(2,1)S(1)} %collective-permute-done.7.refs_1_, bf16[8,1024]{1,0:T(8,128)(2,1)S(1)} %collective-permute-done.8.refs_2_, ...), custom_call_target="tpu_custom_call" | custom-call | flops 1000000 | tf_op jit(solution)/shard_map/pallas_call | solution.py:401
  26.3 0.6 %collective-permute-start.12 = (bf16[8,1024]{1,0:T(8,128)(2,1)S(1)}, bf16[8,1024]{1,0:T(8,128)(2,1)S(1)}, u32[]{:S(2)}, u32[]{:S(2)}) collective-permute-start(bf16[8,1024]{1,0:T(8,128)(2,1)S(1)} %get-tuple-element.31.refs_0_), channel_id=1, source_target_pairs={{0,3},{1,2},{2,1},{3,0},{4,7},{5,6},{6,5},{7,4},{8,11},{9,10},{10,... | collective-permute-start | bytes 49160 | tf_op jit(solution)/shard_map/ppermute | solution.py:414
  26.9 0.6 %collective-permute-start.11 = (bf16[8,1024]{1,0:T(8,128)(2,1)S(1)}, bf16[8,1024]{1,0:T(8,128)(2,1)S(1)}, u32[]{:S(2)}, u32[]{:S(2)}) collective-permute-start(bf16[8,1024]{1,0:T(8,128)(2,1)S(1)} %get-tuple-element.31.refs_0_), channel_id=1, source_target_pairs={{0,2},{1,3},{2,0},{3,1},{4,6},{5,7},{6,4},{7,5},{8,10},{9,11},{10,... | collective-permute-start | bytes 49160 | tf_op jit(solution)/shard_map/ppermute | solution.py:414
  27.5 0.7 %collective-permute-start.10 = (bf16[8,1024]{1,0:T(8,128)(2,1)S(1)}, bf16[8,1024]{1,0:T(8,128)(2,1)S(1)}, u32[]{:S(2)}, u32[]{:S(2)}) collective-permute-start(bf16[8,1024]{1,0:T(8,128)(2,1)S(1)} %get-tuple-element.31.refs_0_), channel_id=1, source_target_pairs={{0,1},{1,0},{2,3},{3,2},{4,5},{5,4},{6,7},{7,6},{8,9},{9,8},{10,11... | collective-permute-start | bytes 49160 | tf_op jit(solution)/shard_map/ppermute | solution.py:414
  28.3 1.3 %collective-permute-done.12.refs_3_ = bf16[8,1024]{1,0:T(8,128)(2,1)S(1)} collective-permute-done((bf16[8,1024]{1,0:T(8,128)(2,1)S(1)}, bf16[8,1024]{1,0:T(8,128)(2,1)S(1)}, u32[]{:S(2)}, u32[]{:S(2)}) %collective-permute-start.12) | collective-permute-done | bytes 16416 | tf_op jit(solution)/shard_map/ppermute | solution.py:414
  29.6 1.1 %collective-permute-done.11.refs_2_ = bf16[8,1024]{1,0:T(8,128)(2,1)S(1)} collective-permute-done((bf16[8,1024]{1,0:T(8,128)(2,1)S(1)}, bf16[8,1024]{1,0:T(8,128)(2,1)S(1)}, u32[]{:S(2)}, u32[]{:S(2)}) %collective-permute-start.11) | collective-permute-done | bytes 16416 | tf_op jit(solution)/shard_map/ppermute | solution.py:414
  30.7 1.1 %shard_map.151 = bf16[32,2,640]{2,1,0:T(2,128)(2,1)S(1)} custom-call(bf16[8,1024]{1,0:T(8,128)(2,1)S(1)} %get-tuple-element.31.refs_0_, bf16[8,1024]{1,0:T(8,128)(2,1)S(1)} %collective-permute-done.10.refs_1_, bf16[8,1024]{1,0:T(8,128)(2,1)S(1)} %collective-permute-done.11.refs_2_, bf16[8,1024]{1,0:T(8,128)(2,1)S(1)} %collective-permute-done.12.refs_3_, ...), custom_call_target="tpu_custom_call" | custom-call | flops 1000000 | tf_op jit(solution)/shard_map/pallas_call | solution.py:401
  31.8 10.6 %all_to_all.5.received_ref = bf16[32,2,640]{2,1,0:T(2,128)(2,1)S(1)} all-to-all(bf16[32,2,640]{2,1,0:T(2,128)(2,1)S(1)} %shard_map.151), channel_id=1, replica_groups={{28,30,29,31,24,26,25,27,20,22,21,23,16,18,17,19,12,14,13,15,8,10,9,11,..., dimensions={0} | all-to-all | bytes 163840 | tf_op jit(solution)/shard_map/all_to_all | solution.py:556
  42.4 0.8 %shard_map.152 = bf16[2,1024]{1,0:T(2,128)(2,1)} custom-call(bf16[32,2,640]{2,1,0:T(2,128)(2,1)S(1)} %all_to_all.5.received_ref), custom_call_target="tpu_custom_call" | custom-call | tf_op jit(solution)/shard_map/pallas_call | solution.py:559
  (25 shorter events, 0.1 us)
Async XLA Ops:
  0.8 12.6 %copy-start.1 = (bf16[2,1024,768]{2,1,0:T(8,128)(2,1)S(1)}, bf16[2,1024,768]{2,1,0:T(8,128)(2,1)}, u32[]{:S(2)}) copy-start(bf16[2,1024,768]{2,1,0:T(8,128)(2,1)} %refs_12_.3) | copy-start | bytes 9437188
  0.8 12.6 %copy-start.3 = (s32[8,512]{1,0:T(8,128)S(1)}, s32[8,512]{1,0:T(8,128)}, u32[]{:S(2)}) copy-start(s32[8,512]{1,0:T(8,128)} %refs_7_.4) | copy-start | bytes 49156
  0.8 12.6 %copy-start.4 = (f32[2,1024]{1,0:T(2,128)S(1)}, f32[2,1024]{1,0:T(2,128)}, u32[]{:S(2)}) copy-start(f32[2,1024]{1,0:T(2,128)} %refs_11_.3) | copy-start | bytes 24580
  0.8 12.6 %copy-start.6 = (f32[2,2,4]{2,1,0:T(2,128)S(1)}, f32[2,2,4]{2,1,0:T(2,128)}, u32[]{:S(2)}) copy-start(f32[2,2,4]{2,1,0:T(2,128)} %refs_14_.1) | copy-start | bytes 196
  0.8 12.6 %copy-start.7 = (f32[1,128]{1,0:T(1,128)S(1)}, f32[1,128]{1,0:T(1,128)}, u32[]{:S(2)}) copy-start(f32[1,128]{1,0:T(1,128)} %constant.8.clone.refs_5_) | copy-start | bytes 1540
  0.8 3.9 %collective-permute-start = (bf16[8,1152]{1,0:T(8,128)(2,1)S(1)}, bf16[8,1152]{1,0:T(8,128)(2,1)S(1)}, u32[]{:S(2)}, u32[]{:S(2)}) collective-permute-start(bf16[8,1152]{1,0:T(8,128)(2,1)S(1)} %shard_map.145.after_ref), channel_id=1, source_target_pairs={{0,5},{1,4},{2,7},{3,6},{4,1},{5,0},{6,3},{7,2},{8,13},{9,12},{10,... | collective-permute-start | bytes 55304 | tf_op jit(solution)/shard_map/ppermute | solution.py:431
  4.8 6.4 %collective-permute-start.3 = (bf16[16,1152]{1,0:T(8,128)(2,1)S(1)}, bf16[16,1152]{1,0:T(8,128)(2,1)S(1)}, u32[]{:S(2)}, u32[]{:S(2)}) collective-permute-start(bf16[16,1152]{1,0:T(8,128)(2,1)S(1)} %pad_maximum_fusion.refs_0_), channel_id=1, source_target_pairs={{0,25},{1,24},{2,27},{3,26},{4,29},{5,28},{6,31},{7,30},{8,17},{9,... | collective-permute-start | bytes 110600 | tf_op jit(solution)/shard_map/ppermute | solution.py:431
  9.0 4.4 %collective-permute-start.2 = (bf16[16,1152]{1,0:T(8,128)(2,1)S(1)}, bf16[16,1152]{1,0:T(8,128)(2,1)S(1)}, u32[]{:S(2)}, u32[]{:S(2)}) collective-permute-start(bf16[16,1152]{1,0:T(8,128)(2,1)S(1)} %pad_maximum_fusion.refs_0_), channel_id=1, source_target_pairs={{0,17},{1,16},{2,19},{3,18},{4,21},{5,20},{6,23},{7,22},{8,25},{9,... | collective-permute-start | bytes 110600 | tf_op jit(solution)/shard_map/ppermute | solution.py:431
  9.0 4.4 %collective-permute-start.1 = (bf16[16,1152]{1,0:T(8,128)(2,1)S(1)}, bf16[16,1152]{1,0:T(8,128)(2,1)S(1)}, u32[]{:S(2)}, u32[]{:S(2)}) collective-permute-start(bf16[16,1152]{1,0:T(8,128)(2,1)S(1)} %pad_maximum_fusion.refs_0_), channel_id=1, source_target_pairs={{0,9},{1,8},{2,11},{3,10},{4,13},{5,12},{6,15},{7,14},{8,1},{9,0},... | collective-permute-start | bytes 110600 | tf_op jit(solution)/shard_map/ppermute | solution.py:431
  9.7 3.8 %copy-start.2 = (bf16[2,256,1024]{2,1,0:T(8,128)(2,1)S(1)}, bf16[2,256,1024]{2,1,0:T(8,128)(2,1)}, u32[]{:S(2)}) copy-start(bf16[2,256,1024]{2,1,0:T(8,128)(2,1)} %refs_13_.3) | copy-start | bytes 3145732
  9.7 10.5 %slice-start = ((s8[8388608]{0:T(1024)(128)(4,1)}), s8[4194304]{0:T(1024)(128)(4,1)S(1)}, s32[]{:S(2)}) async-start(s8[8388608]{0:T(1024)(128)(4,1)} %bitcast.1), calls=%async_computation.1 | async-start | bytes 8388608
  11.2 9.0 %copy-start = (bf16[2,1024,1024]{2,1,0:T(8,128)(2,1)S(1)}, bf16[2,1024,1024]{2,1,0:T(8,128)(2,1)}, u32[]{:S(2)}) copy-start(bf16[2,1024,1024]{2,1,0:T(8,128)(2,1)} %refs_9_.3) | copy-start | bytes 12582916
  11.2 9.0 %copy-start.5 = (f32[2,1024]{1,0:T(2,128)S(1)}, f32[2,1024]{1,0:T(2,128)}, u32[]{:S(2)}) copy-start(f32[2,1024]{1,0:T(2,128)} %refs_7_.5) | copy-start | bytes 24580
  13.4 6.7 %slice-start.1 = ((s8[8388608]{0:T(1024)(128)(4,1)}), s8[4194304]{0:T(1024)(128)(4,1)S(1)}, s32[]{:S(2)}) async-start(s8[8388608]{0:T(1024)(128)(4,1)} %bitcast.1), calls=%async_computation.2 | async-start | bytes 8388608
  14.9 3.2 %collective-permute-start.6 = (bf16[8,1024]{1,0:T(8,128)(2,1)S(1)}, bf16[8,1024]{1,0:T(8,128)(2,1)S(1)}, u32[]{:S(2)}, u32[]{:S(2)}) collective-permute-start(bf16[8,1024]{1,0:T(8,128)(2,1)S(1)} %get-tuple-element.23.refs_0_), channel_id=1, source_target_pairs={{0,3},{1,2},{2,1},{3,0},{4,7},{5,6},{6,5},{7,4},{8,11},{9,10},{10,... | collective-permute-start | bytes 49160 | tf_op jit(solution)/shard_map/ppermute | solution.py:414
  16.4 3.7 %collective-permute-start.5 = (bf16[8,1024]{1,0:T(8,128)(2,1)S(1)}, bf16[8,1024]{1,0:T(8,128)(2,1)S(1)}, u32[]{:S(2)}, u32[]{:S(2)}) collective-permute-start(bf16[8,1024]{1,0:T(8,128)(2,1)S(1)} %get-tuple-element.23.refs_0_), channel_id=1, source_target_pairs={{0,2},{1,3},{2,0},{3,1},{4,6},{5,7},{6,4},{7,5},{8,10},{9,11},{10,... | collective-permute-start | bytes 49160 | tf_op jit(solution)/shard_map/ppermute | solution.py:414
  16.9 3.2 %collective-permute-start.4 = (bf16[8,1024]{1,0:T(8,128)(2,1)S(1)}, bf16[8,1024]{1,0:T(8,128)(2,1)S(1)}, u32[]{:S(2)}, u32[]{:S(2)}) collective-permute-start(bf16[8,1024]{1,0:T(8,128)(2,1)S(1)} %get-tuple-element.23.refs_0_), channel_id=1, source_target_pairs={{0,1},{1,0},{2,3},{3,2},{4,5},{5,4},{6,7},{7,6},{8,9},{9,8},{10,11... | collective-permute-start | bytes 49160 | tf_op jit(solution)/shard_map/ppermute | solution.py:414
  21.1 3.2 %collective-permute-start.9 = (bf16[8,1024]{1,0:T(8,128)(2,1)S(1)}, bf16[8,1024]{1,0:T(8,128)(2,1)S(1)}, u32[]{:S(2)}, u32[]{:S(2)}) collective-permute-start(bf16[8,1024]{1,0:T(8,128)(2,1)S(1)} %get-tuple-element.25.after_ref.refs_0_), channel_id=1, source_target_pairs={{0,3},{1,2},{2,1},{3,0},{4,7},{5,6},{6,5},{7,4},{8,11},{9,10},{10,... | collective-permute-start | bytes 49160 | tf_op jit(solution)/shard_map/ppermute | solution.py:414
  21.1 3.8 %collective-permute-start.8 = (bf16[8,1024]{1,0:T(8,128)(2,1)S(1)}, bf16[8,1024]{1,0:T(8,128)(2,1)S(1)}, u32[]{:S(2)}, u32[]{:S(2)}) collective-permute-start(bf16[8,1024]{1,0:T(8,128)(2,1)S(1)} %get-tuple-element.25.after_ref.refs_0_), channel_id=1, source_target_pairs={{0,2},{1,3},{2,0},{3,1},{4,6},{5,7},{6,4},{7,5},{8,10},{9,11},{10,... | collective-permute-start | bytes 49160 | tf_op jit(solution)/shard_map/ppermute | solution.py:414
  21.8 3.1 %collective-permute-start.7 = (bf16[8,1024]{1,0:T(8,128)(2,1)S(1)}, bf16[8,1024]{1,0:T(8,128)(2,1)S(1)}, u32[]{:S(2)}, u32[]{:S(2)}) collective-permute-start(bf16[8,1024]{1,0:T(8,128)(2,1)S(1)} %get-tuple-element.25.after_ref.refs_0_), channel_id=1, source_target_pairs={{0,1},{1,0},{2,3},{3,2},{4,5},{5,4},{6,7},{7,6},{8,9},{9,8},{10,11... | collective-permute-start | bytes 49160 | tf_op jit(solution)/shard_map/ppermute | solution.py:414
  26.3 3.2 %collective-permute-start.12 = (bf16[8,1024]{1,0:T(8,128)(2,1)S(1)}, bf16[8,1024]{1,0:T(8,128)(2,1)S(1)}, u32[]{:S(2)}, u32[]{:S(2)}) collective-permute-start(bf16[8,1024]{1,0:T(8,128)(2,1)S(1)} %get-tuple-element.31.refs_0_), channel_id=1, source_target_pairs={{0,3},{1,2},{2,1},{3,0},{4,7},{5,6},{6,5},{7,4},{8,11},{9,10},{10,... | collective-permute-start | bytes 49160 | tf_op jit(solution)/shard_map/ppermute | solution.py:414
  26.9 3.7 %collective-permute-start.11 = (bf16[8,1024]{1,0:T(8,128)(2,1)S(1)}, bf16[8,1024]{1,0:T(8,128)(2,1)S(1)}, u32[]{:S(2)}, u32[]{:S(2)}) collective-permute-start(bf16[8,1024]{1,0:T(8,128)(2,1)S(1)} %get-tuple-element.31.refs_0_), channel_id=1, source_target_pairs={{0,2},{1,3},{2,0},{3,1},{4,6},{5,7},{6,4},{7,5},{8,10},{9,11},{10,... | collective-permute-start | bytes 49160 | tf_op jit(solution)/shard_map/ppermute | solution.py:414
  27.5 3.2 %collective-permute-start.10 = (bf16[8,1024]{1,0:T(8,128)(2,1)S(1)}, bf16[8,1024]{1,0:T(8,128)(2,1)S(1)}, u32[]{:S(2)}, u32[]{:S(2)}) collective-permute-start(bf16[8,1024]{1,0:T(8,128)(2,1)S(1)} %get-tuple-element.31.refs_0_), channel_id=1, source_target_pairs={{0,1},{1,0},{2,3},{3,2},{4,5},{5,4},{6,7},{7,6},{8,9},{9,8},{10,11... | collective-permute-start | bytes 49160 | tf_op jit(solution)/shard_map/ppermute | solution.py:414

commit v9 on v8

--- a/solution.py
+++ b/solution.py
@@ -431,13 +431,21 @@
     return lax.ppermute(array, ("req", "head"), pairs)
 
 
-def gather_blocks(block):
-    blocks, ids = [block], [0]
+def gather_ids(count):
+    ids = [0]
+    for masks in gather_stages(count):
+        ids = ids + [mask ^ i for mask in masks for i in ids]
+    return ids
+
+
+def gather_blocks(block, beside):
+    blocks, computed = [block], None
     for masks in gather_stages(lax.axis_size("req")):
         held = blocks[0] if len(blocks) == 1 else jnp.concatenate(blocks, axis=0)
+        if len(blocks) > 1 and computed is None:
+            held, computed = lax.optimization_barrier((held, beside()))
         blocks = [held] + [swap_across(held, mask) for mask in masks]
-        ids = ids + [mask ^ i for mask in masks for i in ids]
-    return blocks, ids
+    return blocks, beside() if computed is None else computed
 
 
 def per_device(
@@ -476,22 +484,26 @@
     exponent = -2.0 * (np.arange(128) % (HD // 2)) / HD
     frequency = jnp.asarray((10000.0**exponent).astype(np.float32)[None, :])
     own_block = lax.axis_index("req").reshape(1)
-    blocks, block_ids = gather_blocks(packed)
     cache_types = [
         ((2, slots, CHUNK, local_width), BF16),
         ((2, cap - CHUNK, local_width), BF16),
     ]
-    pick, place, flag, *cache = call(
-        functools.partial(owner_kernel, share, head_count, block_ids),
-        [(ANY, packed), (HBM, slot_owner), (HBM, own_block), (HBM, kv_cache)],
-        [((slots, total), BF16), ((devices, slots), BF16), ((slots, tail * 2), BF16)]
-        + cache_types,
-        [
-            pltpu.SMEM((slots,), jnp.int32),
-            pltpu.SMEM((1,), jnp.int32),
-            pltpu.SemaphoreType.DMA((4,)),
-        ],
-    )
+    block_ids = gather_ids(lax.axis_size("req"))
+
+    def beside():
+        return call(
+            functools.partial(owner_kernel, share, head_count, block_ids),
+            [(ANY, packed), (HBM, slot_owner), (HBM, own_block), (HBM, kv_cache)],
+            [((slots, total), BF16), ((devices, slots), BF16), ((slots, tail * 2), BF16)]
+            + cache_types,
+            [
+                pltpu.SMEM((slots,), jnp.int32),
+                pltpu.SMEM((1,), jnp.int32),
+                pltpu.SemaphoreType.DMA((4,)),
+            ],
+        )
+
+    blocks, (pick, place, flag, *cache) = gather_blocks(packed, beside)
 
     scratch = [
         pltpu.VMEM((local_heads * slots, cap), F32),
@@ -530,18 +542,18 @@
             )
         parts = exchange(part)
         if not last:
+            cache = call(
+                functools.partial(cache_kernel, layer + 1),
+                [(ANY, part), (HBM, kv_cache)],
+                cache_types,
+                [pltpu.SemaphoreType.DMA((2,))],
+            )
             part, stream = call(
                 functools.partial(feed_forward_kernel, layer, len(parts)),
                 on_chip(*parts, stream, ffn_gain, gate_up_weight, down_weight),
                 [part_type, stream_type],
             )
             parts = exchange(part)
-            cache = call(
-                functools.partial(cache_kernel, layer + 1),
-                [(ANY, part), (HBM, kv_cache)],
-                cache_types,
-                [pltpu.SemaphoreType.DMA((2,))],
-            )
         else:
             (send,) = call(
                 functools.partial(last_feed_forward_kernel, layer, len(parts), head_count),

time: 43.4 us -> 43.4 us (level)
  no operation moved by 1% of the time
where the time goes in v9:
time: 43.4 us; the launch traced here: 43.1 us
  starting transfers between devices  13.1 us (30%)
  blocking collectives  10.6 us (24%)
  waiting for transfers between devices  9.94 us (23%)
  Pallas kernels  9.26 us (21%)
    all_to_all x1, blocking collectives, per_device(): lax.all_to_all(send, ('req', 'head'), 0, 0, axis_index_groups=[order], ti...  10.6 us
    pallas_call x7, Pallas kernels, call(): pl.pallas_call(kernel, out_shape=[pltpu.VMEM(shape, dtype) for shape, dty...  8.5 us
    ppermute x4, starting transfers between devices, swap_across(): return lax.ppermute(array, ('req', 'head'), pairs)  7.25 us
    ppermute x9, waiting for transfers between devices, swap(): return lax.ppermute(array, axis, [(i, i ^ mask) for i in range(count)])  6.21 us
    ppermute x9, starting transfers between devices, swap(): return lax.ppermute(array, axis, [(i, i ^ mask) for i in range(count)])  5.82 us
    ppermute x4, waiting for transfers between devices, swap_across(): return lax.ppermute(array, ('req', 'head'), pairs)  3.72 us
  transfers between devices with their start and end apart: 13, of which 7 were waited for; matrix products, arithmetic and copies ran while one was open for 0% of the time, Pallas kernels for 7%

profile of v9, /device:TPU:0, one launch (start us, length us, event | category | flops | bytes accessed | tf_op | source)
XLA Modules:
  0.0 43.1 jit_solution(14196216373582303254)
XLA Ops:
  0.0 0.8 %shard_map.145.after_ref = bf16[8,1152]{1,0:T(8,128)(2,1)S(1)} custom-call(bf16[8,1024]{1,0:T(8,128)(2,1)} %tokens_ref.1, s32[8]{0:T(128)} %lengths_ref.1, s32[8]{0:T(128)} %positions_ref.1, s32[8]{0:T(128)} %variates_ref.1), custom_call_target="tpu_custom_call" | custom-call | flops 99999997952 | tf_op jit(solution)/shard_map/pallas_call | solution.py:401
  0.8 0.0 copy-start.3
  0.8 0.0 copy-start.4
  0.8 0.0 copy-start.7
  0.8 2.5 %collective-permute-start = (bf16[8,1152]{1,0:T(8,128)(2,1)S(1)}, bf16[8,1152]{1,0:T(8,128)(2,1)S(1)}, u32[]{:S(2)}, u32[]{:S(2)}) collective-permute-start(bf16[8,1152]{1,0:T(8,128)(2,1)S(1)} %shard_map.145.after_ref), channel_id=1, source_target_pairs={{0,5},{1,4},{2,7},{3,6},{4,1},{5,0},{6,3},{7,2},{8,13},{9,12},{10,... | collective-permute-start | bytes 55304 | tf_op jit(solution)/shard_map/ppermute | solution.py:431
  3.3 1.5 %shard_map.146 = (bf16[8,64]{1,0:T(8,128)(2,1)S(1)}, bf16[32,8]{1,0:T(8,128)(2,1)S(1)}, bf16[8,256]{1,0:T(8,128)(2,1)S(1)}, bf16[2,8,128,256]{3,2,1,0:T(8,128)(2,1)S(1)}, bf16[2,384,256]{2,1,0:T(8,128)(2,1)S(1)}) custom-call(bf16[8,1152]{1,0:T(8,128)(2,1)S(1)} %shard_map.145.after_ref, s32[8]{0:T(128)} %owner_ref.1, s32[1]{0:T(128)} %bitcast.own_block_ref, ...), custom_call_target="tpu_custom_call" | custom-call | flops 1000000 | tf_op jit(solution)/shard_map/pallas_call | solution.py:401
  4.8 0.0 copy-start
  4.8 0.0 copy-start.5
  4.9 0.0 slice-start.1
  4.9 4.1 %collective-permute-start.3 = (bf16[16,1152]{1,0:T(8,128)(2,1)S(1)}, bf16[16,1152]{1,0:T(8,128)(2,1)S(1)}, u32[]{:S(2)}, u32[]{:S(2)}) collective-permute-start(bf16[16,1152]{1,0:T(8,128)(2,1)S(1)} %pad_maximum_fusion.refs_0_), channel_id=1, source_target_pairs={{0,25},{1,24},{2,27},{3,26},{4,29},{5,28},{6,31},{7,30},{8,17},{9,... | collective-permute-start | bytes 110600 | tf_op jit(solution)/shard_map/ppermute | solution.py:431
  9.0 0.7 %collective-permute-start.1 = (bf16[16,1152]{1,0:T(8,128)(2,1)S(1)}, bf16[16,1152]{1,0:T(8,128)(2,1)S(1)}, u32[]{:S(2)}, u32[]{:S(2)}) collective-permute-start(bf16[16,1152]{1,0:T(8,128)(2,1)S(1)} %pad_maximum_fusion.refs_0_), channel_id=1, source_target_pairs={{0,9},{1,8},{2,11},{3,10},{4,13},{5,12},{6,15},{7,14},{8,1},{9,0},... | collective-permute-start | bytes 110600 | tf_op jit(solution)/shard_map/ppermute | solution.py:431
  9.7 1.2 %collective-permute-done.3.refs_3_ = bf16[16,1152]{1,0:T(8,128)(2,1)S(1)} collective-permute-done((bf16[16,1152]{1,0:T(8,128)(2,1)S(1)}, bf16[16,1152]{1,0:T(8,128)(2,1)S(1)}, u32[]{:S(2)}, u32[]{:S(2)}) %collective-permute-start.3) | collective-permute-done | bytes 36896 | tf_op jit(solution)/shard_map/ppermute | solution.py:431
  10.9 2.5 %collective-permute-done.2.refs_2_ = bf16[16,1152]{1,0:T(8,128)(2,1)S(1)} collective-permute-done((bf16[16,1152]{1,0:T(8,128)(2,1)S(1)}, bf16[16,1152]{1,0:T(8,128)(2,1)S(1)}, u32[]{:S(2)}, u32[]{:S(2)}) %collective-permute-start.2) | collective-permute-done | bytes 36896 | tf_op jit(solution)/shard_map/ppermute | solution.py:431
  13.4 1.5 %shard_map.147 = (bf16[8,1024]{1,0:T(8,128)(2,1)S(1)}, f32[8,1024]{1,0:T(8,128)S(1)}, f32[8,128]{1,0:T(8,128)S(1)}, f32[8,256]{1,0:T(8,128)S(1)}) custom-call(bf16[16,1152]{1,0:T(8,128)(2,1)S(1)} %pad_maximum_fusion.refs_0_, bf16[16,1152]{1,0:T(8,128)(2,1)S(1)} %collective-permute-done.1.refs_1_, bf16[16,1152]{1,0:T(8,128)(2,1)S(1)} %collective-permute-done.2.refs_2_, ...), custom_call_target="tpu_custom_call" | custom-call | flops 1000000 | tf_op jit(solution)/shard_map/pallas_call | solution.py:401
  14.9 1.5 %collective-permute-start.6 = (bf16[8,1024]{1,0:T(8,128)(2,1)S(1)}, bf16[8,1024]{1,0:T(8,128)(2,1)S(1)}, u32[]{:S(2)}, u32[]{:S(2)}) collective-permute-start(bf16[8,1024]{1,0:T(8,128)(2,1)S(1)} %get-tuple-element.35.refs_0_.after_ref), channel_id=1, source_target_pairs={{0,3},{1,2},{2,1},{3,0},{4,7},{5,6},{6,5},{7,4},{8,11},{9,10},{10,... | collective-permute-start | bytes 49160 | tf_op jit(solution)/shard_map/ppermute | solution.py:414
  16.4 0.5 %collective-permute-start.5 = (bf16[8,1024]{1,0:T(8,128)(2,1)S(1)}, bf16[8,1024]{1,0:T(8,128)(2,1)S(1)}, u32[]{:S(2)}, u32[]{:S(2)}) collective-permute-start(bf16[8,1024]{1,0:T(8,128)(2,1)S(1)} %get-tuple-element.35.refs_0_.after_ref), channel_id=1, source_target_pairs={{0,2},{1,3},{2,0},{3,1},{4,6},{5,7},{6,4},{7,5},{8,10},{9,11},{10,... | collective-permute-start | bytes 49160 | tf_op jit(solution)/shard_map/ppermute | solution.py:414
  16.9 1.2 %collective-permute-done.6.refs_3_ = bf16[8,1024]{1,0:T(8,128)(2,1)S(1)} collective-permute-done((bf16[8,1024]{1,0:T(8,128)(2,1)S(1)}, bf16[8,1024]{1,0:T(8,128)(2,1)S(1)}, u32[]{:S(2)}, u32[]{:S(2)}) %collective-permute-start.6) | collective-permute-done | bytes 16416 | tf_op jit(solution)/shard_map/ppermute | solution.py:414
  18.1 2.0 %collective-permute-done.5.refs_2_ = bf16[8,1024]{1,0:T(8,128)(2,1)S(1)} collective-permute-done((bf16[8,1024]{1,0:T(8,128)(2,1)S(1)}, bf16[8,1024]{1,0:T(8,128)(2,1)S(1)}, u32[]{:S(2)}, u32[]{:S(2)}) %collective-permute-start.5) | collective-permute-done | bytes 16416 | tf_op jit(solution)/shard_map/ppermute | solution.py:414
  20.2 0.9 %shard_map.148 = (bf16[8,1024]{1,0:T(8,128)(2,1)S(1)}, f32[8,1024]{1,0:T(8,128)S(1)}) custom-call(bf16[8,1024]{1,0:T(8,128)(2,1)S(1)} %get-tuple-element.35.refs_0_.after_ref, bf16[8,1024]{1,0:T(8,128)(2,1)S(1)} %collective-permute-done.4.refs_1_, bf16[8,1024]{1,0:T(8,128)(2,1)S(1)} %collective-permute-done.5.refs_2_, ...), custom_call_target="tpu_custom_call" | custom-call | flops 1000000 | tf_op jit(solution)/shard_map/pallas_call | solution.py:401
  21.1 0.7 %collective-permute-start.8 = (bf16[8,1024]{1,0:T(8,128)(2,1)S(1)}, bf16[8,1024]{1,0:T(8,128)(2,1)S(1)}, u32[]{:S(2)}, u32[]{:S(2)}) collective-permute-start(bf16[8,1024]{1,0:T(8,128)(2,1)S(1)} %get-tuple-element.37.refs_0_), channel_id=1, source_target_pairs={{0,2},{1,3},{2,0},{3,1},{4,6},{5,7},{6,4},{7,5},{8,10},{9,11},{10,... | collective-permute-start | bytes 49160 | tf_op jit(solution)/shard_map/ppermute | solution.py:414
  21.8 1.2 %collective-permute-start.7 = (bf16[8,1024]{1,0:T(8,128)(2,1)S(1)}, bf16[8,1024]{1,0:T(8,128)(2,1)S(1)}, u32[]{:S(2)}, u32[]{:S(2)}) collective-permute-start(bf16[8,1024]{1,0:T(8,128)(2,1)S(1)} %get-tuple-element.37.refs_0_), channel_id=1, source_target_pairs={{0,1},{1,0},{2,3},{3,2},{4,5},{5,4},{6,7},{7,6},{8,9},{9,8},{10,11... | collective-permute-start | bytes 49160 | tf_op jit(solution)/shard_map/ppermute | solution.py:414
  23.0 1.3 %shard_map.149 = (bf16[2,8,128,256]{3,2,1,0:T(8,128)(2,1)S(1)}, bf16[2,384,256]{2,1,0:T(8,128)(2,1)S(1)}) custom-call(bf16[8,1024]{1,0:T(8,128)(2,1)S(1)} %get-tuple-element.35.refs_0_.after_ref, bf16[2,2,8,512,256]{4,3,2,1,0:T(8,128)(2,1)} %refs_10_.3), custom_call_target="tpu_custom_call" | custom-call | flops 1000000 | tf_op jit(solution)/shard_map/pallas_call | solution.py:401
  24.3 0.6 %collective-permute-done.8.refs_2_ = bf16[8,1024]{1,0:T(8,128)(2,1)S(1)} collective-permute-done((bf16[8,1024]{1,0:T(8,128)(2,1)S(1)}, bf16[8,1024]{1,0:T(8,128)(2,1)S(1)}, u32[]{:S(2)}, u32[]{:S(2)}) %collective-permute-start.8) | collective-permute-done | bytes 16416 | tf_op jit(solution)/shard_map/ppermute | solution.py:414
  24.9 1.4 %shard_map.150 = (bf16[8,1024]{1,0:T(8,128)(2,1)S(1)}, f32[8,1024]{1,0:T(8,128)S(1)}) custom-call(bf16[8,1024]{1,0:T(8,128)(2,1)S(1)} %get-tuple-element.37.refs_0_, bf16[8,1024]{1,0:T(8,128)(2,1)S(1)} %collective-permute-done.7.refs_1_, bf16[8,1024]{1,0:T(8,128)(2,1)S(1)} %collective-permute-done.8.refs_2_, ...), custom_call_target="tpu_custom_call" | custom-call | flops 1000000 | tf_op jit(solution)/shard_map/pallas_call | solution.py:401
  26.3 0.6 %collective-permute-start.12 = (bf16[8,1024]{1,0:T(8,128)(2,1)S(1)}, bf16[8,1024]{1,0:T(8,128)(2,1)S(1)}, u32[]{:S(2)}, u32[]{:S(2)}) collective-permute-start(bf16[8,1024]{1,0:T(8,128)(2,1)S(1)} %get-tuple-element.43.refs_0_), channel_id=1, source_target_pairs={{0,3},{1,2},{2,1},{3,0},{4,7},{5,6},{6,5},{7,4},{8,11},{9,10},{10,... | collective-permute-start | bytes 49160 | tf_op jit(solution)/shard_map/ppermute | solution.py:414
  26.9 0.6 %collective-permute-start.11 = (bf16[8,1024]{1,0:T(8,128)(2,1)S(1)}, bf16[8,1024]{1,0:T(8,128)(2,1)S(1)}, u32[]{:S(2)}, u32[]{:S(2)}) collective-permute-start(bf16[8,1024]{1,0:T(8,128)(2,1)S(1)} %get-tuple-element.43.refs_0_), channel_id=1, source_target_pairs={{0,2},{1,3},{2,0},{3,1},{4,6},{5,7},{6,4},{7,5},{8,10},{9,11},{10,... | collective-permute-start | bytes 49160 | tf_op jit(solution)/shard_map/ppermute | solution.py:414
  27.5 0.7 %collective-permute-start.10 = (bf16[8,1024]{1,0:T(8,128)(2,1)S(1)}, bf16[8,1024]{1,0:T(8,128)(2,1)S(1)}, u32[]{:S(2)}, u32[]{:S(2)}) collective-permute-start(bf16[8,1024]{1,0:T(8,128)(2,1)S(1)} %get-tuple-element.43.refs_0_), channel_id=1, source_target_pairs={{0,1},{1,0},{2,3},{3,2},{4,5},{5,4},{6,7},{7,6},{8,9},{9,8},{10,11... | collective-permute-start | bytes 49160 | tf_op jit(solution)/shard_map/ppermute | solution.py:414
  28.2 1.3 %collective-permute-done.12.refs_3_ = bf16[8,1024]{1,0:T(8,128)(2,1)S(1)} collective-permute-done((bf16[8,1024]{1,0:T(8,128)(2,1)S(1)}, bf16[8,1024]{1,0:T(8,128)(2,1)S(1)}, u32[]{:S(2)}, u32[]{:S(2)}) %collective-permute-start.12) | collective-permute-done | bytes 16416 | tf_op jit(solution)/shard_map/ppermute | solution.py:414
  29.6 1.1 %collective-permute-done.11.refs_2_ = bf16[8,1024]{1,0:T(8,128)(2,1)S(1)} collective-permute-done((bf16[8,1024]{1,0:T(8,128)(2,1)S(1)}, bf16[8,1024]{1,0:T(8,128)(2,1)S(1)}, u32[]{:S(2)}, u32[]{:S(2)}) %collective-permute-start.11) | collective-permute-done | bytes 16416 | tf_op jit(solution)/shard_map/ppermute | solution.py:414
  30.7 1.1 %shard_map.151 = bf16[32,2,640]{2,1,0:T(2,128)(2,1)S(1)} custom-call(bf16[8,1024]{1,0:T(8,128)(2,1)S(1)} %get-tuple-element.43.refs_0_, bf16[8,1024]{1,0:T(8,128)(2,1)S(1)} %collective-permute-done.10.refs_1_, bf16[8,1024]{1,0:T(8,128)(2,1)S(1)} %collective-permute-done.11.refs_2_, bf16[8,1024]{1,0:T(8,128)(2,1)S(1)} %collective-permute-done.12.refs_3_, ...), custom_call_target="tpu_custom_call" | custom-call | flops 1000000 | tf_op jit(solution)/shard_map/pallas_call | solution.py:401
  31.8 10.6 %all_to_all.5.received_ref = bf16[32,2,640]{2,1,0:T(2,128)(2,1)S(1)} all-to-all(bf16[32,2,640]{2,1,0:T(2,128)(2,1)S(1)} %shard_map.151), channel_id=1, replica_groups={{28,30,29,31,24,26,25,27,20,22,21,23,16,18,17,19,12,14,13,15,8,10,9,11,..., dimensions={0} | all-to-all | bytes 163840 | tf_op jit(solution)/shard_map/all_to_all | solution.py:568
  42.3 0.8 %shard_map.152 = bf16[2,1024]{1,0:T(2,128)(2,1)} custom-call(bf16[32,2,640]{2,1,0:T(2,128)(2,1)S(1)} %all_to_all.5.received_ref), custom_call_target="tpu_custom_call" | custom-call | tf_op jit(solution)/shard_map/pallas_call | solution.py:571
  (25 shorter events, 0.1 us)
Async XLA Ops:
  0.8 12.6 %copy-start.1 = (bf16[2,1024,768]{2,1,0:T(8,128)(2,1)S(1)}, bf16[2,1024,768]{2,1,0:T(8,128)(2,1)}, u32[]{:S(2)}) copy-start(bf16[2,1024,768]{2,1,0:T(8,128)(2,1)} %refs_12_.3) | copy-start | bytes 9437188
  0.8 12.6 %copy-start.3 = (s32[8,512]{1,0:T(8,128)S(1)}, s32[8,512]{1,0:T(8,128)}, u32[]{:S(2)}) copy-start(s32[8,512]{1,0:T(8,128)} %refs_7_.4) | copy-start | bytes 49156
  0.8 12.6 %copy-start.4 = (f32[2,1024]{1,0:T(2,128)S(1)}, f32[2,1024]{1,0:T(2,128)}, u32[]{:S(2)}) copy-start(f32[2,1024]{1,0:T(2,128)} %refs_11_.3) | copy-start | bytes 24580
  0.8 12.6 %copy-start.6 = (f32[2,2,4]{2,1,0:T(2,128)S(1)}, f32[2,2,4]{2,1,0:T(2,128)}, u32[]{:S(2)}) copy-start(f32[2,2,4]{2,1,0:T(2,128)} %refs_14_.1) | copy-start | bytes 196
  0.8 12.6 %copy-start.7 = (f32[1,128]{1,0:T(1,128)S(1)}, f32[1,128]{1,0:T(1,128)}, u32[]{:S(2)}) copy-start(f32[1,128]{1,0:T(1,128)} %constant.8.clone.refs_5_) | copy-start | bytes 1540
  0.8 4.0 %collective-permute-start = (bf16[8,1152]{1,0:T(8,128)(2,1)S(1)}, bf16[8,1152]{1,0:T(8,128)(2,1)S(1)}, u32[]{:S(2)}, u32[]{:S(2)}) collective-permute-start(bf16[8,1152]{1,0:T(8,128)(2,1)S(1)} %shard_map.145.after_ref), channel_id=1, source_target_pairs={{0,5},{1,4},{2,7},{3,6},{4,1},{5,0},{6,3},{7,2},{8,13},{9,12},{10,... | collective-permute-start | bytes 55304 | tf_op jit(solution)/shard_map/ppermute | solution.py:431
  3.3 10.1 %copy-start.2 = (bf16[2,256,1024]{2,1,0:T(8,128)(2,1)S(1)}, bf16[2,256,1024]{2,1,0:T(8,128)(2,1)}, u32[]{:S(2)}) copy-start(bf16[2,256,1024]{2,1,0:T(8,128)(2,1)} %refs_13_.3) | copy-start | bytes 3145732
  3.3 16.8 %slice-start = ((s8[8388608]{0:T(1024)(128)(4,1)}), s8[4194304]{0:T(1024)(128)(4,1)S(1)}, s32[]{:S(2)}) async-start(s8[8388608]{0:T(1024)(128)(4,1)} %bitcast.1), calls=%async_computation.1 | async-start | bytes 8388608
  4.8 15.3 %copy-start = (bf16[2,1024,1024]{2,1,0:T(8,128)(2,1)S(1)}, bf16[2,1024,1024]{2,1,0:T(8,128)(2,1)}, u32[]{:S(2)}) copy-start(bf16[2,1024,1024]{2,1,0:T(8,128)(2,1)} %refs_9_.3) | copy-start | bytes 12582916
  4.8 15.3 %copy-start.5 = (f32[2,1024]{1,0:T(2,128)S(1)}, f32[2,1024]{1,0:T(2,128)}, u32[]{:S(2)}) copy-start(f32[2,1024]{1,0:T(2,128)} %refs_7_.5) | copy-start | bytes 24580
  4.9 15.3 %slice-start.1 = ((s8[8388608]{0:T(1024)(128)(4,1)}), s8[4194304]{0:T(1024)(128)(4,1)S(1)}, s32[]{:S(2)}) async-start(s8[8388608]{0:T(1024)(128)(4,1)} %bitcast.1), calls=%async_computation.2 | async-start | bytes 8388608
  4.9 6.0 %collective-permute-start.3 = (bf16[16,1152]{1,0:T(8,128)(2,1)S(1)}, bf16[16,1152]{1,0:T(8,128)(2,1)S(1)}, u32[]{:S(2)}, u32[]{:S(2)}) collective-permute-start(bf16[16,1152]{1,0:T(8,128)(2,1)S(1)} %pad_maximum_fusion.refs_0_), channel_id=1, source_target_pairs={{0,25},{1,24},{2,27},{3,26},{4,29},{5,28},{6,31},{7,30},{8,17},{9,... | collective-permute-start | bytes 110600 | tf_op jit(solution)/shard_map/ppermute | solution.py:431
  9.0 4.4 %collective-permute-start.2 = (bf16[16,1152]{1,0:T(8,128)(2,1)S(1)}, bf16[16,1152]{1,0:T(8,128)(2,1)S(1)}, u32[]{:S(2)}, u32[]{:S(2)}) collective-permute-start(bf16[16,1152]{1,0:T(8,128)(2,1)S(1)} %pad_maximum_fusion.refs_0_), channel_id=1, source_target_pairs={{0,17},{1,16},{2,19},{3,18},{4,21},{5,20},{6,23},{7,22},{8,25},{9,... | collective-permute-start | bytes 110600 | tf_op jit(solution)/shard_map/ppermute | solution.py:431
  9.0 4.4 %collective-permute-start.1 = (bf16[16,1152]{1,0:T(8,128)(2,1)S(1)}, bf16[16,1152]{1,0:T(8,128)(2,1)S(1)}, u32[]{:S(2)}, u32[]{:S(2)}) collective-permute-start(bf16[16,1152]{1,0:T(8,128)(2,1)S(1)} %pad_maximum_fusion.refs_0_), channel_id=1, source_target_pairs={{0,9},{1,8},{2,11},{3,10},{4,13},{5,12},{6,15},{7,14},{8,1},{9,0},... | collective-permute-start | bytes 110600 | tf_op jit(solution)/shard_map/ppermute | solution.py:431
  14.9 3.2 %collective-permute-start.6 = (bf16[8,1024]{1,0:T(8,128)(2,1)S(1)}, bf16[8,1024]{1,0:T(8,128)(2,1)S(1)}, u32[]{:S(2)}, u32[]{:S(2)}) collective-permute-start(bf16[8,1024]{1,0:T(8,128)(2,1)S(1)} %get-tuple-element.35.refs_0_.after_ref), channel_id=1, source_target_pairs={{0,3},{1,2},{2,1},{3,0},{4,7},{5,6},{6,5},{7,4},{8,11},{9,10},{10,... | collective-permute-start | bytes 49160 | tf_op jit(solution)/shard_map/ppermute | solution.py:414
  16.4 3.7 %collective-permute-start.5 = (bf16[8,1024]{1,0:T(8,128)(2,1)S(1)}, bf16[8,1024]{1,0:T(8,128)(2,1)S(1)}, u32[]{:S(2)}, u32[]{:S(2)}) collective-permute-start(bf16[8,1024]{1,0:T(8,128)(2,1)S(1)} %get-tuple-element.35.refs_0_.after_ref), channel_id=1, source_target_pairs={{0,2},{1,3},{2,0},{3,1},{4,6},{5,7},{6,4},{7,5},{8,10},{9,11},{10,... | collective-permute-start | bytes 49160 | tf_op jit(solution)/shard_map/ppermute | solution.py:414
  16.9 3.2 %collective-permute-start.4 = (bf16[8,1024]{1,0:T(8,128)(2,1)S(1)}, bf16[8,1024]{1,0:T(8,128)(2,1)S(1)}, u32[]{:S(2)}, u32[]{:S(2)}) collective-permute-start(bf16[8,1024]{1,0:T(8,128)(2,1)S(1)} %get-tuple-element.35.refs_0_.after_ref), channel_id=1, source_target_pairs={{0,1},{1,0},{2,3},{3,2},{4,5},{5,4},{6,7},{7,6},{8,9},{9,8},{10,11... | collective-permute-start | bytes 49160 | tf_op jit(solution)/shard_map/ppermute | solution.py:414
  21.1 3.2 %collective-permute-start.9 = (bf16[8,1024]{1,0:T(8,128)(2,1)S(1)}, bf16[8,1024]{1,0:T(8,128)(2,1)S(1)}, u32[]{:S(2)}, u32[]{:S(2)}) collective-permute-start(bf16[8,1024]{1,0:T(8,128)(2,1)S(1)} %get-tuple-element.37.refs_0_), channel_id=1, source_target_pairs={{0,3},{1,2},{2,1},{3,0},{4,7},{5,6},{6,5},{7,4},{8,11},{9,10},{10,... | collective-permute-start | bytes 49160 | tf_op jit(solution)/shard_map/ppermute | solution.py:414
  21.1 3.8 %collective-permute-start.8 = (bf16[8,1024]{1,0:T(8,128)(2,1)S(1)}, bf16[8,1024]{1,0:T(8,128)(2,1)S(1)}, u32[]{:S(2)}, u32[]{:S(2)}) collective-permute-start(bf16[8,1024]{1,0:T(8,128)(2,1)S(1)} %get-tuple-element.37.refs_0_), channel_id=1, source_target_pairs={{0,2},{1,3},{2,0},{3,1},{4,6},{5,7},{6,4},{7,5},{8,10},{9,11},{10,... | collective-permute-start | bytes 49160 | tf_op jit(solution)/shard_map/ppermute | solution.py:414
  21.8 3.1 %collective-permute-start.7 = (bf16[8,1024]{1,0:T(8,128)(2,1)S(1)}, bf16[8,1024]{1,0:T(8,128)(2,1)S(1)}, u32[]{:S(2)}, u32[]{:S(2)}) collective-permute-start(bf16[8,1024]{1,0:T(8,128)(2,1)S(1)} %get-tuple-element.37.refs_0_), channel_id=1, source_target_pairs={{0,1},{1,0},{2,3},{3,2},{4,5},{5,4},{6,7},{7,6},{8,9},{9,8},{10,11... | collective-permute-start | bytes 49160 | tf_op jit(solution)/shard_map/ppermute | solution.py:414
  26.3 3.2 %collective-permute-start.12 = (bf16[8,1024]{1,0:T(8,128)(2,1)S(1)}, bf16[8,1024]{1,0:T(8,128)(2,1)S(1)}, u32[]{:S(2)}, u32[]{:S(2)}) collective-permute-start(bf16[8,1024]{1,0:T(8,128)(2,1)S(1)} %get-tuple-element.43.refs_0_), channel_id=1, source_target_pairs={{0,3},{1,2},{2,1},{3,0},{4,7},{5,6},{6,5},{7,4},{8,11},{9,10},{10,... | collective-permute-start | bytes 49160 | tf_op jit(solution)/shard_map/ppermute | solution.py:414
  26.9 3.7 %collective-permute-start.11 = (bf16[8,1024]{1,0:T(8,128)(2,1)S(1)}, bf16[8,1024]{1,0:T(8,128)(2,1)S(1)}, u32[]{:S(2)}, u32[]{:S(2)}) collective-permute-start(bf16[8,1024]{1,0:T(8,128)(2,1)S(1)} %get-tuple-element.43.refs_0_), channel_id=1, source_target_pairs={{0,2},{1,3},{2,0},{3,1},{4,6},{5,7},{6,4},{7,5},{8,10},{9,11},{10,... | collective-permute-start | bytes 49160 | tf_op jit(solution)/shard_map/ppermute | solution.py:414
  27.5 3.2 %collective-permute-start.10 = (bf16[8,1024]{1,0:T(8,128)(2,1)S(1)}, bf16[8,1024]{1,0:T(8,128)(2,1)S(1)}, u32[]{:S(2)}, u32[]{:S(2)}) collective-permute-start(bf16[8,1024]{1,0:T(8,128)(2,1)S(1)} %get-tuple-element.43.refs_0_), channel_id=1, source_target_pairs={{0,1},{1,0},{2,3},{3,2},{4,5},{5,4},{6,7},{7,6},{8,9},{9,8},{10,11... | collective-permute-start | bytes 49160 | tf_op jit(solution)/shard_map/ppermute | solution.py:414

commit v10 on v8

--- a/solution.py
+++ b/solution.py
@@ -78,7 +78,6 @@
     block_ids,
     after_ref,
     owner_ref,
-    own_block_ref,
     kv_ref,
     pick_ref,
     place_ref,
@@ -86,17 +85,13 @@
     front_ref,
     lead_ref,
     owner,
-    own_block,
     sems,
 ):
-    copies = [
-        pltpu.make_async_copy(owner_ref, owner, sems.at[0]),
-        pltpu.make_async_copy(own_block_ref, own_block, sems.at[1]),
-    ] + cache_copies(0, kv_ref, front_ref, lead_ref, sems, 2)
+    copies = [pltpu.make_async_copy(owner_ref, owner, sems.at[0])]
+    copies += cache_copies(0, kv_ref, front_ref, lead_ref, sems, 1)
     for copy in copies:
         copy.start()
     copies[0].wait()
-    copies[1].wait()
     slots, total = pick_ref.shape
     devices = place_ref.shape[0]
     row, column = iota((slots, total), 0), iota((slots, total), 1)
@@ -105,7 +100,7 @@
     mask = jnp.zeros((slots, total), jnp.int32)
     for k, block_id in enumerate(block_ids):
         mask = jnp.where(column // slots == k, block_id, mask)
-    request_at = (mask ^ own_block[0]) * slots + column % slots
+    request_at = (mask ^ lax.axis_index("req")) * slots + column % slots
     pick = jnp.zeros((slots, total), F32)
     place = jnp.zeros((devices, slots), F32)
     flag = jnp.zeros(flag_ref.shape, F32)
@@ -120,8 +115,8 @@
     pick_ref[...] = pick.astype(BF16)
     place_ref[...] = place.astype(BF16)
     flag_ref[...] = flag.astype(BF16)
+    copies[1].wait()
     copies[2].wait()
-    copies[3].wait()
 
 
 def cache_kernel(layer, after_ref, kv_ref, front_ref, lead_ref, sems):
@@ -382,14 +377,15 @@
     share, width = out_ref.shape
     half = width // 2
     tail = (received_ref.shape[2] - half) // 128
+    halves = [received_ref[:, i, :half].astype(F32) for i in range(2)]
+    placed = []
     for k in range(share):
         lanes = slice(half + k % tail * 128, half + (k % tail + 1) * 128)
         flags = received_ref[:, k // tail, lanes].astype(F32)
         mask = jnp.concatenate([flags] * (half // 128), axis=1)
-        for i in range(2):
-            rows = received_ref[:, i, :half].astype(F32)
-            row = jnp.sum(mask * rows, axis=0, keepdims=True)
-            out_ref[k : k + 1, i * half : (i + 1) * half] = row.astype(BF16)
+        sums = [jnp.sum(mask * rows, axis=0, keepdims=True) for rows in halves]
+        placed.append(jnp.concatenate(sums, axis=1))
+    out_ref[...] = jnp.concatenate(placed, axis=0).astype(BF16)
 
 
 def call(kernel, operands, outs, scratch=(), cost=SHORT):
@@ -475,7 +471,6 @@
     )
     exponent = -2.0 * (np.arange(128) % (HD // 2)) / HD
     frequency = jnp.asarray((10000.0**exponent).astype(np.float32)[None, :])
-    own_block = lax.axis_index("req").reshape(1)
     blocks, block_ids = gather_blocks(packed)
     cache_types = [
         ((2, slots, CHUNK, local_width), BF16),
@@ -483,13 +478,12 @@
     ]
     pick, place, flag, *cache = call(
         functools.partial(owner_kernel, share, head_count, block_ids),
-        [(ANY, packed), (HBM, slot_owner), (HBM, own_block), (HBM, kv_cache)],
+        [(ANY, packed), (HBM, slot_owner), (HBM, kv_cache)],
         [((slots, total), BF16), ((devices, slots), BF16), ((slots, tail * 2), BF16)]
         + cache_types,
         [
             pltpu.SMEM((slots,), jnp.int32),
-            pltpu.SMEM((1,), jnp.int32),
-            pltpu.SemaphoreType.DMA((4,)),
+            pltpu.SemaphoreType.DMA((3,)),
         ],
     )
 

time: 43.4 us -> 43.4 us (level)
  no operation moved by 1% of the time
where the time goes in v10:
time: 43.4 us; the launch traced here: 43.1 us
  starting transfers between devices  13.1 us (30%)
  blocking collectives  10.5 us (24%)
  waiting for transfers between devices  9.89 us (23%)
  Pallas kernels  9.26 us (21%)
    all_to_all x1, blocking collectives, per_device(): lax.all_to_all(send, ('req', 'head'), 0, 0, axis_index_groups=[order], ti...  10.5 us
    pallas_call x7, Pallas kernels, call(): pl.pallas_call(kernel, out_shape=[pltpu.VMEM(shape, dtype) for shape, dty...  8.5 us
    ppermute x4, starting transfers between devices, swap_across(): return lax.ppermute(array, ('req', 'head'), pairs)  7.33 us
    ppermute x9, waiting for transfers between devices, swap(): return lax.ppermute(array, axis, [(i, i ^ mask) for i in range(count)])  6.22 us
    ppermute x9, starting transfers between devices, swap(): return lax.ppermute(array, axis, [(i, i ^ mask) for i in range(count)])  5.81 us
    ppermute x4, waiting for transfers between devices, swap_across(): return lax.ppermute(array, ('req', 'head'), pairs)  3.68 us
  transfers between devices with their start and end apart: 13, of which 7 were waited for; matrix products, arithmetic and copies ran while one was open for 0% of the time, Pallas kernels for 7%

profile of v10, /device:TPU:0, one launch (start us, length us, event | category | flops | bytes accessed | tf_op | source)
XLA Modules:
  0.0 43.1 jit_solution(8441644245446165288)
XLA Ops:
  0.0 0.8 %shard_map.145.after_ref = bf16[8,1152]{1,0:T(8,128)(2,1)S(1)} custom-call(bf16[8,1024]{1,0:T(8,128)(2,1)} %tokens_ref.1, s32[8]{0:T(128)} %lengths_ref.1, s32[8]{0:T(128)} %positions_ref.1, s32[8]{0:T(128)} %variates_ref.1), custom_call_target="tpu_custom_call" | custom-call | flops 99999997952 | tf_op jit(solution)/shard_map/pallas_call | solution.py:397
  0.8 0.0 copy-start.1
  0.8 0.0 copy-start.2
  0.8 0.0 copy-start.3
  0.8 0.0 copy-start.4
  0.8 0.0 copy-start.7
  0.9 2.5 %collective-permute-start = (bf16[8,1152]{1,0:T(8,128)(2,1)S(1)}, bf16[8,1152]{1,0:T(8,128)(2,1)S(1)}, u32[]{:S(2)}, u32[]{:S(2)}) collective-permute-start(bf16[8,1152]{1,0:T(8,128)(2,1)S(1)} %shard_map.145.after_ref), channel_id=1, source_target_pairs={{0,5},{1,4},{2,7},{3,6},{4,1},{5,0},{6,3},{7,2},{8,13},{9,12},{10,... | collective-permute-start | bytes 55304 | tf_op jit(solution)/shard_map/ppermute | solution.py:427
  3.3 1.5 %collective-permute-done = bf16[8,1152]{1,0:T(8,128)(2,1)S(1)} collective-permute-done((bf16[8,1152]{1,0:T(8,128)(2,1)S(1)}, bf16[8,1152]{1,0:T(8,128)(2,1)S(1)}, u32[]{:S(2)}, u32[]{:S(2)}) %collective-permute-start) | collective-permute-done | bytes 18464 | tf_op jit(solution)/shard_map/ppermute | solution.py:427
  4.8 4.2 %collective-permute-start.3 = (bf16[16,1152]{1,0:T(8,128)(2,1)S(1)}, bf16[16,1152]{1,0:T(8,128)(2,1)S(1)}, u32[]{:S(2)}, u32[]{:S(2)}) collective-permute-start(bf16[16,1152]{1,0:T(8,128)(2,1)S(1)} %pad_maximum_fusion.refs_0_), channel_id=1, source_target_pairs={{0,25},{1,24},{2,27},{3,26},{4,29},{5,28},{6,31},{7,30},{8,17},{9,... | collective-permute-start | bytes 110600 | tf_op jit(solution)/shard_map/ppermute | solution.py:427
  9.0 0.7 %collective-permute-start.1 = (bf16[16,1152]{1,0:T(8,128)(2,1)S(1)}, bf16[16,1152]{1,0:T(8,128)(2,1)S(1)}, u32[]{:S(2)}, u32[]{:S(2)}) collective-permute-start(bf16[16,1152]{1,0:T(8,128)(2,1)S(1)} %pad_maximum_fusion.refs_0_), channel_id=1, source_target_pairs={{0,9},{1,8},{2,11},{3,10},{4,13},{5,12},{6,15},{7,14},{8,1},{9,0},... | collective-permute-start | bytes 110600 | tf_op jit(solution)/shard_map/ppermute | solution.py:427
  9.7 1.5 %shard_map.146 = (bf16[8,64]{1,0:T(8,128)(2,1)S(1)}, bf16[32,8]{1,0:T(8,128)(2,1)S(1)}, bf16[8,256]{1,0:T(8,128)(2,1)S(1)}, bf16[2,8,128,256]{3,2,1,0:T(8,128)(2,1)S(1)}, bf16[2,384,256]{2,1,0:T(8,128)(2,1)S(1)}) custom-call(bf16[8,1152]{1,0:T(8,128)(2,1)S(1)} %shard_map.145.after_ref, s32[8]{0:T(128)} %owner_ref.1, bf16[2,2,8,512,256]{4,3,2,1,0:T(8,128)(2,1)} %refs_10_.3), custom_call_target="tpu_custom_call" | custom-call | flops 1000000 | tf_op jit(solution)/shard_map/pallas_call | solution.py:397
  11.2 2.2 %collective-permute-done.2.refs_2_ = bf16[16,1152]{1,0:T(8,128)(2,1)S(1)} collective-permute-done((bf16[16,1152]{1,0:T(8,128)(2,1)S(1)}, bf16[16,1152]{1,0:T(8,128)(2,1)S(1)}, u32[]{:S(2)}, u32[]{:S(2)}) %collective-permute-start.2) | collective-permute-done | bytes 36896 | tf_op jit(solution)/shard_map/ppermute | solution.py:427
  13.4 0.0 slice-start.1
  13.5 1.5 %shard_map.147 = (bf16[8,1024]{1,0:T(8,128)(2,1)S(1)}, f32[8,1024]{1,0:T(8,128)S(1)}, f32[8,128]{1,0:T(8,128)S(1)}, f32[8,256]{1,0:T(8,128)S(1)}) custom-call(bf16[16,1152]{1,0:T(8,128)(2,1)S(1)} %pad_maximum_fusion.refs_0_, bf16[16,1152]{1,0:T(8,128)(2,1)S(1)} %collective-permute-done.1.refs_1_, bf16[16,1152]{1,0:T(8,128)(2,1)S(1)} %collective-permute-done.2.refs_2_, ...), custom_call_target="tpu_custom_call" | custom-call | flops 1000000 | tf_op jit(solution)/shard_map/pallas_call | solution.py:397
  14.9 1.5 %collective-permute-start.6 = (bf16[8,1024]{1,0:T(8,128)(2,1)S(1)}, bf16[8,1024]{1,0:T(8,128)(2,1)S(1)}, u32[]{:S(2)}, u32[]{:S(2)}) collective-permute-start(bf16[8,1024]{1,0:T(8,128)(2,1)S(1)} %get-tuple-element.23.refs_0_), channel_id=1, source_target_pairs={{0,3},{1,2},{2,1},{3,0},{4,7},{5,6},{6,5},{7,4},{8,11},{9,10},{10,... | collective-permute-start | bytes 49160 | tf_op jit(solution)/shard_map/ppermute | solution.py:410
  16.4 0.5 %collective-permute-start.5 = (bf16[8,1024]{1,0:T(8,128)(2,1)S(1)}, bf16[8,1024]{1,0:T(8,128)(2,1)S(1)}, u32[]{:S(2)}, u32[]{:S(2)}) collective-permute-start(bf16[8,1024]{1,0:T(8,128)(2,1)S(1)} %get-tuple-element.23.refs_0_), channel_id=1, source_target_pairs={{0,2},{1,3},{2,0},{3,1},{4,6},{5,7},{6,4},{7,5},{8,10},{9,11},{10,... | collective-permute-start | bytes 49160 | tf_op jit(solution)/shard_map/ppermute | solution.py:410
  17.0 1.2 %collective-permute-done.6.refs_3_ = bf16[8,1024]{1,0:T(8,128)(2,1)S(1)} collective-permute-done((bf16[8,1024]{1,0:T(8,128)(2,1)S(1)}, bf16[8,1024]{1,0:T(8,128)(2,1)S(1)}, u32[]{:S(2)}, u32[]{:S(2)}) %collective-permute-start.6) | collective-permute-done | bytes 16416 | tf_op jit(solution)/shard_map/ppermute | solution.py:410
  18.2 2.0 %collective-permute-done.5.refs_2_ = bf16[8,1024]{1,0:T(8,128)(2,1)S(1)} collective-permute-done((bf16[8,1024]{1,0:T(8,128)(2,1)S(1)}, bf16[8,1024]{1,0:T(8,128)(2,1)S(1)}, u32[]{:S(2)}, u32[]{:S(2)}) %collective-permute-start.5) | collective-permute-done | bytes 16416 | tf_op jit(solution)/shard_map/ppermute | solution.py:410
  20.2 0.9 %shard_map.148 = (bf16[8,1024]{1,0:T(8,128)(2,1)S(1)}, f32[8,1024]{1,0:T(8,128)S(1)}) custom-call(bf16[8,1024]{1,0:T(8,128)(2,1)S(1)} %get-tuple-element.23.refs_0_, bf16[8,1024]{1,0:T(8,128)(2,1)S(1)} %collective-permute-done.4.refs_1_, bf16[8,1024]{1,0:T(8,128)(2,1)S(1)} %collective-permute-done.5.refs_2_, ...), custom_call_target="tpu_custom_call" | custom-call | flops 1000000 | tf_op jit(solution)/shard_map/pallas_call | solution.py:397
  21.1 0.7 %collective-permute-start.8 = (bf16[8,1024]{1,0:T(8,128)(2,1)S(1)}, bf16[8,1024]{1,0:T(8,128)(2,1)S(1)}, u32[]{:S(2)}, u32[]{:S(2)}) collective-permute-start(bf16[8,1024]{1,0:T(8,128)(2,1)S(1)} %get-tuple-element.25.after_ref.refs_0_), channel_id=1, source_target_pairs={{0,2},{1,3},{2,0},{3,1},{4,6},{5,7},{6,4},{7,5},{8,10},{9,11},{10,... | collective-permute-start | bytes 49160 | tf_op jit(solution)/shard_map/ppermute | solution.py:410
  21.8 1.2 %collective-permute-start.7 = (bf16[8,1024]{1,0:T(8,128)(2,1)S(1)}, bf16[8,1024]{1,0:T(8,128)(2,1)S(1)}, u32[]{:S(2)}, u32[]{:S(2)}) collective-permute-start(bf16[8,1024]{1,0:T(8,128)(2,1)S(1)} %get-tuple-element.25.after_ref.refs_0_), channel_id=1, source_target_pairs={{0,1},{1,0},{2,3},{3,2},{4,5},{5,4},{6,7},{7,6},{8,9},{9,8},{10,11... | collective-permute-start | bytes 49160 | tf_op jit(solution)/shard_map/ppermute | solution.py:410
  23.0 1.3 %shard_map.149 = (bf16[2,8,128,256]{3,2,1,0:T(8,128)(2,1)S(1)}, bf16[2,384,256]{2,1,0:T(8,128)(2,1)S(1)}) custom-call(bf16[8,1024]{1,0:T(8,128)(2,1)S(1)} %get-tuple-element.25.after_ref.refs_0_, bf16[2,2,8,512,256]{4,3,2,1,0:T(8,128)(2,1)} %refs_10_.3), custom_call_target="tpu_custom_call" | custom-call | flops 1000000 | tf_op jit(solution)/shard_map/pallas_call | solution.py:397
  24.4 0.6 %collective-permute-done.8.refs_2_ = bf16[8,1024]{1,0:T(8,128)(2,1)S(1)} collective-permute-done((bf16[8,1024]{1,0:T(8,128)(2,1)S(1)}, bf16[8,1024]{1,0:T(8,128)(2,1)S(1)}, u32[]{:S(2)}, u32[]{:S(2)}) %collective-permute-start.8) | collective-permute-done | bytes 16416 | tf_op jit(solution)/shard_map/ppermute | solution.py:410
  24.9 1.4 %shard_map.150 = (bf16[8,1024]{1,0:T(8,128)(2,1)S(1)}, f32[8,1024]{1,0:T(8,128)S(1)}) custom-call(bf16[8,1024]{1,0:T(8,128)(2,1)S(1)} %get-tuple-element.25.after_ref.refs_0_, bf16[8,1024]{1,0:T(8,128)(2,1)S(1)} %collective-permute-done.7.refs_1_, bf16[8,1024]{1,0:T(8,128)(2,1)S(1)} %collective-permute-done.8.refs_2_, ...), custom_call_target="tpu_custom_call" | custom-call | flops 1000000 | tf_op jit(solution)/shard_map/pallas_call | solution.py:397
  26.3 0.6 %collective-permute-start.12 = (bf16[8,1024]{1,0:T(8,128)(2,1)S(1)}, bf16[8,1024]{1,0:T(8,128)(2,1)S(1)}, u32[]{:S(2)}, u32[]{:S(2)}) collective-permute-start(bf16[8,1024]{1,0:T(8,128)(2,1)S(1)} %get-tuple-element.31.refs_0_), channel_id=1, source_target_pairs={{0,3},{1,2},{2,1},{3,0},{4,7},{5,6},{6,5},{7,4},{8,11},{9,10},{10,... | collective-permute-start | bytes 49160 | tf_op jit(solution)/shard_map/ppermute | solution.py:410
  27.0 0.6 %collective-permute-start.11 = (bf16[8,1024]{1,0:T(8,128)(2,1)S(1)}, bf16[8,1024]{1,0:T(8,128)(2,1)S(1)}, u32[]{:S(2)}, u32[]{:S(2)}) collective-permute-start(bf16[8,1024]{1,0:T(8,128)(2,1)S(1)} %get-tuple-element.31.refs_0_), channel_id=1, source_target_pairs={{0,2},{1,3},{2,0},{3,1},{4,6},{5,7},{6,4},{7,5},{8,10},{9,11},{10,... | collective-permute-start | bytes 49160 | tf_op jit(solution)/shard_map/ppermute | solution.py:410
  27.5 0.7 %collective-permute-start.10 = (bf16[8,1024]{1,0:T(8,128)(2,1)S(1)}, bf16[8,1024]{1,0:T(8,128)(2,1)S(1)}, u32[]{:S(2)}, u32[]{:S(2)}) collective-permute-start(bf16[8,1024]{1,0:T(8,128)(2,1)S(1)} %get-tuple-element.31.refs_0_), channel_id=1, source_target_pairs={{0,1},{1,0},{2,3},{3,2},{4,5},{5,4},{6,7},{7,6},{8,9},{9,8},{10,11... | collective-permute-start | bytes 49160 | tf_op jit(solution)/shard_map/ppermute | solution.py:410
  28.3 1.3 %collective-permute-done.12.refs_3_ = bf16[8,1024]{1,0:T(8,128)(2,1)S(1)} collective-permute-done((bf16[8,1024]{1,0:T(8,128)(2,1)S(1)}, bf16[8,1024]{1,0:T(8,128)(2,1)S(1)}, u32[]{:S(2)}, u32[]{:S(2)}) %collective-permute-start.12) | collective-permute-done | bytes 16416 | tf_op jit(solution)/shard_map/ppermute | solution.py:410
  29.6 1.1 %collective-permute-done.11.refs_2_ = bf16[8,1024]{1,0:T(8,128)(2,1)S(1)} collective-permute-done((bf16[8,1024]{1,0:T(8,128)(2,1)S(1)}, bf16[8,1024]{1,0:T(8,128)(2,1)S(1)}, u32[]{:S(2)}, u32[]{:S(2)}) %collective-permute-start.11) | collective-permute-done | bytes 16416 | tf_op jit(solution)/shard_map/ppermute | solution.py:410
  30.7 1.1 %shard_map.151 = bf16[32,2,640]{2,1,0:T(2,128)(2,1)S(1)} custom-call(bf16[8,1024]{1,0:T(8,128)(2,1)S(1)} %get-tuple-element.31.refs_0_, bf16[8,1024]{1,0:T(8,128)(2,1)S(1)} %collective-permute-done.10.refs_1_, bf16[8,1024]{1,0:T(8,128)(2,1)S(1)} %collective-permute-done.11.refs_2_, bf16[8,1024]{1,0:T(8,128)(2,1)S(1)} %collective-permute-done.12.refs_3_, ...), custom_call_target="tpu_custom_call" | custom-call | flops 1000000 | tf_op jit(solution)/shard_map/pallas_call | solution.py:397
  31.8 10.5 %all_to_all.5.received_ref = bf16[32,2,640]{2,1,0:T(2,128)(2,1)S(1)} all-to-all(bf16[32,2,640]{2,1,0:T(2,128)(2,1)S(1)} %shard_map.151), channel_id=1, replica_groups={{28,30,29,31,24,26,25,27,20,22,21,23,16,18,17,19,12,14,13,15,8,10,9,11,..., dimensions={0} | all-to-all | bytes 163840 | tf_op jit(solution)/shard_map/all_to_all | solution.py:550
  42.4 0.8 %shard_map.152 = bf16[2,1024]{1,0:T(2,128)(2,1)} custom-call(bf16[32,2,640]{2,1,0:T(2,128)(2,1)S(1)} %all_to_all.5.received_ref), custom_call_target="tpu_custom_call" | custom-call | tf_op jit(solution)/shard_map/pallas_call | solution.py:553
  (25 shorter events, 0.1 us)
Async XLA Ops:
  0.8 12.6 %copy-start.1 = (bf16[2,1024,768]{2,1,0:T(8,128)(2,1)S(1)}, bf16[2,1024,768]{2,1,0:T(8,128)(2,1)}, u32[]{:S(2)}) copy-start(bf16[2,1024,768]{2,1,0:T(8,128)(2,1)} %refs_12_.3) | copy-start | bytes 9437188
  0.8 12.6 %copy-start.2 = (bf16[2,256,1024]{2,1,0:T(8,128)(2,1)S(1)}, bf16[2,256,1024]{2,1,0:T(8,128)(2,1)}, u32[]{:S(2)}) copy-start(bf16[2,256,1024]{2,1,0:T(8,128)(2,1)} %refs_13_.3) | copy-start | bytes 3145732
  0.8 12.6 %copy-start.3 = (s32[8,512]{1,0:T(8,128)S(1)}, s32[8,512]{1,0:T(8,128)}, u32[]{:S(2)}) copy-start(s32[8,512]{1,0:T(8,128)} %refs_7_.4) | copy-start | bytes 49156
  0.8 12.6 %copy-start.4 = (f32[2,1024]{1,0:T(2,128)S(1)}, f32[2,1024]{1,0:T(2,128)}, u32[]{:S(2)}) copy-start(f32[2,1024]{1,0:T(2,128)} %refs_11_.3) | copy-start | bytes 24580
  0.8 12.6 %copy-start.6 = (f32[2,2,4]{2,1,0:T(2,128)S(1)}, f32[2,2,4]{2,1,0:T(2,128)}, u32[]{:S(2)}) copy-start(f32[2,2,4]{2,1,0:T(2,128)} %refs_14_.1) | copy-start | bytes 196
  0.8 12.6 %copy-start.7 = (f32[1,128]{1,0:T(1,128)S(1)}, f32[1,128]{1,0:T(1,128)}, u32[]{:S(2)}) copy-start(f32[1,128]{1,0:T(1,128)} %constant.2.clone.refs_5_) | copy-start | bytes 1540
  0.9 3.9 %collective-permute-start = (bf16[8,1152]{1,0:T(8,128)(2,1)S(1)}, bf16[8,1152]{1,0:T(8,128)(2,1)S(1)}, u32[]{:S(2)}, u32[]{:S(2)}) collective-permute-start(bf16[8,1152]{1,0:T(8,128)(2,1)S(1)} %shard_map.145.after_ref), channel_id=1, source_target_pairs={{0,5},{1,4},{2,7},{3,6},{4,1},{5,0},{6,3},{7,2},{8,13},{9,12},{10,... | collective-permute-start | bytes 55304 | tf_op jit(solution)/shard_map/ppermute | solution.py:427
  4.8 6.4 %collective-permute-start.3 = (bf16[16,1152]{1,0:T(8,128)(2,1)S(1)}, bf16[16,1152]{1,0:T(8,128)(2,1)S(1)}, u32[]{:S(2)}, u32[]{:S(2)}) collective-permute-start(bf16[16,1152]{1,0:T(8,128)(2,1)S(1)} %pad_maximum_fusion.refs_0_), channel_id=1, source_target_pairs={{0,25},{1,24},{2,27},{3,26},{4,29},{5,28},{6,31},{7,30},{8,17},{9,... | collective-permute-start | bytes 110600 | tf_op jit(solution)/shard_map/ppermute | solution.py:427
  9.0 4.4 %collective-permute-start.2 = (bf16[16,1152]{1,0:T(8,128)(2,1)S(1)}, bf16[16,1152]{1,0:T(8,128)(2,1)S(1)}, u32[]{:S(2)}, u32[]{:S(2)}) collective-permute-start(bf16[16,1152]{1,0:T(8,128)(2,1)S(1)} %pad_maximum_fusion.refs_0_), channel_id=1, source_target_pairs={{0,17},{1,16},{2,19},{3,18},{4,21},{5,20},{6,23},{7,22},{8,25},{9,... | collective-permute-start | bytes 110600 | tf_op jit(solution)/shard_map/ppermute | solution.py:427
  9.0 4.4 %collective-permute-start.1 = (bf16[16,1152]{1,0:T(8,128)(2,1)S(1)}, bf16[16,1152]{1,0:T(8,128)(2,1)S(1)}, u32[]{:S(2)}, u32[]{:S(2)}) collective-permute-start(bf16[16,1152]{1,0:T(8,128)(2,1)S(1)} %pad_maximum_fusion.refs_0_), channel_id=1, source_target_pairs={{0,9},{1,8},{2,11},{3,10},{4,13},{5,12},{6,15},{7,14},{8,1},{9,0},... | collective-permute-start | bytes 110600 | tf_op jit(solution)/shard_map/ppermute | solution.py:427
  9.7 10.5 %slice-start = ((s8[8388608]{0:T(1024)(128)(4,1)}), s8[4194304]{0:T(1024)(128)(4,1)S(1)}, s32[]{:S(2)}) async-start(s8[8388608]{0:T(1024)(128)(4,1)} %bitcast), calls=%async_computation.1 | async-start | bytes 8388608
  11.2 9.0 %copy-start = (bf16[2,1024,1024]{2,1,0:T(8,128)(2,1)S(1)}, bf16[2,1024,1024]{2,1,0:T(8,128)(2,1)}, u32[]{:S(2)}) copy-start(bf16[2,1024,1024]{2,1,0:T(8,128)(2,1)} %refs_9_.3) | copy-start | bytes 12582916
  11.2 9.0 %copy-start.5 = (f32[2,1024]{1,0:T(2,128)S(1)}, f32[2,1024]{1,0:T(2,128)}, u32[]{:S(2)}) copy-start(f32[2,1024]{1,0:T(2,128)} %refs_7_.5) | copy-start | bytes 24580
  13.4 6.7 %slice-start.1 = ((s8[8388608]{0:T(1024)(128)(4,1)}), s8[4194304]{0:T(1024)(128)(4,1)S(1)}, s32[]{:S(2)}) async-start(s8[8388608]{0:T(1024)(128)(4,1)} %bitcast), calls=%async_computation.2 | async-start | bytes 8388608
  14.9 3.2 %collective-permute-start.6 = (bf16[8,1024]{1,0:T(8,128)(2,1)S(1)}, bf16[8,1024]{1,0:T(8,128)(2,1)S(1)}, u32[]{:S(2)}, u32[]{:S(2)}) collective-permute-start(bf16[8,1024]{1,0:T(8,128)(2,1)S(1)} %get-tuple-element.23.refs_0_), channel_id=1, source_target_pairs={{0,3},{1,2},{2,1},{3,0},{4,7},{5,6},{6,5},{7,4},{8,11},{9,10},{10,... | collective-permute-start | bytes 49160 | tf_op jit(solution)/shard_map/ppermute | solution.py:410
  16.4 3.7 %collective-permute-start.5 = (bf16[8,1024]{1,0:T(8,128)(2,1)S(1)}, bf16[8,1024]{1,0:T(8,128)(2,1)S(1)}, u32[]{:S(2)}, u32[]{:S(2)}) collective-permute-start(bf16[8,1024]{1,0:T(8,128)(2,1)S(1)} %get-tuple-element.23.refs_0_), channel_id=1, source_target_pairs={{0,2},{1,3},{2,0},{3,1},{4,6},{5,7},{6,4},{7,5},{8,10},{9,11},{10,... | collective-permute-start | bytes 49160 | tf_op jit(solution)/shard_map/ppermute | solution.py:410
  17.0 3.2 %collective-permute-start.4 = (bf16[8,1024]{1,0:T(8,128)(2,1)S(1)}, bf16[8,1024]{1,0:T(8,128)(2,1)S(1)}, u32[]{:S(2)}, u32[]{:S(2)}) collective-permute-start(bf16[8,1024]{1,0:T(8,128)(2,1)S(1)} %get-tuple-element.23.refs_0_), channel_id=1, source_target_pairs={{0,1},{1,0},{2,3},{3,2},{4,5},{5,4},{6,7},{7,6},{8,9},{9,8},{10,11... | collective-permute-start | bytes 49160 | tf_op jit(solution)/shard_map/ppermute | solution.py:410
  21.1 3.2 %collective-permute-start.9 = (bf16[8,1024]{1,0:T(8,128)(2,1)S(1)}, bf16[8,1024]{1,0:T(8,128)(2,1)S(1)}, u32[]{:S(2)}, u32[]{:S(2)}) collective-permute-start(bf16[8,1024]{1,0:T(8,128)(2,1)S(1)} %get-tuple-element.25.after_ref.refs_0_), channel_id=1, source_target_pairs={{0,3},{1,2},{2,1},{3,0},{4,7},{5,6},{6,5},{7,4},{8,11},{9,10},{10,... | collective-permute-start | bytes 49160 | tf_op jit(solution)/shard_map/ppermute | solution.py:410
  21.1 3.8 %collective-permute-start.8 = (bf16[8,1024]{1,0:T(8,128)(2,1)S(1)}, bf16[8,1024]{1,0:T(8,128)(2,1)S(1)}, u32[]{:S(2)}, u32[]{:S(2)}) collective-permute-start(bf16[8,1024]{1,0:T(8,128)(2,1)S(1)} %get-tuple-element.25.after_ref.refs_0_), channel_id=1, source_target_pairs={{0,2},{1,3},{2,0},{3,1},{4,6},{5,7},{6,4},{7,5},{8,10},{9,11},{10,... | collective-permute-start | bytes 49160 | tf_op jit(solution)/shard_map/ppermute | solution.py:410
  21.8 3.1 %collective-permute-start.7 = (bf16[8,1024]{1,0:T(8,128)(2,1)S(1)}, bf16[8,1024]{1,0:T(8,128)(2,1)S(1)}, u32[]{:S(2)}, u32[]{:S(2)}) collective-permute-start(bf16[8,1024]{1,0:T(8,128)(2,1)S(1)} %get-tuple-element.25.after_ref.refs_0_), channel_id=1, source_target_pairs={{0,1},{1,0},{2,3},{3,2},{4,5},{5,4},{6,7},{7,6},{8,9},{9,8},{10,11... | collective-permute-start | bytes 49160 | tf_op jit(solution)/shard_map/ppermute | solution.py:410
  26.3 3.2 %collective-permute-start.12 = (bf16[8,1024]{1,0:T(8,128)(2,1)S(1)}, bf16[8,1024]{1,0:T(8,128)(2,1)S(1)}, u32[]{:S(2)}, u32[]{:S(2)}) collective-permute-start(bf16[8,1024]{1,0:T(8,128)(2,1)S(1)} %get-tuple-element.31.refs_0_), channel_id=1, source_target_pairs={{0,3},{1,2},{2,1},{3,0},{4,7},{5,6},{6,5},{7,4},{8,11},{9,10},{10,... | collective-permute-start | bytes 49160 | tf_op jit(solution)/shard_map/ppermute | solution.py:410
  27.0 3.7 %collective-permute-start.11 = (bf16[8,1024]{1,0:T(8,128)(2,1)S(1)}, bf16[8,1024]{1,0:T(8,128)(2,1)S(1)}, u32[]{:S(2)}, u32[]{:S(2)}) collective-permute-start(bf16[8,1024]{1,0:T(8,128)(2,1)S(1)} %get-tuple-element.31.refs_0_), channel_id=1, source_target_pairs={{0,2},{1,3},{2,0},{3,1},{4,6},{5,7},{6,4},{7,5},{8,10},{9,11},{10,... | collective-permute-start | bytes 49160 | tf_op jit(solution)/shard_map/ppermute | solution.py:410
  27.5 3.2 %collective-permute-start.10 = (bf16[8,1024]{1,0:T(8,128)(2,1)S(1)}, bf16[8,1024]{1,0:T(8,128)(2,1)S(1)}, u32[]{:S(2)}, u32[]{:S(2)}) collective-permute-start(bf16[8,1024]{1,0:T(8,128)(2,1)S(1)} %get-tuple-element.31.refs_0_), channel_id=1, source_target_pairs={{0,1},{1,0},{2,3},{3,2},{4,5},{5,4},{6,7},{7,6},{8,9},{9,8},{10,11... | collective-permute-start | bytes 49160 | tf_op jit(solution)/shard_map/ppermute | solution.py:410

commit v11 on v10

--- a/solution.py
+++ b/solution.py
@@ -524,18 +524,18 @@
             )
         parts = exchange(part)
         if not last:
-            part, stream = call(
-                functools.partial(feed_forward_kernel, layer, len(parts)),
-                on_chip(*parts, stream, ffn_gain, gate_up_weight, down_weight),
-                [part_type, stream_type],
-            )
-            parts = exchange(part)
             cache = call(
                 functools.partial(cache_kernel, layer + 1),
                 [(ANY, part), (HBM, kv_cache)],
                 cache_types,
                 [pltpu.SemaphoreType.DMA((2,))],
             )
+            part, stream = call(
+                functools.partial(feed_forward_kernel, layer, len(parts)),
+                on_chip(*parts, stream, ffn_gain, gate_up_weight, down_weight),
+                [part_type, stream_type],
+            )
+            parts = exchange(part)
         else:
             (send,) = call(
                 functools.partial(last_feed_forward_kernel, layer, len(parts), head_count),

time: 43.4 us -> 43.4 us (level)
  no operation moved by 1% of the time
where the time goes in v11:
time: 43.4 us; the launch traced here: 43.1 us
  starting transfers between devices  13.1 us (30%)
  blocking collectives  10.6 us (24%)
  waiting for transfers between devices  9.89 us (23%)
  Pallas kernels  9.26 us (21%)
    all_to_all x1, blocking collectives, per_device(): lax.all_to_all(send, ('req', 'head'), 0, 0, axis_index_groups=[order], ti...  10.6 us
    pallas_call x7, Pallas kernels, call(): pl.pallas_call(kernel, out_shape=[pltpu.VMEM(shape, dtype) for shape, dty...  8.5 us
    ppermute x4, starting transfers between devices, swap_across(): return lax.ppermute(array, ('req', 'head'), pairs)  7.33 us
    ppermute x9, waiting for transfers between devices, swap(): return lax.ppermute(array, axis, [(i, i ^ mask) for i in range(count)])  6.21 us
    ppermute x9, starting transfers between devices, swap(): return lax.ppermute(array, axis, [(i, i ^ mask) for i in range(count)])  5.81 us
    ppermute x4, waiting for transfers between devices, swap_across(): return lax.ppermute(array, ('req', 'head'), pairs)  3.68 us
  transfers between devices with their start and end apart: 13, of which 7 were waited for; matrix products, arithmetic and copies ran while one was open for 0% of the time, Pallas kernels for 7%

profile of v11, /device:TPU:0, one launch (start us, length us, event | category | flops | bytes accessed | tf_op | source)
XLA Modules:
  0.0 43.1 jit_solution(5661353410411535037)
XLA Ops:
  0.0 0.8 %shard_map.145.after_ref = bf16[8,1152]{1,0:T(8,128)(2,1)S(1)} custom-call(bf16[8,1024]{1,0:T(8,128)(2,1)} %tokens_ref.1, s32[8]{0:T(128)} %lengths_ref.1, s32[8]{0:T(128)} %positions_ref.1, s32[8]{0:T(128)} %variates_ref.1), custom_call_target="tpu_custom_call" | custom-call | flops 99999997952 | tf_op jit(solution)/shard_map/pallas_call | solution.py:397
  0.8 0.0 copy-start.1
  0.8 0.0 copy-start.2
  0.8 0.0 copy-start.3
  0.8 0.0 copy-start.4
  0.8 0.0 copy-start.7
  0.9 2.5 %collective-permute-start = (bf16[8,1152]{1,0:T(8,128)(2,1)S(1)}, bf16[8,1152]{1,0:T(8,128)(2,1)S(1)}, u32[]{:S(2)}, u32[]{:S(2)}) collective-permute-start(bf16[8,1152]{1,0:T(8,128)(2,1)S(1)} %shard_map.145.after_ref), channel_id=1, source_target_pairs={{0,5},{1,4},{2,7},{3,6},{4,1},{5,0},{6,3},{7,2},{8,13},{9,12},{10,... | collective-permute-start | bytes 55304 | tf_op jit(solution)/shard_map/ppermute | solution.py:427
  3.3 1.5 %collective-permute-done = bf16[8,1152]{1,0:T(8,128)(2,1)S(1)} collective-permute-done((bf16[8,1152]{1,0:T(8,128)(2,1)S(1)}, bf16[8,1152]{1,0:T(8,128)(2,1)S(1)}, u32[]{:S(2)}, u32[]{:S(2)}) %collective-permute-start) | collective-permute-done | bytes 18464 | tf_op jit(solution)/shard_map/ppermute | solution.py:427
  4.8 4.2 %collective-permute-start.3 = (bf16[16,1152]{1,0:T(8,128)(2,1)S(1)}, bf16[16,1152]{1,0:T(8,128)(2,1)S(1)}, u32[]{:S(2)}, u32[]{:S(2)}) collective-permute-start(bf16[16,1152]{1,0:T(8,128)(2,1)S(1)} %pad_maximum_fusion.refs_0_), channel_id=1, source_target_pairs={{0,25},{1,24},{2,27},{3,26},{4,29},{5,28},{6,31},{7,30},{8,17},{9,... | collective-permute-start | bytes 110600 | tf_op jit(solution)/shard_map/ppermute | solution.py:427
  9.0 0.7 %collective-permute-start.1 = (bf16[16,1152]{1,0:T(8,128)(2,1)S(1)}, bf16[16,1152]{1,0:T(8,128)(2,1)S(1)}, u32[]{:S(2)}, u32[]{:S(2)}) collective-permute-start(bf16[16,1152]{1,0:T(8,128)(2,1)S(1)} %pad_maximum_fusion.refs_0_), channel_id=1, source_target_pairs={{0,9},{1,8},{2,11},{3,10},{4,13},{5,12},{6,15},{7,14},{8,1},{9,0},... | collective-permute-start | bytes 110600 | tf_op jit(solution)/shard_map/ppermute | solution.py:427
  9.7 1.5 %shard_map.146 = (bf16[8,64]{1,0:T(8,128)(2,1)S(1)}, bf16[32,8]{1,0:T(8,128)(2,1)S(1)}, bf16[8,256]{1,0:T(8,128)(2,1)S(1)}, bf16[2,8,128,256]{3,2,1,0:T(8,128)(2,1)S(1)}, bf16[2,384,256]{2,1,0:T(8,128)(2,1)S(1)}) custom-call(bf16[8,1152]{1,0:T(8,128)(2,1)S(1)} %shard_map.145.after_ref, s32[8]{0:T(128)} %owner_ref.1, bf16[2,2,8,512,256]{4,3,2,1,0:T(8,128)(2,1)} %refs_10_.3), custom_call_target="tpu_custom_call" | custom-call | flops 1000000 | tf_op jit(solution)/shard_map/pallas_call | solution.py:397
  11.2 2.2 %collective-permute-done.2.refs_2_ = bf16[16,1152]{1,0:T(8,128)(2,1)S(1)} collective-permute-done((bf16[16,1152]{1,0:T(8,128)(2,1)S(1)}, bf16[16,1152]{1,0:T(8,128)(2,1)S(1)}, u32[]{:S(2)}, u32[]{:S(2)}) %collective-permute-start.2) | collective-permute-done | bytes 36896 | tf_op jit(solution)/shard_map/ppermute | solution.py:427
  13.4 0.0 slice-start.1
  13.5 1.5 %shard_map.147 = (bf16[8,1024]{1,0:T(8,128)(2,1)S(1)}, f32[8,1024]{1,0:T(8,128)S(1)}, f32[8,128]{1,0:T(8,128)S(1)}, f32[8,256]{1,0:T(8,128)S(1)}) custom-call(bf16[16,1152]{1,0:T(8,128)(2,1)S(1)} %pad_maximum_fusion.refs_0_, bf16[16,1152]{1,0:T(8,128)(2,1)S(1)} %collective-permute-done.1.refs_1_, bf16[16,1152]{1,0:T(8,128)(2,1)S(1)} %collective-permute-done.2.refs_2_, ...), custom_call_target="tpu_custom_call" | custom-call | flops 1000000 | tf_op jit(solution)/shard_map/pallas_call | solution.py:397
  14.9 1.5 %collective-permute-start.6 = (bf16[8,1024]{1,0:T(8,128)(2,1)S(1)}, bf16[8,1024]{1,0:T(8,128)(2,1)S(1)}, u32[]{:S(2)}, u32[]{:S(2)}) collective-permute-start(bf16[8,1024]{1,0:T(8,128)(2,1)S(1)} %get-tuple-element.23.refs_0_.after_ref), channel_id=1, source_target_pairs={{0,3},{1,2},{2,1},{3,0},{4,7},{5,6},{6,5},{7,4},{8,11},{9,10},{10,... | collective-permute-start | bytes 49160 | tf_op jit(solution)/shard_map/ppermute | solution.py:410
  16.4 0.5 %collective-permute-start.5 = (bf16[8,1024]{1,0:T(8,128)(2,1)S(1)}, bf16[8,1024]{1,0:T(8,128)(2,1)S(1)}, u32[]{:S(2)}, u32[]{:S(2)}) collective-permute-start(bf16[8,1024]{1,0:T(8,128)(2,1)S(1)} %get-tuple-element.23.refs_0_.after_ref), channel_id=1, source_target_pairs={{0,2},{1,3},{2,0},{3,1},{4,6},{5,7},{6,4},{7,5},{8,10},{9,11},{10,... | collective-permute-start | bytes 49160 | tf_op jit(solution)/shard_map/ppermute | solution.py:410
  17.0 1.2 %collective-permute-done.6.refs_3_ = bf16[8,1024]{1,0:T(8,128)(2,1)S(1)} collective-permute-done((bf16[8,1024]{1,0:T(8,128)(2,1)S(1)}, bf16[8,1024]{1,0:T(8,128)(2,1)S(1)}, u32[]{:S(2)}, u32[]{:S(2)}) %collective-permute-start.6) | collective-permute-done | bytes 16416 | tf_op jit(solution)/shard_map/ppermute | solution.py:410
  18.2 2.0 %collective-permute-done.5.refs_2_ = bf16[8,1024]{1,0:T(8,128)(2,1)S(1)} collective-permute-done((bf16[8,1024]{1,0:T(8,128)(2,1)S(1)}, bf16[8,1024]{1,0:T(8,128)(2,1)S(1)}, u32[]{:S(2)}, u32[]{:S(2)}) %collective-permute-start.5) | collective-permute-done | bytes 16416 | tf_op jit(solution)/shard_map/ppermute | solution.py:410
  20.2 0.9 %shard_map.148 = (bf16[8,1024]{1,0:T(8,128)(2,1)S(1)}, f32[8,1024]{1,0:T(8,128)S(1)}) custom-call(bf16[8,1024]{1,0:T(8,128)(2,1)S(1)} %get-tuple-element.23.refs_0_.after_ref, bf16[8,1024]{1,0:T(8,128)(2,1)S(1)} %collective-permute-done.4.refs_1_, bf16[8,1024]{1,0:T(8,128)(2,1)S(1)} %collective-permute-done.5.refs_2_, ...), custom_call_target="tpu_custom_call" | custom-call | flops 1000000 | tf_op jit(solution)/shard_map/pallas_call | solution.py:397
  21.1 0.7 %collective-permute-start.8 = (bf16[8,1024]{1,0:T(8,128)(2,1)S(1)}, bf16[8,1024]{1,0:T(8,128)(2,1)S(1)}, u32[]{:S(2)}, u32[]{:S(2)}) collective-permute-start(bf16[8,1024]{1,0:T(8,128)(2,1)S(1)} %get-tuple-element.25.refs_0_), channel_id=1, source_target_pairs={{0,2},{1,3},{2,0},{3,1},{4,6},{5,7},{6,4},{7,5},{8,10},{9,11},{10,... | collective-permute-start | bytes 49160 | tf_op jit(solution)/shard_map/ppermute | solution.py:410
  21.8 1.2 %collective-permute-start.7 = (bf16[8,1024]{1,0:T(8,128)(2,1)S(1)}, bf16[8,1024]{1,0:T(8,128)(2,1)S(1)}, u32[]{:S(2)}, u32[]{:S(2)}) collective-permute-start(bf16[8,1024]{1,0:T(8,128)(2,1)S(1)} %get-tuple-element.25.refs_0_), channel_id=1, source_target_pairs={{0,1},{1,0},{2,3},{3,2},{4,5},{5,4},{6,7},{7,6},{8,9},{9,8},{10,11... | collective-permute-start | bytes 49160 | tf_op jit(solution)/shard_map/ppermute | solution.py:410
  23.0 1.3 %shard_map.149 = (bf16[2,8,128,256]{3,2,1,0:T(8,128)(2,1)S(1)}, bf16[2,384,256]{2,1,0:T(8,128)(2,1)S(1)}) custom-call(bf16[8,1024]{1,0:T(8,128)(2,1)S(1)} %get-tuple-element.23.refs_0_.after_ref, bf16[2,2,8,512,256]{4,3,2,1,0:T(8,128)(2,1)} %refs_10_.3), custom_call_target="tpu_custom_call" | custom-call | flops 1000000 | tf_op jit(solution)/shard_map/pallas_call | solution.py:397
  24.4 0.6 %collective-permute-done.8.refs_2_ = bf16[8,1024]{1,0:T(8,128)(2,1)S(1)} collective-permute-done((bf16[8,1024]{1,0:T(8,128)(2,1)S(1)}, bf16[8,1024]{1,0:T(8,128)(2,1)S(1)}, u32[]{:S(2)}, u32[]{:S(2)}) %collective-permute-start.8) | collective-permute-done | bytes 16416 | tf_op jit(solution)/shard_map/ppermute | solution.py:410
  24.9 1.4 %shard_map.150 = (bf16[8,1024]{1,0:T(8,128)(2,1)S(1)}, f32[8,1024]{1,0:T(8,128)S(1)}) custom-call(bf16[8,1024]{1,0:T(8,128)(2,1)S(1)} %get-tuple-element.25.refs_0_, bf16[8,1024]{1,0:T(8,128)(2,1)S(1)} %collective-permute-done.7.refs_1_, bf16[8,1024]{1,0:T(8,128)(2,1)S(1)} %collective-permute-done.8.refs_2_, ...), custom_call_target="tpu_custom_call" | custom-call | flops 1000000 | tf_op jit(solution)/shard_map/pallas_call | solution.py:397
  26.3 0.6 %collective-permute-start.12 = (bf16[8,1024]{1,0:T(8,128)(2,1)S(1)}, bf16[8,1024]{1,0:T(8,128)(2,1)S(1)}, u32[]{:S(2)}, u32[]{:S(2)}) collective-permute-start(bf16[8,1024]{1,0:T(8,128)(2,1)S(1)} %get-tuple-element.31.refs_0_), channel_id=1, source_target_pairs={{0,3},{1,2},{2,1},{3,0},{4,7},{5,6},{6,5},{7,4},{8,11},{9,10},{10,... | collective-permute-start | bytes 49160 | tf_op jit(solution)/shard_map/ppermute | solution.py:410
  27.0 0.6 %collective-permute-start.11 = (bf16[8,1024]{1,0:T(8,128)(2,1)S(1)}, bf16[8,1024]{1,0:T(8,128)(2,1)S(1)}, u32[]{:S(2)}, u32[]{:S(2)}) collective-permute-start(bf16[8,1024]{1,0:T(8,128)(2,1)S(1)} %get-tuple-element.31.refs_0_), channel_id=1, source_target_pairs={{0,2},{1,3},{2,0},{3,1},{4,6},{5,7},{6,4},{7,5},{8,10},{9,11},{10,... | collective-permute-start | bytes 49160 | tf_op jit(solution)/shard_map/ppermute | solution.py:410
  27.5 0.7 %collective-permute-start.10 = (bf16[8,1024]{1,0:T(8,128)(2,1)S(1)}, bf16[8,1024]{1,0:T(8,128)(2,1)S(1)}, u32[]{:S(2)}, u32[]{:S(2)}) collective-permute-start(bf16[8,1024]{1,0:T(8,128)(2,1)S(1)} %get-tuple-element.31.refs_0_), channel_id=1, source_target_pairs={{0,1},{1,0},{2,3},{3,2},{4,5},{5,4},{6,7},{7,6},{8,9},{9,8},{10,11... | collective-permute-start | bytes 49160 | tf_op jit(solution)/shard_map/ppermute | solution.py:410
  28.3 1.3 %collective-permute-done.12.refs_3_ = bf16[8,1024]{1,0:T(8,128)(2,1)S(1)} collective-permute-done((bf16[8,1024]{1,0:T(8,128)(2,1)S(1)}, bf16[8,1024]{1,0:T(8,128)(2,1)S(1)}, u32[]{:S(2)}, u32[]{:S(2)}) %collective-permute-start.12) | collective-permute-done | bytes 16416 | tf_op jit(solution)/shard_map/ppermute | solution.py:410
  29.6 1.1 %collective-permute-done.11.refs_2_ = bf16[8,1024]{1,0:T(8,128)(2,1)S(1)} collective-permute-done((bf16[8,1024]{1,0:T(8,128)(2,1)S(1)}, bf16[8,1024]{1,0:T(8,128)(2,1)S(1)}, u32[]{:S(2)}, u32[]{:S(2)}) %collective-permute-start.11) | collective-permute-done | bytes 16416 | tf_op jit(solution)/shard_map/ppermute | solution.py:410
  30.7 1.1 %shard_map.151 = bf16[32,2,640]{2,1,0:T(2,128)(2,1)S(1)} custom-call(bf16[8,1024]{1,0:T(8,128)(2,1)S(1)} %get-tuple-element.31.refs_0_, bf16[8,1024]{1,0:T(8,128)(2,1)S(1)} %collective-permute-done.10.refs_1_, bf16[8,1024]{1,0:T(8,128)(2,1)S(1)} %collective-permute-done.11.refs_2_, bf16[8,1024]{1,0:T(8,128)(2,1)S(1)} %collective-permute-done.12.refs_3_, ...), custom_call_target="tpu_custom_call" | custom-call | flops 1000000 | tf_op jit(solution)/shard_map/pallas_call | solution.py:397
  31.8 10.6 %all_to_all.5.received_ref = bf16[32,2,640]{2,1,0:T(2,128)(2,1)S(1)} all-to-all(bf16[32,2,640]{2,1,0:T(2,128)(2,1)S(1)} %shard_map.151), channel_id=1, replica_groups={{28,30,29,31,24,26,25,27,20,22,21,23,16,18,17,19,12,14,13,15,8,10,9,11,..., dimensions={0} | all-to-all | bytes 163840 | tf_op jit(solution)/shard_map/all_to_all | solution.py:550
  42.4 0.8 %shard_map.152 = bf16[2,1024]{1,0:T(2,128)(2,1)} custom-call(bf16[32,2,640]{2,1,0:T(2,128)(2,1)S(1)} %all_to_all.5.received_ref), custom_call_target="tpu_custom_call" | custom-call | tf_op jit(solution)/shard_map/pallas_call | solution.py:553
  (25 shorter events, 0.1 us)
Async XLA Ops:
  0.8 12.6 %copy-start.1 = (bf16[2,1024,768]{2,1,0:T(8,128)(2,1)S(1)}, bf16[2,1024,768]{2,1,0:T(8,128)(2,1)}, u32[]{:S(2)}) copy-start(bf16[2,1024,768]{2,1,0:T(8,128)(2,1)} %refs_12_.3) | copy-start | bytes 9437188
  0.8 12.6 %copy-start.2 = (bf16[2,256,1024]{2,1,0:T(8,128)(2,1)S(1)}, bf16[2,256,1024]{2,1,0:T(8,128)(2,1)}, u32[]{:S(2)}) copy-start(bf16[2,256,1024]{2,1,0:T(8,128)(2,1)} %refs_13_.3) | copy-start | bytes 3145732
  0.8 12.6 %copy-start.3 = (s32[8,512]{1,0:T(8,128)S(1)}, s32[8,512]{1,0:T(8,128)}, u32[]{:S(2)}) copy-start(s32[8,512]{1,0:T(8,128)} %refs_7_.4) | copy-start | bytes 49156
  0.8 12.6 %copy-start.4 = (f32[2,1024]{1,0:T(2,128)S(1)}, f32[2,1024]{1,0:T(2,128)}, u32[]{:S(2)}) copy-start(f32[2,1024]{1,0:T(2,128)} %refs_11_.3) | copy-start | bytes 24580
  0.8 12.6 %copy-start.6 = (f32[2,2,4]{2,1,0:T(2,128)S(1)}, f32[2,2,4]{2,1,0:T(2,128)}, u32[]{:S(2)}) copy-start(f32[2,2,4]{2,1,0:T(2,128)} %refs_14_.1) | copy-start | bytes 196
  0.8 12.6 %copy-start.7 = (f32[1,128]{1,0:T(1,128)S(1)}, f32[1,128]{1,0:T(1,128)}, u32[]{:S(2)}) copy-start(f32[1,128]{1,0:T(1,128)} %constant.2.clone.refs_5_) | copy-start | bytes 1540
  0.9 3.9 %collective-permute-start = (bf16[8,1152]{1,0:T(8,128)(2,1)S(1)}, bf16[8,1152]{1,0:T(8,128)(2,1)S(1)}, u32[]{:S(2)}, u32[]{:S(2)}) collective-permute-start(bf16[8,1152]{1,0:T(8,128)(2,1)S(1)} %shard_map.145.after_ref), channel_id=1, source_target_pairs={{0,5},{1,4},{2,7},{3,6},{4,1},{5,0},{6,3},{7,2},{8,13},{9,12},{10,... | collective-permute-start | bytes 55304 | tf_op jit(solution)/shard_map/ppermute | solution.py:427
  4.8 6.4 %collective-permute-start.3 = (bf16[16,1152]{1,0:T(8,128)(2,1)S(1)}, bf16[16,1152]{1,0:T(8,128)(2,1)S(1)}, u32[]{:S(2)}, u32[]{:S(2)}) collective-permute-start(bf16[16,1152]{1,0:T(8,128)(2,1)S(1)} %pad_maximum_fusion.refs_0_), channel_id=1, source_target_pairs={{0,25},{1,24},{2,27},{3,26},{4,29},{5,28},{6,31},{7,30},{8,17},{9,... | collective-permute-start | bytes 110600 | tf_op jit(solution)/shard_map/ppermute | solution.py:427
  9.0 4.4 %collective-permute-start.2 = (bf16[16,1152]{1,0:T(8,128)(2,1)S(1)}, bf16[16,1152]{1,0:T(8,128)(2,1)S(1)}, u32[]{:S(2)}, u32[]{:S(2)}) collective-permute-start(bf16[16,1152]{1,0:T(8,128)(2,1)S(1)} %pad_maximum_fusion.refs_0_), channel_id=1, source_target_pairs={{0,17},{1,16},{2,19},{3,18},{4,21},{5,20},{6,23},{7,22},{8,25},{9,... | collective-permute-start | bytes 110600 | tf_op jit(solution)/shard_map/ppermute | solution.py:427
  9.0 4.4 %collective-permute-start.1 = (bf16[16,1152]{1,0:T(8,128)(2,1)S(1)}, bf16[16,1152]{1,0:T(8,128)(2,1)S(1)}, u32[]{:S(2)}, u32[]{:S(2)}) collective-permute-start(bf16[16,1152]{1,0:T(8,128)(2,1)S(1)} %pad_maximum_fusion.refs_0_), channel_id=1, source_target_pairs={{0,9},{1,8},{2,11},{3,10},{4,13},{5,12},{6,15},{7,14},{8,1},{9,0},... | collective-permute-start | bytes 110600 | tf_op jit(solution)/shard_map/ppermute | solution.py:427
  9.7 10.5 %slice-start = ((s8[8388608]{0:T(1024)(128)(4,1)}), s8[4194304]{0:T(1024)(128)(4,1)S(1)}, s32[]{:S(2)}) async-start(s8[8388608]{0:T(1024)(128)(4,1)} %bitcast), calls=%async_computation.1 | async-start | bytes 8388608
  11.2 9.0 %copy-start = (bf16[2,1024,1024]{2,1,0:T(8,128)(2,1)S(1)}, bf16[2,1024,1024]{2,1,0:T(8,128)(2,1)}, u32[]{:S(2)}) copy-start(bf16[2,1024,1024]{2,1,0:T(8,128)(2,1)} %refs_9_.3) | copy-start | bytes 12582916
  11.2 9.0 %copy-start.5 = (f32[2,1024]{1,0:T(2,128)S(1)}, f32[2,1024]{1,0:T(2,128)}, u32[]{:S(2)}) copy-start(f32[2,1024]{1,0:T(2,128)} %refs_7_.5) | copy-start | bytes 24580
  13.4 6.7 %slice-start.1 = ((s8[8388608]{0:T(1024)(128)(4,1)}), s8[4194304]{0:T(1024)(128)(4,1)S(1)}, s32[]{:S(2)}) async-start(s8[8388608]{0:T(1024)(128)(4,1)} %bitcast), calls=%async_computation.2 | async-start | bytes 8388608
  14.9 3.2 %collective-permute-start.6 = (bf16[8,1024]{1,0:T(8,128)(2,1)S(1)}, bf16[8,1024]{1,0:T(8,128)(2,1)S(1)}, u32[]{:S(2)}, u32[]{:S(2)}) collective-permute-start(bf16[8,1024]{1,0:T(8,128)(2,1)S(1)} %get-tuple-element.23.refs_0_.after_ref), channel_id=1, source_target_pairs={{0,3},{1,2},{2,1},{3,0},{4,7},{5,6},{6,5},{7,4},{8,11},{9,10},{10,... | collective-permute-start | bytes 49160 | tf_op jit(solution)/shard_map/ppermute | solution.py:410
  16.4 3.7 %collective-permute-start.5 = (bf16[8,1024]{1,0:T(8,128)(2,1)S(1)}, bf16[8,1024]{1,0:T(8,128)(2,1)S(1)}, u32[]{:S(2)}, u32[]{:S(2)}) collective-permute-start(bf16[8,1024]{1,0:T(8,128)(2,1)S(1)} %get-tuple-element.23.refs_0_.after_ref), channel_id=1, source_target_pairs={{0,2},{1,3},{2,0},{3,1},{4,6},{5,7},{6,4},{7,5},{8,10},{9,11},{10,... | collective-permute-start | bytes 49160 | tf_op jit(solution)/shard_map/ppermute | solution.py:410
  17.0 3.2 %collective-permute-start.4 = (bf16[8,1024]{1,0:T(8,128)(2,1)S(1)}, bf16[8,1024]{1,0:T(8,128)(2,1)S(1)}, u32[]{:S(2)}, u32[]{:S(2)}) collective-permute-start(bf16[8,1024]{1,0:T(8,128)(2,1)S(1)} %get-tuple-element.23.refs_0_.after_ref), channel_id=1, source_target_pairs={{0,1},{1,0},{2,3},{3,2},{4,5},{5,4},{6,7},{7,6},{8,9},{9,8},{10,11... | collective-permute-start | bytes 49160 | tf_op jit(solution)/shard_map/ppermute | solution.py:410
  21.1 3.2 %collective-permute-start.9 = (bf16[8,1024]{1,0:T(8,128)(2,1)S(1)}, bf16[8,1024]{1,0:T(8,128)(2,1)S(1)}, u32[]{:S(2)}, u32[]{:S(2)}) collective-permute-start(bf16[8,1024]{1,0:T(8,128)(2,1)S(1)} %get-tuple-element.25.refs_0_), channel_id=1, source_target_pairs={{0,3},{1,2},{2,1},{3,0},{4,7},{5,6},{6,5},{7,4},{8,11},{9,10},{10,... | collective-permute-start | bytes 49160 | tf_op jit(solution)/shard_map/ppermute | solution.py:410
  21.1 3.8 %collective-permute-start.8 = (bf16[8,1024]{1,0:T(8,128)(2,1)S(1)}, bf16[8,1024]{1,0:T(8,128)(2,1)S(1)}, u32[]{:S(2)}, u32[]{:S(2)}) collective-permute-start(bf16[8,1024]{1,0:T(8,128)(2,1)S(1)} %get-tuple-element.25.refs_0_), channel_id=1, source_target_pairs={{0,2},{1,3},{2,0},{3,1},{4,6},{5,7},{6,4},{7,5},{8,10},{9,11},{10,... | collective-permute-start | bytes 49160 | tf_op jit(solution)/shard_map/ppermute | solution.py:410
  21.8 3.1 %collective-permute-start.7 = (bf16[8,1024]{1,0:T(8,128)(2,1)S(1)}, bf16[8,1024]{1,0:T(8,128)(2,1)S(1)}, u32[]{:S(2)}, u32[]{:S(2)}) collective-permute-start(bf16[8,1024]{1,0:T(8,128)(2,1)S(1)} %get-tuple-element.25.refs_0_), channel_id=1, source_target_pairs={{0,1},{1,0},{2,3},{3,2},{4,5},{5,4},{6,7},{7,6},{8,9},{9,8},{10,11... | collective-permute-start | bytes 49160 | tf_op jit(solution)/shard_map/ppermute | solution.py:410
  26.3 3.2 %collective-permute-start.12 = (bf16[8,1024]{1,0:T(8,128)(2,1)S(1)}, bf16[8,1024]{1,0:T(8,128)(2,1)S(1)}, u32[]{:S(2)}, u32[]{:S(2)}) collective-permute-start(bf16[8,1024]{1,0:T(8,128)(2,1)S(1)} %get-tuple-element.31.refs_0_), channel_id=1, source_target_pairs={{0,3},{1,2},{2,1},{3,0},{4,7},{5,6},{6,5},{7,4},{8,11},{9,10},{10,... | collective-permute-start | bytes 49160 | tf_op jit(solution)/shard_map/ppermute | solution.py:410
  27.0 3.7 %collective-permute-start.11 = (bf16[8,1024]{1,0:T(8,128)(2,1)S(1)}, bf16[8,1024]{1,0:T(8,128)(2,1)S(1)}, u32[]{:S(2)}, u32[]{:S(2)}) collective-permute-start(bf16[8,1024]{1,0:T(8,128)(2,1)S(1)} %get-tuple-element.31.refs_0_), channel_id=1, source_target_pairs={{0,2},{1,3},{2,0},{3,1},{4,6},{5,7},{6,4},{7,5},{8,10},{9,11},{10,... | collective-permute-start | bytes 49160 | tf_op jit(solution)/shard_map/ppermute | solution.py:410
  27.5 3.2 %collective-permute-start.10 = (bf16[8,1024]{1,0:T(8,128)(2,1)S(1)}, bf16[8,1024]{1,0:T(8,128)(2,1)S(1)}, u32[]{:S(2)}, u32[]{:S(2)}) collective-permute-start(bf16[8,1024]{1,0:T(8,128)(2,1)S(1)} %get-tuple-element.31.refs_0_), channel_id=1, source_target_pairs={{0,1},{1,0},{2,3},{3,2},{4,5},{5,4},{6,7},{7,6},{8,9},{9,8},{10,11... | collective-permute-start | bytes 49160 | tf_op jit(solution)/shard_map/ppermute | solution.py:410
